TPU v7x, 32 devices: a whole 2x2x4 slice. The times are simulated.
32 devices in a mesh: rep: 4 (over z), ep: 8 (over y, x, core).
Axes of the slice: x: 2, y: 2, z: 4, core: 2. Of those that a mesh axis runs over, the one named last changes fastest.
Arguments:
- tokens: bfloat16 [4096, 2048], P(('rep', 'ep')), may hold values from -6 to 6
- experts: int32 [4096, 10], P(('rep', 'ep')), may hold values from 0 to 31, all different within a row; in each aligned block of 128 rows (0 to 127, 128 to 255, ...) at most 64 rows name the same one
- gates: bfloat16 [4096, 10], P(('rep', 'ep')), may hold values from 0.099609375 to 0.5
- w_gate: bfloat16 [32, 2048, 512], P('ep'), may hold values from -0.125 to 0.125
- w_up: bfloat16 [32, 2048, 512], P('ep'), may hold values from -0.125 to 0.125
- w_down: bfloat16 [32, 2048, 512], P('ep'), may hold values from -0.25 to 0.25
Outputs:
- mixed: bfloat16 [4096, 2048], P(('rep', 'ep'))
Inputs may be any that keep to these rules, and one draw needn't show every extreme that they name: Each row names 10 different experts. Among the 128 tokens of one device (aligned blocks of rows), no expert is named more than 64 times; in some such blocks one expert is named exactly 64 times.
All inputs are finite; a program needn't handle non-finite values.
Results may differ from a plain program's by a relative error of at most 0.0057.
Values may be sent and summed in bfloat16 or wider, within the bound.
No kernel may reach another device: no remote copies, remote signals or barrier semaphores. Data moves between devices by JAX's collectives and lax.ppermute only.
A program may use at most 128 MiB of HBM per device.

v0:
```python
import jax
import jax.numpy as jnp
from jax import lax
from jax.sharding import PartitionSpec as P


def run_experts(rows, gate_w, up_w, down_w):
    gate_act = jnp.einsum("erd,edf->erf", rows, gate_w, preferred_element_type=jnp.float32)
    up_act = jnp.einsum("erd,edf->erf", rows, up_w, preferred_element_type=jnp.float32)
    hidden = (jax.nn.silu(gate_act) * up_act).astype(jnp.bfloat16)
    return jnp.einsum("erf,edf->erd", hidden, down_w, preferred_element_type=jnp.float32).astype(
        jnp.bfloat16
    )


def body(tokens, experts, gates, w_gate, w_up, w_down):
    n_ep = lax.axis_size("ep")
    tok_dev, width = tokens.shape
    topk = experts.shape[1]
    held = w_gate.shape[0]
    n_experts = held * n_ep
    capacity = 8 * tok_dev * topk // (5 * n_experts)
    slots = n_experts * capacity
    flat = experts.reshape(-1)
    onehot = (flat[:, None] == jnp.arange(n_experts, dtype=jnp.int32)[None, :]).astype(jnp.int32)
    position = jnp.sum(jnp.cumsum(onehot, axis=0) * onehot, axis=1) - 1
    target = (flat * capacity + position).reshape(tok_dev, topk)
    slot_ids = jnp.arange(slots, dtype=jnp.int32)
    matches = slot_ids[:, None, None] == target[None, :, :]
    spread = jnp.any(matches, axis=-1).astype(jnp.bfloat16)
    outgoing = jnp.dot(spread, tokens, preferred_element_type=jnp.float32).astype(jnp.bfloat16)
    by_owner = outgoing.reshape(n_ep, held, capacity, width)
    arrived = lax.all_to_all(by_owner, "ep", split_axis=0, concat_axis=2, tiled=True)
    results = run_experts(arrived[0], w_gate, w_up, w_down)
    returned = lax.all_to_all(results[None], "ep", split_axis=2, concat_axis=0, tiled=True)
    returned = returned.reshape(slots, width)
    weighting = jnp.sum(jnp.where(matches, gates.astype(jnp.float32)[None, :, :], 0.0), axis=-1)
    weighting = weighting.T.astype(jnp.bfloat16)
    mixed = jnp.dot(weighting, returned, preferred_element_type=jnp.float32)
    return mixed.astype(jnp.bfloat16)


def solution(mesh):
    in_specs = (
        P(("rep", "ep"), None),
        P(("rep", "ep"), None),
        P(("rep", "ep"), None),
        P("ep", None, None),
        P("ep", None, None),
        P("ep", None, None),
    )
    out_specs = P(("rep", "ep"), None)
    return jax.shard_map(body, mesh=mesh, in_specs=in_specs, out_specs=out_specs, check_vma=False)
```

profile of v0, /device:TPU:0, one launch (start us, length us, event | category | flops | bytes accessed | tf_op | source)
XLA Modules:
  0.0 288.2 jit_solution(10759536433399477573)
XLA Ops:
  0.0 0.9 copy.50
  0.9 0.1 eq.43
  1.0 0.1 eq.39
  1.2 9.1 %reduce-window.6 = s32[32,10,128]{2,1,0:T(8,128)S(1)} reduce-window(s32[32,10,128]{2,1,0:T(8,128)S(1)} %fusion.3, s32[]{:T(128)} %constant.7.clone.1), window={size=1x1x128 pad=0_0x0_0x127_0}, to_apply=%region_0.0 | reduce-window | flops 5201920 | bytes 327684 | tf_op jit(solution)/shard_map/reduce-window
  10.2 0.1 slice.8
  10.4 0.2 copy.52
  10.6 0.1 copy.53
  10.7 0.1 broadcast_add_fusion
  10.8 0.1 fusion.5
  10.9 0.1 sub.7
  11.1 0.7 multiply_add_fusion
  11.8 1.8 fusion
  13.7 2.3 convolution_convert_fusion
  16.0 99.1 %all_to_all.30 = bf16[8,4,64,2048]{3,2,1,0:T(8,128)(2,1)} all-to-all(bf16[8,4,64,2048]{3,2,1,0:T(8,128)(2,1)S(1)} %bitcast.36), channel_id=1, replica_groups=mesh['rep'=4,'ep'=8] {'ep'}, dimensions={0} | all-to-all | bytes 16777216 | tf_op jit(solution)/shard_map/all_to_all | solution.py:33
  115.1 8.3 %copy.55 = bf16[1,4,8,64,2048]{4,3,2,1,0:T(8,128)(2,1)} copy(bf16[1,4,8,64,2048]{4,3,1,2,0:T(8,128)(2,1)} %bitcast.37) | data formatting | bytes 16777216 | tf_op jit(solution)/shard_map/all_to_all | solution.py:33
  123.4 12.2 %fusion.7 = f32[4,512,512]{2,1,0:T(8,128)} fusion(bf16[4,512,2048]{2,1,0:T(8,128)(2,1)} %bitcast.39, bf16[4,2048,512]{2,1,0:T(8,128)(2,1)} %param.9), kind=kOutput, calls=%fused_computation.19 | convolution fusion | flops 4294967296 | bytes 20971520 | tf_op jit(solution)/shard_map/erd,edf->erf/dot_general | solution.py:8
  135.5 16.3 %convert_bitcast_fusion = bf16[1,4,512,2048]{3,2,1,0:T(8,128)(2,1)} fusion(bf16[4,2048,512]{2,1,0:T(8,128)(2,1)} %param.11, f32[4,512,512]{2,1,0:T(8,128)} %fusion.7, bf16[4,512,2048]{2,1,0:T(8,128)(2,1)} %bitcast.40, bf16[4,2048,512]{2,1,0:T(8,128)(2,1)} %param.10), kind=kOutput, calls=%fused_computation.3 | convolution fusion | flops 8600420352 | bytes 37748736 | tf_op jit(solution)/shard_map/erf,edf->erd/dot_general | solution.py:11
  151.9 12.1 %copy.56 = bf16[1,4,512,2048]{3,1,0,2:T(4,128)(2,1)} copy(bf16[1,4,512,2048]{3,2,1,0:T(8,128)(2,1)} %convert_bitcast_fusion) | data formatting | bytes 16777216 | tf_op jit(solution)/shard_map/broadcast_in_dim | solution.py:35
  164.0 5.3 %all-to-all-start.1 = ((bf16[1,4,512,2048]{3,1,0,2:T(4,128)(2,1)}), bf16[1,4,512,2048]{3,1,0,2:T(4,128)(2,1)}, u32[]{:S(2)}, u32[]{:S(2)}) async-start(bf16[1,4,512,2048]{3,1,0,2:T(4,128)(2,1)} %copy.56), calls=%async_computation.1 | async-start | bytes 16777216 | tf_op jit(solution)/shard_map/all_to_all | solution.py:35
  169.4 1.1 select_reduce_fusion
  170.5 92.7 %all-to-all-done.1 = bf16[1,4,512,2048]{3,1,0,2:T(4,128)(2,1)} async-done(((bf16[1,4,512,2048]{3,1,0,2:T(4,128)(2,1)}), bf16[1,4,512,2048]{3,1,0,2:T(4,128)(2,1)}, u32[]{:S(2)}, u32[]{:S(2)}) %all-to-all-start.1) | async-done | bytes 8388640 | tf_op jit(solution)/shard_map/all_to_all | solution.py:35
  263.2 11.2 %copy.57 = bf16[1,4,512,2048]{3,2,1,0:T(8,128)(2,1)} copy(bf16[1,4,512,2048]{3,1,0,2:T(4,128)(2,1)} %all-to-all-done.1) | data formatting | bytes 16777216 | tf_op jit(solution)/shard_map/all_to_all | solution.py:35
  274.4 8.3 %copy.58 = bf16[8,1,4,64,2048]{4,3,2,0,1:T(8,128)(2,1)} copy(bf16[8,1,4,64,2048]{4,3,0,2,1:T(8,128)(2,1)} %bitcast.38) | data formatting | bytes 16777216 | tf_op jit(solution)/shard_map/all_to_all | solution.py:35
  282.7 5.5 %convolution_convert_fusion.1 = bf16[128,2048]{1,0:T(8,128)(2,1)} fusion(bf16[2048,2048]{1,0:T(8,128)(2,1)} %bitcast.35, bf16[2048,128]{1,0:T(8,128)(2,1)S(1)} %select_reduce_fusion), kind=kOutput, calls=%fused_computation.6 | convolution fusion | flops 1074003968 | bytes 9437184 | tf_op jit(solution)/shard_map/dot_general | solution.py:39
  (11 shorter events, 0.1 us)
Async XLA Ops:
  0.0 13.7 %copy-start = (bf16[128,2048]{1,0:T(8,128)(2,1)S(1)}, bf16[128,2048]{1,0:T(8,128)(2,1)}, u32[]{:S(2)}) copy-start(bf16[128,2048]{1,0:T(8,128)(2,1)} %param.6) | copy-start | bytes 1572868
  164.0 5.3 %copy-start.2 = (bf16[128,10]{0,1:T(8,128)(2,1)S(1)}, bf16[128,10]{0,1:T(8,128)(2,1)}, u32[]{:S(2)}) copy-start(bf16[128,10]{0,1:T(8,128)(2,1)} %param.8) | copy-start | bytes 7684
  164.0 99.2 %all-to-all-start.1 = ((bf16[1,4,512,2048]{3,1,0,2:T(4,128)(2,1)}), bf16[1,4,512,2048]{3,1,0,2:T(4,128)(2,1)}, u32[]{:S(2)}, u32[]{:S(2)}) async-start(bf16[1,4,512,2048]{3,1,0,2:T(4,128)(2,1)} %copy.56), calls=%async_computation.1 | async-start | bytes 16777216 | tf_op jit(solution)/shard_map/all_to_all | solution.py:35
  282.7 5.5 %copy-start.1 = (bf16[128,2048]{1,0:T(8,128)(2,1)S(1)}, bf16[128,2048]{1,0:T(8,128)(2,1)}, u32[]{:S(2)}) copy-start(bf16[128,2048]{1,0:T(8,128)(2,1)} %param.6) | copy-start | bytes 1572868
where the time goes:
time: 289 us; the launch traced here: 288 us
  blocking collectives  99.1 us (34%)
  waiting for transfers between devices  92.7 us (32%)
  local copies, waits for them, and re-layouts  41.6 us (14%)
  matrix products  36.4 us (13%)
  other arithmetic  13 us (4%)
  starting transfers between devices  5.31 us (2%)
    all_to_all x1, blocking collectives, body(): lax.all_to_all(by_owner, 'ep', split_axis=0, concat_axis=2, tiled=True)  99.1 us
    all_to_all x1, waiting for transfers between devices, body(): lax.all_to_all(results[None], 'ep', split_axis=2, concat_axis=0, tiled=True)  92.7 us
    all_to_all x2, local copies, waits for them, and re-layouts, body(): lax.all_to_all(results[None], 'ep', split_axis=2, concat_axis=0, tiled=True)  19.5 us
    dot_general x1, matrix products, run_experts(): jnp.einsum('erf,edf->erd', hidden, down_w, preferred_element_type=jnp.flo...  16.3 us
    dot_general x1, matrix products, run_experts(): jnp.einsum('erd,edf->erf', rows, gate_w, preferred_element_type=jnp.float32)  12.2 us
    broadcast_in_dim x1, local copies, waits for them, and re-layouts, body(): results[None]  12.1 us
    another operation x3, other arithmetic  9.24 us
    all_to_all x1, local copies, waits for them, and re-layouts, body(): lax.all_to_all(by_owner, 'ep', split_axis=0, concat_axis=2, tiled=True)  8.27 us
  transfers between devices with their start and end apart: 1, of which 1 were waited for; matrix products, arithmetic and copies ran while one was open for 0% of the time, Pallas kernels for 0%

commit v1 on v0

v1 whole, which is shorter than its diff:
```python
import functools

import jax
import jax.numpy as jnp
from jax import lax
from jax.experimental import pallas as pl
from jax.experimental.pallas import tpu as pltpu
from jax.sharding import PartitionSpec as P

MIB = 2**20
LANES = 128
NT = (((1,), (1,)), ((), ()))
VMEM_SPEC = pl.BlockSpec(memory_space=pltpu.VMEM)
ANY_SPEC = pl.BlockSpec(memory_space=pl.ANY)


def flip(x, mask):
    n = lax.axis_size("ep")
    return lax.ppermute(x, "ep", [(i, i ^ mask) for i in range(n)])


def prepare_kernel(tokens, experts, gates, out, table, sems):
    width = tokens.shape[1]
    rows = pltpu.make_async_copy(tokens, out.at[:, pl.ds(0, width)], sems.at[0])
    rows.start()
    lanes, count = table.shape[1], table.shape[0]
    ids = lax.broadcasted_iota(jnp.int32, (lanes, count), 0)
    chosen = experts[...]
    weight = gates[...].astype(jnp.float32)
    total = jnp.zeros((lanes, count), jnp.float32)
    for k in range(chosen.shape[0]):
        total += jnp.where(ids == chosen[k : k + 1, :], weight[k : k + 1, :], 0.0)
    table[...] = total.T.astype(jnp.bfloat16)
    last = pltpu.make_async_copy(table, out.at[:, pl.ds(width, lanes)], sems.at[1])
    last.start()
    rows.wait()
    last.wait()


def prepare(tokens, experts, gates, lanes):
    count, width = tokens.shape
    return pl.pallas_call(
        prepare_kernel,
        in_specs=[ANY_SPEC, VMEM_SPEC, VMEM_SPEC],
        out_specs=ANY_SPEC,
        out_shape=jax.ShapeDtypeStruct((count, width + lanes), jnp.bfloat16),
        scratch_shapes=[pltpu.VMEM((count, lanes), jnp.bfloat16), pltpu.SemaphoreType.DMA((2,))],
        name="prepare",
    )(tokens, experts.T, gates.T)


def hidden_of(rows, gate_w, up_w, weight):
    gate_act = jnp.dot(rows, gate_w, preferred_element_type=jnp.float32)
    up_act = jnp.dot(rows, up_w, preferred_element_type=jnp.float32)
    return (gate_act / (1.0 + jnp.exp(-gate_act)) * up_act * weight).astype(jnp.bfloat16)


def gather_inputs(first, second, rows, held):
    count = first.shape[0]
    width = rows.shape[1]
    rows[:count] = first[:, :width]
    rows[count:] = second[:, :width]
    table = jnp.concatenate([first[:, width:], second[:, width:]], axis=0).astype(jnp.float32)
    lane = lax.broadcasted_iota(jnp.int32, table.shape, 1)
    base = lax.axis_index("ep") * held
    return [
        jnp.sum(jnp.where(lane == base + e, table, 0.0), axis=1, keepdims=True) for e in range(held)
    ]


def down_all(hidden, w_down, mine, other, tile=512):
    held, width, units = w_down.shape
    count = mine.shape[0]
    for start in range(0, width, tile):
        total = None
        for e in range(held):
            part = lax.dot_general(
                hidden[:, e * units : (e + 1) * units],
                w_down[e, start : start + tile, :],
                NT,
                preferred_element_type=jnp.float32,
            )
            total = part if total is None else total + part
        total = total.astype(jnp.bfloat16)
        mine[:, start : start + tile] = total[:count]
        other[:, start : start + tile] = total[count:]


def first_kernel(first, second, gate_hbm, up_hbm, down_hbm, mine, other, w_gate, w_up, w_down, rows, hidden, sems):
    held, _, units = w_gate.shape
    order = [(gate_hbm, w_gate, e, 0) for e in range(held)]
    order = [c for e in range(held) for c in ((gate_hbm, w_gate, e, 0), (up_hbm, w_up, e, 1))]
    order += [(down_hbm, w_down, e, 2) for e in range(held)]
    copies = {}
    for src, dst, e, which in order:
        copies[e, which] = pltpu.make_async_copy(src.at[e], dst.at[e], sems.at[which, e])
        copies[e, which].start()
    weights = gather_inputs(first, second, rows, held)
    for e in range(held):
        copies[e, 0].wait()
        copies[e, 1].wait()
        hidden[:, e * units : (e + 1) * units] = hidden_of(rows[...], w_gate[e], w_up[e], weights[e])
    for e in range(held):
        copies[e, 2].wait()
    down_all(hidden, w_down, mine, other)


def chunk_kernel(first, second, w_gate, w_up, w_down, mine, other, rows, hidden):
    held, _, units = w_gate.shape
    weights = gather_inputs(first, second, rows, held)
    for e in range(held):
        hidden[:, e * units : (e + 1) * units] = hidden_of(rows[...], w_gate[e], w_up[e], weights[e])
    down_all(hidden, w_down, mine, other)


def scratch_of(first, w_gate):
    count = first.shape[0]
    held, width, units = w_gate.shape
    return [pltpu.VMEM((2 * count, width), jnp.bfloat16), pltpu.VMEM((2 * count, held * units), jnp.bfloat16)]


def cost_of(first, w_gate):
    held, width, units = w_gate.shape
    flops = 2 * 2 * first.shape[0] * 3 * held * width * units
    return pl.CostEstimate(flops=flops, bytes_accessed=4 * first.size, transcendentals=0)


def first_chunk(first, second, w_gate, w_up, w_down):
    half = jax.ShapeDtypeStruct((first.shape[0], w_gate.shape[1]), jnp.bfloat16)
    kept = [pltpu.VMEM(w.shape, w.dtype) for w in (w_gate, w_up, w_down)]
    return pl.pallas_call(
        first_kernel,
        in_specs=[VMEM_SPEC] * 2 + [ANY_SPEC] * 3,
        out_specs=[VMEM_SPEC] * 5,
        out_shape=[half, half] + kept,
        scratch_shapes=scratch_of(first, w_gate) + [pltpu.SemaphoreType.DMA((3, w_gate.shape[0]))],
        compiler_params=pltpu.CompilerParams(vmem_limit_bytes=16 * MIB),
        cost_estimate=cost_of(first, w_gate),
        name="first_chunk",
    )(first, second, w_gate, w_up, w_down)


def chunk(first, second, weights):
    half = jax.ShapeDtypeStruct((first.shape[0], weights[0].shape[1]), jnp.bfloat16)
    return pl.pallas_call(
        chunk_kernel,
        in_specs=[VMEM_SPEC] * 5,
        out_specs=[VMEM_SPEC] * 2,
        out_shape=[half, half],
        scratch_shapes=scratch_of(first, weights[0]),
        compiler_params=pltpu.CompilerParams(vmem_limit_bytes=16 * MIB),
        cost_estimate=cost_of(first, weights[0]),
        name="chunk",
    )(first, second, *weights)


def body(tokens, experts, gates, w_gate, w_up, w_down):
    n_ep = lax.axis_size("ep")
    n_experts = w_gate.shape[0] * n_ep
    lanes = -(-n_experts // LANES) * LANES
    mixed_rows = prepare(tokens, experts, gates, lanes)
    arrived = {d: flip(mixed_rows, 2 * d) for d in range(1, n_ep // 2)}
    mine, other, *weights = first_chunk(mixed_rows, flip(mixed_rows, 1), w_gate, w_up, w_down)
    total = mine.astype(jnp.float32) + flip(other, 1).astype(jnp.float32)
    returned = []
    for d, rows in arrived.items():
        mine, other = chunk(rows, flip(rows, 1), weights)
        pair = mine.astype(jnp.float32) + flip(other, 1).astype(jnp.float32)
        returned.append(flip(pair.astype(jnp.bfloat16), 2 * d))
    for part in returned:
        total = total + part.astype(jnp.float32)
    return total.astype(jnp.bfloat16)


def solution(mesh):
    in_specs = (
        P(("rep", "ep"), None),
        P(("rep", "ep"), None),
        P(("rep", "ep"), None),
        P("ep", None, None),
        P("ep", None, None),
        P("ep", None, None),
    )
    out_specs = P(("rep", "ep"), None)
    return jax.shard_map(body, mesh=mesh, in_specs=in_specs, out_specs=out_specs, check_vma=False)
```

time: 289 us -> 113 us (0.39)
  blocking collectives: 99.1 us -> 0 us
  waiting for transfers between devices: 92.7 us -> 34.7 us
  Pallas kernels: 0 us -> 47.3 us
  matrix products: 36.4 us -> 0 us
  local copies, waits for them, and re-layouts: 41.6 us -> 17.7 us
  other arithmetic: 13 us -> 1.6 us
  starting transfers between devices: 5.31 us -> 11.1 us
    all_to_all x1 -> x0, blocking collectives: 99.1 us -> none  [body(): lax.all_to_all(by_owner, 'ep', split_axis=0, concat_axis=2, tiled=True)]
    all_to_all x1 -> x0, waiting for transfers between devices: 92.7 us -> none  [body(): lax.all_to_all(results[None], 'ep', split_axis=2, concat_axis=0, tiled=True)]
    pallas_call x0 -> x5, Pallas kernels: none -> 47.3 us  [the longest x3 20.4 us: chunk(): pl.pallas_call(chunk_kernel, in_specs=[VMEM_SPEC] * 5, out_specs=[VMEM_SP...]
    dot_general x4 -> x0, matrix products: 36.4 us -> none  [the longest x1 16.3 us: run_experts(): jnp.einsum('erf,edf->erd', hidden, down_w, preferred_element_type=jnp.flo...]
    ppermute x0 -> x14, waiting for transfers between devices: none -> 34.7 us  [flip(): return lax.ppermute(x, 'ep', [(i, i ^ mask) for i in range(n)])]
    all_to_all x3 -> x0, local copies, waits for them, and re-layouts: 27.8 us -> none  [the longest x2 19.5 us: body(): lax.all_to_all(results[None], 'ep', split_axis=2, concat_axis=0, tiled=True)]
    unnamed x7 -> x12, local copies, waits for them, and re-layouts: 0.87 us -> 17.7 us
    broadcast_in_dim x1 -> x0, local copies, waits for them, and re-layouts: 12.1 us -> none  [body(): results[None]]
  transfers between devices with their start and end apart: 1 -> 14, of which waited for: 1 -> 3; matrix products, arithmetic and copies ran while one was open for 0% -> 0% of each run, Pallas kernels for 0% -> 26%
where the time goes in v1:
time: 113 us; the launch traced here: 112 us
  Pallas kernels  47.3 us (42%)
  waiting for transfers between devices  34.7 us (31%)
  local copies, waits for them, and re-layouts  17.7 us (16%)
  starting transfers between devices  11.1 us (10%)
  other arithmetic  1.6 us (1%)
    ppermute x14, waiting for transfers between devices, flip(): return lax.ppermute(x, 'ep', [(i, i ^ mask) for i in range(n)])  34.7 us
    pallas_call x3, Pallas kernels, chunk(): pl.pallas_call(chunk_kernel, in_specs=[VMEM_SPEC] * 5, out_specs=[VMEM_SP...  20.4 us
    pallas_call x1, Pallas kernels, prepare(): pl.pallas_call(prepare_kernel, in_specs=[ANY_SPEC, VMEM_SPEC, VMEM_SPEC],...  17.7 us
    unnamed x12, local copies, waits for them, and re-layouts  17.7 us
    ppermute x14, starting transfers between devices, flip(): return lax.ppermute(x, 'ep', [(i, i ^ mask) for i in range(n)])  11.1 us
    pallas_call x1, Pallas kernels, first_chunk(): pl.pallas_call(first_kernel, in_specs=[VMEM_SPEC] * 2 + [ANY_SPEC] * 3, o...  9.22 us
  transfers between devices with their start and end apart: 14, of which 3 were waited for; matrix products, arithmetic and copies ran while one was open for 0% of the time, Pallas kernels for 26%

profile of v1, /device:TPU:0, one launch (start us, length us, event | category | flops | bytes accessed | tf_op | source)
XLA Modules:
  0.0 112.4 jit_solution(11278329328950564622)
XLA Ops:
  0.0 17.7 %prepare.1.first = bf16[128,2176]{1,0:T(8,128)(2,1)} custom-call(bf16[128,2048]{1,0:T(8,128)(2,1)} %tokens.1, s32[10,128]{1,0:T(8,128)} %bitcast.2, bf16[10,128]{1,0:T(8,128)(2,1)} %bitcast.3), custom_call_target="tpu_custom_call" | custom-call | tf_op jit(solution)/shard_map/prepare/pallas_call | solution.py:42
  17.7 3.0 %collective-permute-start.2 = (bf16[128,2176]{1,0:T(8,128)(2,1)}, bf16[128,2176]{1,0:T(8,128)(2,1)S(1)}, u32[]{:S(2)}, u32[]{:S(2)}) collective-permute-start(bf16[128,2176]{1,0:T(8,128)(2,1)} %prepare.1.first), channel_id=1, source_target_pairs={{0,2},{1,3},{2,0},{3,1},{4,6},{5,7},{6,4},{7,5},{8,10},{9,11},{10,... | collective-permute-start | bytes 1671176 | tf_op jit(solution)/shard_map/ppermute | solution.py:19
  20.7 1.5 %collective-permute-start.6 = (bf16[128,2176]{1,0:T(8,128)(2,1)}, bf16[128,2176]{1,0:T(8,128)(2,1)S(1)}, u32[]{:S(2)}, u32[]{:S(2)}) collective-permute-start(bf16[128,2176]{1,0:T(8,128)(2,1)} %prepare.1.first), channel_id=1, source_target_pairs={{0,4},{1,5},{2,6},{3,7},{4,0},{5,1},{6,2},{7,3},{8,12},{9,13},{10,... | collective-permute-start | bytes 1671176 | tf_op jit(solution)/shard_map/ppermute | solution.py:19
  22.4 12.0 %collective-permute-done.2.first = bf16[128,2176]{1,0:T(8,128)(2,1)S(1)} collective-permute-done((bf16[128,2176]{1,0:T(8,128)(2,1)}, bf16[128,2176]{1,0:T(8,128)(2,1)S(1)}, u32[]{:S(2)}, u32[]{:S(2)}) %collective-permute-start.2) | collective-permute-done | bytes 557088 | tf_op jit(solution)/shard_map/ppermute | solution.py:19
  34.4 3.4 %copy-done.4 = bf16[4,2048,512]{2,1,0:T(8,128)(2,1)S(1)} copy-done((bf16[4,2048,512]{2,1,0:T(8,128)(2,1)S(1)}, bf16[4,2048,512]{2,1,0:T(8,128)(2,1)}, u32[]{:S(2)}) %copy-start.4) | copy-done | bytes 8388632
  37.8 1.1 copy-done.5
  38.8 9.2 %first_chunk.1 = (bf16[128,2048]{1,0:T(8,128)(2,1)S(1)}, bf16[128,2048]{1,0:T(8,128)(2,1)S(1)}, bf16[4,2048,512]{2,1,0:T(8,128)(2,1)S(1)}, bf16[4,2048,512]{2,1,0:T(8,128)(2,1)S(1)}, bf16[4,2048,512]{2,1,0:T(8,128)(2,1)S(1)}) custom-call(bf16[128,2176]{1,0:T(8,128)(2,1)S(1)} %copy-done.5, bf16[128,2176]{1,0:T(8,128)(2,1)S(1)} %collective-permute-done.second, ...), custom_call_target="tpu_custom_call" | custom-call | flops 6442450944 | bytes 1114112 | tf_op jit(solution)/shard_map/first_chunk/pallas_call | solution.py:131
  48.1 3.2 %copy-done = bf16[4,2048,512]{2,1,0:T(8,128)(2,1)} copy-done((bf16[4,2048,512]{2,1,0:T(8,128)(2,1)}, bf16[4,2048,512]{2,1,0:T(8,128)(2,1)S(1)}, u32[]{:S(2)}) %copy-start) | copy-done | bytes 8388632
  51.3 3.2 %copy-done.2 = bf16[4,2048,512]{2,1,0:T(8,128)(2,1)} copy-done((bf16[4,2048,512]{2,1,0:T(8,128)(2,1)}, bf16[4,2048,512]{2,1,0:T(8,128)(2,1)S(1)}, u32[]{:S(2)}) %copy-start.2) | copy-done | bytes 8388632
  54.5 0.5 collective-permute-start.1
  55.0 0.5 collective-permute-start.11
  55.5 3.4 %copy-done.1 = bf16[4,2048,512]{2,1,0:T(8,128)(2,1)S(1)} copy-done((bf16[4,2048,512]{2,1,0:T(8,128)(2,1)S(1)}, bf16[4,2048,512]{2,1,0:T(8,128)(2,1)}, u32[]{:S(2)}) %copy-start.1) | copy-done | bytes 8388632
  58.9 3.4 %copy-done.3 = bf16[4,2048,512]{2,1,0:T(8,128)(2,1)S(1)} copy-done((bf16[4,2048,512]{2,1,0:T(8,128)(2,1)S(1)}, bf16[4,2048,512]{2,1,0:T(8,128)(2,1)}, u32[]{:S(2)}) %copy-start.3) | copy-done | bytes 8388632
  62.3 6.7 %chunk.3 = (bf16[128,2048]{1,0:T(8,128)(2,1)S(1)}, bf16[128,2048]{1,0:T(8,128)(2,1)S(1)}) custom-call(bf16[128,2176]{1,0:T(8,128)(2,1)S(1)} %collective-permute-done.2.first, bf16[128,2176]{1,0:T(8,128)(2,1)S(1)} %collective-permute-done.3.second, bf16[4,2048,512]{2,1,0:T(8,128)(2,1)S(1)} %get-tuple-element.18.w_gate, bf16[4,2048,512]{2,1,0:T(8,128)(2,1)S(1)} %copy-done.1, ...), custom_call_target="tpu_custom_call" | custom-call | flops 6442450944 | bytes 1114112 | tf_op jit(solution)/shard_map/chunk/pallas_call | solution.py:145
  69.2 6.9 %chunk.4 = (bf16[128,2048]{1,0:T(8,128)(2,1)S(1)}, bf16[128,2048]{1,0:T(8,128)(2,1)S(1)}) custom-call(bf16[128,2176]{1,0:T(8,128)(2,1)S(1)} %collective-permute-done.6.first, bf16[128,2176]{1,0:T(8,128)(2,1)S(1)} %collective-permute-done.7.second, bf16[4,2048,512]{2,1,0:T(8,128)(2,1)S(1)} %get-tuple-element.18.w_gate, bf16[4,2048,512]{2,1,0:T(8,128)(2,1)S(1)} %copy-done.1, ...), custom_call_target="tpu_custom_call" | custom-call | flops 6442450944 | bytes 1114112 | tf_op jit(solution)/shard_map/chunk/pallas_call | solution.py:145
  76.1 0.5 collective-permute-start.8
  76.6 6.7 %chunk.5 = (bf16[128,2048]{1,0:T(8,128)(2,1)S(1)}, bf16[128,2048]{1,0:T(8,128)(2,1)S(1)}) custom-call(bf16[128,2176]{1,0:T(8,128)(2,1)S(1)} %collective-permute-done.10.first, bf16[128,2176]{1,0:T(8,128)(2,1)S(1)} %collective-permute-done.11.second, bf16[4,2048,512]{2,1,0:T(8,128)(2,1)S(1)} %get-tuple-element.18.w_gate, bf16[4,2048,512]{2,1,0:T(8,128)(2,1)S(1)} %copy-done.1, ...), custom_call_target="tpu_custom_call" | custom-call | flops 6442450944 | bytes 1114112 | tf_op jit(solution)/shard_map/chunk/pallas_call | solution.py:145
  83.4 0.1 collective-permute-start.12
  83.7 2.1 %collective-permute-start.5 = (bf16[128,2048]{1,0:T(8,128)(2,1)S(1)}, bf16[128,2048]{1,0:T(8,128)(2,1)S(1)}, u32[]{:S(2)}, u32[]{:S(2)}) collective-permute-start(bf16[128,2048]{1,0:T(8,128)(2,1)S(1)} %add_convert_fusion.3), channel_id=1, source_target_pairs={{0,2},{1,3},{2,0},{3,1},{4,6},{5,7},{6,4},{7,5},{8,10},{9,11},{10,... | collective-permute-start | bytes 1572872 | tf_op jit(solution)/shard_map/ppermute | solution.py:19
  85.9 1.6 %collective-permute-start.9 = (bf16[128,2048]{1,0:T(8,128)(2,1)S(1)}, bf16[128,2048]{1,0:T(8,128)(2,1)S(1)}, u32[]{:S(2)}, u32[]{:S(2)}) collective-permute-start(bf16[128,2048]{1,0:T(8,128)(2,1)S(1)} %add_convert_fusion.2), channel_id=1, source_target_pairs={{0,4},{1,5},{2,6},{3,7},{4,0},{5,1},{6,2},{7,3},{8,12},{9,13},{10,... | collective-permute-start | bytes 1572872 | tf_op jit(solution)/shard_map/ppermute | solution.py:19
  87.6 0.9 collective-permute-start.13
  88.6 10.0 %collective-permute-done.5 = bf16[128,2048]{1,0:T(8,128)(2,1)S(1)} collective-permute-done((bf16[128,2048]{1,0:T(8,128)(2,1)S(1)}, bf16[128,2048]{1,0:T(8,128)(2,1)S(1)}, u32[]{:S(2)}, u32[]{:S(2)}) %collective-permute-start.5) | collective-permute-done | bytes 524320 | tf_op jit(solution)/shard_map/ppermute | solution.py:19
  98.6 12.6 %collective-permute-done.9 = bf16[128,2048]{1,0:T(8,128)(2,1)S(1)} collective-permute-done((bf16[128,2048]{1,0:T(8,128)(2,1)S(1)}, bf16[128,2048]{1,0:T(8,128)(2,1)S(1)}, u32[]{:S(2)}, u32[]{:S(2)}) %collective-permute-start.9) | collective-permute-done | bytes 524320 | tf_op jit(solution)/shard_map/ppermute | solution.py:19
  111.2 1.2 %add_convert_fusion = bf16[128,2048]{1,0:T(8,128)(2,1)} fusion(bf16[128,2048]{1,0:T(8,128)(2,1)S(1)} %collective-permute-done.13, bf16[128,2048]{1,0:T(8,128)(2,1)S(1)} %collective-permute-done.9, bf16[128,2048]{1,0:T(8,128)(2,1)S(1)} %collective-permute-done.5, bf16[128,2048]{1,0:T(8,128)(2,1)S(1)} %collective-permute-done.1, ...), kind=kLoop, calls=%fused_computation | loop fusion | flops 2621440 | bytes 3145728 | tf_op jit(solution)/shard_map/convert_element_type | solution.py:172
  (25 shorter events, 0.7 us)
Async XLA Ops:
  17.7 16.7 %collective-permute-start.2 = (bf16[128,2176]{1,0:T(8,128)(2,1)}, bf16[128,2176]{1,0:T(8,128)(2,1)S(1)}, u32[]{:S(2)}, u32[]{:S(2)}) collective-permute-start(bf16[128,2176]{1,0:T(8,128)(2,1)} %prepare.1.first), channel_id=1, source_target_pairs={{0,2},{1,3},{2,0},{3,1},{4,6},{5,7},{6,4},{7,5},{8,10},{9,11},{10,... | collective-permute-start | bytes 1671176 | tf_op jit(solution)/shard_map/ppermute | solution.py:19
  20.7 13.7 %collective-permute-start = (bf16[128,2176]{1,0:T(8,128)(2,1)}, bf16[128,2176]{1,0:T(8,128)(2,1)S(1)}, u32[]{:S(2)}, u32[]{:S(2)}) collective-permute-start(bf16[128,2176]{1,0:T(8,128)(2,1)} %prepare.1.first), channel_id=1, source_target_pairs={{0,1},{1,0},{2,3},{3,2},{4,5},{5,4},{6,7},{7,6},{8,9},{9,8},{10,11... | collective-permute-start | bytes 1671176 | tf_op jit(solution)/shard_map/ppermute | solution.py:19
  20.7 34.3 %collective-permute-start.6 = (bf16[128,2176]{1,0:T(8,128)(2,1)}, bf16[128,2176]{1,0:T(8,128)(2,1)S(1)}, u32[]{:S(2)}, u32[]{:S(2)}) collective-permute-start(bf16[128,2176]{1,0:T(8,128)(2,1)} %prepare.1.first), channel_id=1, source_target_pairs={{0,4},{1,5},{2,6},{3,7},{4,0},{5,1},{6,2},{7,3},{8,12},{9,13},{10,... | collective-permute-start | bytes 1671176 | tf_op jit(solution)/shard_map/ppermute | solution.py:19
  22.2 32.8 %collective-permute-start.10 = (bf16[128,2176]{1,0:T(8,128)(2,1)}, bf16[128,2176]{1,0:T(8,128)(2,1)S(1)}, u32[]{:S(2)}, u32[]{:S(2)}) collective-permute-start(bf16[128,2176]{1,0:T(8,128)(2,1)} %prepare.1.first), channel_id=1, source_target_pairs={{0,6},{1,7},{2,4},{3,5},{4,2},{5,3},{6,0},{7,1},{8,14},{9,15},{10,... | collective-permute-start | bytes 1671176 | tf_op jit(solution)/shard_map/ppermute | solution.py:19
  34.4 21.2 %collective-permute-start.3 = (bf16[128,2176]{1,0:T(8,128)(2,1)S(1)}, bf16[128,2176]{1,0:T(8,128)(2,1)S(1)}, u32[]{:S(2)}, u32[]{:S(2)}) collective-permute-start(bf16[128,2176]{1,0:T(8,128)(2,1)S(1)} %collective-permute-done.2.first), channel_id=1, source_target_pairs={{0,1},{1,0},{2,3},{3,2},{4,5},{5,4},{6,7},{7,6},{8,9},{9,8},{10,11... | collective-permute-start | bytes 1671176 | tf_op jit(solution)/shard_map/ppermute | solution.py:19
  34.4 3.4 %copy-start.4 = (bf16[4,2048,512]{2,1,0:T(8,128)(2,1)S(1)}, bf16[4,2048,512]{2,1,0:T(8,128)(2,1)}, u32[]{:S(2)}) copy-start(bf16[4,2048,512]{2,1,0:T(8,128)(2,1)} %gate_hbm.1) | copy-start | bytes 25165828
  37.8 1.1 copy-start.5
  48.0 3.3 %copy-start = (bf16[4,2048,512]{2,1,0:T(8,128)(2,1)}, bf16[4,2048,512]{2,1,0:T(8,128)(2,1)S(1)}, u32[]{:S(2)}) copy-start(bf16[4,2048,512]{2,1,0:T(8,128)(2,1)S(1)} %get-tuple-element.19.w_up) | copy-start | bytes 25165828
  51.3 3.2 %copy-start.2 = (bf16[4,2048,512]{2,1,0:T(8,128)(2,1)}, bf16[4,2048,512]{2,1,0:T(8,128)(2,1)S(1)}, u32[]{:S(2)}) copy-start(bf16[4,2048,512]{2,1,0:T(8,128)(2,1)S(1)} %get-tuple-element.20.w_down) | copy-start | bytes 25165828
  54.5 34.1 %collective-permute-start.1 = (bf16[128,2048]{1,0:T(8,128)(2,1)S(1)}, bf16[128,2048]{1,0:T(8,128)(2,1)S(1)}, u32[]{:S(2)}, u32[]{:S(2)}) collective-permute-start(bf16[128,2048]{1,0:T(8,128)(2,1)S(1)} %get-tuple-element.17), channel_id=1, source_target_pairs={{0,1},{1,0},{2,3},{3,2},{4,5},{5,4},{6,7},{7,6},{8,9},{9,8},{10,11... | collective-permute-start | bytes 1572872 | tf_op jit(solution)/shard_map/ppermute | solution.py:19
  55.0 14.2 %collective-permute-start.7 = (bf16[128,2176]{1,0:T(8,128)(2,1)S(1)}, bf16[128,2176]{1,0:T(8,128)(2,1)S(1)}, u32[]{:S(2)}, u32[]{:S(2)}) collective-permute-start(bf16[128,2176]{1,0:T(8,128)(2,1)S(1)} %collective-permute-done.6.first), channel_id=1, source_target_pairs={{0,1},{1,0},{2,3},{3,2},{4,5},{5,4},{6,7},{7,6},{8,9},{9,8},{10,11... | collective-permute-start | bytes 1671176 | tf_op jit(solution)/shard_map/ppermute | solution.py:19
  55.0 21.6 %collective-permute-start.11 = (bf16[128,2176]{1,0:T(8,128)(2,1)S(1)}, bf16[128,2176]{1,0:T(8,128)(2,1)S(1)}, u32[]{:S(2)}, u32[]{:S(2)}) collective-permute-start(bf16[128,2176]{1,0:T(8,128)(2,1)S(1)} %collective-permute-done.10.first), channel_id=1, source_target_pairs={{0,1},{1,0},{2,3},{3,2},{4,5},{5,4},{6,7},{7,6},{8,9},{9,8},{10,11... | collective-permute-start | bytes 1671176 | tf_op jit(solution)/shard_map/ppermute | solution.py:19
  55.5 3.4 %copy-start.1 = (bf16[4,2048,512]{2,1,0:T(8,128)(2,1)S(1)}, bf16[4,2048,512]{2,1,0:T(8,128)(2,1)}, u32[]{:S(2)}) copy-start(bf16[4,2048,512]{2,1,0:T(8,128)(2,1)} %copy-done) | copy-start | bytes 25165828
  58.9 3.4 %copy-start.3 = (bf16[4,2048,512]{2,1,0:T(8,128)(2,1)S(1)}, bf16[4,2048,512]{2,1,0:T(8,128)(2,1)}, u32[]{:S(2)}) copy-start(bf16[4,2048,512]{2,1,0:T(8,128)(2,1)} %copy-done.2) | copy-start | bytes 25165828
  69.1 14.5 %collective-permute-start.4 = (bf16[128,2048]{1,0:T(8,128)(2,1)S(1)}, bf16[128,2048]{1,0:T(8,128)(2,1)S(1)}, u32[]{:S(2)}, u32[]{:S(2)}) collective-permute-start(bf16[128,2048]{1,0:T(8,128)(2,1)S(1)} %get-tuple-element.22), channel_id=1, source_target_pairs={{0,1},{1,0},{2,3},{3,2},{4,5},{5,4},{6,7},{7,6},{8,9},{9,8},{10,11... | collective-permute-start | bytes 1572872 | tf_op jit(solution)/shard_map/ppermute | solution.py:19
  76.1 9.7 %collective-permute-start.8 = (bf16[128,2048]{1,0:T(8,128)(2,1)S(1)}, bf16[128,2048]{1,0:T(8,128)(2,1)S(1)}, u32[]{:S(2)}, u32[]{:S(2)}) collective-permute-start(bf16[128,2048]{1,0:T(8,128)(2,1)S(1)} %get-tuple-element.24), channel_id=1, source_target_pairs={{0,1},{1,0},{2,3},{3,2},{4,5},{5,4},{6,7},{7,6},{8,9},{9,8},{10,11... | collective-permute-start | bytes 1572872 | tf_op jit(solution)/shard_map/ppermute | solution.py:19
  83.4 4.1 %collective-permute-start.12 = (bf16[128,2048]{1,0:T(8,128)(2,1)S(1)}, bf16[128,2048]{1,0:T(8,128)(2,1)S(1)}, u32[]{:S(2)}, u32[]{:S(2)}) collective-permute-start(bf16[128,2048]{1,0:T(8,128)(2,1)S(1)} %get-tuple-element.26), channel_id=1, source_target_pairs={{0,1},{1,0},{2,3},{3,2},{4,5},{5,4},{6,7},{7,6},{8,9},{9,8},{10,11... | collective-permute-start | bytes 1572872 | tf_op jit(solution)/shard_map/ppermute | solution.py:19
  83.7 14.9 %collective-permute-start.5 = (bf16[128,2048]{1,0:T(8,128)(2,1)S(1)}, bf16[128,2048]{1,0:T(8,128)(2,1)S(1)}, u32[]{:S(2)}, u32[]{:S(2)}) collective-permute-start(bf16[128,2048]{1,0:T(8,128)(2,1)S(1)} %add_convert_fusion.3), channel_id=1, source_target_pairs={{0,2},{1,3},{2,0},{3,1},{4,6},{5,7},{6,4},{7,5},{8,10},{9,11},{10,... | collective-permute-start | bytes 1572872 | tf_op jit(solution)/shard_map/ppermute | solution.py:19
  85.9 25.3 %collective-permute-start.9 = (bf16[128,2048]{1,0:T(8,128)(2,1)S(1)}, bf16[128,2048]{1,0:T(8,128)(2,1)S(1)}, u32[]{:S(2)}, u32[]{:S(2)}) collective-permute-start(bf16[128,2048]{1,0:T(8,128)(2,1)S(1)} %add_convert_fusion.2), channel_id=1, source_target_pairs={{0,4},{1,5},{2,6},{3,7},{4,0},{5,1},{6,2},{7,3},{8,12},{9,13},{10,... | collective-permute-start | bytes 1572872 | tf_op jit(solution)/shard_map/ppermute | solution.py:19
  87.6 23.6 %collective-permute-start.13 = (bf16[128,2048]{1,0:T(8,128)(2,1)S(1)}, bf16[128,2048]{1,0:T(8,128)(2,1)S(1)}, u32[]{:S(2)}, u32[]{:S(2)}) collective-permute-start(bf16[128,2048]{1,0:T(8,128)(2,1)S(1)} %add_convert_fusion.1), channel_id=1, source_target_pairs={{0,6},{1,7},{2,4},{3,5},{4,2},{5,3},{6,0},{7,1},{8,14},{9,15},{10,... | collective-permute-start | bytes 1572872 | tf_op jit(solution)/shard_map/ppermute | solution.py:19

commit v2 on v1

v2 whole, which is shorter than its diff:
```python
import functools

import jax
import jax.numpy as jnp
from jax import lax
from jax.experimental import pallas as pl
from jax.experimental.pallas import tpu as pltpu
from jax.sharding import PartitionSpec as P

MIB = 2**20
LANES = 128
NT = (((1,), (1,)), ((), ()))
VMEM_SPEC = pl.BlockSpec(memory_space=pltpu.VMEM)
HBM_SPEC = pl.BlockSpec(memory_space=pltpu.HBM)
CORE = 1


def flip(x, mask):
    n = lax.axis_size("ep")
    return lax.ppermute(x, "ep", [(i, i ^ mask) for i in range(n)])


def after(x, *others):
    return lax.optimization_barrier((x, *others))[0]


def in_vmem(*arrays):
    return [pltpu.with_memory_space_constraint(a, pltpu.VMEM) for a in arrays]


def in_hbm(*arrays):
    return [pltpu.with_memory_space_constraint(a, pltpu.HBM) for a in arrays]


def params(limit=16):
    return pltpu.CompilerParams(vmem_limit_bytes=limit * MIB)


def prepare_kernel(tokens, experts, gates, whole, low, high, chosen, weight, sems):
    count, width = tokens.shape
    half = count // 2
    lanes = whole.shape[1] - width
    copies = [
        pltpu.make_async_copy(experts, chosen, sems.at[0]),
        pltpu.make_async_copy(gates, weight, sems.at[1]),
        pltpu.make_async_copy(tokens.at[pl.ds(0, half)], low.at[:, pl.ds(0, width)], sems.at[2]),
        pltpu.make_async_copy(tokens.at[pl.ds(half, half)], high.at[:, pl.ds(0, width)], sems.at[3]),
        pltpu.make_async_copy(tokens, whole.at[:, pl.ds(0, width)], sems.at[4]),
    ]
    for copy in copies:
        copy.start()
    copies[0].wait()
    copies[1].wait()
    ids = lax.broadcasted_iota(jnp.int32, (lanes, count), 0)
    total = jnp.zeros((lanes, count), jnp.float32)
    for k in range(chosen.shape[0]):
        gate = weight[k : k + 1, :].astype(jnp.float32)
        total += jnp.where(ids == chosen[k : k + 1, :], gate, 0.0)
    table = total.T.astype(jnp.bfloat16)
    whole[:, width:] = table
    low[:, width:] = table[:half]
    high[:, width:] = table[half:]
    for copy in copies[2:]:
        copy.wait()


def prepare(tokens, experts, gates, lanes):
    count, width = tokens.shape
    rows = [(count, width + lanes), (count // 2, width + lanes), (count // 2, width + lanes)]
    return pl.pallas_call(
        prepare_kernel,
        in_specs=[HBM_SPEC] * 3,
        out_specs=[VMEM_SPEC] * 3,
        out_shape=[pltpu.VMEM(shape, jnp.bfloat16) for shape in rows],
        scratch_shapes=[
            pltpu.VMEM(experts.shape[::-1], jnp.int32),
            pltpu.VMEM(gates.shape[::-1], jnp.bfloat16),
            pltpu.SemaphoreType.DMA((5,)),
        ],
        compiler_params=params(4),
        name="prepare",
    )(*in_hbm(tokens, experts.T, gates.T))


def gather_inputs(parts, rows, held):
    width = rows.shape[1]
    tables, start = [], 0
    for part in parts:
        rows[start : start + part.shape[0]] = part[:, :width]
        tables.append(part[:, width:])
        start += part.shape[0]
    table = jnp.concatenate(tables, axis=0).astype(jnp.float32)
    lane = lax.broadcasted_iota(jnp.int32, table.shape, 1)
    base = lax.axis_index("ep") * held
    return [
        jnp.sum(jnp.where(lane == base + e, table, 0.0), axis=1, keepdims=True) for e in range(held)
    ]


def hidden_of(rows, gate_w, up_w, weight):
    gate_act = jnp.dot(rows, gate_w, preferred_element_type=jnp.float32)
    up_act = jnp.dot(rows, up_w, preferred_element_type=jnp.float32)
    return (gate_act / (1.0 + jnp.exp(-gate_act)) * up_act * weight).astype(jnp.bfloat16)


def down_all(hidden, w_down, mine, other, tile=512):
    held, width, units = w_down.shape
    count = mine.shape[0]
    for start in range(0, width, tile):
        total = None
        for e in range(held):
            part = lax.dot_general(
                hidden[:, e * units : (e + 1) * units],
                w_down[e, start : start + tile, :],
                NT,
                preferred_element_type=jnp.float32,
            )
            total = part if total is None else total + part
        total = total.astype(jnp.bfloat16)
        mine[:, start : start + tile] = total[:count]
        other[:, start : start + tile] = total[count:]


def load_kernel(own, twin, gate_hbm, up_hbm, w_gate, w_up, hidden, rows, sems):
    held, _, units = w_gate.shape
    copies = []
    for e in range(held):
        for which, (src, dst) in enumerate(((gate_hbm, w_gate), (up_hbm, w_up))):
            copies.append(pltpu.make_async_copy(src.at[e], dst.at[e], sems.at[which, e]))
            copies[-1].start()
    weights = gather_inputs([own, twin], rows, held)
    for e in range(held):
        copies[2 * e].wait()
        copies[2 * e + 1].wait()
        hidden[:, e * units : (e + 1) * units] = hidden_of(rows[...], w_gate[e], w_up[e], weights[e])


def load(own, twin, w_gate, w_up):
    count = 2 * own.shape[0]
    held, width, units = w_gate.shape
    return pl.pallas_call(
        load_kernel,
        in_specs=[VMEM_SPEC] * 2 + [HBM_SPEC] * 2,
        out_specs=[VMEM_SPEC] * 3,
        out_shape=[pltpu.VMEM(w_gate.shape, w_gate.dtype)] * 2 + [pltpu.VMEM((count, held * units), jnp.bfloat16)],
        scratch_shapes=[pltpu.VMEM((count, width), jnp.bfloat16), pltpu.SemaphoreType.DMA((2, held))],
        compiler_params=params(),
        name="load",
    )(own, twin, *in_hbm(w_gate, w_up))


def first_kernel(*refs, parts):
    inputs, (w_gate, w_up, down_hbm, mine, other, w_down, rows, hidden, sem) = refs[:parts], refs[parts:]
    copy = pltpu.make_async_copy(down_hbm, w_down, sem)
    copy.start()
    held, _, units = w_gate.shape
    weights = gather_inputs(inputs, rows, held)
    for e in range(held):
        hidden[:, e * units : (e + 1) * units] = hidden_of(rows[...], w_gate[e], w_up[e], weights[e])
    copy.wait()
    down_all(hidden, w_down, mine, other)


def chunk_kernel(*refs, parts):
    inputs, (w_gate, w_up, w_down, mine, other, rows, hidden) = refs[:parts], refs[parts:]
    held, _, units = w_gate.shape
    weights = gather_inputs(inputs, rows, held)
    for e in range(held):
        hidden[:, e * units : (e + 1) * units] = hidden_of(rows[...], w_gate[e], w_up[e], weights[e])
    down_all(hidden, w_down, mine, other)


def shapes_of(parts, w_gate):
    count = sum(part.shape[0] for part in parts)
    held, width, units = w_gate.shape
    halves = [pltpu.VMEM((count // 2, width), jnp.bfloat16)] * 2
    scratch = [pltpu.VMEM((count, width), jnp.bfloat16), pltpu.VMEM((count, held * units), jnp.bfloat16)]
    return halves, scratch


def first_chunk(parts, w_gate, w_up, w_down):
    halves, scratch = shapes_of(parts, w_gate)
    return pl.pallas_call(
        functools.partial(first_kernel, parts=len(parts)),
        in_specs=[VMEM_SPEC] * (len(parts) + 2) + [HBM_SPEC],
        out_specs=[VMEM_SPEC] * 3,
        out_shape=halves + [pltpu.VMEM(w_down.shape, w_down.dtype)],
        scratch_shapes=scratch + [pltpu.SemaphoreType.DMA],
        compiler_params=params(),
        name="first_chunk",
    )(*in_vmem(*parts, w_gate, w_up), *in_hbm(w_down))


def chunk(parts, w_gate, w_up, w_down):
    halves, scratch = shapes_of(parts, w_gate)
    return pl.pallas_call(
        functools.partial(chunk_kernel, parts=len(parts)),
        in_specs=[VMEM_SPEC] * (len(parts) + 3),
        out_specs=[VMEM_SPEC] * 2,
        out_shape=halves,
        scratch_shapes=scratch,
        compiler_params=params(),
        name="chunk",
    )(*in_vmem(*parts, w_gate, w_up, w_down))


def finish_own(hidden, w_down):
    half = pltpu.VMEM((hidden.shape[0] // 2, w_down.shape[1]), jnp.bfloat16)
    return pl.pallas_call(
        down_all,
        in_specs=[VMEM_SPEC] * 2,
        out_specs=[VMEM_SPEC] * 2,
        out_shape=[half, half],
        compiler_params=params(),
        name="finish_own",
    )(*in_vmem(hidden, w_down))


def add_kernel(*refs):
    *inputs, low, high = refs
    half = low.shape[0]
    for out, block in ((low, slice(0, half)), (high, slice(half, 2 * half))):
        total = inputs[0][block].astype(jnp.float32)
        for part in inputs[1:]:
            total += part[block].astype(jnp.float32)
        out[...] = total.astype(out.dtype)


def add_halves(first, second):
    half = pltpu.VMEM((first.shape[0] // 2, first.shape[1]), first.dtype)
    return pl.pallas_call(
        add_kernel,
        in_specs=[VMEM_SPEC] * 2,
        out_specs=[VMEM_SPEC] * 2,
        out_shape=[half, half],
        compiler_params=params(8),
        name="add_halves",
    )(*in_vmem(first, second))


def add_relay_kernel(first, second, low_relay, high_relay, low, high):
    half = low.shape[0]
    for out, relay, block in ((low, low_relay, slice(0, half)), (high, high_relay, slice(half, 2 * half))):
        total = first[block].astype(jnp.float32) + second[block].astype(jnp.float32)
        out[...] = (total + relay[...].astype(jnp.float32)).astype(out.dtype)


def add_relay(first, second, low_relay, high_relay):
    half = pltpu.VMEM(low_relay.shape, first.dtype)
    return pl.pallas_call(
        add_relay_kernel,
        in_specs=[VMEM_SPEC] * 4,
        out_specs=[VMEM_SPEC] * 2,
        out_shape=[half, half],
        compiler_params=params(8),
        name="add_relay",
    )(*in_vmem(first, second, low_relay, high_relay))


def finish_kernel(mine, twin, low_parts, high_parts, out):
    half = low_parts[0].shape[0]
    for parts, block in ((low_parts, slice(0, half)), (high_parts, slice(half, 2 * half))):
        total = mine[block].astype(jnp.float32) + twin[block].astype(jnp.float32)
        for part in parts:
            total += part[...].astype(jnp.float32)
        out[block] = total.astype(out.dtype)


def finish(mine, twin, low_parts, high_parts):
    parts = [*low_parts, *high_parts]

    def kernel(mine, twin, *refs):
        finish_kernel(mine, twin, refs[: len(low_parts)], refs[len(low_parts) : -1], refs[-1])

    return pl.pallas_call(
        kernel,
        in_specs=[VMEM_SPEC] * (2 + len(parts)),
        out_specs=VMEM_SPEC,
        out_shape=jax.ShapeDtypeStruct(mine.shape, mine.dtype),
        compiler_params=params(8),
        name="finish",
    )(*in_vmem(mine, twin, *parts))


def on_four_chips(whole, low, high, w_gate, w_up, w_down):
    x, y = 2, 4
    near_x, near_y = flip(low, x), flip(high, y)
    w_gate, w_up, hidden = load(whole, flip(whole, CORE), w_gate, w_up)
    near_x, near_y, hidden = lax.optimization_barrier((near_x, near_y, hidden))
    far_low, far_high = flip(near_x, y), flip(near_y, x)
    parts = [near_x, near_y, flip(near_x, CORE), flip(near_y, CORE)]
    low, high = lax.optimization_barrier((low, high, near_x, near_y))[:2]
    next_x, next_y = flip(high, x), flip(low, y)
    mine_near, other_near, w_down = first_chunk(parts, w_gate, w_up, w_down)
    weights = (w_gate, w_up, w_down)
    far_low, far_high, hidden, _ = lax.optimization_barrier((far_low, far_high, hidden, mine_near))
    parts = [far_low, far_high, flip(far_low, CORE), flip(far_high, CORE)]
    mine_own, other_own = finish_own(hidden, w_down)
    twin_own = flip(other_own, CORE)
    sum_x, sum_y = add_halves(mine_near, flip(other_near, CORE))
    back_x, back_y = flip(sum_x, x), flip(sum_y, y)
    mine_far, other_far = chunk([after(parts[0], mine_own), *parts[1:]], *weights)
    next_x, next_y, _ = lax.optimization_barrier((next_x, next_y, mine_far))
    relay_low, relay_high = add_halves(mine_far, flip(other_far, CORE))
    relay_low, relay_high = flip(relay_low, x), flip(relay_high, y)
    mine_next, other_next = chunk([next_x, next_y, flip(next_x, CORE), flip(next_y, CORE)], *weights)
    sum_x, sum_y = add_relay(mine_next, flip(other_next, CORE), relay_high, relay_low)
    last_x, last_y = flip(sum_x, x), flip(sum_y, y)
    return finish(mine_own, twin_own, [back_x, last_y], [back_y, last_x])


def on_any_chips(whole, low, high, w_gate, w_up, w_down):
    offsets = range(2, lax.axis_size("ep"), 2)
    arrived = [flip(whole, d) for d in offsets]
    w_gate, w_up, hidden = load(whole, flip(whole, CORE), w_gate, w_up)
    low_parts, high_parts = [], []
    weights = None
    for d, rows in zip(offsets, arrived):
        parts = [rows, flip(rows, CORE)]
        if weights is None:
            mine, other, w_down = first_chunk(parts, w_gate, w_up, w_down)
            weights = (w_gate, w_up, w_down)
        else:
            mine, other = chunk(parts, *weights)
        low, high = add_halves(mine, flip(other, CORE))
        low_parts.append(flip(low, d))
        high_parts.append(flip(high, d))
    mine, other = finish_own(hidden, w_down)
    return finish(mine, flip(other, CORE), low_parts, high_parts)


def body(tokens, experts, gates, w_gate, w_up, w_down):
    n_ep = lax.axis_size("ep")
    n_experts = w_gate.shape[0] * n_ep
    lanes = -(-n_experts // LANES) * LANES
    whole, low, high = prepare(tokens, experts, gates, lanes)
    run = on_four_chips if n_ep == 8 else on_any_chips
    return run(whole, low, high, w_gate, w_up, w_down)


def solution(mesh):
    in_specs = (
        P(("rep", "ep"), None),
        P(("rep", "ep"), None),
        P(("rep", "ep"), None),
        P("ep", None, None),
        P("ep", None, None),
        P("ep", None, None),
    )
    out_specs = P(("rep", "ep"), None)
    return jax.shard_map(body, mesh=mesh, in_specs=in_specs, out_specs=out_specs, check_vma=False)
```

time: 113 us -> 67.1 us (0.59)
  waiting for transfers between devices: 34.7 us -> 16.5 us
  local copies, waits for them, and re-layouts: 17.7 us -> 0 us
  Pallas kernels: 47.3 us -> 33 us
  starting transfers between devices: 11.1 us -> 17.2 us
  other arithmetic: 1.6 us -> 0 us
    ppermute x14 -> x23, waiting for transfers between devices: 34.7 us -> 16.5 us  [flip(): return lax.ppermute(x, 'ep', [(i, i ^ mask) for i in range(n)])]
    unnamed x12 -> x0, local copies, waits for them, and re-layouts: 17.7 us -> none
    pallas_call x5 -> x10, Pallas kernels: 47.3 us -> 33 us  [the longest x2 13.7 us: chunk(): pl.pallas_call(functools.partial(chunk_kernel, parts=len(parts)), in_spec...]
    ppermute x14 -> x23, starting transfers between devices: 11.1 us -> 17.2 us  [flip(): return lax.ppermute(x, 'ep', [(i, i ^ mask) for i in range(n)])]
    convert_element_type x4 -> x0, other arithmetic: 1.6 us -> none  [the longest x1 1.22 us: body(): return total.astype(jnp.bfloat16)]
  transfers between devices with their start and end apart: 14 -> 23, of which waited for: 3 -> 8; matrix products, arithmetic and copies ran while one was open for 0% -> 0% of each run, Pallas kernels for 26% -> 46%
where the time goes in v2:
time: 67.1 us; the launch traced here: 66.9 us
  Pallas kernels  33 us (49%)
  starting transfers between devices  17.2 us (26%)
  waiting for transfers between devices  16.5 us (25%)
    ppermute x23, starting transfers between devices, flip(): return lax.ppermute(x, 'ep', [(i, i ^ mask) for i in range(n)])  17.2 us
    ppermute x23, waiting for transfers between devices, flip(): return lax.ppermute(x, 'ep', [(i, i ^ mask) for i in range(n)])  16.5 us
    pallas_call x2, Pallas kernels, chunk(): pl.pallas_call(functools.partial(chunk_kernel, parts=len(parts)), in_spec...  13.7 us
    pallas_call x1, Pallas kernels, load(): pl.pallas_call(load_kernel, in_specs=[VMEM_SPEC] * 2 + [HBM_SPEC] * 2, ou...  7.32 us
    pallas_call x1, Pallas kernels, first_chunk(): pl.pallas_call(functools.partial(first_kernel, parts=len(parts)), in_spec...  6.92 us
    pallas_call x1, Pallas kernels, finish_own(): pl.pallas_call(down_all, in_specs=[VMEM_SPEC] * 2, out_specs=[VMEM_SPEC]...  2.36 us
  transfers between devices with their start and end apart: 23, of which 8 were waited for; matrix products, arithmetic and copies ran while one was open for 0% of the time, Pallas kernels for 46%

profile of v2, /device:TPU:0, one launch (start us, length us, event | category | flops | bytes accessed | tf_op | source)
XLA Modules:
  0.0 66.9 jit_solution(16569528514799696664)
XLA Ops:
  0.0 1.3 %prepare.1 = (bf16[128,2176]{1,0:T(8,128)(2,1)S(1)}, bf16[64,2176]{1,0:T(8,128)(2,1)S(1)}, bf16[64,2176]{1,0:T(8,128)(2,1)S(1)}) custom-call(bf16[128,2048]{1,0:T(8,128)(2,1)} %tokens.1, s32[10,128]{1,0:T(8,128)} %bitcast.2, bf16[10,128]{1,0:T(8,128)(2,1)} %bitcast.3), custom_call_target="tpu_custom_call" | custom-call | tf_op jit(solution)/shard_map/prepare/pallas_call | solution.py:70
  1.8 2.6 %collective-permute-start = (bf16[64,2176]{1,0:T(8,128)(2,1)S(1)}, bf16[64,2176]{1,0:T(8,128)(2,1)S(1)}, u32[]{:S(2)}, u32[]{:S(2)}) collective-permute-start(bf16[64,2176]{1,0:T(8,128)(2,1)S(1)} %get-tuple-element.54), channel_id=1, source_target_pairs={{0,2},{1,3},{2,0},{3,1},{4,6},{5,7},{6,4},{7,5},{8,10},{9,11},{10,... | collective-permute-start | bytes 835592 | tf_op jit(solution)/shard_map/ppermute | solution.py:20
  4.4 1.5 %collective-permute-start.1 = (bf16[64,2176]{1,0:T(8,128)(2,1)S(1)}, bf16[64,2176]{1,0:T(8,128)(2,1)S(1)}, u32[]{:S(2)}, u32[]{:S(2)}) collective-permute-start(bf16[64,2176]{1,0:T(8,128)(2,1)S(1)} %get-tuple-element.53), channel_id=1, source_target_pairs={{0,4},{1,5},{2,6},{3,7},{4,0},{5,1},{6,2},{7,3},{8,12},{9,13},{10,... | collective-permute-start | bytes 835592 | tf_op jit(solution)/shard_map/ppermute | solution.py:20
  5.9 7.3 %load.1 = (bf16[4,2048,512]{2,1,0:T(8,128)(2,1)S(1)}, bf16[4,2048,512]{2,1,0:T(8,128)(2,1)S(1)}, bf16[256,2048]{1,0:T(8,128)(2,1)S(1)}) custom-call(bf16[128,2176]{1,0:T(8,128)(2,1)S(1)} %get-tuple-element.39.own, bf16[128,2176]{1,0:T(8,128)(2,1)S(1)} %collective-permute-done.2.twin, bf16[4,2048,512]{2,1,0:T(8,128)(2,1)} %gate_hbm.1, ...), custom_call_target="tpu_custom_call" | custom-call | tf_op jit(solution)/shard_map/load/pallas_call | solution.py:141
  13.8 1.3 %collective-permute-start.3 = (bf16[64,2176]{1,0:T(8,128)(2,1)S(1)}, bf16[64,2176]{1,0:T(8,128)(2,1)S(1)}, u32[]{:S(2)}, u32[]{:S(2)}) collective-permute-start(bf16[64,2176]{1,0:T(8,128)(2,1)S(1)} %collective-permute-done.refs_0_), channel_id=1, source_target_pairs={{0,4},{1,5},{2,6},{3,7},{4,0},{5,1},{6,2},{7,3},{8,12},{9,13},{10,... | collective-permute-start | bytes 835592 | tf_op jit(solution)/shard_map/ppermute | solution.py:20
  15.7 6.9 %first_chunk.1 = (bf16[128,2048]{1,0:T(8,128)(2,1)S(1)}, bf16[128,2048]{1,0:T(8,128)(2,1)S(1)}, bf16[4,2048,512]{2,1,0:T(8,128)(2,1)S(1)}) custom-call(bf16[64,2176]{1,0:T(8,128)(2,1)S(1)} %collective-permute-done.refs_0_, bf16[64,2176]{1,0:T(8,128)(2,1)S(1)} %collective-permute-done.1.refs_1_, bf16[64,2176]{1,0:T(8,128)(2,1)S(1)} %collective-permute-done.5.refs_2_, ...), custom_call_target="tpu_custom_call" | custom-call | tf_op jit(solution)/shard_map/first_chunk/pallas_call | solution.py:183
  22.6 0.8 %collective-permute-done.4.refs_1_ = bf16[64,2176]{1,0:T(8,128)(2,1)S(1)} collective-permute-done((bf16[64,2176]{1,0:T(8,128)(2,1)S(1)}, bf16[64,2176]{1,0:T(8,128)(2,1)S(1)}, u32[]{:S(2)}, u32[]{:S(2)}) %collective-permute-start.4) | collective-permute-done | bytes 278560 | tf_op jit(solution)/shard_map/ppermute | solution.py:20
  23.9 0.8 %collective-permute-start.10 = (bf16[64,2176]{1,0:T(8,128)(2,1)S(1)}, bf16[64,2176]{1,0:T(8,128)(2,1)S(1)}, u32[]{:S(2)}, u32[]{:S(2)}) collective-permute-start(bf16[64,2176]{1,0:T(8,128)(2,1)S(1)} %get-tuple-element.53), channel_id=1, source_target_pairs={{0,2},{1,3},{2,0},{3,1},{4,6},{5,7},{6,4},{7,5},{8,10},{9,11},{10,... | collective-permute-start | bytes 835592 | tf_op jit(solution)/shard_map/ppermute | solution.py:20
  24.7 0.7 %collective-permute-start.11 = (bf16[64,2176]{1,0:T(8,128)(2,1)S(1)}, bf16[64,2176]{1,0:T(8,128)(2,1)S(1)}, u32[]{:S(2)}, u32[]{:S(2)}) collective-permute-start(bf16[64,2176]{1,0:T(8,128)(2,1)S(1)} %get-tuple-element.54), channel_id=1, source_target_pairs={{0,4},{1,5},{2,6},{3,7},{4,0},{5,1},{6,2},{7,3},{8,12},{9,13},{10,... | collective-permute-start | bytes 835592 | tf_op jit(solution)/shard_map/ppermute | solution.py:20
  25.4 2.4 %finish_own.1 = (bf16[128,2048]{1,0:T(8,128)(2,1)S(1)}, bf16[128,2048]{1,0:T(8,128)(2,1)S(1)}) custom-call(bf16[256,2048]{1,0:T(8,128)(2,1)S(1)} %get-tuple-element.47.hidden, bf16[4,2048,512]{2,1,0:T(8,128)(2,1)S(1)} %get-tuple-element.48.w_down.refs_6_), custom_call_target="tpu_custom_call" | custom-call | tf_op jit(solution)/shard_map/finish_own/pallas_call | solution.py:209
  27.8 6.9 %chunk.2 = (bf16[128,2048]{1,0:T(8,128)(2,1)S(1)}, bf16[128,2048]{1,0:T(8,128)(2,1)S(1)}) custom-call(bf16[64,2176]{1,0:T(8,128)(2,1)S(1)} %collective-permute-done.3.refs_0_, bf16[64,2176]{1,0:T(8,128)(2,1)S(1)} %collective-permute-done.4.refs_1_, bf16[64,2176]{1,0:T(8,128)(2,1)S(1)} %collective-permute-done.12.refs_2_, ...), custom_call_target="tpu_custom_call" | custom-call | tf_op jit(solution)/shard_map/chunk/pallas_call | solution.py:196
  36.8 6.7 %chunk.3 = (bf16[128,2048]{1,0:T(8,128)(2,1)S(1)}, bf16[128,2048]{1,0:T(8,128)(2,1)S(1)}) custom-call(bf16[64,2176]{1,0:T(8,128)(2,1)S(1)} %collective-permute-done.10.refs_0_, bf16[64,2176]{1,0:T(8,128)(2,1)S(1)} %collective-permute-done.11.refs_1_, bf16[64,2176]{1,0:T(8,128)(2,1)S(1)} %collective-permute-done.14.refs_2_, ...), custom_call_target="tpu_custom_call" | custom-call | tf_op jit(solution)/shard_map/chunk/pallas_call | solution.py:196
  43.8 1.4 %collective-permute-start.18 = (bf16[64,2048]{1,0:T(8,128)(2,1)S(1)}, bf16[64,2048]{1,0:T(8,128)(2,1)S(1)}, u32[]{:S(2)}, u32[]{:S(2)}) collective-permute-start(bf16[64,2048]{1,0:T(8,128)(2,1)S(1)} %get-tuple-element.64), channel_id=1, source_target_pairs={{0,4},{1,5},{2,6},{3,7},{4,0},{5,1},{6,2},{7,3},{8,12},{9,13},{10,... | collective-permute-start | bytes 786440 | tf_op jit(solution)/shard_map/ppermute | solution.py:20
  45.2 1.3 %collective-permute-start.19 = (bf16[64,2048]{1,0:T(8,128)(2,1)S(1)}, bf16[64,2048]{1,0:T(8,128)(2,1)S(1)}, u32[]{:S(2)}, u32[]{:S(2)}) collective-permute-start(bf16[64,2048]{1,0:T(8,128)(2,1)S(1)} %get-tuple-element.65), channel_id=1, source_target_pairs={{0,2},{1,3},{2,0},{3,1},{4,6},{5,7},{6,4},{7,5},{8,10},{9,11},{10,... | collective-permute-start | bytes 786440 | tf_op jit(solution)/shard_map/ppermute | solution.py:20
  46.6 0.8 %collective-permute-start.9 = (bf16[64,2048]{1,0:T(8,128)(2,1)S(1)}, bf16[64,2048]{1,0:T(8,128)(2,1)S(1)}, u32[]{:S(2)}, u32[]{:S(2)}) collective-permute-start(bf16[64,2048]{1,0:T(8,128)(2,1)S(1)} %get-tuple-element.52), channel_id=1, source_target_pairs={{0,2},{1,3},{2,0},{3,1},{4,6},{5,7},{6,4},{7,5},{8,10},{9,11},{10,... | collective-permute-start | bytes 786440 | tf_op jit(solution)/shard_map/ppermute | solution.py:20
  47.5 5.0 %collective-permute-done.18.low_relay = bf16[64,2048]{1,0:T(8,128)(2,1)S(1)} collective-permute-done((bf16[64,2048]{1,0:T(8,128)(2,1)S(1)}, bf16[64,2048]{1,0:T(8,128)(2,1)S(1)}, u32[]{:S(2)}, u32[]{:S(2)}) %collective-permute-start.18) | collective-permute-done | bytes 262176 | tf_op jit(solution)/shard_map/ppermute | solution.py:20
  52.5 1.3 %collective-permute-start.21 = (bf16[64,2048]{1,0:T(8,128)(2,1)S(1)}, bf16[64,2048]{1,0:T(8,128)(2,1)S(1)}, u32[]{:S(2)}, u32[]{:S(2)}) collective-permute-start(bf16[64,2048]{1,0:T(8,128)(2,1)S(1)} %get-tuple-element.67), channel_id=1, source_target_pairs={{0,4},{1,5},{2,6},{3,7},{4,0},{5,1},{6,2},{7,3},{8,12},{9,13},{10,... | collective-permute-start | bytes 786440 | tf_op jit(solution)/shard_map/ppermute | solution.py:20
  53.8 0.6 collective-permute-done.19.high_relay
  54.6 0.8 %collective-permute-start.20 = (bf16[64,2048]{1,0:T(8,128)(2,1)S(1)}, bf16[64,2048]{1,0:T(8,128)(2,1)S(1)}, u32[]{:S(2)}, u32[]{:S(2)}) collective-permute-start(bf16[64,2048]{1,0:T(8,128)(2,1)S(1)} %get-tuple-element.66), channel_id=1, source_target_pairs={{0,4},{1,5},{2,6},{3,7},{4,0},{5,1},{6,2},{7,3},{8,12},{9,13},{10,... | collective-permute-start | bytes 786440 | tf_op jit(solution)/shard_map/ppermute | solution.py:20
  55.4 1.3 %collective-permute-start.22 = (bf16[64,2048]{1,0:T(8,128)(2,1)S(1)}, bf16[64,2048]{1,0:T(8,128)(2,1)S(1)}, u32[]{:S(2)}, u32[]{:S(2)}) collective-permute-start(bf16[64,2048]{1,0:T(8,128)(2,1)S(1)} %get-tuple-element.68), channel_id=1, source_target_pairs={{0,2},{1,3},{2,0},{3,1},{4,6},{5,7},{6,4},{7,5},{8,10},{9,11},{10,... | collective-permute-start | bytes 786440 | tf_op jit(solution)/shard_map/ppermute | solution.py:20
  56.7 3.3 %collective-permute-done.9.refs_0_ = bf16[64,2048]{1,0:T(8,128)(2,1)S(1)} collective-permute-done((bf16[64,2048]{1,0:T(8,128)(2,1)S(1)}, bf16[64,2048]{1,0:T(8,128)(2,1)S(1)}, u32[]{:S(2)}, u32[]{:S(2)}) %collective-permute-start.9) | collective-permute-done | bytes 262176 | tf_op jit(solution)/shard_map/ppermute | solution.py:20
  60.0 1.7 %collective-permute-done.21.refs_2_ = bf16[64,2048]{1,0:T(8,128)(2,1)S(1)} collective-permute-done((bf16[64,2048]{1,0:T(8,128)(2,1)S(1)}, bf16[64,2048]{1,0:T(8,128)(2,1)S(1)}, u32[]{:S(2)}, u32[]{:S(2)}) %collective-permute-start.21) | collective-permute-done | bytes 262176 | tf_op jit(solution)/shard_map/ppermute | solution.py:20
  61.7 4.2 %collective-permute-done.20.refs_1_ = bf16[64,2048]{1,0:T(8,128)(2,1)S(1)} collective-permute-done((bf16[64,2048]{1,0:T(8,128)(2,1)S(1)}, bf16[64,2048]{1,0:T(8,128)(2,1)S(1)}, u32[]{:S(2)}, u32[]{:S(2)}) %collective-permute-start.20) | collective-permute-done | bytes 262176 | tf_op jit(solution)/shard_map/ppermute | solution.py:20
  65.9 1.1 %finish.1 = bf16[128,2048]{1,0:T(8,128)(2,1)} custom-call(bf16[128,2048]{1,0:T(8,128)(2,1)S(1)} %get-tuple-element.49.mine, bf16[128,2048]{1,0:T(8,128)(2,1)S(1)} %collective-permute-done.7.twin, bf16[64,2048]{1,0:T(8,128)(2,1)S(1)} %collective-permute-done.9.refs_0_, bf16[64,2048]{1,0:T(8,128)(2,1)S(1)} %collective-permute-done.20.refs_1_, ...), custom_call_target="tpu_custom_call" | custom-call | tf_op jit(solution)/shard_map/finish/pallas_call | solution.py:275
  (32 shorter events, 4.8 us)
Async XLA Ops:
  1.3 4.6 %collective-permute-start.2 = (bf16[128,2176]{1,0:T(8,128)(2,1)S(1)}, bf16[128,2176]{1,0:T(8,128)(2,1)S(1)}, u32[]{:S(2)}, u32[]{:S(2)}) collective-permute-start(bf16[128,2176]{1,0:T(8,128)(2,1)S(1)} %get-tuple-element.39.own), channel_id=1, source_target_pairs={{0,1},{1,0},{2,3},{3,2},{4,5},{5,4},{6,7},{7,6},{8,9},{9,8},{10,11... | collective-permute-start | bytes 1671176 | tf_op jit(solution)/shard_map/ppermute | solution.py:20
  1.8 11.4 %collective-permute-start = (bf16[64,2176]{1,0:T(8,128)(2,1)S(1)}, bf16[64,2176]{1,0:T(8,128)(2,1)S(1)}, u32[]{:S(2)}, u32[]{:S(2)}) collective-permute-start(bf16[64,2176]{1,0:T(8,128)(2,1)S(1)} %get-tuple-element.54), channel_id=1, source_target_pairs={{0,2},{1,3},{2,0},{3,1},{4,6},{5,7},{6,4},{7,5},{8,10},{9,11},{10,... | collective-permute-start | bytes 835592 | tf_op jit(solution)/shard_map/ppermute | solution.py:20
  4.4 8.9 %collective-permute-start.1 = (bf16[64,2176]{1,0:T(8,128)(2,1)S(1)}, bf16[64,2176]{1,0:T(8,128)(2,1)S(1)}, u32[]{:S(2)}, u32[]{:S(2)}) collective-permute-start(bf16[64,2176]{1,0:T(8,128)(2,1)S(1)} %get-tuple-element.53), channel_id=1, source_target_pairs={{0,4},{1,5},{2,6},{3,7},{4,0},{5,1},{6,2},{7,3},{8,12},{9,13},{10,... | collective-permute-start | bytes 835592 | tf_op jit(solution)/shard_map/ppermute | solution.py:20
  13.2 2.5 %collective-permute-start.5 = (bf16[64,2176]{1,0:T(8,128)(2,1)S(1)}, bf16[64,2176]{1,0:T(8,128)(2,1)S(1)}, u32[]{:S(2)}, u32[]{:S(2)}) collective-permute-start(bf16[64,2176]{1,0:T(8,128)(2,1)S(1)} %collective-permute-done.refs_0_), channel_id=1, source_target_pairs={{0,1},{1,0},{2,3},{3,2},{4,5},{5,4},{6,7},{7,6},{8,9},{9,8},{10,11... | collective-permute-start | bytes 835592 | tf_op jit(solution)/shard_map/ppermute | solution.py:20
  13.3 2.4 %collective-permute-start.6 = (bf16[64,2176]{1,0:T(8,128)(2,1)S(1)}, bf16[64,2176]{1,0:T(8,128)(2,1)S(1)}, u32[]{:S(2)}, u32[]{:S(2)}) collective-permute-start(bf16[64,2176]{1,0:T(8,128)(2,1)S(1)} %collective-permute-done.1.refs_1_), channel_id=1, source_target_pairs={{0,1},{1,0},{2,3},{3,2},{4,5},{5,4},{6,7},{7,6},{8,9},{9,8},{10,11... | collective-permute-start | bytes 835592 | tf_op jit(solution)/shard_map/ppermute | solution.py:20
  13.8 8.8 %collective-permute-start.3 = (bf16[64,2176]{1,0:T(8,128)(2,1)S(1)}, bf16[64,2176]{1,0:T(8,128)(2,1)S(1)}, u32[]{:S(2)}, u32[]{:S(2)}) collective-permute-start(bf16[64,2176]{1,0:T(8,128)(2,1)S(1)} %collective-permute-done.refs_0_), channel_id=1, source_target_pairs={{0,4},{1,5},{2,6},{3,7},{4,0},{5,1},{6,2},{7,3},{8,12},{9,13},{10,... | collective-permute-start | bytes 835592 | tf_op jit(solution)/shard_map/ppermute | solution.py:20
  15.1 8.3 %collective-permute-start.4 = (bf16[64,2176]{1,0:T(8,128)(2,1)S(1)}, bf16[64,2176]{1,0:T(8,128)(2,1)S(1)}, u32[]{:S(2)}, u32[]{:S(2)}) collective-permute-start(bf16[64,2176]{1,0:T(8,128)(2,1)S(1)} %collective-permute-done.1.refs_1_), channel_id=1, source_target_pairs={{0,2},{1,3},{2,0},{3,1},{4,6},{5,7},{6,4},{7,5},{8,10},{9,11},{10,... | collective-permute-start | bytes 835592 | tf_op jit(solution)/shard_map/ppermute | solution.py:20
  23.4 4.3 %collective-permute-start.12 = (bf16[64,2176]{1,0:T(8,128)(2,1)S(1)}, bf16[64,2176]{1,0:T(8,128)(2,1)S(1)}, u32[]{:S(2)}, u32[]{:S(2)}) collective-permute-start(bf16[64,2176]{1,0:T(8,128)(2,1)S(1)} %collective-permute-done.3.refs_0_), channel_id=1, source_target_pairs={{0,1},{1,0},{2,3},{3,2},{4,5},{5,4},{6,7},{7,6},{8,9},{9,8},{10,11... | collective-permute-start | bytes 835592 | tf_op jit(solution)/shard_map/ppermute | solution.py:20
  23.4 4.4 %collective-permute-start.13 = (bf16[64,2176]{1,0:T(8,128)(2,1)S(1)}, bf16[64,2176]{1,0:T(8,128)(2,1)S(1)}, u32[]{:S(2)}, u32[]{:S(2)}) collective-permute-start(bf16[64,2176]{1,0:T(8,128)(2,1)S(1)} %collective-permute-done.4.refs_1_), channel_id=1, source_target_pairs={{0,1},{1,0},{2,3},{3,2},{4,5},{5,4},{6,7},{7,6},{8,9},{9,8},{10,11... | collective-permute-start | bytes 835592 | tf_op jit(solution)/shard_map/ppermute | solution.py:20
  23.9 10.8 %collective-permute-start.10 = (bf16[64,2176]{1,0:T(8,128)(2,1)S(1)}, bf16[64,2176]{1,0:T(8,128)(2,1)S(1)}, u32[]{:S(2)}, u32[]{:S(2)}) collective-permute-start(bf16[64,2176]{1,0:T(8,128)(2,1)S(1)} %get-tuple-element.53), channel_id=1, source_target_pairs={{0,2},{1,3},{2,0},{3,1},{4,6},{5,7},{6,4},{7,5},{8,10},{9,11},{10,... | collective-permute-start | bytes 835592 | tf_op jit(solution)/shard_map/ppermute | solution.py:20
  24.7 10.1 %collective-permute-start.11 = (bf16[64,2176]{1,0:T(8,128)(2,1)S(1)}, bf16[64,2176]{1,0:T(8,128)(2,1)S(1)}, u32[]{:S(2)}, u32[]{:S(2)}) collective-permute-start(bf16[64,2176]{1,0:T(8,128)(2,1)S(1)} %get-tuple-element.54), channel_id=1, source_target_pairs={{0,4},{1,5},{2,6},{3,7},{4,0},{5,1},{6,2},{7,3},{8,12},{9,13},{10,... | collective-permute-start | bytes 835592 | tf_op jit(solution)/shard_map/ppermute | solution.py:20
  34.7 1.6 %collective-permute-start.14 = (bf16[64,2176]{1,0:T(8,128)(2,1)S(1)}, bf16[64,2176]{1,0:T(8,128)(2,1)S(1)}, u32[]{:S(2)}, u32[]{:S(2)}) collective-permute-start(bf16[64,2176]{1,0:T(8,128)(2,1)S(1)} %collective-permute-done.10.refs_0_), channel_id=1, source_target_pairs={{0,1},{1,0},{2,3},{3,2},{4,5},{5,4},{6,7},{7,6},{8,9},{9,8},{10,11... | collective-permute-start | bytes 835592 | tf_op jit(solution)/shard_map/ppermute | solution.py:20
  34.8 1.9 %collective-permute-start.15 = (bf16[64,2176]{1,0:T(8,128)(2,1)S(1)}, bf16[64,2176]{1,0:T(8,128)(2,1)S(1)}, u32[]{:S(2)}, u32[]{:S(2)}) collective-permute-start(bf16[64,2176]{1,0:T(8,128)(2,1)S(1)} %collective-permute-done.11.refs_1_), channel_id=1, source_target_pairs={{0,1},{1,0},{2,3},{3,2},{4,5},{5,4},{6,7},{7,6},{8,9},{9,8},{10,11... | collective-permute-start | bytes 835592 | tf_op jit(solution)/shard_map/ppermute | solution.py:20
  35.3 8.4 %collective-permute-start.17 = (bf16[128,2048]{1,0:T(8,128)(2,1)S(1)}, bf16[128,2048]{1,0:T(8,128)(2,1)S(1)}, u32[]{:S(2)}, u32[]{:S(2)}) collective-permute-start(bf16[128,2048]{1,0:T(8,128)(2,1)S(1)} %get-tuple-element.63), channel_id=1, source_target_pairs={{0,1},{1,0},{2,3},{3,2},{4,5},{5,4},{6,7},{7,6},{8,9},{9,8},{10,11... | collective-permute-start | bytes 1572872 | tf_op jit(solution)/shard_map/ppermute | solution.py:20
  35.4 11.1 %collective-permute-start.8 = (bf16[128,2048]{1,0:T(8,128)(2,1)S(1)}, bf16[128,2048]{1,0:T(8,128)(2,1)S(1)}, u32[]{:S(2)}, u32[]{:S(2)}) collective-permute-start(bf16[128,2048]{1,0:T(8,128)(2,1)S(1)} %get-tuple-element.51), channel_id=1, source_target_pairs={{0,1},{1,0},{2,3},{3,2},{4,5},{5,4},{6,7},{7,6},{8,9},{9,8},{10,11... | collective-permute-start | bytes 1572872 | tf_op jit(solution)/shard_map/ppermute | solution.py:20
  43.5 10.9 %collective-permute-start.16 = (bf16[128,2048]{1,0:T(8,128)(2,1)S(1)}, bf16[128,2048]{1,0:T(8,128)(2,1)S(1)}, u32[]{:S(2)}, u32[]{:S(2)}) collective-permute-start(bf16[128,2048]{1,0:T(8,128)(2,1)S(1)} %get-tuple-element.62), channel_id=1, source_target_pairs={{0,1},{1,0},{2,3},{3,2},{4,5},{5,4},{6,7},{7,6},{8,9},{9,8},{10,11... | collective-permute-start | bytes 1572872 | tf_op jit(solution)/shard_map/ppermute | solution.py:20
  43.8 8.6 %collective-permute-start.18 = (bf16[64,2048]{1,0:T(8,128)(2,1)S(1)}, bf16[64,2048]{1,0:T(8,128)(2,1)S(1)}, u32[]{:S(2)}, u32[]{:S(2)}) collective-permute-start(bf16[64,2048]{1,0:T(8,128)(2,1)S(1)} %get-tuple-element.64), channel_id=1, source_target_pairs={{0,4},{1,5},{2,6},{3,7},{4,0},{5,1},{6,2},{7,3},{8,12},{9,13},{10,... | collective-permute-start | bytes 786440 | tf_op jit(solution)/shard_map/ppermute | solution.py:20
  45.2 9.2 %collective-permute-start.19 = (bf16[64,2048]{1,0:T(8,128)(2,1)S(1)}, bf16[64,2048]{1,0:T(8,128)(2,1)S(1)}, u32[]{:S(2)}, u32[]{:S(2)}) collective-permute-start(bf16[64,2048]{1,0:T(8,128)(2,1)S(1)} %get-tuple-element.65), channel_id=1, source_target_pairs={{0,2},{1,3},{2,0},{3,1},{4,6},{5,7},{6,4},{7,5},{8,10},{9,11},{10,... | collective-permute-start | bytes 786440 | tf_op jit(solution)/shard_map/ppermute | solution.py:20
  46.5 10.2 %collective-permute-start.7 = (bf16[128,2048]{1,0:T(8,128)(2,1)S(1)}, bf16[128,2048]{1,0:T(8,128)(2,1)S(1)}, u32[]{:S(2)}, u32[]{:S(2)}) collective-permute-start(bf16[128,2048]{1,0:T(8,128)(2,1)S(1)} %get-tuple-element.50), channel_id=1, source_target_pairs={{0,1},{1,0},{2,3},{3,2},{4,5},{5,4},{6,7},{7,6},{8,9},{9,8},{10,11... | collective-permute-start | bytes 1572872 | tf_op jit(solution)/shard_map/ppermute | solution.py:20
  46.6 13.4 %collective-permute-start.9 = (bf16[64,2048]{1,0:T(8,128)(2,1)S(1)}, bf16[64,2048]{1,0:T(8,128)(2,1)S(1)}, u32[]{:S(2)}, u32[]{:S(2)}) collective-permute-start(bf16[64,2048]{1,0:T(8,128)(2,1)S(1)} %get-tuple-element.52), channel_id=1, source_target_pairs={{0,2},{1,3},{2,0},{3,1},{4,6},{5,7},{6,4},{7,5},{8,10},{9,11},{10,... | collective-permute-start | bytes 786440 | tf_op jit(solution)/shard_map/ppermute | solution.py:20
  52.5 9.2 %collective-permute-start.21 = (bf16[64,2048]{1,0:T(8,128)(2,1)S(1)}, bf16[64,2048]{1,0:T(8,128)(2,1)S(1)}, u32[]{:S(2)}, u32[]{:S(2)}) collective-permute-start(bf16[64,2048]{1,0:T(8,128)(2,1)S(1)} %get-tuple-element.67), channel_id=1, source_target_pairs={{0,4},{1,5},{2,6},{3,7},{4,0},{5,1},{6,2},{7,3},{8,12},{9,13},{10,... | collective-permute-start | bytes 786440 | tf_op jit(solution)/shard_map/ppermute | solution.py:20
  54.6 11.3 %collective-permute-start.20 = (bf16[64,2048]{1,0:T(8,128)(2,1)S(1)}, bf16[64,2048]{1,0:T(8,128)(2,1)S(1)}, u32[]{:S(2)}, u32[]{:S(2)}) collective-permute-start(bf16[64,2048]{1,0:T(8,128)(2,1)S(1)} %get-tuple-element.66), channel_id=1, source_target_pairs={{0,4},{1,5},{2,6},{3,7},{4,0},{5,1},{6,2},{7,3},{8,12},{9,13},{10,... | collective-permute-start | bytes 786440 | tf_op jit(solution)/shard_map/ppermute | solution.py:20
  55.4 10.5 %collective-permute-start.22 = (bf16[64,2048]{1,0:T(8,128)(2,1)S(1)}, bf16[64,2048]{1,0:T(8,128)(2,1)S(1)}, u32[]{:S(2)}, u32[]{:S(2)}) collective-permute-start(bf16[64,2048]{1,0:T(8,128)(2,1)S(1)} %get-tuple-element.68), channel_id=1, source_target_pairs={{0,2},{1,3},{2,0},{3,1},{4,6},{5,7},{6,4},{7,5},{8,10},{9,11},{10,... | collective-permute-start | bytes 786440 | tf_op jit(solution)/shard_map/ppermute | solution.py:20

commit v3 on v2

v3 whole, which is shorter than its diff:
```python
import functools

import jax
import jax.numpy as jnp
from jax import lax
from jax.experimental import pallas as pl
from jax.experimental.pallas import tpu as pltpu
from jax.sharding import PartitionSpec as P

MIB = 2**20
LANES = 128
NT = (((1,), (1,)), ((), ()))
VMEM_SPEC = pl.BlockSpec(memory_space=pltpu.VMEM)
HBM_SPEC = pl.BlockSpec(memory_space=pltpu.HBM)
CORE = 1
COST = pl.CostEstimate(flops=0, bytes_accessed=0, transcendentals=0)


def flip(x, mask):
    n = lax.axis_size("ep")
    return lax.ppermute(x, "ep", [(i, i ^ mask) for i in range(n)])


def after(x, *others):
    return lax.optimization_barrier((x, *others))[0]


def in_vmem(*arrays):
    return [pltpu.with_memory_space_constraint(a, pltpu.VMEM) for a in arrays]


def in_hbm(*arrays):
    return [pltpu.with_memory_space_constraint(a, pltpu.HBM) for a in arrays]


def params(limit=6):
    return pltpu.CompilerParams(vmem_limit_bytes=limit * MIB)


def prepare_kernel(tokens, experts, gates, whole, low, high, chosen, weight, sems):
    count, width = tokens.shape
    half = count // 2
    lanes = whole.shape[1] - width
    copies = [
        pltpu.make_async_copy(experts, chosen, sems.at[0]),
        pltpu.make_async_copy(gates, weight, sems.at[1]),
        pltpu.make_async_copy(tokens.at[pl.ds(0, half)], low.at[:, pl.ds(0, width)], sems.at[2]),
        pltpu.make_async_copy(tokens.at[pl.ds(half, half)], high.at[:, pl.ds(0, width)], sems.at[3]),
        pltpu.make_async_copy(tokens, whole.at[:, pl.ds(0, width)], sems.at[4]),
    ]
    for copy in copies:
        copy.start()
    copies[0].wait()
    copies[1].wait()
    ids = lax.broadcasted_iota(jnp.int32, (lanes, count), 0)
    total = jnp.zeros((lanes, count), jnp.float32)
    for k in range(chosen.shape[0]):
        gate = weight[k : k + 1, :].astype(jnp.float32)
        total += jnp.where(ids == chosen[k : k + 1, :], gate, 0.0)
    table = total.T.astype(jnp.bfloat16)
    whole[:, width:] = table
    low[:, width:] = table[:half]
    high[:, width:] = table[half:]
    for copy in copies[2:]:
        copy.wait()


def prepare(tokens, experts, gates, lanes):
    count, width = tokens.shape
    rows = [(count, width + lanes), (count // 2, width + lanes), (count // 2, width + lanes)]
    return pl.pallas_call(
        prepare_kernel,
        in_specs=[HBM_SPEC] * 3,
        out_specs=[VMEM_SPEC] * 3,
        out_shape=[pltpu.VMEM(shape, jnp.bfloat16) for shape in rows],
        scratch_shapes=[
            pltpu.VMEM(experts.shape[::-1], jnp.int32),
            pltpu.VMEM(gates.shape[::-1], jnp.bfloat16),
            pltpu.SemaphoreType.DMA((5,)),
        ],
        cost_estimate=pl.CostEstimate(flops=10**11, bytes_accessed=10**8, transcendentals=0),
        compiler_params=params(4),
        name="prepare",
    )(*in_hbm(tokens, experts.T, gates.T))


def gather_inputs(parts, rows, held):
    width = rows.shape[1]
    tables, start = [], 0
    for part in parts:
        rows[start : start + part.shape[0]] = part[:, :width]
        tables.append(part[:, width:])
        start += part.shape[0]
    table = jnp.concatenate(tables, axis=0).astype(jnp.float32)
    lane = lax.broadcasted_iota(jnp.int32, table.shape, 1)
    base = lax.axis_index("ep") * held
    return [
        jnp.sum(jnp.where(lane == base + e, table, 0.0), axis=1, keepdims=True) for e in range(held)
    ]


def hidden_of(rows, gate_w, up_w, weight):
    gate_act = jnp.dot(rows, gate_w, preferred_element_type=jnp.float32)
    up_act = jnp.dot(rows, up_w, preferred_element_type=jnp.float32)
    return (gate_act / (1.0 + jnp.exp(-gate_act)) * up_act * weight).astype(jnp.bfloat16)


def down_all(hidden, w_down, mine, *others, tile=512):
    held, width, units = w_down.shape
    count, piece = mine.shape[0], others[0].shape[0]
    for start in range(0, width, tile):
        total = None
        for e in range(held):
            part = lax.dot_general(
                hidden[:, e * units : (e + 1) * units],
                w_down[e, start : start + tile, :],
                NT,
                preferred_element_type=jnp.float32,
            )
            total = part if total is None else total + part
        total = total.astype(jnp.bfloat16)
        mine[:, start : start + tile] = total[:count]
        for i, other in enumerate(others):
            first = count + i * piece
            other[:, start : start + tile] = total[first : first + piece]


def hidden_kernel(*refs, parts):
    inputs, (w_gate, w_up, hidden, rows) = refs[:parts], refs[parts:]
    held, _, units = w_gate.shape
    weights = gather_inputs(inputs, rows, held)
    for e in range(held):
        hidden[:, e * units : (e + 1) * units] = hidden_of(rows[...], w_gate[e], w_up[e], weights[e])


def hidden_units(parts, w_gate, w_up):
    count = sum(part.shape[0] for part in parts)
    held, width, units = w_gate.shape
    return pl.pallas_call(
        functools.partial(hidden_kernel, parts=len(parts)),
        in_specs=[VMEM_SPEC] * (len(parts) + 2),
        out_specs=VMEM_SPEC,
        out_shape=pltpu.VMEM((count, held * units), jnp.bfloat16),
        scratch_shapes=[pltpu.VMEM((count, width), jnp.bfloat16)],
        cost_estimate=COST,
        compiler_params=params(),
        name="hidden_units",
    )(*in_vmem(*parts, w_gate, w_up))


def chunk_kernel(*refs, parts):
    inputs, (w_gate, w_up, w_down), refs = refs[:parts], refs[parts : parts + 3], refs[parts + 3 :]
    mine, *others, rows, hidden = refs
    held, _, units = w_gate.shape
    weights = gather_inputs(inputs, rows, held)
    for e in range(held):
        hidden[:, e * units : (e + 1) * units] = hidden_of(rows[...], w_gate[e], w_up[e], weights[e])
    down_all(hidden, w_down, mine, *others)


def sum_shapes(count, width, pieces):
    pieces = [pltpu.VMEM((count // 2 // pieces, width), jnp.bfloat16)] * pieces
    return [pltpu.VMEM((count // 2, width), jnp.bfloat16), *pieces]


def scratch_of(count, w_gate):
    held, width, units = w_gate.shape
    return [pltpu.VMEM((count, width), jnp.bfloat16), pltpu.VMEM((count, held * units), jnp.bfloat16)]


def chunk(parts, w_gate, w_up, w_down, pieces=1):
    count = sum(part.shape[0] for part in parts)
    mine, *others = pl.pallas_call(
        functools.partial(chunk_kernel, parts=len(parts)),
        in_specs=[VMEM_SPEC] * (len(parts) + 3),
        out_specs=[VMEM_SPEC] * (1 + pieces),
        out_shape=sum_shapes(count, w_gate.shape[1], pieces),
        scratch_shapes=scratch_of(count, w_gate),
        cost_estimate=COST,
        compiler_params=params(),
        name="chunk",
    )(*in_vmem(*parts, w_gate, w_up, w_down))
    return mine, others


def down_units(hidden, w_down, pieces=1):
    mine, *others = pl.pallas_call(
        down_all,
        in_specs=[VMEM_SPEC] * 2,
        out_specs=[VMEM_SPEC] * (1 + pieces),
        out_shape=sum_shapes(hidden.shape[0], w_down.shape[1], pieces),
        cost_estimate=COST,
        compiler_params=params(),
        name="down_units",
    )(*in_vmem(hidden, w_down))
    return mine, others


def swap(others):
    return [flip(other, CORE) for other in others]


def add_kernel(mine, *refs):
    *twins, low, high = refs
    half, piece = low.shape[0], twins[0].shape[0]
    step = min(half, piece)
    for first in range(0, 2 * half, step):
        out, at = (low, first) if first < half else (high, first - half)
        twin = twins[first // piece][first % piece : first % piece + step]
        total = mine[first : first + step].astype(jnp.float32) + twin.astype(jnp.float32)
        out[at : at + step] = total.astype(out.dtype)


def add_halves(mine, twins):
    half = pltpu.VMEM((mine.shape[0] // 2, mine.shape[1]), jnp.bfloat16)
    return pl.pallas_call(
        add_kernel,
        in_specs=[VMEM_SPEC] * (1 + len(twins)),
        out_specs=[VMEM_SPEC] * 2,
        out_shape=[half, half],
        cost_estimate=COST,
        compiler_params=params(8),
        name="add_halves",
    )(*in_vmem(mine, *twins))


def add_relay_kernel(mine, low, high, out):
    half = low.shape[0]
    out[:half] = mine[:half].astype(jnp.float32) + low[...].astype(jnp.float32)
    out[half:] = mine[half:].astype(jnp.float32) + high[...].astype(jnp.float32)


def add_relay(mine, low, high):
    return pl.pallas_call(
        add_relay_kernel,
        in_specs=[VMEM_SPEC] * 3,
        out_specs=VMEM_SPEC,
        out_shape=pltpu.VMEM(mine.shape, jnp.float32),
        cost_estimate=COST,
        compiler_params=params(8),
        name="add_relay",
    )(*in_vmem(mine, low, high))


def join_kernel(first, second, out):
    half = first.shape[0]
    out[:half] = first[...]
    out[half:] = second[...]


def join(first, second):
    return pl.pallas_call(
        join_kernel,
        in_specs=[VMEM_SPEC] * 2,
        out_specs=VMEM_SPEC,
        out_shape=pltpu.VMEM((2 * first.shape[0], first.shape[1]), first.dtype),
        cost_estimate=COST,
        compiler_params=params(8),
        name="join",
    )(*in_vmem(first, second))


def finish_kernel(mine, *refs, twins, lows):
    out = refs[-1]
    pieces, low_parts, high_parts = refs[:twins], refs[twins : twins + lows], refs[twins + lows : -1]
    half, piece = low_parts[0].shape[0], pieces[0].shape[0]
    step = min(half, piece)
    for first in range(0, 2 * half, step):
        parts, at = (low_parts, first) if first < half else (high_parts, first - half)
        twin = pieces[first // piece][first % piece : first % piece + step]
        total = mine[first : first + step].astype(jnp.float32) + twin.astype(jnp.float32)
        for part in parts:
            total += part[at : at + step].astype(jnp.float32)
        out[first : first + step] = total.astype(out.dtype)


def finish(mine, twins, low_parts, high_parts):
    parts = [*twins, *low_parts, *high_parts]
    return pl.pallas_call(
        functools.partial(finish_kernel, twins=len(twins), lows=len(low_parts)),
        in_specs=[VMEM_SPEC] * (1 + len(parts)),
        out_specs=VMEM_SPEC,
        out_shape=jax.ShapeDtypeStruct(mine.shape, mine.dtype),
        cost_estimate=COST,
        compiler_params=params(8),
        name="finish",
    )(*in_vmem(mine, *parts))


def on_four_chips(whole, low, high, w_gate, w_up, w_down):
    x, y = 2, 4
    near_x, near_y = flip(low, x), flip(high, y)
    weights = (w_gate, w_up, w_down)
    hidden = hidden_units([whole, flip(whole, CORE)], w_gate, w_up)
    near_x, near_y, hidden = lax.optimization_barrier((near_x, near_y, hidden))
    far_low, far_high = flip(near_x, y), flip(near_y, x)
    parts = [near_x, near_y, flip(near_x, CORE), flip(near_y, CORE)]
    mine_near, other_near = chunk(parts, *weights)
    far_low, far_high, mine_near, low, high = lax.optimization_barrier((far_low, far_high, mine_near, low, high))
    parts = [far_low, far_high, flip(far_low, CORE), flip(far_high, CORE)]
    next_x, next_y = flip(high, x), flip(low, y)
    sum_x, sum_y = add_halves(mine_near, swap(other_near))
    sum_x, sum_y, *parts = lax.optimization_barrier((sum_x, sum_y, *parts))
    back_x, back_y = flip(sum_x, x), flip(sum_y, y)
    mine_far, other_far = chunk(parts, *weights, pieces=2)
    next_x, next_y, mine_far = lax.optimization_barrier((next_x, next_y, mine_far))
    rows = join(next_x, next_y)
    parts = [rows, flip(rows, CORE)]
    relay_low, relay_high = add_halves(mine_far, swap(other_far))
    relay_low, relay_high, *parts = lax.optimization_barrier((relay_low, relay_high, *parts))
    relay_low, relay_high = flip(relay_low, x), flip(relay_high, y)
    mine_next, other_next = chunk(parts, *weights, pieces=2)
    mine_next, hidden, back_x, back_y = lax.optimization_barrier((mine_next, hidden, back_x, back_y))
    mine_own, other_own = down_units(hidden, w_down)
    mine_next, mine_own = lax.optimization_barrier((mine_next, mine_own))
    sum_x, sum_y = add_halves(add_relay(mine_next, relay_high, relay_low), swap(other_next))
    last_x, last_y = flip(sum_x, x), flip(sum_y, y)
    return finish(mine_own, swap(other_own), [back_x, last_y], [back_y, last_x])


def on_any_chips(whole, low, high, *weights):
    offsets = range(2, lax.axis_size("ep"), 2)
    arrived = [flip(whole, d) for d in offsets]
    mine_own, other_own = chunk([whole, flip(whole, CORE)], *weights)
    low_parts, high_parts = [], []
    for d, rows in zip(offsets, arrived):
        mine, others = chunk([rows, flip(rows, CORE)], *weights)
        low, high = add_halves(mine, swap(others))
        low_parts.append(flip(low, d))
        high_parts.append(flip(high, d))
    return finish(mine_own, swap(other_own), low_parts, high_parts)


def body(tokens, experts, gates, w_gate, w_up, w_down):
    n_ep = lax.axis_size("ep")
    n_experts = w_gate.shape[0] * n_ep
    lanes = -(-n_experts // LANES) * LANES
    whole, low, high = prepare(tokens, experts, gates, lanes)
    run = on_four_chips if n_ep == 8 else on_any_chips
    return run(whole, low, high, w_gate, w_up, w_down)


def solution(mesh):
    in_specs = (
        P(("rep", "ep"), None),
        P(("rep", "ep"), None),
        P(("rep", "ep"), None),
        P("ep", None, None),
        P("ep", None, None),
        P("ep", None, None),
    )
    out_specs = P(("rep", "ep"), None)
    return jax.shard_map(body, mesh=mesh, in_specs=in_specs, out_specs=out_specs, check_vma=False)
```

time: 67.1 us -> 59.1 us (0.88)
  waiting for transfers between devices: 16.5 us -> 12.7 us
  Pallas kernels: 33 us -> 30.2 us
  starting transfers between devices: 17.2 us -> 15.8 us
    pallas_call x7 -> x8, Pallas kernels: 18.1 us -> 8.42 us  [the longest x1 4.54 us: hidden_units(): pl.pallas_call(functools.partial(hidden_kernel, parts=len(parts)), in_spe...]
    pallas_call x2 -> x3, Pallas kernels: 13.7 us -> 20.4 us  [chunk(): pl.pallas_call(functools.partial(chunk_kernel, parts=len(parts)), in_spec...]
    ppermute x23 -> x24, waiting for transfers between devices: 16.5 us -> 12.7 us  [flip(): return lax.ppermute(x, 'ep', [(i, i ^ mask) for i in range(n)])]
    ppermute x23 -> x24, starting transfers between devices: 17.2 us -> 15.8 us  [flip(): return lax.ppermute(x, 'ep', [(i, i ^ mask) for i in range(n)])]
  transfers between devices with their start and end apart: 23 -> 24, of which waited for: 8 -> 10; matrix products, arithmetic and copies ran while one was open for 0% -> 0% of each run, Pallas kernels for 46% -> 47%
where the time goes in v3:
time: 59.1 us; the launch traced here: 59 us
  Pallas kernels  30.2 us (51%)
  starting transfers between devices  15.8 us (27%)
  waiting for transfers between devices  12.7 us (21%)
    pallas_call x3, Pallas kernels, chunk(): pl.pallas_call(functools.partial(chunk_kernel, parts=len(parts)), in_spec...  20.4 us
    ppermute x24, starting transfers between devices, flip(): return lax.ppermute(x, 'ep', [(i, i ^ mask) for i in range(n)])  15.8 us
    ppermute x24, waiting for transfers between devices, flip(): return lax.ppermute(x, 'ep', [(i, i ^ mask) for i in range(n)])  12.7 us
    pallas_call x1, Pallas kernels, hidden_units(): pl.pallas_call(functools.partial(hidden_kernel, parts=len(parts)), in_spe...  4.54 us
    pallas_call x1, Pallas kernels, down_units(): pl.pallas_call(down_all, in_specs=[VMEM_SPEC] * 2, out_specs=[VMEM_SPEC]...  2.36 us
    pallas_call x1, Pallas kernels, prepare(): pl.pallas_call(prepare_kernel, in_specs=[HBM_SPEC] * 3, out_specs=[VMEM_S...  1.42 us
  transfers between devices with their start and end apart: 24, of which 10 were waited for; matrix products, arithmetic and copies ran while one was open for 0% of the time, Pallas kernels for 47%

profile of v3, /device:TPU:0, one launch (start us, length us, event | category | flops | bytes accessed | tf_op | source)
XLA Modules:
  0.0 59.0 jit_solution(7719418819361603755)
XLA Ops:
  0.0 1.4 %prepare.1 = (bf16[128,2176]{1,0:T(8,128)(2,1)S(1)}, bf16[64,2176]{1,0:T(8,128)(2,1)S(1)}, bf16[64,2176]{1,0:T(8,128)(2,1)S(1)}) custom-call(bf16[128,2048]{1,0:T(8,128)(2,1)} %tokens.1, s32[10,128]{1,0:T(8,128)} %bitcast.4, bf16[10,128]{1,0:T(8,128)(2,1)} %bitcast.5), custom_call_target="tpu_custom_call" | custom-call | flops 99999997952 | bytes 100000000 | tf_op jit(solution)/shard_map/prepare/pallas_call | solution.py:71
  2.0 2.6 %collective-permute-start = (bf16[64,2176]{1,0:T(8,128)(2,1)S(1)}, bf16[64,2176]{1,0:T(8,128)(2,1)S(1)}, u32[]{:S(2)}, u32[]{:S(2)}) collective-permute-start(bf16[64,2176]{1,0:T(8,128)(2,1)S(1)} %get-tuple-element.58), channel_id=1, source_target_pairs={{0,2},{1,3},{2,0},{3,1},{4,6},{5,7},{6,4},{7,5},{8,10},{9,11},{10,... | collective-permute-start | bytes 835592 | tf_op jit(solution)/shard_map/ppermute | solution.py:21
  4.5 1.5 %collective-permute-start.1 = (bf16[64,2176]{1,0:T(8,128)(2,1)S(1)}, bf16[64,2176]{1,0:T(8,128)(2,1)S(1)}, u32[]{:S(2)}, u32[]{:S(2)}) collective-permute-start(bf16[64,2176]{1,0:T(8,128)(2,1)S(1)} %get-tuple-element.57), channel_id=1, source_target_pairs={{0,4},{1,5},{2,6},{3,7},{4,0},{5,1},{6,2},{7,3},{8,12},{9,13},{10,... | collective-permute-start | bytes 835592 | tf_op jit(solution)/shard_map/ppermute | solution.py:21
  6.1 4.5 %hidden_units.1.hidden = bf16[256,2048]{1,0:T(8,128)(2,1)S(1)} custom-call(bf16[128,2176]{1,0:T(8,128)(2,1)S(1)} %get-tuple-element.53.refs_0_, bf16[128,2176]{1,0:T(8,128)(2,1)S(1)} %collective-permute-done.2.refs_1_, bf16[4,2048,512]{2,1,0:T(8,128)(2,1)S(1)} %copy-done, bf16[4,2048,512]{2,1,0:T(8,128)(2,1)S(1)} %copy-done.1), custom_call_target="tpu_custom_call" | custom-call | tf_op jit(solution)/shard_map/hidden_units/pallas_call | solution.py:139
  10.7 1.1 %collective-permute-done.refs_0_ = bf16[64,2176]{1,0:T(8,128)(2,1)S(1)} collective-permute-done((bf16[64,2176]{1,0:T(8,128)(2,1)S(1)}, bf16[64,2176]{1,0:T(8,128)(2,1)S(1)}, u32[]{:S(2)}, u32[]{:S(2)}) %collective-permute-start) | collective-permute-done | bytes 278560 | tf_op jit(solution)/shard_map/ppermute | solution.py:21
  11.8 1.5 %collective-permute-done.1.refs_1_ = bf16[64,2176]{1,0:T(8,128)(2,1)S(1)} collective-permute-done((bf16[64,2176]{1,0:T(8,128)(2,1)S(1)}, bf16[64,2176]{1,0:T(8,128)(2,1)S(1)}, u32[]{:S(2)}, u32[]{:S(2)}) %collective-permute-start.1) | collective-permute-done | bytes 278560 | tf_op jit(solution)/shard_map/ppermute | solution.py:21
  13.8 1.5 %collective-permute-start.3 = (bf16[64,2176]{1,0:T(8,128)(2,1)S(1)}, bf16[64,2176]{1,0:T(8,128)(2,1)S(1)}, u32[]{:S(2)}, u32[]{:S(2)}) collective-permute-start(bf16[64,2176]{1,0:T(8,128)(2,1)S(1)} %collective-permute-done.refs_0_), channel_id=1, source_target_pairs={{0,4},{1,5},{2,6},{3,7},{4,0},{5,1},{6,2},{7,3},{8,12},{9,13},{10,... | collective-permute-start | bytes 835592 | tf_op jit(solution)/shard_map/ppermute | solution.py:21
  15.8 6.7 %chunk.3 = (bf16[128,2048]{1,0:T(8,128)(2,1)S(1)}, bf16[128,2048]{1,0:T(8,128)(2,1)S(1)}) custom-call(bf16[64,2176]{1,0:T(8,128)(2,1)S(1)} %collective-permute-done.refs_0_, bf16[64,2176]{1,0:T(8,128)(2,1)S(1)} %collective-permute-done.1.refs_1_, bf16[64,2176]{1,0:T(8,128)(2,1)S(1)} %collective-permute-done.5.refs_2_, ...), custom_call_target="tpu_custom_call" | custom-call | tf_op jit(solution)/shard_map/chunk/pallas_call | solution.py:173
  22.7 0.9 %collective-permute-done.4.refs_1_ = bf16[64,2176]{1,0:T(8,128)(2,1)S(1)} collective-permute-done((bf16[64,2176]{1,0:T(8,128)(2,1)S(1)}, bf16[64,2176]{1,0:T(8,128)(2,1)S(1)}, u32[]{:S(2)}, u32[]{:S(2)}) %collective-permute-start.4) | collective-permute-done | bytes 278560 | tf_op jit(solution)/shard_map/ppermute | solution.py:21
  24.1 0.7 %collective-permute-start.7 = (bf16[64,2176]{1,0:T(8,128)(2,1)S(1)}, bf16[64,2176]{1,0:T(8,128)(2,1)S(1)}, u32[]{:S(2)}, u32[]{:S(2)}) collective-permute-start(bf16[64,2176]{1,0:T(8,128)(2,1)S(1)} %get-tuple-element.57), channel_id=1, source_target_pairs={{0,2},{1,3},{2,0},{3,1},{4,6},{5,7},{6,4},{7,5},{8,10},{9,11},{10,... | collective-permute-start | bytes 835592 | tf_op jit(solution)/shard_map/ppermute | solution.py:21
  25.5 6.9 %chunk.4 = (bf16[128,2048]{1,0:T(8,128)(2,1)S(1)}, bf16[64,2048]{1,0:T(8,128)(2,1)S(1)}, bf16[64,2048]{1,0:T(8,128)(2,1)S(1)}) custom-call(bf16[64,2176]{1,0:T(8,128)(2,1)S(1)} %collective-permute-done.3.refs_0_, bf16[64,2176]{1,0:T(8,128)(2,1)S(1)} %collective-permute-done.4.refs_1_, bf16[64,2176]{1,0:T(8,128)(2,1)S(1)} %collective-permute-done.10.refs_2_, ...), custom_call_target="tpu_custom_call" | custom-call | tf_op jit(solution)/shard_map/chunk/pallas_call | solution.py:173
  32.6 0.8 %collective-permute-done.8.second = bf16[64,2176]{1,0:T(8,128)(2,1)S(1)} collective-permute-done((bf16[64,2176]{1,0:T(8,128)(2,1)S(1)}, bf16[64,2176]{1,0:T(8,128)(2,1)S(1)}, u32[]{:S(2)}, u32[]{:S(2)}) %collective-permute-start.8) | collective-permute-done | bytes 278560 | tf_op jit(solution)/shard_map/ppermute | solution.py:21
  34.2 0.9 %collective-permute-start.15 = (bf16[64,2048]{1,0:T(8,128)(2,1)S(1)}, bf16[64,2048]{1,0:T(8,128)(2,1)S(1)}, u32[]{:S(2)}, u32[]{:S(2)}) collective-permute-start(bf16[64,2048]{1,0:T(8,128)(2,1)S(1)} %get-tuple-element.81), channel_id=1, source_target_pairs={{0,2},{1,3},{2,0},{3,1},{4,6},{5,7},{6,4},{7,5},{8,10},{9,11},{10,... | collective-permute-start | bytes 786440 | tf_op jit(solution)/shard_map/ppermute | solution.py:21
  35.1 0.9 %collective-permute-start.16 = (bf16[64,2048]{1,0:T(8,128)(2,1)S(1)}, bf16[64,2048]{1,0:T(8,128)(2,1)S(1)}, u32[]{:S(2)}, u32[]{:S(2)}) collective-permute-start(bf16[64,2048]{1,0:T(8,128)(2,1)S(1)} %get-tuple-element.82), channel_id=1, source_target_pairs={{0,4},{1,5},{2,6},{3,7},{4,0},{5,1},{6,2},{7,3},{8,12},{9,13},{10,... | collective-permute-start | bytes 786440 | tf_op jit(solution)/shard_map/ppermute | solution.py:21
  36.4 0.9 %collective-permute-start.18 = (bf16[64,2048]{1,0:T(8,128)(2,1)S(1)}, bf16[64,2048]{1,0:T(8,128)(2,1)S(1)}, u32[]{:S(2)}, u32[]{:S(2)}) collective-permute-start(bf16[64,2048]{1,0:T(8,128)(2,1)S(1)} %get-tuple-element.90), channel_id=1, source_target_pairs={{0,4},{1,5},{2,6},{3,7},{4,0},{5,1},{6,2},{7,3},{8,12},{9,13},{10,... | collective-permute-start | bytes 786440 | tf_op jit(solution)/shard_map/ppermute | solution.py:21
  37.3 1.1 %collective-permute-start.19 = (bf16[64,2048]{1,0:T(8,128)(2,1)S(1)}, bf16[64,2048]{1,0:T(8,128)(2,1)S(1)}, u32[]{:S(2)}, u32[]{:S(2)}) collective-permute-start(bf16[64,2048]{1,0:T(8,128)(2,1)S(1)} %get-tuple-element.91), channel_id=1, source_target_pairs={{0,2},{1,3},{2,0},{3,1},{4,6},{5,7},{6,4},{7,5},{8,10},{9,11},{10,... | collective-permute-start | bytes 786440 | tf_op jit(solution)/shard_map/ppermute | solution.py:21
  38.4 6.7 %chunk.5 = (bf16[128,2048]{1,0:T(8,128)(2,1)S(1)}, bf16[64,2048]{1,0:T(8,128)(2,1)S(1)}, bf16[64,2048]{1,0:T(8,128)(2,1)S(1)}) custom-call(bf16[128,2176]{1,0:T(8,128)(2,1)S(1)} %join.1.refs_0_, bf16[128,2176]{1,0:T(8,128)(2,1)S(1)} %collective-permute-done.14.refs_1_, bf16[4,2048,512]{2,1,0:T(8,128)(2,1)S(1)} %copy-done, ...), custom_call_target="tpu_custom_call" | custom-call | tf_op jit(solution)/shard_map/chunk/pallas_call | solution.py:173
  45.8 2.4 %down_units.1 = (bf16[128,2048]{1,0:T(8,128)(2,1)S(1)}, bf16[128,2048]{1,0:T(8,128)(2,1)S(1)}) custom-call(bf16[256,2048]{1,0:T(8,128)(2,1)S(1)} %hidden_units.1.hidden, bf16[4,2048,512]{2,1,0:T(8,128)(2,1)S(1)} %bitcast.3), custom_call_target="tpu_custom_call" | custom-call | tf_op jit(solution)/shard_map/down_units/pallas_call | solution.py:187
  48.3 0.8 %collective-permute-done.18.low = bf16[64,2048]{1,0:T(8,128)(2,1)S(1)} collective-permute-done((bf16[64,2048]{1,0:T(8,128)(2,1)S(1)}, bf16[64,2048]{1,0:T(8,128)(2,1)S(1)}, u32[]{:S(2)}, u32[]{:S(2)}) %collective-permute-start.18) | collective-permute-done | bytes 262176 | tf_op jit(solution)/shard_map/ppermute | solution.py:21
  49.3 0.9 %collective-permute-start.22 = (bf16[64,2048]{1,0:T(8,128)(2,1)S(1)}, bf16[64,2048]{1,0:T(8,128)(2,1)S(1)}, u32[]{:S(2)}, u32[]{:S(2)}) collective-permute-start(bf16[64,2048]{1,0:T(8,128)(2,1)S(1)} %get-tuple-element.94), channel_id=1, source_target_pairs={{0,4},{1,5},{2,6},{3,7},{4,0},{5,1},{6,2},{7,3},{8,12},{9,13},{10,... | collective-permute-start | bytes 786440 | tf_op jit(solution)/shard_map/ppermute | solution.py:21
  50.2 0.8 %collective-permute-start.23 = (bf16[64,2048]{1,0:T(8,128)(2,1)S(1)}, bf16[64,2048]{1,0:T(8,128)(2,1)S(1)}, u32[]{:S(2)}, u32[]{:S(2)}) collective-permute-start(bf16[64,2048]{1,0:T(8,128)(2,1)S(1)} %get-tuple-element.96), channel_id=1, source_target_pairs={{0,2},{1,3},{2,0},{3,1},{4,6},{5,7},{6,4},{7,5},{8,10},{9,11},{10,... | collective-permute-start | bytes 786440 | tf_op jit(solution)/shard_map/ppermute | solution.py:21
  51.0 6.2 %collective-permute-done.22.refs_2_ = bf16[64,2048]{1,0:T(8,128)(2,1)S(1)} collective-permute-done((bf16[64,2048]{1,0:T(8,128)(2,1)S(1)}, bf16[64,2048]{1,0:T(8,128)(2,1)S(1)}, u32[]{:S(2)}, u32[]{:S(2)}) %collective-permute-start.22) | collective-permute-done | bytes 262176 | tf_op jit(solution)/shard_map/ppermute | solution.py:21
  57.2 0.7 %collective-permute-done.23.refs_4_ = bf16[64,2048]{1,0:T(8,128)(2,1)S(1)} collective-permute-done((bf16[64,2048]{1,0:T(8,128)(2,1)S(1)}, bf16[64,2048]{1,0:T(8,128)(2,1)S(1)}, u32[]{:S(2)}, u32[]{:S(2)}) %collective-permute-start.23) | collective-permute-done | bytes 262176 | tf_op jit(solution)/shard_map/ppermute | solution.py:21
  57.9 1.1 %finish.1 = bf16[128,2048]{1,0:T(8,128)(2,1)} custom-call(bf16[128,2048]{1,0:T(8,128)(2,1)S(1)} %get-tuple-element.86.mine, bf16[128,2048]{1,0:T(8,128)(2,1)S(1)} %collective-permute-done.17.refs_0_, bf16[64,2048]{1,0:T(8,128)(2,1)S(1)} %collective-permute-done.15.refs_1_, bf16[64,2048]{1,0:T(8,128)(2,1)S(1)} %collective-permute-done.22.refs_2_, ...), custom_call_target="tpu_custom_call" | custom-call | tf_op jit(solution)/shard_map/finish/pallas_call | solution.py:279
  (45 shorter events, 5.2 us)
Async XLA Ops:
  1.4 4.6 %collective-permute-start.2 = (bf16[128,2176]{1,0:T(8,128)(2,1)S(1)}, bf16[128,2176]{1,0:T(8,128)(2,1)S(1)}, u32[]{:S(2)}, u32[]{:S(2)}) collective-permute-start(bf16[128,2176]{1,0:T(8,128)(2,1)S(1)} %get-tuple-element.53.refs_0_), channel_id=1, source_target_pairs={{0,1},{1,0},{2,3},{3,2},{4,5},{5,4},{6,7},{7,6},{8,9},{9,8},{10,11... | collective-permute-start | bytes 1671176 | tf_op jit(solution)/shard_map/ppermute | solution.py:21
  2.0 9.8 %collective-permute-start = (bf16[64,2176]{1,0:T(8,128)(2,1)S(1)}, bf16[64,2176]{1,0:T(8,128)(2,1)S(1)}, u32[]{:S(2)}, u32[]{:S(2)}) collective-permute-start(bf16[64,2176]{1,0:T(8,128)(2,1)S(1)} %get-tuple-element.58), channel_id=1, source_target_pairs={{0,2},{1,3},{2,0},{3,1},{4,6},{5,7},{6,4},{7,5},{8,10},{9,11},{10,... | collective-permute-start | bytes 835592 | tf_op jit(solution)/shard_map/ppermute | solution.py:21
  4.5 8.7 %collective-permute-start.1 = (bf16[64,2176]{1,0:T(8,128)(2,1)S(1)}, bf16[64,2176]{1,0:T(8,128)(2,1)S(1)}, u32[]{:S(2)}, u32[]{:S(2)}) collective-permute-start(bf16[64,2176]{1,0:T(8,128)(2,1)S(1)} %get-tuple-element.57), channel_id=1, source_target_pairs={{0,4},{1,5},{2,6},{3,7},{4,0},{5,1},{6,2},{7,3},{8,12},{9,13},{10,... | collective-permute-start | bytes 835592 | tf_op jit(solution)/shard_map/ppermute | solution.py:21
  13.3 2.6 %collective-permute-start.5 = (bf16[64,2176]{1,0:T(8,128)(2,1)S(1)}, bf16[64,2176]{1,0:T(8,128)(2,1)S(1)}, u32[]{:S(2)}, u32[]{:S(2)}) collective-permute-start(bf16[64,2176]{1,0:T(8,128)(2,1)S(1)} %collective-permute-done.refs_0_), channel_id=1, source_target_pairs={{0,1},{1,0},{2,3},{3,2},{4,5},{5,4},{6,7},{7,6},{8,9},{9,8},{10,11... | collective-permute-start | bytes 835592 | tf_op jit(solution)/shard_map/ppermute | solution.py:21
  13.3 2.6 %collective-permute-start.6 = (bf16[64,2176]{1,0:T(8,128)(2,1)S(1)}, bf16[64,2176]{1,0:T(8,128)(2,1)S(1)}, u32[]{:S(2)}, u32[]{:S(2)}) collective-permute-start(bf16[64,2176]{1,0:T(8,128)(2,1)S(1)} %collective-permute-done.1.refs_1_), channel_id=1, source_target_pairs={{0,1},{1,0},{2,3},{3,2},{4,5},{5,4},{6,7},{7,6},{8,9},{9,8},{10,11... | collective-permute-start | bytes 835592 | tf_op jit(solution)/shard_map/ppermute | solution.py:21
  13.8 8.9 %collective-permute-start.3 = (bf16[64,2176]{1,0:T(8,128)(2,1)S(1)}, bf16[64,2176]{1,0:T(8,128)(2,1)S(1)}, u32[]{:S(2)}, u32[]{:S(2)}) collective-permute-start(bf16[64,2176]{1,0:T(8,128)(2,1)S(1)} %collective-permute-done.refs_0_), channel_id=1, source_target_pairs={{0,4},{1,5},{2,6},{3,7},{4,0},{5,1},{6,2},{7,3},{8,12},{9,13},{10,... | collective-permute-start | bytes 835592 | tf_op jit(solution)/shard_map/ppermute | solution.py:21
  15.3 8.3 %collective-permute-start.4 = (bf16[64,2176]{1,0:T(8,128)(2,1)S(1)}, bf16[64,2176]{1,0:T(8,128)(2,1)S(1)}, u32[]{:S(2)}, u32[]{:S(2)}) collective-permute-start(bf16[64,2176]{1,0:T(8,128)(2,1)S(1)} %collective-permute-done.1.refs_1_), channel_id=1, source_target_pairs={{0,2},{1,3},{2,0},{3,1},{4,6},{5,7},{6,4},{7,5},{8,10},{9,11},{10,... | collective-permute-start | bytes 835592 | tf_op jit(solution)/shard_map/ppermute | solution.py:21
  22.6 2.7 %collective-permute-start.9 = (bf16[128,2048]{1,0:T(8,128)(2,1)S(1)}, bf16[128,2048]{1,0:T(8,128)(2,1)S(1)}, u32[]{:S(2)}, u32[]{:S(2)}) collective-permute-start(bf16[128,2048]{1,0:T(8,128)(2,1)S(1)} %get-tuple-element.60), channel_id=1, source_target_pairs={{0,1},{1,0},{2,3},{3,2},{4,5},{5,4},{6,7},{7,6},{8,9},{9,8},{10,11... | collective-permute-start | bytes 1572872 | tf_op jit(solution)/shard_map/ppermute | solution.py:21
  23.6 1.8 %collective-permute-start.10 = (bf16[64,2176]{1,0:T(8,128)(2,1)S(1)}, bf16[64,2176]{1,0:T(8,128)(2,1)S(1)}, u32[]{:S(2)}, u32[]{:S(2)}) collective-permute-start(bf16[64,2176]{1,0:T(8,128)(2,1)S(1)} %collective-permute-done.3.refs_0_), channel_id=1, source_target_pairs={{0,1},{1,0},{2,3},{3,2},{4,5},{5,4},{6,7},{7,6},{8,9},{9,8},{10,11... | collective-permute-start | bytes 835592 | tf_op jit(solution)/shard_map/ppermute | solution.py:21
  23.6 2.0 %collective-permute-start.11 = (bf16[64,2176]{1,0:T(8,128)(2,1)S(1)}, bf16[64,2176]{1,0:T(8,128)(2,1)S(1)}, u32[]{:S(2)}, u32[]{:S(2)}) collective-permute-start(bf16[64,2176]{1,0:T(8,128)(2,1)S(1)} %collective-permute-done.4.refs_1_), channel_id=1, source_target_pairs={{0,1},{1,0},{2,3},{3,2},{4,5},{5,4},{6,7},{7,6},{8,9},{9,8},{10,11... | collective-permute-start | bytes 835592 | tf_op jit(solution)/shard_map/ppermute | solution.py:21
  24.1 8.6 %collective-permute-start.7 = (bf16[64,2176]{1,0:T(8,128)(2,1)S(1)}, bf16[64,2176]{1,0:T(8,128)(2,1)S(1)}, u32[]{:S(2)}, u32[]{:S(2)}) collective-permute-start(bf16[64,2176]{1,0:T(8,128)(2,1)S(1)} %get-tuple-element.57), channel_id=1, source_target_pairs={{0,2},{1,3},{2,0},{3,1},{4,6},{5,7},{6,4},{7,5},{8,10},{9,11},{10,... | collective-permute-start | bytes 835592 | tf_op jit(solution)/shard_map/ppermute | solution.py:21
  24.8 8.7 %collective-permute-start.8 = (bf16[64,2176]{1,0:T(8,128)(2,1)S(1)}, bf16[64,2176]{1,0:T(8,128)(2,1)S(1)}, u32[]{:S(2)}, u32[]{:S(2)}) collective-permute-start(bf16[64,2176]{1,0:T(8,128)(2,1)S(1)} %get-tuple-element.58), channel_id=1, source_target_pairs={{0,4},{1,5},{2,6},{3,7},{4,0},{5,1},{6,2},{7,3},{8,12},{9,13},{10,... | collective-permute-start | bytes 835592 | tf_op jit(solution)/shard_map/ppermute | solution.py:21
  33.5 2.9 %collective-permute-start.14 = (bf16[128,2176]{1,0:T(8,128)(2,1)S(1)}, bf16[128,2176]{1,0:T(8,128)(2,1)S(1)}, u32[]{:S(2)}, u32[]{:S(2)}) collective-permute-start(bf16[128,2176]{1,0:T(8,128)(2,1)S(1)} %join.1.refs_0_), channel_id=1, source_target_pairs={{0,1},{1,0},{2,3},{3,2},{4,5},{5,4},{6,7},{7,6},{8,9},{9,8},{10,11... | collective-permute-start | bytes 1671176 | tf_op jit(solution)/shard_map/ppermute | solution.py:21
  33.6 2.4 %collective-permute-start.12 = (bf16[64,2048]{1,0:T(8,128)(2,1)S(1)}, bf16[64,2048]{1,0:T(8,128)(2,1)S(1)}, u32[]{:S(2)}, u32[]{:S(2)}) collective-permute-start(bf16[64,2048]{1,0:T(8,128)(2,1)S(1)} %get-tuple-element.71), channel_id=1, source_target_pairs={{0,1},{1,0},{2,3},{3,2},{4,5},{5,4},{6,7},{7,6},{8,9},{9,8},{10,11... | collective-permute-start | bytes 786440 | tf_op jit(solution)/shard_map/ppermute | solution.py:21
  34.1 2.2 %collective-permute-start.13 = (bf16[64,2048]{1,0:T(8,128)(2,1)S(1)}, bf16[64,2048]{1,0:T(8,128)(2,1)S(1)}, u32[]{:S(2)}, u32[]{:S(2)}) collective-permute-start(bf16[64,2048]{1,0:T(8,128)(2,1)S(1)} %get-tuple-element.72), channel_id=1, source_target_pairs={{0,1},{1,0},{2,3},{3,2},{4,5},{5,4},{6,7},{7,6},{8,9},{9,8},{10,11... | collective-permute-start | bytes 786440 | tf_op jit(solution)/shard_map/ppermute | solution.py:21
  34.2 11.1 %collective-permute-start.15 = (bf16[64,2048]{1,0:T(8,128)(2,1)S(1)}, bf16[64,2048]{1,0:T(8,128)(2,1)S(1)}, u32[]{:S(2)}, u32[]{:S(2)}) collective-permute-start(bf16[64,2048]{1,0:T(8,128)(2,1)S(1)} %get-tuple-element.81), channel_id=1, source_target_pairs={{0,2},{1,3},{2,0},{3,1},{4,6},{5,7},{6,4},{7,5},{8,10},{9,11},{10,... | collective-permute-start | bytes 786440 | tf_op jit(solution)/shard_map/ppermute | solution.py:21
  35.1 10.7 %collective-permute-start.16 = (bf16[64,2048]{1,0:T(8,128)(2,1)S(1)}, bf16[64,2048]{1,0:T(8,128)(2,1)S(1)}, u32[]{:S(2)}, u32[]{:S(2)}) collective-permute-start(bf16[64,2048]{1,0:T(8,128)(2,1)S(1)} %get-tuple-element.82), channel_id=1, source_target_pairs={{0,4},{1,5},{2,6},{3,7},{4,0},{5,1},{6,2},{7,3},{8,12},{9,13},{10,... | collective-permute-start | bytes 786440 | tf_op jit(solution)/shard_map/ppermute | solution.py:21
  36.4 12.7 %collective-permute-start.18 = (bf16[64,2048]{1,0:T(8,128)(2,1)S(1)}, bf16[64,2048]{1,0:T(8,128)(2,1)S(1)}, u32[]{:S(2)}, u32[]{:S(2)}) collective-permute-start(bf16[64,2048]{1,0:T(8,128)(2,1)S(1)} %get-tuple-element.90), channel_id=1, source_target_pairs={{0,4},{1,5},{2,6},{3,7},{4,0},{5,1},{6,2},{7,3},{8,12},{9,13},{10,... | collective-permute-start | bytes 786440 | tf_op jit(solution)/shard_map/ppermute | solution.py:21
  37.3 11.8 %collective-permute-start.19 = (bf16[64,2048]{1,0:T(8,128)(2,1)S(1)}, bf16[64,2048]{1,0:T(8,128)(2,1)S(1)}, u32[]{:S(2)}, u32[]{:S(2)}) collective-permute-start(bf16[64,2048]{1,0:T(8,128)(2,1)S(1)} %get-tuple-element.91), channel_id=1, source_target_pairs={{0,2},{1,3},{2,0},{3,1},{4,6},{5,7},{6,4},{7,5},{8,10},{9,11},{10,... | collective-permute-start | bytes 786440 | tf_op jit(solution)/shard_map/ppermute | solution.py:21
  45.2 4.0 %collective-permute-start.20 = (bf16[64,2048]{1,0:T(8,128)(2,1)S(1)}, bf16[64,2048]{1,0:T(8,128)(2,1)S(1)}, u32[]{:S(2)}, u32[]{:S(2)}) collective-permute-start(bf16[64,2048]{1,0:T(8,128)(2,1)S(1)} %get-tuple-element.92), channel_id=1, source_target_pairs={{0,1},{1,0},{2,3},{3,2},{4,5},{5,4},{6,7},{7,6},{8,9},{9,8},{10,11... | collective-permute-start | bytes 786440 | tf_op jit(solution)/shard_map/ppermute | solution.py:21
  45.3 3.9 %collective-permute-start.21 = (bf16[64,2048]{1,0:T(8,128)(2,1)S(1)}, bf16[64,2048]{1,0:T(8,128)(2,1)S(1)}, u32[]{:S(2)}, u32[]{:S(2)}) collective-permute-start(bf16[64,2048]{1,0:T(8,128)(2,1)S(1)} %get-tuple-element.93), channel_id=1, source_target_pairs={{0,1},{1,0},{2,3},{3,2},{4,5},{5,4},{6,7},{7,6},{8,9},{9,8},{10,11... | collective-permute-start | bytes 786440 | tf_op jit(solution)/shard_map/ppermute | solution.py:21
  48.1 9.8 %collective-permute-start.17 = (bf16[128,2048]{1,0:T(8,128)(2,1)S(1)}, bf16[128,2048]{1,0:T(8,128)(2,1)S(1)}, u32[]{:S(2)}, u32[]{:S(2)}) collective-permute-start(bf16[128,2048]{1,0:T(8,128)(2,1)S(1)} %get-tuple-element.87), channel_id=1, source_target_pairs={{0,1},{1,0},{2,3},{3,2},{4,5},{5,4},{6,7},{7,6},{8,9},{9,8},{10,11... | collective-permute-start | bytes 1572872 | tf_op jit(solution)/shard_map/ppermute | solution.py:21
  49.3 7.9 %collective-permute-start.22 = (bf16[64,2048]{1,0:T(8,128)(2,1)S(1)}, bf16[64,2048]{1,0:T(8,128)(2,1)S(1)}, u32[]{:S(2)}, u32[]{:S(2)}) collective-permute-start(bf16[64,2048]{1,0:T(8,128)(2,1)S(1)} %get-tuple-element.94), channel_id=1, source_target_pairs={{0,4},{1,5},{2,6},{3,7},{4,0},{5,1},{6,2},{7,3},{8,12},{9,13},{10,... | collective-permute-start | bytes 786440 | tf_op jit(solution)/shard_map/ppermute | solution.py:21
  50.2 7.7 %collective-permute-start.23 = (bf16[64,2048]{1,0:T(8,128)(2,1)S(1)}, bf16[64,2048]{1,0:T(8,128)(2,1)S(1)}, u32[]{:S(2)}, u32[]{:S(2)}) collective-permute-start(bf16[64,2048]{1,0:T(8,128)(2,1)S(1)} %get-tuple-element.96), channel_id=1, source_target_pairs={{0,2},{1,3},{2,0},{3,1},{4,6},{5,7},{6,4},{7,5},{8,10},{9,11},{10,... | collective-permute-start | bytes 786440 | tf_op jit(solution)/shard_map/ppermute | solution.py:21
  (4 other events, 34.8 us)

commit v4 on v0

v4 whole, which is shorter than its diff:
```python
import functools

import jax
import jax.numpy as jnp
from jax import lax
from jax.experimental import pallas as pl
from jax.experimental.pallas import tpu as pltpu
from jax.sharding import PartitionSpec as P

MIB = 2**20
LANES = 128
NT = (((1,), (1,)), ((), ()))
VMEM_SPEC = pl.BlockSpec(memory_space=pltpu.VMEM)
HBM_SPEC = pl.BlockSpec(memory_space=pltpu.HBM)
CORE = 1
LONG = pl.CostEstimate(flops=10**11, bytes_accessed=10**8, transcendentals=0)
COST = pl.CostEstimate(flops=0, bytes_accessed=0, transcendentals=0)


def flip(x, mask):
    n = lax.axis_size("ep")
    return lax.ppermute(x, "ep", [(i, i ^ mask) for i in range(n)])


def cross(x, even, odd):
    n = lax.axis_size("ep")
    return lax.ppermute(x, "ep", [(i, i ^ (odd if i % 2 else even)) for i in range(n)])


def in_vmem(*arrays):
    return [pltpu.with_memory_space_constraint(a, pltpu.VMEM) for a in arrays]


def in_hbm(*arrays):
    return [pltpu.with_memory_space_constraint(a, pltpu.HBM) for a in arrays]


def params(limit=6):
    return pltpu.CompilerParams(vmem_limit_bytes=limit * MIB)


def prepare_kernel(tokens, experts, gates, out, chosen, weight, sems):
    count, width = tokens.shape
    lanes = out.shape[1] - width
    copies = [
        pltpu.make_async_copy(experts, chosen, sems.at[0]),
        pltpu.make_async_copy(gates, weight, sems.at[1]),
        pltpu.make_async_copy(tokens, out.at[:, pl.ds(0, width)], sems.at[2]),
    ]
    for copy in copies:
        copy.start()
    copies[0].wait()
    copies[1].wait()
    ids = lax.broadcasted_iota(jnp.int32, (lanes, count), 0)
    total = jnp.zeros((lanes, count), jnp.float32)
    for k in range(chosen.shape[0]):
        gate = weight[k : k + 1, :].astype(jnp.float32)
        total += jnp.where(ids == chosen[k : k + 1, :], gate, 0.0)
    out[:, width:] = total.T.astype(jnp.bfloat16)
    copies[2].wait()


def prepare(tokens, experts, gates, lanes):
    count, width = tokens.shape
    return pl.pallas_call(
        prepare_kernel,
        in_specs=[HBM_SPEC] * 3,
        out_specs=VMEM_SPEC,
        out_shape=pltpu.VMEM((count, width + lanes), jnp.bfloat16),
        scratch_shapes=[
            pltpu.VMEM(experts.shape[::-1], jnp.int32),
            pltpu.VMEM(gates.shape[::-1], jnp.bfloat16),
            pltpu.SemaphoreType.DMA((3,)),
        ],
        cost_estimate=LONG,
        compiler_params=params(4),
        name="prepare",
    )(*in_hbm(tokens, experts.T, gates.T))


def gather_inputs(parts, rows, held):
    width = rows.shape[1]
    tables, start = [], 0
    for part in parts:
        rows[start : start + part.shape[0]] = part[:, :width]
        tables.append(part[:, width:])
        start += part.shape[0]
    table = jnp.concatenate(tables, axis=0).astype(jnp.float32)
    lane = lax.broadcasted_iota(jnp.int32, table.shape, 1)
    base = lax.axis_index("ep") * held
    return [
        jnp.sum(jnp.where(lane == base + e, table, 0.0), axis=1, keepdims=True) for e in range(held)
    ]


def gated_of(rows, gate_w, weight):
    gate_act = jnp.dot(rows, gate_w, preferred_element_type=jnp.float32)
    return gate_act / (1.0 + jnp.exp(-gate_act)) * weight


def hidden_of(rows, gate_w, up_w, weight):
    up_act = jnp.dot(rows, up_w, preferred_element_type=jnp.float32)
    return (gated_of(rows, gate_w, weight) * up_act).astype(jnp.bfloat16)


def down_all(hidden, w_down, mine, other, tile=512):
    held, width, units = w_down.shape
    count = mine.shape[0]
    for start in range(0, width, tile):
        total = None
        for e in range(held):
            part = lax.dot_general(
                hidden[:, e * units : (e + 1) * units],
                w_down[e, start : start + tile, :],
                NT,
                preferred_element_type=jnp.float32,
            )
            total = part if total is None else total + part
        total = total.astype(jnp.bfloat16)
        mine[:, start : start + tile] = total[:count]
        other[:, start : start + tile] = total[count:]


def gated_kernel(*refs, parts):
    inputs, (w_gate, gated, rows) = refs[:parts], refs[parts:]
    held, _, units = w_gate.shape
    weights = gather_inputs(inputs, rows, held)
    for e in range(held):
        gated[:, e * units : (e + 1) * units] = gated_of(rows[...], w_gate[e], weights[e])


def gated_units(parts, w_gate):
    count = sum(part.shape[0] for part in parts)
    held, width, units = w_gate.shape
    return pl.pallas_call(
        functools.partial(gated_kernel, parts=len(parts)),
        in_specs=[VMEM_SPEC] * (len(parts) + 1),
        out_specs=[VMEM_SPEC] * 2,
        out_shape=[pltpu.VMEM((count, held * units), jnp.float32), pltpu.VMEM((count, width), jnp.bfloat16)],
        cost_estimate=COST,
        compiler_params=params(),
        name="gated_units",
    )(*in_vmem(*parts, w_gate))


def hidden_kernel(gated, rows, w_up, hidden):
    held, _, units = w_up.shape
    for e in range(held):
        block = slice(e * units, (e + 1) * units)
        up_act = jnp.dot(rows[...], w_up[e], preferred_element_type=jnp.float32)
        hidden[:, block] = (gated[:, block] * up_act).astype(jnp.bfloat16)


def hidden_units(gated, rows, w_up):
    return pl.pallas_call(
        hidden_kernel,
        in_specs=[VMEM_SPEC] * 3,
        out_specs=VMEM_SPEC,
        out_shape=pltpu.VMEM(gated.shape, jnp.bfloat16),
        cost_estimate=COST,
        compiler_params=params(),
        name="hidden_units",
    )(*in_vmem(gated, rows, w_up))


def units_kernel(*refs, parts):
    inputs, (w_gate, w_up, hidden, rows) = refs[:parts], refs[parts:]
    held, _, units = w_gate.shape
    weights = gather_inputs(inputs, rows, held)
    for e in range(held):
        hidden[:, e * units : (e + 1) * units] = hidden_of(rows[...], w_gate[e], w_up[e], weights[e])


def units_of(parts, w_gate, w_up):
    count = sum(part.shape[0] for part in parts)
    held, width, units = w_gate.shape
    return pl.pallas_call(
        functools.partial(units_kernel, parts=len(parts)),
        in_specs=[VMEM_SPEC] * (len(parts) + 2),
        out_specs=VMEM_SPEC,
        out_shape=pltpu.VMEM((count, held * units), jnp.bfloat16),
        scratch_shapes=[pltpu.VMEM((count, width), jnp.bfloat16)],
        cost_estimate=COST,
        compiler_params=params(),
        name="units_of",
    )(*in_vmem(*parts, w_gate, w_up))


def rest_kernel(first, part, w_gate, w_up, w_down, mine, other, rows, hidden):
    held, _, units = w_gate.shape
    count = first.shape[0]
    weights = gather_inputs([part], rows, held)
    for e in range(held):
        block = slice(e * units, (e + 1) * units)
        hidden[:count, block] = first[:, block]
        hidden[count:, block] = hidden_of(rows[...], w_gate[e], w_up[e], weights[e])
    down_all(hidden, w_down, mine, other)


def rest_of(first, part, w_gate, w_up, w_down):
    count = part.shape[0]
    held, width, units = w_gate.shape
    return pl.pallas_call(
        rest_kernel,
        in_specs=[VMEM_SPEC] * 5,
        out_specs=[VMEM_SPEC] * 2,
        out_shape=[pltpu.VMEM((count, width), jnp.bfloat16)] * 2,
        scratch_shapes=[
            pltpu.VMEM((count, width), jnp.bfloat16),
            pltpu.VMEM((2 * count, held * units), jnp.bfloat16),
        ],
        cost_estimate=COST,
        compiler_params=params(),
        name="rest_of",
    )(*in_vmem(first, part, w_gate, w_up, w_down))


def down_units(hidden, w_down):
    half = pltpu.VMEM((hidden.shape[0] // 2, w_down.shape[1]), jnp.bfloat16)
    return pl.pallas_call(
        down_all,
        in_specs=[VMEM_SPEC] * 2,
        out_specs=[VMEM_SPEC] * 2,
        out_shape=[half, half],
        cost_estimate=COST,
        compiler_params=params(),
        name="down_units",
    )(*in_vmem(hidden, w_down))


def add_kernel(*refs):
    *parts, out = refs
    width = parts[0].shape[1]
    total = parts[0][...].astype(jnp.float32)
    for part in parts[1:]:
        total += part[:, :width].astype(jnp.float32)
    out[:, :width] = total.astype(out.dtype)
    if out.shape[1] > width:
        out[:, width:] = jnp.zeros((out.shape[0], out.shape[1] - width), out.dtype)


def add(*parts, dtype=jnp.bfloat16, spare=0, cost=COST):
    count, width = parts[0].shape
    return pl.pallas_call(
        add_kernel,
        in_specs=[VMEM_SPEC] * len(parts),
        out_specs=VMEM_SPEC,
        out_shape=pltpu.VMEM((count, width + spare), dtype),
        cost_estimate=cost,
        compiler_params=params(8),
        name="add",
    )(*in_vmem(*parts))


def finish(*parts):
    count, width = parts[0].shape
    return pl.pallas_call(
        add_kernel,
        in_specs=[VMEM_SPEC] * len(parts),
        out_specs=VMEM_SPEC,
        out_shape=jax.ShapeDtypeStruct((count, width), jnp.bfloat16),
        cost_estimate=COST,
        compiler_params=params(8),
        name="finish",
    )(*in_vmem(*parts))


def on_four_chips(own, w_gate, w_up, w_down):
    x, y = 2, 4
    barrier = lax.optimization_barrier
    weights = (w_gate, w_up, w_down)
    near = cross(own, x, y)
    hidden = hidden_units(*gated_units([own, flip(own, CORE)], w_gate), w_up)
    near, hidden = barrier((near, hidden))

    far = cross(near, y, x)
    mine_near, other_near = rest_of(units_of([near], w_gate, w_up), flip(near, CORE), *weights)
    far, own, mine_near = barrier((far, own, mine_near))

    following = cross(own, y, x)
    far_twin = flip(far, CORE)
    sum_near = add(mine_near, flip(other_near, CORE), spare=2 * LANES, cost=LONG)
    sum_near, far_twin = barrier((sum_near, far_twin))
    units = units_of([far, far_twin], w_gate, w_up)
    sum_near, units = barrier((sum_near, units))
    back = cross(sum_near, x, y)
    mine_far, other_far = down_units(units, w_down)
    following, mine_far = barrier((following, mine_far))

    following_twin = flip(following, CORE)
    first = units_of([following], w_gate, w_up)
    mine_far, first = barrier((mine_far, first))
    sum_far = add(mine_far, flip(other_far, CORE))
    sum_far, following_twin, first = barrier((sum_far, following_twin, first))
    relay = cross(sum_far, x, y)
    first, back = barrier((first, back))
    mine_last, other_last = rest_of(first, following_twin, *weights)
    mine_last, hidden = barrier((mine_last, hidden))

    mine_own, other_own = down_units(hidden, w_down)
    mine_last, mine_own = barrier((mine_last, mine_own))
    sum_last = add(add(mine_last, relay, dtype=jnp.float32), flip(other_last, CORE))
    last = cross(sum_last, y, x)
    return finish(mine_own, flip(other_own, CORE), back, last)


def on_any_chips(own, *weights):
    offsets = range(2, lax.axis_size("ep"), 2)
    arrived = [flip(own, d) for d in offsets]
    parts = []
    for d, rows in zip([0, *offsets], [own, *arrived]):
        mine, other = rest_of(units_of([rows], *weights[:2]), flip(rows, CORE), *weights)
        other = flip(other, CORE)
        parts += [flip(add(mine, other), d)] if d else [mine, other]
    return finish(*parts)


def body(tokens, experts, gates, w_gate, w_up, w_down):
    n_ep = lax.axis_size("ep")
    n_experts = w_gate.shape[0] * n_ep
    lanes = -(-n_experts // LANES) * LANES
    own = prepare(tokens, experts, gates, lanes)
    run = on_four_chips if n_ep == 8 else on_any_chips
    return run(own, w_gate, w_up, w_down)


def solution(mesh):
    in_specs = (
        P(("rep", "ep"), None),
        P(("rep", "ep"), None),
        P(("rep", "ep"), None),
        P("ep", None, None),
        P("ep", None, None),
        P("ep", None, None),
    )
    out_specs = P(("rep", "ep"), None)
    return jax.shard_map(body, mesh=mesh, in_specs=in_specs, out_specs=out_specs, check_vma=False)
```

time: 289 us -> 56.8 us (0.20)
  blocking collectives: 99.1 us -> 0 us
  waiting for transfers between devices: 92.7 us -> 12.2 us
  local copies, waits for them, and re-layouts: 41.6 us -> 0.03 us
  matrix products: 36.4 us -> 0 us
  Pallas kernels: 0 us -> 31.2 us
  other arithmetic: 13 us -> 0.01 us
  starting transfers between devices: 5.31 us -> 13 us
    all_to_all x1 -> x0, blocking collectives: 99.1 us -> none  [body(): lax.all_to_all(by_owner, 'ep', split_axis=0, concat_axis=2, tiled=True)]
    all_to_all x1 -> x0, waiting for transfers between devices: 92.7 us -> none  [body(): lax.all_to_all(results[None], 'ep', split_axis=2, concat_axis=0, tiled=True)]
    dot_general x4 -> x0, matrix products: 36.4 us -> none  [the longest x1 16.3 us: run_experts(): jnp.einsum('erf,edf->erd', hidden, down_w, preferred_element_type=jnp.flo...]
    pallas_call x0 -> x15, Pallas kernels: none -> 31.2 us  [the longest x3 9.6 us: units_of(): pl.pallas_call(functools.partial(units_kernel, parts=len(parts)), in_spec...]
    all_to_all x3 -> x0, local copies, waits for them, and re-layouts: 27.8 us -> none  [the longest x2 19.5 us: body(): lax.all_to_all(results[None], 'ep', split_axis=2, concat_axis=0, tiled=True)]
    ppermute x0 -> x14, starting transfers between devices: none -> 13 us  [the longest x6 10.8 us: cross(): lax.ppermute(x, 'ep', [(i, i ^ (odd if i % 2 else even)) for i in range(n)])]
    ppermute x0 -> x14, waiting for transfers between devices: none -> 12.2 us  [the longest x6 12 us: cross(): lax.ppermute(x, 'ep', [(i, i ^ (odd if i % 2 else even)) for i in range(n)])]
    broadcast_in_dim x1 -> x0, local copies, waits for them, and re-layouts: 12.1 us -> none  [body(): results[None]]
  transfers between devices with their start and end apart: 1 -> 14, of which waited for: 1 -> 5; matrix products, arithmetic and copies ran while one was open for 0% -> 0% of each run, Pallas kernels for 0% -> 51%
where the time goes in v4:
time: 56.8 us; the launch traced here: 56.7 us
  Pallas kernels  31.2 us (55%)
  starting transfers between devices  13 us (23%)
  waiting for transfers between devices  12.2 us (21%)
    ppermute x6, waiting for transfers between devices, cross(): lax.ppermute(x, 'ep', [(i, i ^ (odd if i % 2 else even)) for i in range(n)])  12 us
    ppermute x6, starting transfers between devices, cross(): lax.ppermute(x, 'ep', [(i, i ^ (odd if i % 2 else even)) for i in range(n)])  10.8 us
    pallas_call x3, Pallas kernels, units_of(): pl.pallas_call(functools.partial(units_kernel, parts=len(parts)), in_spec...  9.6 us
    pallas_call x2, Pallas kernels, rest_of(): pl.pallas_call(rest_kernel, in_specs=[VMEM_SPEC] * 5, out_specs=[VMEM_SPE...  9.23 us
    pallas_call x2, Pallas kernels, down_units(): pl.pallas_call(down_all, in_specs=[VMEM_SPEC] * 2, out_specs=[VMEM_SPEC]...  4.72 us
    pallas_call x1, Pallas kernels, gated_units(): pl.pallas_call(functools.partial(gated_kernel, parts=len(parts)), in_spec...  2.55 us
    pallas_call x1, Pallas kernels, hidden_units(): pl.pallas_call(hidden_kernel, in_specs=[VMEM_SPEC] * 3, out_specs=VMEM_SP...  2.32 us
    ppermute x8, starting transfers between devices, flip(): return lax.ppermute(x, 'ep', [(i, i ^ mask) for i in range(n)])  2.15 us
  transfers between devices with their start and end apart: 14, of which 5 were waited for; matrix products, arithmetic and copies ran while one was open for 0% of the time, Pallas kernels for 51%

profile of v4, /device:TPU:0, one launch (start us, length us, event | category | flops | bytes accessed | tf_op | source)
XLA Modules:
  0.0 56.7 jit_solution(1991168685826235232)
XLA Ops:
  0.0 1.3 %prepare.1.refs_0_ = bf16[128,2176]{1,0:T(8,128)(2,1)S(1)} custom-call(bf16[128,2048]{1,0:T(8,128)(2,1)} %tokens.1, s32[10,128]{1,0:T(8,128)} %bitcast.6, bf16[10,128]{1,0:T(8,128)(2,1)} %bitcast.7), custom_call_target="tpu_custom_call" | custom-call | flops 99999997952 | bytes 100000000 | tf_op jit(solution)/shard_map/prepare/pallas_call | solution.py:65
  1.3 0.5 collective-permute-start.1
  1.8 2.6 %collective-permute-start = (bf16[128,2176]{1,0:T(8,128)(2,1)S(1)}, bf16[128,2176]{1,0:T(8,128)(2,1)S(1)}, u32[]{:S(2)}, u32[]{:S(2)}) collective-permute-start(bf16[128,2176]{1,0:T(8,128)(2,1)S(1)} %prepare.1.refs_0_), channel_id=1, source_target_pairs={{0,2},{1,5},{2,0},{3,7},{4,6},{5,1},{6,4},{7,3},{8,10},{9,13},{10,... | collective-permute-start | bytes 1671176 | tf_op jit(solution)/shard_map/ppermute | solution.py:27
  4.4 2.6 %gated_units.1 = (f32[256,2048]{1,0:T(8,128)S(1)}, bf16[256,2048]{1,0:T(8,128)(2,1)S(1)}) custom-call(bf16[128,2176]{1,0:T(8,128)(2,1)S(1)} %prepare.1.refs_0_, bf16[128,2176]{1,0:T(8,128)(2,1)S(1)} %collective-permute-done.1.refs_1_, bf16[4,2048,512]{2,1,0:T(8,128)(2,1)S(1)} %copy-done), custom_call_target="tpu_custom_call" | custom-call | tf_op jit(solution)/shard_map/gated_units/pallas_call | solution.py:135
  7.0 2.3 %hidden_units.1.hidden = bf16[256,2048]{1,0:T(8,128)(2,1)S(1)} custom-call(f32[256,2048]{1,0:T(8,128)S(1)} %get-tuple-element.37.gated, bf16[256,2048]{1,0:T(8,128)(2,1)S(1)} %get-tuple-element.38.rows, bf16[4,2048,512]{2,1,0:T(8,128)(2,1)S(1)} %bitcast.3), custom_call_target="tpu_custom_call" | custom-call | tf_op jit(solution)/shard_map/hidden_units/pallas_call | solution.py:155
  9.3 2.6 %collective-permute-done.refs_0_ = bf16[128,2176]{1,0:T(8,128)(2,1)S(1)} collective-permute-done((bf16[128,2176]{1,0:T(8,128)(2,1)S(1)}, bf16[128,2176]{1,0:T(8,128)(2,1)S(1)}, u32[]{:S(2)}, u32[]{:S(2)}) %collective-permute-start) | collective-permute-done | bytes 557088 | tf_op jit(solution)/shard_map/ppermute | solution.py:27
  11.9 2.0 %collective-permute-start.2 = (bf16[128,2176]{1,0:T(8,128)(2,1)S(1)}, bf16[128,2176]{1,0:T(8,128)(2,1)S(1)}, u32[]{:S(2)}, u32[]{:S(2)}) collective-permute-start(bf16[128,2176]{1,0:T(8,128)(2,1)S(1)} %collective-permute-done.refs_0_), channel_id=1, source_target_pairs={{0,4},{1,3},{2,6},{3,1},{4,0},{5,7},{6,2},{7,5},{8,12},{9,11},{10,... | collective-permute-start | bytes 1671176 | tf_op jit(solution)/shard_map/ppermute | solution.py:27
  13.9 2.4 %units_of.3.first = bf16[128,2048]{1,0:T(8,128)(2,1)S(1)} custom-call(bf16[128,2176]{1,0:T(8,128)(2,1)S(1)} %collective-permute-done.refs_0_, bf16[4,2048,512]{2,1,0:T(8,128)(2,1)S(1)} %copy-done, bf16[4,2048,512]{2,1,0:T(8,128)(2,1)S(1)} %bitcast.3), custom_call_target="tpu_custom_call" | custom-call | tf_op jit(solution)/shard_map/units_of/pallas_call | solution.py:177
  16.4 4.6 %rest_of.2 = (bf16[128,2048]{1,0:T(8,128)(2,1)S(1)}, bf16[128,2048]{1,0:T(8,128)(2,1)S(1)}) custom-call(bf16[128,2048]{1,0:T(8,128)(2,1)S(1)} %units_of.3.first, bf16[128,2176]{1,0:T(8,128)(2,1)S(1)} %collective-permute-done.3.part, bf16[4,2048,512]{2,1,0:T(8,128)(2,1)S(1)} %copy-done, bf16[4,2048,512]{2,1,0:T(8,128)(2,1)S(1)} %bitcast.3, ...), custom_call_target="tpu_custom_call" | custom-call | tf_op jit(solution)/shard_map/rest_of/pallas_call | solution.py:203
  21.0 0.3 collective-permute-start.5
  21.6 1.9 %collective-permute-start.4 = (bf16[128,2176]{1,0:T(8,128)(2,1)S(1)}, bf16[128,2176]{1,0:T(8,128)(2,1)S(1)}, u32[]{:S(2)}, u32[]{:S(2)}) collective-permute-start(bf16[128,2176]{1,0:T(8,128)(2,1)S(1)} %prepare.1.refs_0_), channel_id=1, source_target_pairs={{0,4},{1,3},{2,6},{3,1},{4,0},{5,7},{6,2},{7,5},{8,12},{9,11},{10,... | collective-permute-start | bytes 1671176 | tf_op jit(solution)/shard_map/ppermute | solution.py:27
  23.8 4.8 %units_of.4.hidden = bf16[256,2048]{1,0:T(8,128)(2,1)S(1)} custom-call(bf16[128,2176]{1,0:T(8,128)(2,1)S(1)} %collective-permute-done.2.refs_0_, bf16[128,2176]{1,0:T(8,128)(2,1)S(1)} %collective-permute-done.6.refs_1_, bf16[4,2048,512]{2,1,0:T(8,128)(2,1)S(1)} %copy-done, bf16[4,2048,512]{2,1,0:T(8,128)(2,1)S(1)} %bitcast.3), custom_call_target="tpu_custom_call" | custom-call | tf_op jit(solution)/shard_map/units_of/pallas_call | solution.py:177
  28.6 1.7 %collective-permute-start.9 = (bf16[128,2304]{1,0:T(8,128)(2,1)S(1)}, bf16[128,2304]{1,0:T(8,128)(2,1)S(1)}, u32[]{:S(2)}, u32[]{:S(2)}) collective-permute-start(bf16[128,2304]{1,0:T(8,128)(2,1)S(1)} %add.4), channel_id=1, source_target_pairs={{0,2},{1,5},{2,0},{3,7},{4,6},{5,1},{6,4},{7,3},{8,10},{9,13},{10,... | collective-permute-start | bytes 1769480 | tf_op jit(solution)/shard_map/ppermute | solution.py:27
  30.2 2.4 %down_units.2 = (bf16[128,2048]{1,0:T(8,128)(2,1)S(1)}, bf16[128,2048]{1,0:T(8,128)(2,1)S(1)}) custom-call(bf16[256,2048]{1,0:T(8,128)(2,1)S(1)} %units_of.4.hidden, bf16[4,2048,512]{2,1,0:T(8,128)(2,1)S(1)} %bitcast.5), custom_call_target="tpu_custom_call" | custom-call | tf_op jit(solution)/shard_map/down_units/pallas_call | solution.py:220
  32.7 0.5 collective-permute-start.7
  33.2 2.4 %units_of.5.first = bf16[128,2048]{1,0:T(8,128)(2,1)S(1)} custom-call(bf16[128,2176]{1,0:T(8,128)(2,1)S(1)} %collective-permute-done.4.refs_0_, bf16[4,2048,512]{2,1,0:T(8,128)(2,1)S(1)} %copy-done, bf16[4,2048,512]{2,1,0:T(8,128)(2,1)S(1)} %bitcast.3), custom_call_target="tpu_custom_call" | custom-call | tf_op jit(solution)/shard_map/units_of/pallas_call | solution.py:177
  35.8 1.0 %collective-permute-start.11 = (bf16[128,2048]{1,0:T(8,128)(2,1)S(1)}, bf16[128,2048]{1,0:T(8,128)(2,1)S(1)}, u32[]{:S(2)}, u32[]{:S(2)}) collective-permute-start(bf16[128,2048]{1,0:T(8,128)(2,1)S(1)} %add.5), channel_id=1, source_target_pairs={{0,2},{1,5},{2,0},{3,7},{4,6},{5,1},{6,4},{7,3},{8,10},{9,13},{10,... | collective-permute-start | bytes 1572872 | tf_op jit(solution)/shard_map/ppermute | solution.py:27
  36.8 1.8 %collective-permute-done.9.refs_2_ = bf16[128,2304]{1,0:T(8,128)(2,1)S(1)} collective-permute-done((bf16[128,2304]{1,0:T(8,128)(2,1)S(1)}, bf16[128,2304]{1,0:T(8,128)(2,1)S(1)}, u32[]{:S(2)}, u32[]{:S(2)}) %collective-permute-start.9) | collective-permute-done | bytes 589856 | tf_op jit(solution)/shard_map/ppermute | solution.py:27
  38.5 4.6 %rest_of.3 = (bf16[128,2048]{1,0:T(8,128)(2,1)S(1)}, bf16[128,2048]{1,0:T(8,128)(2,1)S(1)}) custom-call(bf16[128,2048]{1,0:T(8,128)(2,1)S(1)} %units_of.5.first, bf16[128,2176]{1,0:T(8,128)(2,1)S(1)} %collective-permute-done.8.part, bf16[4,2048,512]{2,1,0:T(8,128)(2,1)S(1)} %copy-done, bf16[4,2048,512]{2,1,0:T(8,128)(2,1)S(1)} %bitcast.3, ...), custom_call_target="tpu_custom_call" | custom-call | tf_op jit(solution)/shard_map/rest_of/pallas_call | solution.py:203
  43.2 2.4 %down_units.3 = (bf16[128,2048]{1,0:T(8,128)(2,1)S(1)}, bf16[128,2048]{1,0:T(8,128)(2,1)S(1)}) custom-call(bf16[256,2048]{1,0:T(8,128)(2,1)S(1)} %hidden_units.1.hidden, bf16[4,2048,512]{2,1,0:T(8,128)(2,1)S(1)} %bitcast.5), custom_call_target="tpu_custom_call" | custom-call | tf_op jit(solution)/shard_map/down_units/pallas_call | solution.py:220
  45.6 0.6 collective-permute-start.10
  46.4 1.7 %collective-permute-start.13 = (bf16[128,2048]{1,0:T(8,128)(2,1)S(1)}, bf16[128,2048]{1,0:T(8,128)(2,1)S(1)}, u32[]{:S(2)}, u32[]{:S(2)}) collective-permute-start(bf16[128,2048]{1,0:T(8,128)(2,1)S(1)} %add.7), channel_id=1, source_target_pairs={{0,4},{1,3},{2,6},{3,1},{4,0},{5,7},{6,2},{7,5},{8,12},{9,11},{10,... | collective-permute-start | bytes 1572872 | tf_op jit(solution)/shard_map/ppermute | solution.py:27
  48.1 7.5 %collective-permute-done.13.refs_3_ = bf16[128,2048]{1,0:T(8,128)(2,1)S(1)} collective-permute-done((bf16[128,2048]{1,0:T(8,128)(2,1)S(1)}, bf16[128,2048]{1,0:T(8,128)(2,1)S(1)}, u32[]{:S(2)}, u32[]{:S(2)}) %collective-permute-start.13) | collective-permute-done | bytes 524320 | tf_op jit(solution)/shard_map/ppermute | solution.py:27
  55.6 1.0 %finish.1 = bf16[128,2048]{1,0:T(8,128)(2,1)} custom-call(bf16[128,2048]{1,0:T(8,128)(2,1)S(1)} %get-tuple-element.63.refs_0_, bf16[128,2048]{1,0:T(8,128)(2,1)S(1)} %collective-permute-done.10.refs_1_, bf16[128,2304]{1,0:T(8,128)(2,1)S(1)} %collective-permute-done.9.refs_2_, bf16[128,2048]{1,0:T(8,128)(2,1)S(1)} %collective-permute-done.13.refs_3_), custom_call_target="tpu_custom_call" | custom-call | tf_op jit(solution)/shard_map/finish/pallas_call | solution.py:257
  (31 shorter events, 1.1 us)
Async XLA Ops:
  0.0 6.9 %slice-start = ((s8[8388608]{0:T(1024)(128)(4,1)}), s8[4194304]{0:T(1024)(128)(4,1)S(1)}, s32[]{:S(2)}) async-start(s8[8388608]{0:T(1024)(128)(4,1)} %bitcast.2), calls=%async_computation | async-start | bytes 8388608
  0.0 4.4 %copy-start = (bf16[4,2048,512]{2,1,0:T(8,128)(2,1)S(1)}, bf16[4,2048,512]{2,1,0:T(8,128)(2,1)}, u32[]{:S(2)}) copy-start(bf16[4,2048,512]{2,1,0:T(8,128)(2,1)} %w_gate.3) | copy-start | bytes 25165828
  0.0 6.9 %slice-start.1 = ((s8[8388608]{0:T(1024)(128)(4,1)}), s8[4194304]{0:T(1024)(128)(4,1)S(1)}, s32[]{:S(2)}) async-start(s8[8388608]{0:T(1024)(128)(4,1)} %bitcast.2), calls=%async_computation.1 | async-start | bytes 8388608
  1.3 3.1 %collective-permute-start.1 = (bf16[128,2176]{1,0:T(8,128)(2,1)S(1)}, bf16[128,2176]{1,0:T(8,128)(2,1)S(1)}, u32[]{:S(2)}, u32[]{:S(2)}) collective-permute-start(bf16[128,2176]{1,0:T(8,128)(2,1)S(1)} %prepare.1.refs_0_), channel_id=1, source_target_pairs={{0,1},{1,0},{2,3},{3,2},{4,5},{5,4},{6,7},{7,6},{8,9},{9,8},{10,11... | collective-permute-start | bytes 1671176 | tf_op jit(solution)/shard_map/ppermute | solution.py:22
  1.8 10.1 %collective-permute-start = (bf16[128,2176]{1,0:T(8,128)(2,1)S(1)}, bf16[128,2176]{1,0:T(8,128)(2,1)S(1)}, u32[]{:S(2)}, u32[]{:S(2)}) collective-permute-start(bf16[128,2176]{1,0:T(8,128)(2,1)S(1)} %prepare.1.refs_0_), channel_id=1, source_target_pairs={{0,2},{1,5},{2,0},{3,7},{4,6},{5,1},{6,4},{7,3},{8,10},{9,13},{10,... | collective-permute-start | bytes 1671176 | tf_op jit(solution)/shard_map/ppermute | solution.py:27
  7.0 9.4 %slice-start.2 = ((s8[8388608]{0:T(1024)(128)(4,1)}), s8[4194304]{0:T(1024)(128)(4,1)S(1)}, s32[]{:S(2)}) async-start(s8[8388608]{0:T(1024)(128)(4,1)} %bitcast.4), calls=%async_computation.2 | async-start | bytes 8388608
  9.3 7.1 %slice-start.3 = ((s8[8388608]{0:T(1024)(128)(4,1)}), s8[4194304]{0:T(1024)(128)(4,1)S(1)}, s32[]{:S(2)}) async-start(s8[8388608]{0:T(1024)(128)(4,1)} %bitcast.4), calls=%async_computation.3 | async-start | bytes 8388608
  11.9 4.5 %collective-permute-start.3 = (bf16[128,2176]{1,0:T(8,128)(2,1)S(1)}, bf16[128,2176]{1,0:T(8,128)(2,1)S(1)}, u32[]{:S(2)}, u32[]{:S(2)}) collective-permute-start(bf16[128,2176]{1,0:T(8,128)(2,1)S(1)} %collective-permute-done.refs_0_), channel_id=1, source_target_pairs={{0,1},{1,0},{2,3},{3,2},{4,5},{5,4},{6,7},{7,6},{8,9},{9,8},{10,11... | collective-permute-start | bytes 1671176 | tf_op jit(solution)/shard_map/ppermute | solution.py:22
  11.9 9.6 %collective-permute-start.2 = (bf16[128,2176]{1,0:T(8,128)(2,1)S(1)}, bf16[128,2176]{1,0:T(8,128)(2,1)S(1)}, u32[]{:S(2)}, u32[]{:S(2)}) collective-permute-start(bf16[128,2176]{1,0:T(8,128)(2,1)S(1)} %collective-permute-done.refs_0_), channel_id=1, source_target_pairs={{0,4},{1,3},{2,6},{3,1},{4,0},{5,7},{6,2},{7,5},{8,12},{9,11},{10,... | collective-permute-start | bytes 1671176 | tf_op jit(solution)/shard_map/ppermute | solution.py:27
  21.0 2.5 %collective-permute-start.5 = (bf16[128,2048]{1,0:T(8,128)(2,1)S(1)}, bf16[128,2048]{1,0:T(8,128)(2,1)S(1)}, u32[]{:S(2)}, u32[]{:S(2)}) collective-permute-start(bf16[128,2048]{1,0:T(8,128)(2,1)S(1)} %get-tuple-element.43), channel_id=1, source_target_pairs={{0,1},{1,0},{2,3},{3,2},{4,5},{5,4},{6,7},{7,6},{8,9},{9,8},{10,11... | collective-permute-start | bytes 1572872 | tf_op jit(solution)/shard_map/ppermute | solution.py:22
  21.4 2.4 %collective-permute-start.6 = (bf16[128,2176]{1,0:T(8,128)(2,1)S(1)}, bf16[128,2176]{1,0:T(8,128)(2,1)S(1)}, u32[]{:S(2)}, u32[]{:S(2)}) collective-permute-start(bf16[128,2176]{1,0:T(8,128)(2,1)S(1)} %collective-permute-done.2.refs_0_), channel_id=1, source_target_pairs={{0,1},{1,0},{2,3},{3,2},{4,5},{5,4},{6,7},{7,6},{8,9},{9,8},{10,11... | collective-permute-start | bytes 1671176 | tf_op jit(solution)/shard_map/ppermute | solution.py:22
  21.6 11.0 %collective-permute-start.4 = (bf16[128,2176]{1,0:T(8,128)(2,1)S(1)}, bf16[128,2176]{1,0:T(8,128)(2,1)S(1)}, u32[]{:S(2)}, u32[]{:S(2)}) collective-permute-start(bf16[128,2176]{1,0:T(8,128)(2,1)S(1)} %prepare.1.refs_0_), channel_id=1, source_target_pairs={{0,4},{1,3},{2,6},{3,1},{4,0},{5,7},{6,2},{7,5},{8,12},{9,11},{10,... | collective-permute-start | bytes 1671176 | tf_op jit(solution)/shard_map/ppermute | solution.py:27
  28.6 9.9 %collective-permute-start.9 = (bf16[128,2304]{1,0:T(8,128)(2,1)S(1)}, bf16[128,2304]{1,0:T(8,128)(2,1)S(1)}, u32[]{:S(2)}, u32[]{:S(2)}) collective-permute-start(bf16[128,2304]{1,0:T(8,128)(2,1)S(1)} %add.4), channel_id=1, source_target_pairs={{0,2},{1,5},{2,0},{3,7},{4,6},{5,1},{6,4},{7,3},{8,10},{9,13},{10,... | collective-permute-start | bytes 1769480 | tf_op jit(solution)/shard_map/ppermute | solution.py:27
  32.6 3.1 %collective-permute-start.8 = (bf16[128,2176]{1,0:T(8,128)(2,1)S(1)}, bf16[128,2176]{1,0:T(8,128)(2,1)S(1)}, u32[]{:S(2)}, u32[]{:S(2)}) collective-permute-start(bf16[128,2176]{1,0:T(8,128)(2,1)S(1)} %collective-permute-done.4.refs_0_), channel_id=1, source_target_pairs={{0,1},{1,0},{2,3},{3,2},{4,5},{5,4},{6,7},{7,6},{8,9},{9,8},{10,11... | collective-permute-start | bytes 1671176 | tf_op jit(solution)/shard_map/ppermute | solution.py:22
  32.7 2.9 %collective-permute-start.7 = (bf16[128,2048]{1,0:T(8,128)(2,1)S(1)}, bf16[128,2048]{1,0:T(8,128)(2,1)S(1)}, u32[]{:S(2)}, u32[]{:S(2)}) collective-permute-start(bf16[128,2048]{1,0:T(8,128)(2,1)S(1)} %get-tuple-element.52), channel_id=1, source_target_pairs={{0,1},{1,0},{2,3},{3,2},{4,5},{5,4},{6,7},{7,6},{8,9},{9,8},{10,11... | collective-permute-start | bytes 1572872 | tf_op jit(solution)/shard_map/ppermute | solution.py:22
  35.8 10.4 %collective-permute-start.11 = (bf16[128,2048]{1,0:T(8,128)(2,1)S(1)}, bf16[128,2048]{1,0:T(8,128)(2,1)S(1)}, u32[]{:S(2)}, u32[]{:S(2)}) collective-permute-start(bf16[128,2048]{1,0:T(8,128)(2,1)S(1)} %add.5), channel_id=1, source_target_pairs={{0,2},{1,5},{2,0},{3,7},{4,6},{5,1},{6,4},{7,3},{8,10},{9,13},{10,... | collective-permute-start | bytes 1572872 | tf_op jit(solution)/shard_map/ppermute | solution.py:27
  43.1 3.1 %collective-permute-start.12 = (bf16[128,2048]{1,0:T(8,128)(2,1)S(1)}, bf16[128,2048]{1,0:T(8,128)(2,1)S(1)}, u32[]{:S(2)}, u32[]{:S(2)}) collective-permute-start(bf16[128,2048]{1,0:T(8,128)(2,1)S(1)} %get-tuple-element.68), channel_id=1, source_target_pairs={{0,1},{1,0},{2,3},{3,2},{4,5},{5,4},{6,7},{7,6},{8,9},{9,8},{10,11... | collective-permute-start | bytes 1572872 | tf_op jit(solution)/shard_map/ppermute | solution.py:22
  45.6 2.5 %collective-permute-start.10 = (bf16[128,2048]{1,0:T(8,128)(2,1)S(1)}, bf16[128,2048]{1,0:T(8,128)(2,1)S(1)}, u32[]{:S(2)}, u32[]{:S(2)}) collective-permute-start(bf16[128,2048]{1,0:T(8,128)(2,1)S(1)} %get-tuple-element.64), channel_id=1, source_target_pairs={{0,1},{1,0},{2,3},{3,2},{4,5},{5,4},{6,7},{7,6},{8,9},{9,8},{10,11... | collective-permute-start | bytes 1572872 | tf_op jit(solution)/shard_map/ppermute | solution.py:22
  46.4 9.2 %collective-permute-start.13 = (bf16[128,2048]{1,0:T(8,128)(2,1)S(1)}, bf16[128,2048]{1,0:T(8,128)(2,1)S(1)}, u32[]{:S(2)}, u32[]{:S(2)}) collective-permute-start(bf16[128,2048]{1,0:T(8,128)(2,1)S(1)} %add.7), channel_id=1, source_target_pairs={{0,4},{1,3},{2,6},{3,1},{4,0},{5,7},{6,2},{7,5},{8,12},{9,11},{10,... | collective-permute-start | bytes 1572872 | tf_op jit(solution)/shard_map/ppermute | solution.py:27

commit v5 on v4

--- a/solution.py
+++ b/solution.py
@@ -13,6 +13,8 @@
 VMEM_SPEC = pl.BlockSpec(memory_space=pltpu.VMEM)
 HBM_SPEC = pl.BlockSpec(memory_space=pltpu.HBM)
 CORE = 1
+MEDIUM = pl.CostEstimate(flops=0, bytes_accessed=3 * 10**6, transcendentals=0)
+RELAY = pl.CostEstimate(flops=2 * 10**9, bytes_accessed=3 * 10**6, transcendentals=0)
 LONG = pl.CostEstimate(flops=10**11, bytes_accessed=10**8, transcendentals=0)
 COST = pl.CostEstimate(flops=0, bytes_accessed=0, transcendentals=0)
 
@@ -39,13 +41,14 @@
     return pltpu.CompilerParams(vmem_limit_bytes=limit * MIB)
 
 
-def prepare_kernel(tokens, experts, gates, out, chosen, weight, sems):
+def prepare_kernel(tokens, experts, gates, out, wide, chosen, weight, sems):
     count, width = tokens.shape
     lanes = out.shape[1] - width
     copies = [
         pltpu.make_async_copy(experts, chosen, sems.at[0]),
         pltpu.make_async_copy(gates, weight, sems.at[1]),
         pltpu.make_async_copy(tokens, out.at[:, pl.ds(0, width)], sems.at[2]),
+        pltpu.make_async_copy(tokens, wide.at[:, pl.ds(0, width)], sems.at[3]),
     ]
     for copy in copies:
         copy.start()
@@ -56,8 +59,12 @@
     for k in range(chosen.shape[0]):
         gate = weight[k : k + 1, :].astype(jnp.float32)
         total += jnp.where(ids == chosen[k : k + 1, :], gate, 0.0)
-    out[:, width:] = total.T.astype(jnp.bfloat16)
+    table = total.T.astype(jnp.bfloat16)
+    out[:, width:] = table
+    wide[:, width : width + lanes] = table
+    wide[:, width + lanes :] = jnp.zeros((count, wide.shape[1] - width - lanes), jnp.bfloat16)
     copies[2].wait()
+    copies[3].wait()
 
 
 def prepare(tokens, experts, gates, lanes):
@@ -65,12 +72,12 @@
     return pl.pallas_call(
         prepare_kernel,
         in_specs=[HBM_SPEC] * 3,
-        out_specs=VMEM_SPEC,
-        out_shape=pltpu.VMEM((count, width + lanes), jnp.bfloat16),
+        out_specs=[VMEM_SPEC] * 2,
+        out_shape=[pltpu.VMEM((count, width + lanes + spare), jnp.bfloat16) for spare in (0, LANES)],
         scratch_shapes=[
             pltpu.VMEM(experts.shape[::-1], jnp.int32),
             pltpu.VMEM(gates.shape[::-1], jnp.bfloat16),
-            pltpu.SemaphoreType.DMA((3,)),
+            pltpu.SemaphoreType.DMA((4,)),
         ],
         cost_estimate=LONG,
         compiler_params=params(4),
@@ -103,9 +110,9 @@
     return (gated_of(rows, gate_w, weight) * up_act).astype(jnp.bfloat16)
 
 
-def down_all(hidden, w_down, mine, other, tile=512):
+def down_all(hidden, w_down, mine, *others, tile=512):
     held, width, units = w_down.shape
-    count = mine.shape[0]
+    count, piece = mine.shape[0], others[0].shape[0]
     for start in range(0, width, tile):
         total = None
         for e in range(held):
@@ -118,7 +125,9 @@
             total = part if total is None else total + part
         total = total.astype(jnp.bfloat16)
         mine[:, start : start + tile] = total[:count]
-        other[:, start : start + tile] = total[count:]
+        for i, other in enumerate(others):
+            row = count + i * piece
+            other[:, start : start + tile] = total[row : row + piece]
 
 
 def gated_kernel(*refs, parts):
@@ -164,26 +173,26 @@
 
 
 def units_kernel(*refs, parts):
-    inputs, (w_gate, w_up, hidden, rows) = refs[:parts], refs[parts:]
+    inputs, (w_gate, w_up), (hidden, rows) = refs[:parts], refs[parts : parts + 2], refs[-2:]
     held, _, units = w_gate.shape
     weights = gather_inputs(inputs, rows, held)
     for e in range(held):
         hidden[:, e * units : (e + 1) * units] = hidden_of(rows[...], w_gate[e], w_up[e], weights[e])
 
 
-def units_of(parts, w_gate, w_up):
+def units_of(parts, w_gate, w_up, *others):
     count = sum(part.shape[0] for part in parts)
     held, width, units = w_gate.shape
     return pl.pallas_call(
         functools.partial(units_kernel, parts=len(parts)),
-        in_specs=[VMEM_SPEC] * (len(parts) + 2),
+        in_specs=[VMEM_SPEC] * (len(parts) + 2 + len(others)),
         out_specs=VMEM_SPEC,
         out_shape=pltpu.VMEM((count, held * units), jnp.bfloat16),
         scratch_shapes=[pltpu.VMEM((count, width), jnp.bfloat16)],
         cost_estimate=COST,
         compiler_params=params(),
         name="units_of",
-    )(*in_vmem(*parts, w_gate, w_up))
+    )(*in_vmem(*parts, w_gate, w_up, *others))
 
 
 def rest_kernel(first, part, w_gate, w_up, w_down, mine, other, rows, hidden):
@@ -215,6 +224,49 @@
     )(*in_vmem(first, part, w_gate, w_up, w_down))
 
 
+def sums_kernel(first, second, w_down, mine, *refs):
+    *others, hidden = refs
+    count = first.shape[0]
+    hidden[:count] = first[...]
+    hidden[count:] = second[...]
+    down_all(hidden, w_down, mine, *others)
+
+
+def sums_of(first, second, w_down, pieces=1):
+    count, width = first.shape[0], w_down.shape[1]
+    others = [pltpu.VMEM((count // pieces, width), jnp.bfloat16)] * pieces
+    return pl.pallas_call(
+        sums_kernel,
+        in_specs=[VMEM_SPEC] * 3,
+        out_specs=[VMEM_SPEC] * (1 + pieces),
+        out_shape=[pltpu.VMEM((count, width), jnp.bfloat16), *others],
+        scratch_shapes=[pltpu.VMEM((2 * count, first.shape[1]), jnp.bfloat16)],
+        cost_estimate=COST,
+        compiler_params=params(),
+        name="sums_of",
+    )(*in_vmem(first, second, w_down))
+
+
+def join_kernel(mine, *refs):
+    *others, out = refs
+    piece = others[0].shape[0]
+    for i, other in enumerate(others):
+        rows = slice(i * piece, (i + 1) * piece)
+        out[rows] = (mine[rows].astype(jnp.float32) + other[...].astype(jnp.float32)).astype(out.dtype)
+
+
+def add_pieces(mine, others):
+    return pl.pallas_call(
+        join_kernel,
+        in_specs=[VMEM_SPEC] * (1 + len(others)),
+        out_specs=VMEM_SPEC,
+        out_shape=pltpu.VMEM(mine.shape, mine.dtype),
+        cost_estimate=COST,
+        compiler_params=params(8),
+        name="add_pieces",
+    )(*in_vmem(mine, *others))
+
+
 def down_units(hidden, w_down):
     half = pltpu.VMEM((hidden.shape[0] // 2, w_down.shape[1]), jnp.bfloat16)
     return pl.pallas_call(
@@ -252,6 +304,22 @@
     )(*in_vmem(*parts))
 
 
+def trim_kernel(rows, out):
+    out[...] = rows[:, : out.shape[1]]
+
+
+def trim(rows, columns):
+    return pl.pallas_call(
+        trim_kernel,
+        in_specs=[VMEM_SPEC],
+        out_specs=VMEM_SPEC,
+        out_shape=pltpu.VMEM((rows.shape[0], columns), rows.dtype),
+        cost_estimate=COST,
+        compiler_params=params(8),
+        name="trim",
+    )(*in_vmem(rows))
+
+
 def finish(*parts):
     count, width = parts[0].shape
     return pl.pallas_call(
@@ -265,7 +333,7 @@
     )(*in_vmem(*parts))
 
 
-def on_four_chips(own, w_gate, w_up, w_down):
+def on_four_chips(own, wide, w_gate, w_up, w_down):
     x, y = 2, 4
     barrier = lax.optimization_barrier
     weights = (w_gate, w_up, w_down)
@@ -274,37 +342,39 @@
     near, hidden = barrier((near, hidden))
 
     far = cross(near, y, x)
-    mine_near, other_near = rest_of(units_of([near], w_gate, w_up), flip(near, CORE), *weights)
-    far, own, mine_near = barrier((far, own, mine_near))
-
-    following = cross(own, y, x)
+    mine_near, other_near = rest_of(units_of([near], *weights), flip(near, CORE), *weights)
+    following = cross(wide, y, x)
+    far, mine_near = barrier((far, mine_near))
+
     far_twin = flip(far, CORE)
-    sum_near = add(mine_near, flip(other_near, CORE), spare=2 * LANES, cost=LONG)
-    sum_near, far_twin = barrier((sum_near, far_twin))
-    units = units_of([far, far_twin], w_gate, w_up)
-    sum_near, units = barrier((sum_near, units))
+    first = units_of([far], w_gate, w_up)
+    first, far_twin = barrier((first, far_twin))
+    second = units_of([far_twin], w_gate, w_up)
+    mine_near, second = barrier((mine_near, second))
+    sum_near = add(mine_near, flip(other_near, CORE))
     back = cross(sum_near, x, y)
-    mine_far, other_far = down_units(units, w_down)
-    following, mine_far = barrier((following, mine_far))
-
+    following, second = barrier((following, second))
+    mine_far, *other_far = sums_of(first, second, w_down, pieces=2)
+
+    following = trim(following, own.shape[1])
     following_twin = flip(following, CORE)
     first = units_of([following], w_gate, w_up)
     mine_far, first = barrier((mine_far, first))
-    sum_far = add(mine_far, flip(other_far, CORE))
+    sum_far = add_pieces(mine_far, [flip(other, CORE) for other in other_far])
     sum_far, following_twin, first = barrier((sum_far, following_twin, first))
     relay = cross(sum_far, x, y)
-    first, back = barrier((first, back))
-    mine_last, other_last = rest_of(first, following_twin, *weights)
+    second = units_of([following_twin], w_gate, w_up)
+    second, back = barrier((second, back))
+    mine_last, other_last = sums_of(first, second, w_down)
     mine_last, hidden = barrier((mine_last, hidden))
-
     mine_own, other_own = down_units(hidden, w_down)
     mine_last, mine_own = barrier((mine_last, mine_own))
-    sum_last = add(add(mine_last, relay, dtype=jnp.float32), flip(other_last, CORE))
+    sum_last = add(add(mine_last, relay, dtype=jnp.float32, cost=RELAY), flip(other_last, CORE))
     last = cross(sum_last, y, x)
     return finish(mine_own, flip(other_own, CORE), back, last)
 
 
-def on_any_chips(own, *weights):
+def on_any_chips(own, _, *weights):
     offsets = range(2, lax.axis_size("ep"), 2)
     arrived = [flip(own, d) for d in offsets]
     parts = []
@@ -319,9 +389,9 @@
     n_ep = lax.axis_size("ep")
     n_experts = w_gate.shape[0] * n_ep
     lanes = -(-n_experts // LANES) * LANES
-    own = prepare(tokens, experts, gates, lanes)
+    own, wide = prepare(tokens, experts, gates, lanes)
     run = on_four_chips if n_ep == 8 else on_any_chips
-    return run(own, w_gate, w_up, w_down)
+    return run(own, wide, w_gate, w_up, w_down)
 
 
 def solution(mesh):

time: 56.8 us -> 55.7 us (0.981)
  starting transfers between devices: 13 us -> 12 us
    pallas_call x1 -> x5, Pallas kernels: 1.25 us -> 6.3 us  [the longest x2 4.71 us: sums_of(): pl.pallas_call(sums_kernel, in_specs=[VMEM_SPEC] * 3, out_specs=[VMEM_SPE...]
    pallas_call x2 -> x1, Pallas kernels: 9.23 us -> 4.61 us  [rest_of(): pl.pallas_call(rest_kernel, in_specs=[VMEM_SPEC] * 5, out_specs=[VMEM_SPE...]
    pallas_call x3 -> x5, Pallas kernels: 9.6 us -> 12 us  [units_of(): pl.pallas_call(functools.partial(units_kernel, parts=len(parts)), in_spec...]
    pallas_call x2 -> x1, Pallas kernels: 4.72 us -> 2.36 us  [down_units(): pl.pallas_call(down_all, in_specs=[VMEM_SPEC] * 2, out_specs=[VMEM_SPEC]...]
    ppermute x6, starting transfers between devices: 10.8 us -> 9.64 us  [cross(): lax.ppermute(x, 'ep', [(i, i ^ (odd if i % 2 else even)) for i in range(n)])]
    ppermute x8 -> x9, starting transfers between devices: 2.15 us -> 2.33 us  [flip(): return lax.ppermute(x, 'ep', [(i, i ^ mask) for i in range(n)])]
  transfers between devices with their start and end apart: 14 -> 15, of which waited for: 5 -> 6; matrix products, arithmetic and copies ran while one was open for 0% -> 0% of each run, Pallas kernels for 51% -> 52%
where the time goes in v5:
time: 55.7 us; the launch traced here: 55.5 us
  Pallas kernels  31.6 us (57%)
  starting transfers between devices  12 us (22%)
  waiting for transfers between devices  11.7 us (21%)
    pallas_call x5, Pallas kernels, units_of(): pl.pallas_call(functools.partial(units_kernel, parts=len(parts)), in_spec...  12 us
    ppermute x6, waiting for transfers between devices, cross(): lax.ppermute(x, 'ep', [(i, i ^ (odd if i % 2 else even)) for i in range(n)])  11.5 us
    ppermute x6, starting transfers between devices, cross(): lax.ppermute(x, 'ep', [(i, i ^ (odd if i % 2 else even)) for i in range(n)])  9.64 us
    pallas_call x2, Pallas kernels, sums_of(): pl.pallas_call(sums_kernel, in_specs=[VMEM_SPEC] * 3, out_specs=[VMEM_SPE...  4.71 us
    pallas_call x1, Pallas kernels, rest_of(): pl.pallas_call(rest_kernel, in_specs=[VMEM_SPEC] * 5, out_specs=[VMEM_SPE...  4.61 us
    pallas_call x1, Pallas kernels, gated_units(): pl.pallas_call(functools.partial(gated_kernel, parts=len(parts)), in_spec...  2.55 us
    pallas_call x1, Pallas kernels, down_units(): pl.pallas_call(down_all, in_specs=[VMEM_SPEC] * 2, out_specs=[VMEM_SPEC]...  2.36 us
    ppermute x9, starting transfers between devices, flip(): return lax.ppermute(x, 'ep', [(i, i ^ mask) for i in range(n)])  2.33 us
  transfers between devices with their start and end apart: 15, of which 6 were waited for; matrix products, arithmetic and copies ran while one was open for 0% of the time, Pallas kernels for 52%

profile of v5, /device:TPU:0, one launch (start us, length us, event | category | flops | bytes accessed | tf_op | source)
XLA Modules:
  0.0 55.5 jit_solution(9663435184381688625)
XLA Ops:
  0.0 1.4 %prepare.1 = (bf16[128,2176]{1,0:T(8,128)(2,1)S(1)}, bf16[128,2304]{1,0:T(8,128)(2,1)S(1)}) custom-call(bf16[128,2048]{1,0:T(8,128)(2,1)} %tokens.1, s32[10,128]{1,0:T(8,128)} %bitcast.6, bf16[10,128]{1,0:T(8,128)(2,1)} %bitcast.7), custom_call_target="tpu_custom_call" | custom-call | flops 99999997952 | bytes 100000000 | tf_op jit(solution)/shard_map/prepare/pallas_call | solution.py:72
  1.4 0.5 collective-permute-start.1
  2.0 2.6 %collective-permute-start = (bf16[128,2176]{1,0:T(8,128)(2,1)S(1)}, bf16[128,2176]{1,0:T(8,128)(2,1)S(1)}, u32[]{:S(2)}, u32[]{:S(2)}) collective-permute-start(bf16[128,2176]{1,0:T(8,128)(2,1)S(1)} %get-tuple-element.39.refs_0_), channel_id=1, source_target_pairs={{0,2},{1,5},{2,0},{3,7},{4,6},{5,1},{6,4},{7,3},{8,10},{9,13},{10,... | collective-permute-start | bytes 1671176 | tf_op jit(solution)/shard_map/ppermute | solution.py:29
  4.5 2.6 %gated_units.1 = (f32[256,2048]{1,0:T(8,128)S(1)}, bf16[256,2048]{1,0:T(8,128)(2,1)S(1)}) custom-call(bf16[128,2176]{1,0:T(8,128)(2,1)S(1)} %get-tuple-element.39.refs_0_, bf16[128,2176]{1,0:T(8,128)(2,1)S(1)} %collective-permute-done.1.refs_1_, bf16[4,2048,512]{2,1,0:T(8,128)(2,1)S(1)} %copy-done), custom_call_target="tpu_custom_call" | custom-call | tf_op jit(solution)/shard_map/gated_units/pallas_call | solution.py:144
  7.1 2.3 %hidden_units.1.hidden = bf16[256,2048]{1,0:T(8,128)(2,1)S(1)} custom-call(f32[256,2048]{1,0:T(8,128)S(1)} %get-tuple-element.40.gated, bf16[256,2048]{1,0:T(8,128)(2,1)S(1)} %get-tuple-element.41.rows, bf16[4,2048,512]{2,1,0:T(8,128)(2,1)S(1)} %bitcast.3), custom_call_target="tpu_custom_call" | custom-call | tf_op jit(solution)/shard_map/hidden_units/pallas_call | solution.py:164
  9.5 2.6 %collective-permute-done.refs_0_ = bf16[128,2176]{1,0:T(8,128)(2,1)S(1)} collective-permute-done((bf16[128,2176]{1,0:T(8,128)(2,1)S(1)}, bf16[128,2176]{1,0:T(8,128)(2,1)S(1)}, u32[]{:S(2)}, u32[]{:S(2)}) %collective-permute-start) | collective-permute-done | bytes 557088 | tf_op jit(solution)/shard_map/ppermute | solution.py:29
  12.0 2.0 %collective-permute-start.2 = (bf16[128,2176]{1,0:T(8,128)(2,1)S(1)}, bf16[128,2176]{1,0:T(8,128)(2,1)S(1)}, u32[]{:S(2)}, u32[]{:S(2)}) collective-permute-start(bf16[128,2176]{1,0:T(8,128)(2,1)S(1)} %collective-permute-done.refs_0_), channel_id=1, source_target_pairs={{0,4},{1,3},{2,6},{3,1},{4,0},{5,7},{6,2},{7,5},{8,12},{9,11},{10,... | collective-permute-start | bytes 1671176 | tf_op jit(solution)/shard_map/ppermute | solution.py:29
  14.1 2.4 %units_of.5.first = bf16[128,2048]{1,0:T(8,128)(2,1)S(1)} custom-call(bf16[128,2176]{1,0:T(8,128)(2,1)S(1)} %collective-permute-done.refs_0_, bf16[4,2048,512]{2,1,0:T(8,128)(2,1)S(1)} %copy-done, bf16[4,2048,512]{2,1,0:T(8,128)(2,1)S(1)} %bitcast.3, bf16[4,2048,512]{2,1,0:T(8,128)(2,1)S(1)} %bitcast.5), custom_call_target="tpu_custom_call" | custom-call | tf_op jit(solution)/shard_map/units_of/pallas_call | solution.py:186
  16.6 4.6 %rest_of.1 = (bf16[128,2048]{1,0:T(8,128)(2,1)S(1)}, bf16[128,2048]{1,0:T(8,128)(2,1)S(1)}) custom-call(bf16[128,2048]{1,0:T(8,128)(2,1)S(1)} %units_of.5.first, bf16[128,2176]{1,0:T(8,128)(2,1)S(1)} %collective-permute-done.3.part, bf16[4,2048,512]{2,1,0:T(8,128)(2,1)S(1)} %copy-done, bf16[4,2048,512]{2,1,0:T(8,128)(2,1)S(1)} %bitcast.3, ...), custom_call_target="tpu_custom_call" | custom-call | tf_op jit(solution)/shard_map/rest_of/pallas_call | solution.py:212
  21.6 0.5 collective-permute-start.9
  22.1 2.4 %units_of.6.first = bf16[128,2048]{1,0:T(8,128)(2,1)S(1)} custom-call(bf16[128,2176]{1,0:T(8,128)(2,1)S(1)} %collective-permute-done.2.refs_0_, bf16[4,2048,512]{2,1,0:T(8,128)(2,1)S(1)} %copy-done, bf16[4,2048,512]{2,1,0:T(8,128)(2,1)S(1)} %bitcast.3), custom_call_target="tpu_custom_call" | custom-call | tf_op jit(solution)/shard_map/units_of/pallas_call | solution.py:186
  24.7 2.4 %units_of.7.second = bf16[128,2048]{1,0:T(8,128)(2,1)S(1)} custom-call(bf16[128,2176]{1,0:T(8,128)(2,1)S(1)} %collective-permute-done.4.refs_0_, bf16[4,2048,512]{2,1,0:T(8,128)(2,1)S(1)} %copy-done, bf16[4,2048,512]{2,1,0:T(8,128)(2,1)S(1)} %bitcast.3), custom_call_target="tpu_custom_call" | custom-call | tf_op jit(solution)/shard_map/units_of/pallas_call | solution.py:186
  27.1 0.8 %collective-permute-done.5.rows = bf16[128,2304]{1,0:T(8,128)(2,1)S(1)} collective-permute-done((bf16[128,2304]{1,0:T(8,128)(2,1)S(1)}, bf16[128,2304]{1,0:T(8,128)(2,1)S(1)}, u32[]{:S(2)}, u32[]{:S(2)}) %collective-permute-start.5) | collective-permute-done | bytes 589856 | tf_op jit(solution)/shard_map/ppermute | solution.py:29
  28.2 2.1 %collective-permute-start.10 = (bf16[128,2048]{1,0:T(8,128)(2,1)S(1)}, bf16[128,2048]{1,0:T(8,128)(2,1)S(1)}, u32[]{:S(2)}, u32[]{:S(2)}) collective-permute-start(bf16[128,2048]{1,0:T(8,128)(2,1)S(1)} %add.3), channel_id=1, source_target_pairs={{0,2},{1,5},{2,0},{3,7},{4,6},{5,1},{6,4},{7,3},{8,10},{9,13},{10,... | collective-permute-start | bytes 1572872 | tf_op jit(solution)/shard_map/ppermute | solution.py:29
  30.2 2.4 %sums_of.2 = (bf16[128,2048]{1,0:T(8,128)(2,1)S(1)}, bf16[64,2048]{1,0:T(8,128)(2,1)S(1)}, bf16[64,2048]{1,0:T(8,128)(2,1)S(1)}) custom-call(bf16[128,2048]{1,0:T(8,128)(2,1)S(1)} %units_of.6.first, bf16[128,2048]{1,0:T(8,128)(2,1)S(1)} %units_of.7.second, bf16[4,2048,512]{2,1,0:T(8,128)(2,1)S(1)} %bitcast.5), custom_call_target="tpu_custom_call" | custom-call | tf_op jit(solution)/shard_map/sums_of/pallas_call | solution.py:238
  33.2 2.4 %units_of.8.first = bf16[128,2048]{1,0:T(8,128)(2,1)S(1)} custom-call(bf16[128,2176]{1,0:T(8,128)(2,1)S(1)} %trim.1.refs_0_, bf16[4,2048,512]{2,1,0:T(8,128)(2,1)S(1)} %copy-done, bf16[4,2048,512]{2,1,0:T(8,128)(2,1)S(1)} %bitcast.3), custom_call_target="tpu_custom_call" | custom-call | tf_op jit(solution)/shard_map/units_of/pallas_call | solution.py:186
  35.8 1.4 %collective-permute-start.12 = (bf16[128,2048]{1,0:T(8,128)(2,1)S(1)}, bf16[128,2048]{1,0:T(8,128)(2,1)S(1)}, u32[]{:S(2)}, u32[]{:S(2)}) collective-permute-start(bf16[128,2048]{1,0:T(8,128)(2,1)S(1)} %add_pieces.1), channel_id=1, source_target_pairs={{0,2},{1,5},{2,0},{3,7},{4,6},{5,1},{6,4},{7,3},{8,10},{9,13},{10,... | collective-permute-start | bytes 1572872 | tf_op jit(solution)/shard_map/ppermute | solution.py:29
  37.1 2.4 %units_of.9.second = bf16[128,2048]{1,0:T(8,128)(2,1)S(1)} custom-call(bf16[128,2176]{1,0:T(8,128)(2,1)S(1)} %collective-permute-done.8.refs_0_, bf16[4,2048,512]{2,1,0:T(8,128)(2,1)S(1)} %copy-done, bf16[4,2048,512]{2,1,0:T(8,128)(2,1)S(1)} %bitcast.3), custom_call_target="tpu_custom_call" | custom-call | tf_op jit(solution)/shard_map/units_of/pallas_call | solution.py:186
  39.5 2.4 %sums_of.3 = (bf16[128,2048]{1,0:T(8,128)(2,1)S(1)}, bf16[128,2048]{1,0:T(8,128)(2,1)S(1)}) custom-call(bf16[128,2048]{1,0:T(8,128)(2,1)S(1)} %units_of.8.first, bf16[128,2048]{1,0:T(8,128)(2,1)S(1)} %units_of.9.second, bf16[4,2048,512]{2,1,0:T(8,128)(2,1)S(1)} %bitcast.5), custom_call_target="tpu_custom_call" | custom-call | tf_op jit(solution)/shard_map/sums_of/pallas_call | solution.py:238
  42.0 2.4 %down_units.1 = (bf16[128,2048]{1,0:T(8,128)(2,1)S(1)}, bf16[128,2048]{1,0:T(8,128)(2,1)S(1)}) custom-call(bf16[256,2048]{1,0:T(8,128)(2,1)S(1)} %hidden_units.1.hidden, bf16[4,2048,512]{2,1,0:T(8,128)(2,1)S(1)} %bitcast.5), custom_call_target="tpu_custom_call" | custom-call | tf_op jit(solution)/shard_map/down_units/pallas_call | solution.py:272
  44.4 0.6 collective-permute-start.11
  45.2 1.6 %collective-permute-start.14 = (bf16[128,2048]{1,0:T(8,128)(2,1)S(1)}, bf16[128,2048]{1,0:T(8,128)(2,1)S(1)}, u32[]{:S(2)}, u32[]{:S(2)}) collective-permute-start(bf16[128,2048]{1,0:T(8,128)(2,1)S(1)} %add.5), channel_id=1, source_target_pairs={{0,4},{1,3},{2,6},{3,1},{4,0},{5,7},{6,2},{7,5},{8,12},{9,11},{10,... | collective-permute-start | bytes 1572872 | tf_op jit(solution)/shard_map/ppermute | solution.py:29
  46.8 7.7 %collective-permute-done.14.refs_3_ = bf16[128,2048]{1,0:T(8,128)(2,1)S(1)} collective-permute-done((bf16[128,2048]{1,0:T(8,128)(2,1)S(1)}, bf16[128,2048]{1,0:T(8,128)(2,1)S(1)}, u32[]{:S(2)}, u32[]{:S(2)}) %collective-permute-start.14) | collective-permute-done | bytes 524320 | tf_op jit(solution)/shard_map/ppermute | solution.py:29
  54.5 1.0 %finish.1 = bf16[128,2048]{1,0:T(8,128)(2,1)} custom-call(bf16[128,2048]{1,0:T(8,128)(2,1)S(1)} %get-tuple-element.67.refs_0_, bf16[128,2048]{1,0:T(8,128)(2,1)S(1)} %collective-permute-done.11.refs_1_, bf16[128,2048]{1,0:T(8,128)(2,1)S(1)} %collective-permute-done.10.refs_2_, bf16[128,2048]{1,0:T(8,128)(2,1)S(1)} %collective-permute-done.14.refs_3_), custom_call_target="tpu_custom_call" | custom-call | tf_op jit(solution)/shard_map/finish/pallas_call | solution.py:325
  (36 shorter events, 2.0 us)
Async XLA Ops:
  0.0 7.1 %slice-start = ((s8[8388608]{0:T(1024)(128)(4,1)}), s8[4194304]{0:T(1024)(128)(4,1)S(1)}, s32[]{:S(2)}) async-start(s8[8388608]{0:T(1024)(128)(4,1)} %bitcast.2), calls=%async_computation | async-start | bytes 8388608
  0.0 4.5 %copy-start = (bf16[4,2048,512]{2,1,0:T(8,128)(2,1)S(1)}, bf16[4,2048,512]{2,1,0:T(8,128)(2,1)}, u32[]{:S(2)}) copy-start(bf16[4,2048,512]{2,1,0:T(8,128)(2,1)} %refs_1_.9) | copy-start | bytes 25165828
  0.0 7.1 %slice-start.1 = ((s8[8388608]{0:T(1024)(128)(4,1)}), s8[4194304]{0:T(1024)(128)(4,1)S(1)}, s32[]{:S(2)}) async-start(s8[8388608]{0:T(1024)(128)(4,1)} %bitcast.2), calls=%async_computation.1 | async-start | bytes 8388608
  1.4 3.1 %collective-permute-start.1 = (bf16[128,2176]{1,0:T(8,128)(2,1)S(1)}, bf16[128,2176]{1,0:T(8,128)(2,1)S(1)}, u32[]{:S(2)}, u32[]{:S(2)}) collective-permute-start(bf16[128,2176]{1,0:T(8,128)(2,1)S(1)} %get-tuple-element.39.refs_0_), channel_id=1, source_target_pairs={{0,1},{1,0},{2,3},{3,2},{4,5},{5,4},{6,7},{7,6},{8,9},{9,8},{10,11... | collective-permute-start | bytes 1671176 | tf_op jit(solution)/shard_map/ppermute | solution.py:24
  2.0 10.1 %collective-permute-start = (bf16[128,2176]{1,0:T(8,128)(2,1)S(1)}, bf16[128,2176]{1,0:T(8,128)(2,1)S(1)}, u32[]{:S(2)}, u32[]{:S(2)}) collective-permute-start(bf16[128,2176]{1,0:T(8,128)(2,1)S(1)} %get-tuple-element.39.refs_0_), channel_id=1, source_target_pairs={{0,2},{1,5},{2,0},{3,7},{4,6},{5,1},{6,4},{7,3},{8,10},{9,13},{10,... | collective-permute-start | bytes 1671176 | tf_op jit(solution)/shard_map/ppermute | solution.py:29
  4.5 9.6 %slice-start.2 = ((s8[8388608]{0:T(1024)(128)(4,1)}), s8[4194304]{0:T(1024)(128)(4,1)S(1)}, s32[]{:S(2)}) async-start(s8[8388608]{0:T(1024)(128)(4,1)} %bitcast.4), calls=%async_computation.2 | async-start | bytes 8388608
  7.1 7.0 %slice-start.3 = ((s8[8388608]{0:T(1024)(128)(4,1)}), s8[4194304]{0:T(1024)(128)(4,1)S(1)}, s32[]{:S(2)}) async-start(s8[8388608]{0:T(1024)(128)(4,1)} %bitcast.4), calls=%async_computation.3 | async-start | bytes 8388608
  12.0 4.5 %collective-permute-start.3 = (bf16[128,2176]{1,0:T(8,128)(2,1)S(1)}, bf16[128,2176]{1,0:T(8,128)(2,1)S(1)}, u32[]{:S(2)}, u32[]{:S(2)}) collective-permute-start(bf16[128,2176]{1,0:T(8,128)(2,1)S(1)} %collective-permute-done.refs_0_), channel_id=1, source_target_pairs={{0,1},{1,0},{2,3},{3,2},{4,5},{5,4},{6,7},{7,6},{8,9},{9,8},{10,11... | collective-permute-start | bytes 1671176 | tf_op jit(solution)/shard_map/ppermute | solution.py:24
  12.0 9.6 %collective-permute-start.2 = (bf16[128,2176]{1,0:T(8,128)(2,1)S(1)}, bf16[128,2176]{1,0:T(8,128)(2,1)S(1)}, u32[]{:S(2)}, u32[]{:S(2)}) collective-permute-start(bf16[128,2176]{1,0:T(8,128)(2,1)S(1)} %collective-permute-done.refs_0_), channel_id=1, source_target_pairs={{0,4},{1,3},{2,6},{3,1},{4,0},{5,7},{6,2},{7,5},{8,12},{9,11},{10,... | collective-permute-start | bytes 1671176 | tf_op jit(solution)/shard_map/ppermute | solution.py:29
  14.1 13.8 %collective-permute-start.5 = (bf16[128,2304]{1,0:T(8,128)(2,1)S(1)}, bf16[128,2304]{1,0:T(8,128)(2,1)S(1)}, u32[]{:S(2)}, u32[]{:S(2)}) collective-permute-start(bf16[128,2304]{1,0:T(8,128)(2,1)S(1)} %get-tuple-element.46), channel_id=1, source_target_pairs={{0,4},{1,3},{2,6},{3,1},{4,0},{5,7},{6,2},{7,5},{8,12},{9,11},{10,... | collective-permute-start | bytes 1769480 | tf_op jit(solution)/shard_map/ppermute | solution.py:29
  21.6 3.1 %collective-permute-start.4 = (bf16[128,2176]{1,0:T(8,128)(2,1)S(1)}, bf16[128,2176]{1,0:T(8,128)(2,1)S(1)}, u32[]{:S(2)}, u32[]{:S(2)}) collective-permute-start(bf16[128,2176]{1,0:T(8,128)(2,1)S(1)} %collective-permute-done.2.refs_0_), channel_id=1, source_target_pairs={{0,1},{1,0},{2,3},{3,2},{4,5},{5,4},{6,7},{7,6},{8,9},{9,8},{10,11... | collective-permute-start | bytes 1671176 | tf_op jit(solution)/shard_map/ppermute | solution.py:24
  21.6 6.4 %collective-permute-start.9 = (bf16[128,2048]{1,0:T(8,128)(2,1)S(1)}, bf16[128,2048]{1,0:T(8,128)(2,1)S(1)}, u32[]{:S(2)}, u32[]{:S(2)}) collective-permute-start(bf16[128,2048]{1,0:T(8,128)(2,1)S(1)} %get-tuple-element.60), channel_id=1, source_target_pairs={{0,1},{1,0},{2,3},{3,2},{4,5},{5,4},{6,7},{7,6},{8,9},{9,8},{10,11... | collective-permute-start | bytes 1572872 | tf_op jit(solution)/shard_map/ppermute | solution.py:24
  28.0 7.8 %collective-permute-start.8 = (bf16[128,2176]{1,0:T(8,128)(2,1)S(1)}, bf16[128,2176]{1,0:T(8,128)(2,1)S(1)}, u32[]{:S(2)}, u32[]{:S(2)}) collective-permute-start(bf16[128,2176]{1,0:T(8,128)(2,1)S(1)} %trim.1.refs_0_), channel_id=1, source_target_pairs={{0,1},{1,0},{2,3},{3,2},{4,5},{5,4},{6,7},{7,6},{8,9},{9,8},{10,11... | collective-permute-start | bytes 1671176 | tf_op jit(solution)/shard_map/ppermute | solution.py:24
  28.2 11.4 %collective-permute-start.10 = (bf16[128,2048]{1,0:T(8,128)(2,1)S(1)}, bf16[128,2048]{1,0:T(8,128)(2,1)S(1)}, u32[]{:S(2)}, u32[]{:S(2)}) collective-permute-start(bf16[128,2048]{1,0:T(8,128)(2,1)S(1)} %add.3), channel_id=1, source_target_pairs={{0,2},{1,5},{2,0},{3,7},{4,6},{5,1},{6,4},{7,3},{8,10},{9,13},{10,... | collective-permute-start | bytes 1572872 | tf_op jit(solution)/shard_map/ppermute | solution.py:29
  32.6 3.0 %collective-permute-start.6 = (bf16[64,2048]{1,0:T(8,128)(2,1)S(1)}, bf16[64,2048]{1,0:T(8,128)(2,1)S(1)}, u32[]{:S(2)}, u32[]{:S(2)}) collective-permute-start(bf16[64,2048]{1,0:T(8,128)(2,1)S(1)} %get-tuple-element.54), channel_id=1, source_target_pairs={{0,1},{1,0},{2,3},{3,2},{4,5},{5,4},{6,7},{7,6},{8,9},{9,8},{10,11... | collective-permute-start | bytes 786440 | tf_op jit(solution)/shard_map/ppermute | solution.py:24
  32.9 2.7 %collective-permute-start.7 = (bf16[64,2048]{1,0:T(8,128)(2,1)S(1)}, bf16[64,2048]{1,0:T(8,128)(2,1)S(1)}, u32[]{:S(2)}, u32[]{:S(2)}) collective-permute-start(bf16[64,2048]{1,0:T(8,128)(2,1)S(1)} %get-tuple-element.55), channel_id=1, source_target_pairs={{0,1},{1,0},{2,3},{3,2},{4,5},{5,4},{6,7},{7,6},{8,9},{9,8},{10,11... | collective-permute-start | bytes 786440 | tf_op jit(solution)/shard_map/ppermute | solution.py:24
  35.8 9.2 %collective-permute-start.12 = (bf16[128,2048]{1,0:T(8,128)(2,1)S(1)}, bf16[128,2048]{1,0:T(8,128)(2,1)S(1)}, u32[]{:S(2)}, u32[]{:S(2)}) collective-permute-start(bf16[128,2048]{1,0:T(8,128)(2,1)S(1)} %add_pieces.1), channel_id=1, source_target_pairs={{0,2},{1,5},{2,0},{3,7},{4,6},{5,1},{6,4},{7,3},{8,10},{9,13},{10,... | collective-permute-start | bytes 1572872 | tf_op jit(solution)/shard_map/ppermute | solution.py:29
  41.9 3.2 %collective-permute-start.13 = (bf16[128,2048]{1,0:T(8,128)(2,1)S(1)}, bf16[128,2048]{1,0:T(8,128)(2,1)S(1)}, u32[]{:S(2)}, u32[]{:S(2)}) collective-permute-start(bf16[128,2048]{1,0:T(8,128)(2,1)S(1)} %get-tuple-element.72), channel_id=1, source_target_pairs={{0,1},{1,0},{2,3},{3,2},{4,5},{5,4},{6,7},{7,6},{8,9},{9,8},{10,11... | collective-permute-start | bytes 1572872 | tf_op jit(solution)/shard_map/ppermute | solution.py:24
  44.4 2.5 %collective-permute-start.11 = (bf16[128,2048]{1,0:T(8,128)(2,1)S(1)}, bf16[128,2048]{1,0:T(8,128)(2,1)S(1)}, u32[]{:S(2)}, u32[]{:S(2)}) collective-permute-start(bf16[128,2048]{1,0:T(8,128)(2,1)S(1)} %get-tuple-element.68), channel_id=1, source_target_pairs={{0,1},{1,0},{2,3},{3,2},{4,5},{5,4},{6,7},{7,6},{8,9},{9,8},{10,11... | collective-permute-start | bytes 1572872 | tf_op jit(solution)/shard_map/ppermute | solution.py:24
  45.2 9.2 %collective-permute-start.14 = (bf16[128,2048]{1,0:T(8,128)(2,1)S(1)}, bf16[128,2048]{1,0:T(8,128)(2,1)S(1)}, u32[]{:S(2)}, u32[]{:S(2)}) collective-permute-start(bf16[128,2048]{1,0:T(8,128)(2,1)S(1)} %add.5), channel_id=1, source_target_pairs={{0,4},{1,3},{2,6},{3,1},{4,0},{5,7},{6,2},{7,5},{8,12},{9,11},{10,... | collective-permute-start | bytes 1572872 | tf_op jit(solution)/shard_map/ppermute | solution.py:29

commit v6 on v5

--- a/solution.py
+++ b/solution.py
@@ -13,6 +13,8 @@
 VMEM_SPEC = pl.BlockSpec(memory_space=pltpu.VMEM)
 HBM_SPEC = pl.BlockSpec(memory_space=pltpu.HBM)
 CORE = 1
+PACK = 16
+SPARE = 4 * LANES
 MEDIUM = pl.CostEstimate(flops=0, bytes_accessed=3 * 10**6, transcendentals=0)
 RELAY = pl.CostEstimate(flops=2 * 10**9, bytes_accessed=3 * 10**6, transcendentals=0)
 LONG = pl.CostEstimate(flops=10**11, bytes_accessed=10**8, transcendentals=0)
@@ -41,43 +43,56 @@
     return pltpu.CompilerParams(vmem_limit_bytes=limit * MIB)
 
 
-def prepare_kernel(tokens, experts, gates, out, wide, chosen, weight, sems):
+def prepare_kernel(tokens, experts, gates, low, high, table, chosen, weight, sems, *, n_experts):
     count, width = tokens.shape
-    lanes = out.shape[1] - width
+    groups = count // PACK
+    half = groups // 2
     copies = [
         pltpu.make_async_copy(experts, chosen, sems.at[0]),
         pltpu.make_async_copy(gates, weight, sems.at[1]),
-        pltpu.make_async_copy(tokens, out.at[:, pl.ds(0, width)], sems.at[2]),
-        pltpu.make_async_copy(tokens, wide.at[:, pl.ds(0, width)], sems.at[3]),
     ]
+    for j in range(groups):
+        rows = tokens.at[pl.ds(j * PACK, PACK)]
+        place = (low if j < half else high).at[:, pl.ds(j % half * width, width)]
+        copies.append(pltpu.make_async_copy(rows, place, sems.at[2 + j]))
     for copy in copies:
         copy.start()
     copies[0].wait()
     copies[1].wait()
-    ids = lax.broadcasted_iota(jnp.int32, (lanes, count), 0)
-    total = jnp.zeros((lanes, count), jnp.float32)
+    ids = lax.broadcasted_iota(jnp.int32, (-(-n_experts // LANES) * LANES, count), 0)
+    total = jnp.zeros(ids.shape, jnp.float32)
     for k in range(chosen.shape[0]):
         gate = weight[k : k + 1, :].astype(jnp.float32)
         total += jnp.where(ids == chosen[k : k + 1, :], gate, 0.0)
-    table = total.T.astype(jnp.bfloat16)
-    out[:, width:] = table
-    wide[:, width : width + lanes] = table
-    wide[:, width + lanes :] = jnp.zeros((count, wide.shape[1] - width - lanes), jnp.bfloat16)
-    copies[2].wait()
-    copies[3].wait()
-
-
-def prepare(tokens, experts, gates, lanes):
+    total = total.T
+    blocks = [total[j * PACK : (j + 1) * PACK, :n_experts] for j in range(groups)]
+    for out, first, last in ((low, 0, half), (high, half, groups), (table, 0, groups)):
+        start = 0 if out is table else half * width
+        spare = out.shape[1] - start - (last - first) * n_experts
+        values = blocks[first:last] + ([jnp.zeros((PACK, spare), jnp.float32)] if spare else [])
+        out[:, start:] = jnp.concatenate(values, axis=1).astype(jnp.bfloat16)
+    for copy in copies[2:]:
+        copy.wait()
+
+
+def table_lanes(groups, n_experts):
+    return -(-groups * n_experts // LANES) * LANES
+
+
+def prepare(tokens, experts, gates, n_experts):
     count, width = tokens.shape
-    return pl.pallas_call(
-        prepare_kernel,
+    groups = count // PACK
+    half = groups // 2 * width + table_lanes(groups // 2, n_experts)
+    lanes = [half, half, table_lanes(groups, n_experts)]
+    return pl.pallas_call(
+        functools.partial(prepare_kernel, n_experts=n_experts),
         in_specs=[HBM_SPEC] * 3,
-        out_specs=[VMEM_SPEC] * 2,
-        out_shape=[pltpu.VMEM((count, width + lanes + spare), jnp.bfloat16) for spare in (0, LANES)],
+        out_specs=[VMEM_SPEC] * 3,
+        out_shape=[pltpu.VMEM((PACK, size), jnp.bfloat16) for size in lanes],
         scratch_shapes=[
             pltpu.VMEM(experts.shape[::-1], jnp.int32),
             pltpu.VMEM(gates.shape[::-1], jnp.bfloat16),
-            pltpu.SemaphoreType.DMA((4,)),
+            pltpu.SemaphoreType.DMA((2 + groups,)),
         ],
         cost_estimate=LONG,
         compiler_params=params(4),
@@ -85,19 +100,69 @@
     )(*in_hbm(tokens, experts.T, gates.T))
 
 
+def join_kernel(low, high, table, out, *, width):
+    part = low.shape[1] // width * width
+    out[:, :part] = low[:, :part]
+    out[:, part : 2 * part] = high[:, :part]
+    out[:, 2 * part : 2 * part + table.shape[1]] = table[...]
+    if out.shape[1] > 2 * part + table.shape[1]:
+        spare = out.shape[1] - 2 * part - table.shape[1]
+        out[:, 2 * part + table.shape[1] :] = jnp.zeros((PACK, spare), out.dtype)
+
+
+def join(low, high, table, width, spare=0):
+    lanes = low.shape[1] // width * width * 2 + table.shape[1] + spare
+    return pl.pallas_call(
+        functools.partial(join_kernel, width=width),
+        in_specs=[VMEM_SPEC] * 3,
+        out_specs=VMEM_SPEC,
+        out_shape=pltpu.VMEM((PACK, lanes), low.dtype),
+        cost_estimate=COST,
+        compiler_params=params(4),
+        name="join",
+    )(*in_vmem(low, high, table))
+
+
+def pack_kernel(rows, table, out):
+    width = rows.shape[1]
+    for j in range(rows.shape[0] // PACK):
+        out[:, j * width : (j + 1) * width] = rows[j * PACK : (j + 1) * PACK]
+    out[:, rows.shape[0] // PACK * width :] = table[...]
+
+
+def pack(rows, table):
+    return pl.pallas_call(
+        pack_kernel,
+        in_specs=[VMEM_SPEC] * 2,
+        out_specs=VMEM_SPEC,
+        out_shape=pltpu.VMEM((PACK, rows.size // PACK + table.shape[1]), rows.dtype),
+        cost_estimate=COST,
+        compiler_params=params(4),
+        name="pack",
+    )(*in_vmem(rows, table))
+
+
+def rows_in(part, width):
+    return part.shape[1] // width * PACK
+
+
 def gather_inputs(parts, rows, held):
     width = rows.shape[1]
-    tables, start = [], 0
+    n_experts = held * lax.axis_size("ep")
+    base = lax.axis_index("ep") * held
+    columns = [[] for _ in range(held)]
+    start = 0
     for part in parts:
-        rows[start : start + part.shape[0]] = part[:, :width]
-        tables.append(part[:, width:])
-        start += part.shape[0]
-    table = jnp.concatenate(tables, axis=0).astype(jnp.float32)
-    lane = lax.broadcasted_iota(jnp.int32, table.shape, 1)
-    base = lax.axis_index("ep") * held
-    return [
-        jnp.sum(jnp.where(lane == base + e, table, 0.0), axis=1, keepdims=True) for e in range(held)
-    ]
+        groups = part.shape[1] // width
+        table = part[:, groups * width :].astype(jnp.float32)
+        lane = lax.broadcasted_iota(jnp.int32, table.shape, 1)
+        for j in range(groups):
+            rows[start : start + PACK] = part[:, j * width : (j + 1) * width]
+            start += PACK
+            for e in range(held):
+                gate = jnp.where(lane == j * n_experts + base + e, table, 0.0)
+                columns[e].append(jnp.sum(gate, axis=1, keepdims=True))
+    return [jnp.concatenate(column, axis=0) for column in columns]
 
 
 def gated_of(rows, gate_w, weight):
@@ -139,8 +204,8 @@
 
 
 def gated_units(parts, w_gate):
-    count = sum(part.shape[0] for part in parts)
     held, width, units = w_gate.shape
+    count = sum(rows_in(part, width) for part in parts)
     return pl.pallas_call(
         functools.partial(gated_kernel, parts=len(parts)),
         in_specs=[VMEM_SPEC] * (len(parts) + 1),
@@ -181,8 +246,8 @@
 
 
 def units_of(parts, w_gate, w_up, *others):
-    count = sum(part.shape[0] for part in parts)
     held, width, units = w_gate.shape
+    count = sum(rows_in(part, width) for part in parts)
     return pl.pallas_call(
         functools.partial(units_kernel, parts=len(parts)),
         in_specs=[VMEM_SPEC] * (len(parts) + 2 + len(others)),
@@ -207,8 +272,8 @@
 
 
 def rest_of(first, part, w_gate, w_up, w_down):
-    count = part.shape[0]
     held, width, units = w_gate.shape
+    count = rows_in(part, width)
     return pl.pallas_call(
         rest_kernel,
         in_specs=[VMEM_SPEC] * 5,
@@ -247,7 +312,7 @@
     )(*in_vmem(first, second, w_down))
 
 
-def join_kernel(mine, *refs):
+def pieces_kernel(mine, *refs):
     *others, out = refs
     piece = others[0].shape[0]
     for i, other in enumerate(others):
@@ -257,7 +322,7 @@
 
 def add_pieces(mine, others):
     return pl.pallas_call(
-        join_kernel,
+        pieces_kernel,
         in_specs=[VMEM_SPEC] * (1 + len(others)),
         out_specs=VMEM_SPEC,
         out_shape=pltpu.VMEM(mine.shape, mine.dtype),
@@ -267,13 +332,14 @@
     )(*in_vmem(mine, *others))
 
 
-def down_units(hidden, w_down):
-    half = pltpu.VMEM((hidden.shape[0] // 2, w_down.shape[1]), jnp.bfloat16)
+def down_units(hidden, w_down, pieces=1):
+    count, width = hidden.shape[0] // 2, w_down.shape[1]
+    others = [pltpu.VMEM((count // pieces, width), jnp.bfloat16)] * pieces
     return pl.pallas_call(
         down_all,
         in_specs=[VMEM_SPEC] * 2,
-        out_specs=[VMEM_SPEC] * 2,
-        out_shape=[half, half],
+        out_specs=[VMEM_SPEC] * (1 + pieces),
+        out_shape=[pltpu.VMEM((count, width), jnp.bfloat16), *others],
         cost_estimate=COST,
         compiler_params=params(),
         name="down_units",
@@ -304,46 +370,54 @@
     )(*in_vmem(*parts))
 
 
-def trim_kernel(rows, out):
-    out[...] = rows[:, : out.shape[1]]
-
-
-def trim(rows, columns):
-    return pl.pallas_call(
-        trim_kernel,
-        in_specs=[VMEM_SPEC],
-        out_specs=VMEM_SPEC,
-        out_shape=pltpu.VMEM((rows.shape[0], columns), rows.dtype),
-        cost_estimate=COST,
-        compiler_params=params(8),
-        name="trim",
-    )(*in_vmem(rows))
-
-
-def finish(*parts):
+def finish_kernel(*refs, pieces):
+    *parts, out, block, sems = refs
+    twins, parts = parts[:pieces], parts[pieces:]
+    count = block.shape[1]
+    copies = []
+    for i in range(block.shape[0]):
+        start = i * count
+        rows = pl.ds(start, count)
+        size = twins[0].shape[0]
+        total = twins[start // size][pl.ds(start % size, count)].astype(jnp.float32)
+        for part in parts:
+            total += part[rows].astype(jnp.float32)
+        block[i] = total.astype(block.dtype)
+        copies.append(pltpu.make_async_copy(block.at[i], out.at[rows], sems.at[i]))
+        copies[-1].start()
+    for copy in copies:
+        copy.wait()
+
+
+def finish(twins, *parts, blocks=4):
     count, width = parts[0].shape
     return pl.pallas_call(
-        add_kernel,
-        in_specs=[VMEM_SPEC] * len(parts),
-        out_specs=VMEM_SPEC,
+        functools.partial(finish_kernel, pieces=len(twins)),
+        in_specs=[VMEM_SPEC] * (len(twins) + len(parts)),
+        out_specs=HBM_SPEC,
         out_shape=jax.ShapeDtypeStruct((count, width), jnp.bfloat16),
+        scratch_shapes=[
+            pltpu.VMEM((blocks, count // blocks, width), jnp.bfloat16),
+            pltpu.SemaphoreType.DMA((blocks,)),
+        ],
         cost_estimate=COST,
         compiler_params=params(8),
         name="finish",
-    )(*in_vmem(*parts))
-
-
-def on_four_chips(own, wide, w_gate, w_up, w_down):
+    )(*in_vmem(*twins, *parts))
+
+
+def on_four_chips(tokens, low, high, table, w_gate, w_up, w_down):
     x, y = 2, 4
     barrier = lax.optimization_barrier
     weights = (w_gate, w_up, w_down)
-    near = cross(own, x, y)
-    hidden = hidden_units(*gated_units([own, flip(own, CORE)], w_gate), w_up)
-    near, hidden = barrier((near, hidden))
+    near_rows, near_table = cross(tokens, x, y), cross(table, x, y)
+    gated, rows = gated_units([low, high, flip(low, CORE), flip(high, CORE)], w_gate)
+    near_table, near_rows, gated = barrier((near_table, near_rows, gated))
+    near = pack(near_rows, near_table)
 
     far = cross(near, y, x)
     mine_near, other_near = rest_of(units_of([near], *weights), flip(near, CORE), *weights)
-    following = cross(wide, y, x)
+    following = cross(join(low, high, table, tokens.shape[1], SPARE), y, x)
     far, mine_near = barrier((far, mine_near))
 
     far_twin = flip(far, CORE)
@@ -356,7 +430,6 @@
     following, second = barrier((following, second))
     mine_far, *other_far = sums_of(first, second, w_down, pieces=2)
 
-    following = trim(following, own.shape[1])
     following_twin = flip(following, CORE)
     first = units_of([following], w_gate, w_up)
     mine_far, first = barrier((mine_far, first))
@@ -366,15 +439,17 @@
     second = units_of([following_twin], w_gate, w_up)
     second, back = barrier((second, back))
     mine_last, other_last = sums_of(first, second, w_down)
+    mine_last, gated = barrier((mine_last, gated))
+    hidden = hidden_units(gated, rows, w_up)
     mine_last, hidden = barrier((mine_last, hidden))
-    mine_own, other_own = down_units(hidden, w_down)
-    mine_last, mine_own = barrier((mine_last, mine_own))
     sum_last = add(add(mine_last, relay, dtype=jnp.float32, cost=RELAY), flip(other_last, CORE))
     last = cross(sum_last, y, x)
-    return finish(mine_own, flip(other_own, CORE), back, last)
-
-
-def on_any_chips(own, _, *weights):
+    mine_own, *other_own = down_units(hidden, w_down, pieces=2)
+    return finish([flip(other, CORE) for other in other_own], mine_own, back, last)
+
+
+def on_any_chips(tokens, low, high, table, *weights):
+    own = join(low, high, table, tokens.shape[1])
     offsets = range(2, lax.axis_size("ep"), 2)
     arrived = [flip(own, d) for d in offsets]
     parts = []
@@ -382,16 +457,15 @@
         mine, other = rest_of(units_of([rows], *weights[:2]), flip(rows, CORE), *weights)
         other = flip(other, CORE)
         parts += [flip(add(mine, other), d)] if d else [mine, other]
-    return finish(*parts)
+    return finish(parts[:1], *parts[1:])
 
 
 def body(tokens, experts, gates, w_gate, w_up, w_down):
     n_ep = lax.axis_size("ep")
     n_experts = w_gate.shape[0] * n_ep
-    lanes = -(-n_experts // LANES) * LANES
-    own, wide = prepare(tokens, experts, gates, lanes)
+    packed = prepare(tokens, experts, gates, n_experts)
     run = on_four_chips if n_ep == 8 else on_any_chips
-    return run(own, wide, w_gate, w_up, w_down)
+    return run(tokens, *packed, w_gate, w_up, w_down)
 
 
 def solution(mesh):

time: 55.7 us -> 53.5 us (0.961)
  waiting for transfers between devices: 11.7 us -> 7.1 us
  starting transfers between devices: 12 us -> 13.3 us
    ppermute x6 -> x7, waiting for transfers between devices: 11.5 us -> 4.91 us  [cross(): lax.ppermute(x, 'ep', [(i, i ^ (odd if i % 2 else even)) for i in range(n)])]
    ppermute x9 -> x11, waiting for transfers between devices: 0.2 us -> 2.18 us  [flip(): return lax.ppermute(x, 'ep', [(i, i ^ mask) for i in range(n)])]
    ppermute x6 -> x7, starting transfers between devices: 9.64 us -> 10.7 us  [cross(): lax.ppermute(x, 'ep', [(i, i ^ (odd if i % 2 else even)) for i in range(n)])]
    ppermute x9 -> x11, starting transfers between devices: 2.33 us -> 2.65 us  [flip(): return lax.ppermute(x, 'ep', [(i, i ^ mask) for i in range(n)])]
    pallas_call x4 -> x5, Pallas kernels: 2.63 us -> 2.49 us  [the longest x1 1.34 us: prepare(): pl.pallas_call(functools.partial(prepare_kernel, n_experts=n_experts), in...]
  transfers between devices with their start and end apart: 15 -> 18, of which waited for: 6 -> 7; matrix products, arithmetic and copies ran while one was open for 0% -> 0% of each run, Pallas kernels for 52% -> 58%
where the time goes in v6:
time: 53.5 us; the launch traced here: 53.4 us
  Pallas kernels  32.1 us (60%)
  starting transfers between devices  13.3 us (25%)
  waiting for transfers between devices  7.1 us (13%)
    pallas_call x5, Pallas kernels, units_of(): pl.pallas_call(functools.partial(units_kernel, parts=len(parts)), in_spec...  12.6 us
    ppermute x7, starting transfers between devices, cross(): lax.ppermute(x, 'ep', [(i, i ^ (odd if i % 2 else even)) for i in range(n)])  10.7 us
    ppermute x7, waiting for transfers between devices, cross(): lax.ppermute(x, 'ep', [(i, i ^ (odd if i % 2 else even)) for i in range(n)])  4.91 us
    pallas_call x2, Pallas kernels, sums_of(): pl.pallas_call(sums_kernel, in_specs=[VMEM_SPEC] * 3, out_specs=[VMEM_SPE...  4.71 us
    pallas_call x1, Pallas kernels, rest_of(): pl.pallas_call(rest_kernel, in_specs=[VMEM_SPEC] * 5, out_specs=[VMEM_SPE...  4.62 us
    ppermute x11, starting transfers between devices, flip(): return lax.ppermute(x, 'ep', [(i, i ^ mask) for i in range(n)])  2.65 us
    pallas_call x1, Pallas kernels, gated_units(): pl.pallas_call(functools.partial(gated_kernel, parts=len(parts)), in_spec...  2.64 us
    pallas_call x1, Pallas kernels, down_units(): pl.pallas_call(down_all, in_specs=[VMEM_SPEC] * 2, out_specs=[VMEM_SPEC]...  2.36 us
  transfers between devices with their start and end apart: 18, of which 7 were waited for; matrix products, arithmetic and copies ran while one was open for 0% of the time, Pallas kernels for 58%

profile of v6, /device:TPU:0, one launch (start us, length us, event | category | flops | bytes accessed | tf_op | source)
XLA Modules:
  0.0 53.4 jit_solution(10295157541141213941)
XLA Ops:
  0.0 2.9 %collective-permute-start.1 = (bf16[128,2048]{1,0:T(8,128)(2,1)}, bf16[128,2048]{1,0:T(8,128)(2,1)S(1)}, u32[]{:S(2)}, u32[]{:S(2)}) collective-permute-start(bf16[128,2048]{1,0:T(8,128)(2,1)} %tokens.1), channel_id=1, source_target_pairs={{0,2},{1,5},{2,0},{3,7},{4,6},{5,1},{6,4},{7,3},{8,10},{9,13},{10,... | collective-permute-start | bytes 1572872 | tf_op jit(solution)/shard_map/ppermute | solution.py:31
  3.0 1.3 %prepare.1 = (bf16[16,8320]{1,0:T(8,128)(2,1)S(1)}, bf16[16,8320]{1,0:T(8,128)(2,1)S(1)}, bf16[16,256]{1,0:T(8,128)(2,1)S(1)}) custom-call(bf16[128,2048]{1,0:T(8,128)(2,1)} %tokens.1, s32[10,128]{1,0:T(8,128)} %bitcast.6, bf16[10,128]{1,0:T(8,128)(2,1)} %bitcast.7), custom_call_target="tpu_custom_call" | custom-call | flops 99999997952 | bytes 100000000 | tf_op jit(solution)/shard_map/prepare/pallas_call | solution.py:87
  4.4 0.5 collective-permute-start.3
  4.9 0.6 %collective-permute-start = (bf16[16,256]{1,0:T(8,128)(2,1)S(1)}, bf16[16,256]{1,0:T(8,128)(2,1)S(1)}, u32[]{:S(2)}, u32[]{:S(2)}) collective-permute-start(bf16[16,256]{1,0:T(8,128)(2,1)S(1)} %get-tuple-element.42.table), channel_id=1, source_target_pairs={{0,2},{1,5},{2,0},{3,7},{4,6},{5,1},{6,4},{7,3},{8,10},{9,13},{10,... | collective-permute-start | bytes 24584 | tf_op jit(solution)/shard_map/ppermute | solution.py:31
  6.8 2.6 %gated_units.1 = (f32[256,2048]{1,0:T(8,128)S(1)}, bf16[256,2048]{1,0:T(8,128)(2,1)S(1)}) custom-call(bf16[16,8320]{1,0:T(8,128)(2,1)S(1)} %get-tuple-element.43.refs_0_.low, bf16[16,8320]{1,0:T(8,128)(2,1)S(1)} %get-tuple-element.44.refs_1_.high, bf16[16,8320]{1,0:T(8,128)(2,1)S(1)} %collective-permute-done.2.refs_2_, ...), custom_call_target="tpu_custom_call" | custom-call | tf_op jit(solution)/shard_map/gated_units/pallas_call | solution.py:209
  9.4 1.0 %collective-permute-done.table = bf16[16,256]{1,0:T(8,128)(2,1)S(1)} collective-permute-done((bf16[16,256]{1,0:T(8,128)(2,1)S(1)}, bf16[16,256]{1,0:T(8,128)(2,1)S(1)}, u32[]{:S(2)}, u32[]{:S(2)}) %collective-permute-start) | collective-permute-done | bytes 8224 | tf_op jit(solution)/shard_map/ppermute | solution.py:31
  10.5 2.1 %collective-permute-start.4 = (bf16[16,16640]{1,0:T(8,128)(2,1)S(1)}, bf16[16,16640]{1,0:T(8,128)(2,1)S(1)}, u32[]{:S(2)}, u32[]{:S(2)}) collective-permute-start(bf16[16,16640]{1,0:T(8,128)(2,1)S(1)} %pack.1.refs_0_), channel_id=1, source_target_pairs={{0,4},{1,3},{2,6},{3,1},{4,0},{5,7},{6,2},{7,5},{8,12},{9,11},{10,... | collective-permute-start | bytes 1597448 | tf_op jit(solution)/shard_map/ppermute | solution.py:31
  12.8 2.5 %units_of.5.first = bf16[128,2048]{1,0:T(8,128)(2,1)S(1)} custom-call(bf16[16,16640]{1,0:T(8,128)(2,1)S(1)} %pack.1.refs_0_, bf16[4,2048,512]{2,1,0:T(8,128)(2,1)S(1)} %copy-done, bf16[4,2048,512]{2,1,0:T(8,128)(2,1)S(1)} %bitcast.3, bf16[4,2048,512]{2,1,0:T(8,128)(2,1)S(1)} %bitcast.5), custom_call_target="tpu_custom_call" | custom-call | tf_op jit(solution)/shard_map/units_of/pallas_call | solution.py:251
  15.3 4.6 %rest_of.1 = (bf16[128,2048]{1,0:T(8,128)(2,1)S(1)}, bf16[128,2048]{1,0:T(8,128)(2,1)S(1)}) custom-call(bf16[128,2048]{1,0:T(8,128)(2,1)S(1)} %units_of.5.first, bf16[16,16640]{1,0:T(8,128)(2,1)S(1)} %collective-permute-done.5.part, bf16[4,2048,512]{2,1,0:T(8,128)(2,1)S(1)} %copy-done, bf16[4,2048,512]{2,1,0:T(8,128)(2,1)S(1)} %bitcast.3, ...), custom_call_target="tpu_custom_call" | custom-call | tf_op jit(solution)/shard_map/rest_of/pallas_call | solution.py:277
  20.5 2.5 %units_of.6.first = bf16[128,2048]{1,0:T(8,128)(2,1)S(1)} custom-call(bf16[16,16640]{1,0:T(8,128)(2,1)S(1)} %collective-permute-done.4.refs_0_, bf16[4,2048,512]{2,1,0:T(8,128)(2,1)S(1)} %copy-done, bf16[4,2048,512]{2,1,0:T(8,128)(2,1)S(1)} %bitcast.3), custom_call_target="tpu_custom_call" | custom-call | tf_op jit(solution)/shard_map/units_of/pallas_call | solution.py:251
  23.0 2.7 %units_of.7.second = bf16[128,2048]{1,0:T(8,128)(2,1)S(1)} custom-call(bf16[16,16640]{1,0:T(8,128)(2,1)S(1)} %collective-permute-done.6.refs_0_, bf16[4,2048,512]{2,1,0:T(8,128)(2,1)S(1)} %copy-done, bf16[4,2048,512]{2,1,0:T(8,128)(2,1)S(1)} %bitcast.3), custom_call_target="tpu_custom_call" | custom-call | tf_op jit(solution)/shard_map/units_of/pallas_call | solution.py:251
  26.0 2.0 %collective-permute-start.12 = (bf16[128,2048]{1,0:T(8,128)(2,1)S(1)}, bf16[128,2048]{1,0:T(8,128)(2,1)S(1)}, u32[]{:S(2)}, u32[]{:S(2)}) collective-permute-start(bf16[128,2048]{1,0:T(8,128)(2,1)S(1)} %add.3), channel_id=1, source_target_pairs={{0,2},{1,5},{2,0},{3,7},{4,6},{5,1},{6,4},{7,3},{8,10},{9,13},{10,... | collective-permute-start | bytes 1572872 | tf_op jit(solution)/shard_map/ppermute | solution.py:31
  28.0 2.4 %sums_of.2 = (bf16[128,2048]{1,0:T(8,128)(2,1)S(1)}, bf16[64,2048]{1,0:T(8,128)(2,1)S(1)}, bf16[64,2048]{1,0:T(8,128)(2,1)S(1)}) custom-call(bf16[128,2048]{1,0:T(8,128)(2,1)S(1)} %units_of.6.first, bf16[128,2048]{1,0:T(8,128)(2,1)S(1)} %units_of.7.second, bf16[4,2048,512]{2,1,0:T(8,128)(2,1)S(1)} %bitcast.5), custom_call_target="tpu_custom_call" | custom-call | tf_op jit(solution)/shard_map/sums_of/pallas_call | solution.py:303
  30.9 2.5 %units_of.8.first = bf16[128,2048]{1,0:T(8,128)(2,1)S(1)} custom-call(bf16[16,17152]{1,0:T(8,128)(2,1)S(1)} %collective-permute-done.7.refs_0_, bf16[4,2048,512]{2,1,0:T(8,128)(2,1)S(1)} %copy-done, bf16[4,2048,512]{2,1,0:T(8,128)(2,1)S(1)} %bitcast.3), custom_call_target="tpu_custom_call" | custom-call | tf_op jit(solution)/shard_map/units_of/pallas_call | solution.py:251
  33.6 1.3 %collective-permute-start.15 = (bf16[128,2048]{1,0:T(8,128)(2,1)S(1)}, bf16[128,2048]{1,0:T(8,128)(2,1)S(1)}, u32[]{:S(2)}, u32[]{:S(2)}) collective-permute-start(bf16[128,2048]{1,0:T(8,128)(2,1)S(1)} %add_pieces.1), channel_id=1, source_target_pairs={{0,2},{1,5},{2,0},{3,7},{4,6},{5,1},{6,4},{7,3},{8,10},{9,13},{10,... | collective-permute-start | bytes 1572872 | tf_op jit(solution)/shard_map/ppermute | solution.py:31
  34.9 2.5 %units_of.9.second = bf16[128,2048]{1,0:T(8,128)(2,1)S(1)} custom-call(bf16[16,17152]{1,0:T(8,128)(2,1)S(1)} %collective-permute-done.10.refs_0_, bf16[4,2048,512]{2,1,0:T(8,128)(2,1)S(1)} %copy-done, bf16[4,2048,512]{2,1,0:T(8,128)(2,1)S(1)} %bitcast.3), custom_call_target="tpu_custom_call" | custom-call | tf_op jit(solution)/shard_map/units_of/pallas_call | solution.py:251
  37.4 2.4 %sums_of.3 = (bf16[128,2048]{1,0:T(8,128)(2,1)S(1)}, bf16[128,2048]{1,0:T(8,128)(2,1)S(1)}) custom-call(bf16[128,2048]{1,0:T(8,128)(2,1)S(1)} %units_of.8.first, bf16[128,2048]{1,0:T(8,128)(2,1)S(1)} %units_of.9.second, bf16[4,2048,512]{2,1,0:T(8,128)(2,1)S(1)} %bitcast.5), custom_call_target="tpu_custom_call" | custom-call | tf_op jit(solution)/shard_map/sums_of/pallas_call | solution.py:303
  39.9 2.3 %hidden_units.1.hidden = bf16[256,2048]{1,0:T(8,128)(2,1)S(1)} custom-call(f32[256,2048]{1,0:T(8,128)S(1)} %get-tuple-element.69.gated, bf16[256,2048]{1,0:T(8,128)(2,1)S(1)} %get-tuple-element.70.rows, bf16[4,2048,512]{2,1,0:T(8,128)(2,1)S(1)} %bitcast.3), custom_call_target="tpu_custom_call" | custom-call | tf_op jit(solution)/shard_map/hidden_units/pallas_call | solution.py:229
  42.3 0.6 %collective-permute-done.15.refs_1_ = bf16[128,2048]{1,0:T(8,128)(2,1)S(1)} collective-permute-done((bf16[128,2048]{1,0:T(8,128)(2,1)S(1)}, bf16[128,2048]{1,0:T(8,128)(2,1)S(1)}, u32[]{:S(2)}, u32[]{:S(2)}) %collective-permute-start.15) | collective-permute-done | bytes 524320 | tf_op jit(solution)/shard_map/ppermute | solution.py:31
  43.1 1.6 %collective-permute-start.17 = (bf16[128,2048]{1,0:T(8,128)(2,1)S(1)}, bf16[128,2048]{1,0:T(8,128)(2,1)S(1)}, u32[]{:S(2)}, u32[]{:S(2)}) collective-permute-start(bf16[128,2048]{1,0:T(8,128)(2,1)S(1)} %add.5), channel_id=1, source_target_pairs={{0,4},{1,3},{2,6},{3,1},{4,0},{5,7},{6,2},{7,5},{8,12},{9,11},{10,... | collective-permute-start | bytes 1572872 | tf_op jit(solution)/shard_map/ppermute | solution.py:31
  44.7 2.4 %down_units.1 = (bf16[128,2048]{1,0:T(8,128)(2,1)S(1)}, bf16[64,2048]{1,0:T(8,128)(2,1)S(1)}, bf16[64,2048]{1,0:T(8,128)(2,1)S(1)}) custom-call(bf16[256,2048]{1,0:T(8,128)(2,1)S(1)} %hidden_units.1.hidden, bf16[4,2048,512]{2,1,0:T(8,128)(2,1)S(1)} %bitcast.5), custom_call_target="tpu_custom_call" | custom-call | tf_op jit(solution)/shard_map/down_units/pallas_call | solution.py:338
  47.6 1.0 %collective-permute-done.13.refs_0_ = bf16[64,2048]{1,0:T(8,128)(2,1)S(1)} collective-permute-done((bf16[64,2048]{1,0:T(8,128)(2,1)S(1)}, bf16[64,2048]{1,0:T(8,128)(2,1)S(1)}, u32[]{:S(2)}, u32[]{:S(2)}) %collective-permute-start.13) | collective-permute-done | bytes 262176 | tf_op jit(solution)/shard_map/ppermute | solution.py:26
  49.0 3.3 %collective-permute-done.17.refs_4_ = bf16[128,2048]{1,0:T(8,128)(2,1)S(1)} collective-permute-done((bf16[128,2048]{1,0:T(8,128)(2,1)S(1)}, bf16[128,2048]{1,0:T(8,128)(2,1)S(1)}, u32[]{:S(2)}, u32[]{:S(2)}) %collective-permute-start.17) | collective-permute-done | bytes 524320 | tf_op jit(solution)/shard_map/ppermute | solution.py:31
  52.3 0.9 %finish.1 = bf16[128,2048]{1,0:T(8,128)(2,1)} custom-call(bf16[64,2048]{1,0:T(8,128)(2,1)S(1)} %collective-permute-done.13.refs_0_, bf16[64,2048]{1,0:T(8,128)(2,1)S(1)} %collective-permute-done.14.refs_1_, bf16[128,2048]{1,0:T(8,128)(2,1)S(1)} %get-tuple-element.74.refs_2_, bf16[128,2048]{1,0:T(8,128)(2,1)S(1)} %collective-permute-done.12.refs_3_, ...), custom_call_target="tpu_custom_call" | custom-call | tf_op jit(solution)/shard_map/finish/pallas_call | solution.py:394
  (43 shorter events, 4.4 us)
Async XLA Ops:
  0.0 10.4 %collective-permute-start.1 = (bf16[128,2048]{1,0:T(8,128)(2,1)}, bf16[128,2048]{1,0:T(8,128)(2,1)S(1)}, u32[]{:S(2)}, u32[]{:S(2)}) collective-permute-start(bf16[128,2048]{1,0:T(8,128)(2,1)} %tokens.1), channel_id=1, source_target_pairs={{0,2},{1,5},{2,0},{3,7},{4,6},{5,1},{6,4},{7,3},{8,10},{9,13},{10,... | collective-permute-start | bytes 1572872 | tf_op jit(solution)/shard_map/ppermute | solution.py:31
  2.9 9.8 %slice-start = ((s8[8388608]{0:T(1024)(128)(4,1)}), s8[4194304]{0:T(1024)(128)(4,1)S(1)}, s32[]{:S(2)}) async-start(s8[8388608]{0:T(1024)(128)(4,1)} %bitcast.2), calls=%async_computation | async-start | bytes 8388608
  2.9 9.8 %slice-start.2 = ((s8[8388608]{0:T(1024)(128)(4,1)}), s8[4194304]{0:T(1024)(128)(4,1)S(1)}, s32[]{:S(2)}) async-start(s8[8388608]{0:T(1024)(128)(4,1)} %bitcast.4), calls=%async_computation.2 | async-start | bytes 8388608
  2.9 3.8 %copy-start = (bf16[4,2048,512]{2,1,0:T(8,128)(2,1)S(1)}, bf16[4,2048,512]{2,1,0:T(8,128)(2,1)}, u32[]{:S(2)}) copy-start(bf16[4,2048,512]{2,1,0:T(8,128)(2,1)} %refs_1_.9) | copy-start | bytes 25165828
  2.9 9.8 %slice-start.1 = ((s8[8388608]{0:T(1024)(128)(4,1)}), s8[4194304]{0:T(1024)(128)(4,1)S(1)}, s32[]{:S(2)}) async-start(s8[8388608]{0:T(1024)(128)(4,1)} %bitcast.2), calls=%async_computation.1 | async-start | bytes 8388608
  3.0 9.8 %slice-start.3 = ((s8[8388608]{0:T(1024)(128)(4,1)}), s8[4194304]{0:T(1024)(128)(4,1)S(1)}, s32[]{:S(2)}) async-start(s8[8388608]{0:T(1024)(128)(4,1)} %bitcast.4), calls=%async_computation.3 | async-start | bytes 8388608
  4.3 1.6 %collective-permute-start.2 = (bf16[16,8320]{1,0:T(8,128)(2,1)S(1)}, bf16[16,8320]{1,0:T(8,128)(2,1)S(1)}, u32[]{:S(2)}, u32[]{:S(2)}) collective-permute-start(bf16[16,8320]{1,0:T(8,128)(2,1)S(1)} %get-tuple-element.43.refs_0_.low), channel_id=1, source_target_pairs={{0,1},{1,0},{2,3},{3,2},{4,5},{5,4},{6,7},{7,6},{8,9},{9,8},{10,11... | collective-permute-start | bytes 798728 | tf_op jit(solution)/shard_map/ppermute | solution.py:26
  4.4 1.9 %collective-permute-start.3 = (bf16[16,8320]{1,0:T(8,128)(2,1)S(1)}, bf16[16,8320]{1,0:T(8,128)(2,1)S(1)}, u32[]{:S(2)}, u32[]{:S(2)}) collective-permute-start(bf16[16,8320]{1,0:T(8,128)(2,1)S(1)} %get-tuple-element.44.refs_1_.high), channel_id=1, source_target_pairs={{0,1},{1,0},{2,3},{3,2},{4,5},{5,4},{6,7},{7,6},{8,9},{9,8},{10,11... | collective-permute-start | bytes 798728 | tf_op jit(solution)/shard_map/ppermute | solution.py:26
  4.9 5.5 %collective-permute-start = (bf16[16,256]{1,0:T(8,128)(2,1)S(1)}, bf16[16,256]{1,0:T(8,128)(2,1)S(1)}, u32[]{:S(2)}, u32[]{:S(2)}) collective-permute-start(bf16[16,256]{1,0:T(8,128)(2,1)S(1)} %get-tuple-element.42.table), channel_id=1, source_target_pairs={{0,2},{1,5},{2,0},{3,7},{4,6},{5,1},{6,4},{7,3},{8,10},{9,13},{10,... | collective-permute-start | bytes 24584 | tf_op jit(solution)/shard_map/ppermute | solution.py:31
  10.4 4.9 %collective-permute-start.5 = (bf16[16,16640]{1,0:T(8,128)(2,1)S(1)}, bf16[16,16640]{1,0:T(8,128)(2,1)S(1)}, u32[]{:S(2)}, u32[]{:S(2)}) collective-permute-start(bf16[16,16640]{1,0:T(8,128)(2,1)S(1)} %pack.1.refs_0_), channel_id=1, source_target_pairs={{0,1},{1,0},{2,3},{3,2},{4,5},{5,4},{6,7},{7,6},{8,9},{9,8},{10,11... | collective-permute-start | bytes 1597448 | tf_op jit(solution)/shard_map/ppermute | solution.py:26
  10.5 9.4 %collective-permute-start.4 = (bf16[16,16640]{1,0:T(8,128)(2,1)S(1)}, bf16[16,16640]{1,0:T(8,128)(2,1)S(1)}, u32[]{:S(2)}, u32[]{:S(2)}) collective-permute-start(bf16[16,16640]{1,0:T(8,128)(2,1)S(1)} %pack.1.refs_0_), channel_id=1, source_target_pairs={{0,4},{1,3},{2,6},{3,1},{4,0},{5,7},{6,2},{7,5},{8,12},{9,11},{10,... | collective-permute-start | bytes 1597448 | tf_op jit(solution)/shard_map/ppermute | solution.py:31
  12.7 13.1 %collective-permute-start.7 = (bf16[16,17152]{1,0:T(8,128)(2,1)S(1)}, bf16[16,17152]{1,0:T(8,128)(2,1)S(1)}, u32[]{:S(2)}, u32[]{:S(2)}) collective-permute-start(bf16[16,17152]{1,0:T(8,128)(2,1)S(1)} %join.1), channel_id=1, source_target_pairs={{0,4},{1,3},{2,6},{3,1},{4,0},{5,7},{6,2},{7,5},{8,12},{9,11},{10,... | collective-permute-start | bytes 1646600 | tf_op jit(solution)/shard_map/ppermute | solution.py:31
  19.9 3.1 %collective-permute-start.6 = (bf16[16,16640]{1,0:T(8,128)(2,1)S(1)}, bf16[16,16640]{1,0:T(8,128)(2,1)S(1)}, u32[]{:S(2)}, u32[]{:S(2)}) collective-permute-start(bf16[16,16640]{1,0:T(8,128)(2,1)S(1)} %collective-permute-done.4.refs_0_), channel_id=1, source_target_pairs={{0,1},{1,0},{2,3},{3,2},{4,5},{5,4},{6,7},{7,6},{8,9},{9,8},{10,11... | collective-permute-start | bytes 1597448 | tf_op jit(solution)/shard_map/ppermute | solution.py:26
  20.1 5.8 %collective-permute-start.11 = (bf16[128,2048]{1,0:T(8,128)(2,1)S(1)}, bf16[128,2048]{1,0:T(8,128)(2,1)S(1)}, u32[]{:S(2)}, u32[]{:S(2)}) collective-permute-start(bf16[128,2048]{1,0:T(8,128)(2,1)S(1)} %get-tuple-element.64), channel_id=1, source_target_pairs={{0,1},{1,0},{2,3},{3,2},{4,5},{5,4},{6,7},{7,6},{8,9},{9,8},{10,11... | collective-permute-start | bytes 1572872 | tf_op jit(solution)/shard_map/ppermute | solution.py:26
  25.8 7.8 %collective-permute-start.10 = (bf16[16,17152]{1,0:T(8,128)(2,1)S(1)}, bf16[16,17152]{1,0:T(8,128)(2,1)S(1)}, u32[]{:S(2)}, u32[]{:S(2)}) collective-permute-start(bf16[16,17152]{1,0:T(8,128)(2,1)S(1)} %collective-permute-done.7.refs_0_), channel_id=1, source_target_pairs={{0,1},{1,0},{2,3},{3,2},{4,5},{5,4},{6,7},{7,6},{8,9},{9,8},{10,11... | collective-permute-start | bytes 1646600 | tf_op jit(solution)/shard_map/ppermute | solution.py:26
  26.0 11.4 %collective-permute-start.12 = (bf16[128,2048]{1,0:T(8,128)(2,1)S(1)}, bf16[128,2048]{1,0:T(8,128)(2,1)S(1)}, u32[]{:S(2)}, u32[]{:S(2)}) collective-permute-start(bf16[128,2048]{1,0:T(8,128)(2,1)S(1)} %add.3), channel_id=1, source_target_pairs={{0,2},{1,5},{2,0},{3,7},{4,6},{5,1},{6,4},{7,3},{8,10},{9,13},{10,... | collective-permute-start | bytes 1572872 | tf_op jit(solution)/shard_map/ppermute | solution.py:31
  30.4 3.1 %collective-permute-start.8 = (bf16[64,2048]{1,0:T(8,128)(2,1)S(1)}, bf16[64,2048]{1,0:T(8,128)(2,1)S(1)}, u32[]{:S(2)}, u32[]{:S(2)}) collective-permute-start(bf16[64,2048]{1,0:T(8,128)(2,1)S(1)} %get-tuple-element.58), channel_id=1, source_target_pairs={{0,1},{1,0},{2,3},{3,2},{4,5},{5,4},{6,7},{7,6},{8,9},{9,8},{10,11... | collective-permute-start | bytes 786440 | tf_op jit(solution)/shard_map/ppermute | solution.py:26
  30.7 2.8 %collective-permute-start.9 = (bf16[64,2048]{1,0:T(8,128)(2,1)S(1)}, bf16[64,2048]{1,0:T(8,128)(2,1)S(1)}, u32[]{:S(2)}, u32[]{:S(2)}) collective-permute-start(bf16[64,2048]{1,0:T(8,128)(2,1)S(1)} %get-tuple-element.59), channel_id=1, source_target_pairs={{0,1},{1,0},{2,3},{3,2},{4,5},{5,4},{6,7},{7,6},{8,9},{9,8},{10,11... | collective-permute-start | bytes 786440 | tf_op jit(solution)/shard_map/ppermute | solution.py:26
  33.6 9.2 %collective-permute-start.15 = (bf16[128,2048]{1,0:T(8,128)(2,1)S(1)}, bf16[128,2048]{1,0:T(8,128)(2,1)S(1)}, u32[]{:S(2)}, u32[]{:S(2)}) collective-permute-start(bf16[128,2048]{1,0:T(8,128)(2,1)S(1)} %add_pieces.1), channel_id=1, source_target_pairs={{0,2},{1,5},{2,0},{3,7},{4,6},{5,1},{6,4},{7,3},{8,10},{9,13},{10,... | collective-permute-start | bytes 1572872 | tf_op jit(solution)/shard_map/ppermute | solution.py:31
  39.8 3.2 %collective-permute-start.16 = (bf16[128,2048]{1,0:T(8,128)(2,1)S(1)}, bf16[128,2048]{1,0:T(8,128)(2,1)S(1)}, u32[]{:S(2)}, u32[]{:S(2)}) collective-permute-start(bf16[128,2048]{1,0:T(8,128)(2,1)S(1)} %get-tuple-element.78), channel_id=1, source_target_pairs={{0,1},{1,0},{2,3},{3,2},{4,5},{5,4},{6,7},{7,6},{8,9},{9,8},{10,11... | collective-permute-start | bytes 1572872 | tf_op jit(solution)/shard_map/ppermute | solution.py:26
  43.1 9.2 %collective-permute-start.17 = (bf16[128,2048]{1,0:T(8,128)(2,1)S(1)}, bf16[128,2048]{1,0:T(8,128)(2,1)S(1)}, u32[]{:S(2)}, u32[]{:S(2)}) collective-permute-start(bf16[128,2048]{1,0:T(8,128)(2,1)S(1)} %add.5), channel_id=1, source_target_pairs={{0,4},{1,3},{2,6},{3,1},{4,0},{5,7},{6,2},{7,5},{8,12},{9,11},{10,... | collective-permute-start | bytes 1572872 | tf_op jit(solution)/shard_map/ppermute | solution.py:31
  47.0 1.6 %collective-permute-start.13 = (bf16[64,2048]{1,0:T(8,128)(2,1)S(1)}, bf16[64,2048]{1,0:T(8,128)(2,1)S(1)}, u32[]{:S(2)}, u32[]{:S(2)}) collective-permute-start(bf16[64,2048]{1,0:T(8,128)(2,1)S(1)} %get-tuple-element.72), channel_id=1, source_target_pairs={{0,1},{1,0},{2,3},{3,2},{4,5},{5,4},{6,7},{7,6},{8,9},{9,8},{10,11... | collective-permute-start | bytes 786440 | tf_op jit(solution)/shard_map/ppermute | solution.py:26
  47.1 1.9 %collective-permute-start.14 = (bf16[64,2048]{1,0:T(8,128)(2,1)S(1)}, bf16[64,2048]{1,0:T(8,128)(2,1)S(1)}, u32[]{:S(2)}, u32[]{:S(2)}) collective-permute-start(bf16[64,2048]{1,0:T(8,128)(2,1)S(1)} %get-tuple-element.73), channel_id=1, source_target_pairs={{0,1},{1,0},{2,3},{3,2},{4,5},{5,4},{6,7},{7,6},{8,9},{9,8},{10,11... | collective-permute-start | bytes 786440 | tf_op jit(solution)/shard_map/ppermute | solution.py:26

commit v7 on v6

--- a/solution.py
+++ b/solution.py
@@ -14,7 +14,7 @@
 HBM_SPEC = pl.BlockSpec(memory_space=pltpu.HBM)
 CORE = 1
 PACK = 16
-SPARE = 4 * LANES
+SPARE = LANES
 MEDIUM = pl.CostEstimate(flops=0, bytes_accessed=3 * 10**6, transcendentals=0)
 RELAY = pl.CostEstimate(flops=2 * 10**9, bytes_accessed=3 * 10**6, transcendentals=0)
 LONG = pl.CostEstimate(flops=10**11, bytes_accessed=10**8, transcendentals=0)
@@ -167,7 +167,7 @@
 
 def gated_of(rows, gate_w, weight):
     gate_act = jnp.dot(rows, gate_w, preferred_element_type=jnp.float32)
-    return gate_act / (1.0 + jnp.exp(-gate_act)) * weight
+    return gate_act * (0.5 * jnp.tanh(0.5 * gate_act) + 0.5) * weight
 
 
 def hidden_of(rows, gate_w, up_w, weight):

time: 53.5 us -> 53.3 us (level)
  transfers between devices with their start and end apart: 18 -> 18, of which waited for: 7 -> 8; matrix products, arithmetic and copies ran while one was open for 0% -> 0% of each run, Pallas kernels for 58% -> 58%
where the time goes in v7:
time: 53.3 us; the launch traced here: 53.2 us
  Pallas kernels  31.7 us (59%)
  starting transfers between devices  13.2 us (25%)
  waiting for transfers between devices  7.36 us (14%)
    pallas_call x5, Pallas kernels, units_of(): pl.pallas_call(functools.partial(units_kernel, parts=len(parts)), in_spec...  12.3 us
    ppermute x7, starting transfers between devices, cross(): lax.ppermute(x, 'ep', [(i, i ^ (odd if i % 2 else even)) for i in range(n)])  10.8 us
    ppermute x7, waiting for transfers between devices, cross(): lax.ppermute(x, 'ep', [(i, i ^ (odd if i % 2 else even)) for i in range(n)])  5.18 us
    pallas_call x2, Pallas kernels, sums_of(): pl.pallas_call(sums_kernel, in_specs=[VMEM_SPEC] * 3, out_specs=[VMEM_SPE...  4.71 us
    pallas_call x1, Pallas kernels, rest_of(): pl.pallas_call(rest_kernel, in_specs=[VMEM_SPEC] * 5, out_specs=[VMEM_SPE...  4.62 us
    pallas_call x1, Pallas kernels, gated_units(): pl.pallas_call(functools.partial(gated_kernel, parts=len(parts)), in_spec...  2.63 us
    ppermute x11, starting transfers between devices, flip(): return lax.ppermute(x, 'ep', [(i, i ^ mask) for i in range(n)])  2.43 us
    pallas_call x1, Pallas kernels, down_units(): pl.pallas_call(down_all, in_specs=[VMEM_SPEC] * 2, out_specs=[VMEM_SPEC]...  2.36 us
  transfers between devices with their start and end apart: 18, of which 8 were waited for; matrix products, arithmetic and copies ran while one was open for 0% of the time, Pallas kernels for 58%

profile of v7, /device:TPU:0, one launch (start us, length us, event | category | flops | bytes accessed | tf_op | source)
XLA Modules:
  0.0 53.2 jit_solution(5884293071910590855)
XLA Ops:
  0.0 2.9 %collective-permute-start.1 = (bf16[128,2048]{1,0:T(8,128)(2,1)}, bf16[128,2048]{1,0:T(8,128)(2,1)S(1)}, u32[]{:S(2)}, u32[]{:S(2)}) collective-permute-start(bf16[128,2048]{1,0:T(8,128)(2,1)} %tokens.1), channel_id=1, source_target_pairs={{0,2},{1,5},{2,0},{3,7},{4,6},{5,1},{6,4},{7,3},{8,10},{9,13},{10,... | collective-permute-start | bytes 1572872 | tf_op jit(solution)/shard_map/ppermute | solution.py:31
  3.0 1.3 %prepare.1 = (bf16[16,8320]{1,0:T(8,128)(2,1)S(1)}, bf16[16,8320]{1,0:T(8,128)(2,1)S(1)}, bf16[16,256]{1,0:T(8,128)(2,1)S(1)}) custom-call(bf16[128,2048]{1,0:T(8,128)(2,1)} %tokens.1, s32[10,128]{1,0:T(8,128)} %bitcast.6, bf16[10,128]{1,0:T(8,128)(2,1)} %bitcast.7), custom_call_target="tpu_custom_call" | custom-call | flops 99999997952 | bytes 100000000 | tf_op jit(solution)/shard_map/prepare/pallas_call | solution.py:87
  4.9 0.6 %collective-permute-start = (bf16[16,256]{1,0:T(8,128)(2,1)S(1)}, bf16[16,256]{1,0:T(8,128)(2,1)S(1)}, u32[]{:S(2)}, u32[]{:S(2)}) collective-permute-start(bf16[16,256]{1,0:T(8,128)(2,1)S(1)} %get-tuple-element.42.table), channel_id=1, source_target_pairs={{0,2},{1,5},{2,0},{3,7},{4,6},{5,1},{6,4},{7,3},{8,10},{9,13},{10,... | collective-permute-start | bytes 24584 | tf_op jit(solution)/shard_map/ppermute | solution.py:31
  6.8 2.6 %gated_units.1 = (f32[256,2048]{1,0:T(8,128)S(1)}, bf16[256,2048]{1,0:T(8,128)(2,1)S(1)}) custom-call(bf16[16,8320]{1,0:T(8,128)(2,1)S(1)} %get-tuple-element.43.refs_0_.low, bf16[16,8320]{1,0:T(8,128)(2,1)S(1)} %get-tuple-element.44.refs_1_.high, bf16[16,8320]{1,0:T(8,128)(2,1)S(1)} %collective-permute-done.2.refs_2_, ...), custom_call_target="tpu_custom_call" | custom-call | tf_op jit(solution)/shard_map/gated_units/pallas_call | solution.py:209
  9.4 1.0 %collective-permute-done.table = bf16[16,256]{1,0:T(8,128)(2,1)S(1)} collective-permute-done((bf16[16,256]{1,0:T(8,128)(2,1)S(1)}, bf16[16,256]{1,0:T(8,128)(2,1)S(1)}, u32[]{:S(2)}, u32[]{:S(2)}) %collective-permute-start) | collective-permute-done | bytes 8224 | tf_op jit(solution)/shard_map/ppermute | solution.py:31
  10.5 2.1 %collective-permute-start.4 = (bf16[16,16640]{1,0:T(8,128)(2,1)S(1)}, bf16[16,16640]{1,0:T(8,128)(2,1)S(1)}, u32[]{:S(2)}, u32[]{:S(2)}) collective-permute-start(bf16[16,16640]{1,0:T(8,128)(2,1)S(1)} %pack.1.refs_0_), channel_id=1, source_target_pairs={{0,4},{1,3},{2,6},{3,1},{4,0},{5,7},{6,2},{7,5},{8,12},{9,11},{10,... | collective-permute-start | bytes 1597448 | tf_op jit(solution)/shard_map/ppermute | solution.py:31
  12.8 2.4 %units_of.5.first = bf16[128,2048]{1,0:T(8,128)(2,1)S(1)} custom-call(bf16[16,16640]{1,0:T(8,128)(2,1)S(1)} %pack.1.refs_0_, bf16[4,2048,512]{2,1,0:T(8,128)(2,1)S(1)} %copy-done, bf16[4,2048,512]{2,1,0:T(8,128)(2,1)S(1)} %bitcast.3, bf16[4,2048,512]{2,1,0:T(8,128)(2,1)S(1)} %bitcast.5), custom_call_target="tpu_custom_call" | custom-call | tf_op jit(solution)/shard_map/units_of/pallas_call | solution.py:251
  15.2 4.6 %rest_of.1 = (bf16[128,2048]{1,0:T(8,128)(2,1)S(1)}, bf16[128,2048]{1,0:T(8,128)(2,1)S(1)}) custom-call(bf16[128,2048]{1,0:T(8,128)(2,1)S(1)} %units_of.5.first, bf16[16,16640]{1,0:T(8,128)(2,1)S(1)} %collective-permute-done.5.part, bf16[4,2048,512]{2,1,0:T(8,128)(2,1)S(1)} %copy-done, bf16[4,2048,512]{2,1,0:T(8,128)(2,1)S(1)} %bitcast.3, ...), custom_call_target="tpu_custom_call" | custom-call | tf_op jit(solution)/shard_map/rest_of/pallas_call | solution.py:277
  20.4 2.4 %units_of.6.first = bf16[128,2048]{1,0:T(8,128)(2,1)S(1)} custom-call(bf16[16,16640]{1,0:T(8,128)(2,1)S(1)} %collective-permute-done.4.refs_0_, bf16[4,2048,512]{2,1,0:T(8,128)(2,1)S(1)} %copy-done, bf16[4,2048,512]{2,1,0:T(8,128)(2,1)S(1)} %bitcast.3), custom_call_target="tpu_custom_call" | custom-call | tf_op jit(solution)/shard_map/units_of/pallas_call | solution.py:251
  22.9 2.6 %units_of.7.second = bf16[128,2048]{1,0:T(8,128)(2,1)S(1)} custom-call(bf16[16,16640]{1,0:T(8,128)(2,1)S(1)} %collective-permute-done.6.refs_0_, bf16[4,2048,512]{2,1,0:T(8,128)(2,1)S(1)} %copy-done, bf16[4,2048,512]{2,1,0:T(8,128)(2,1)S(1)} %bitcast.3), custom_call_target="tpu_custom_call" | custom-call | tf_op jit(solution)/shard_map/units_of/pallas_call | solution.py:251
  25.8 2.0 %collective-permute-start.12 = (bf16[128,2048]{1,0:T(8,128)(2,1)S(1)}, bf16[128,2048]{1,0:T(8,128)(2,1)S(1)}, u32[]{:S(2)}, u32[]{:S(2)}) collective-permute-start(bf16[128,2048]{1,0:T(8,128)(2,1)S(1)} %add.3), channel_id=1, source_target_pairs={{0,2},{1,5},{2,0},{3,7},{4,6},{5,1},{6,4},{7,3},{8,10},{9,13},{10,... | collective-permute-start | bytes 1572872 | tf_op jit(solution)/shard_map/ppermute | solution.py:31
  27.8 2.4 %sums_of.2 = (bf16[128,2048]{1,0:T(8,128)(2,1)S(1)}, bf16[64,2048]{1,0:T(8,128)(2,1)S(1)}, bf16[64,2048]{1,0:T(8,128)(2,1)S(1)}) custom-call(bf16[128,2048]{1,0:T(8,128)(2,1)S(1)} %units_of.6.first, bf16[128,2048]{1,0:T(8,128)(2,1)S(1)} %units_of.7.second, bf16[4,2048,512]{2,1,0:T(8,128)(2,1)S(1)} %bitcast.5), custom_call_target="tpu_custom_call" | custom-call | tf_op jit(solution)/shard_map/sums_of/pallas_call | solution.py:303
  30.8 2.5 %units_of.8.first = bf16[128,2048]{1,0:T(8,128)(2,1)S(1)} custom-call(bf16[16,16768]{1,0:T(8,128)(2,1)S(1)} %collective-permute-done.7.refs_0_, bf16[4,2048,512]{2,1,0:T(8,128)(2,1)S(1)} %copy-done, bf16[4,2048,512]{2,1,0:T(8,128)(2,1)S(1)} %bitcast.3), custom_call_target="tpu_custom_call" | custom-call | tf_op jit(solution)/shard_map/units_of/pallas_call | solution.py:251
  33.4 1.4 %collective-permute-start.15 = (bf16[128,2048]{1,0:T(8,128)(2,1)S(1)}, bf16[128,2048]{1,0:T(8,128)(2,1)S(1)}, u32[]{:S(2)}, u32[]{:S(2)}) collective-permute-start(bf16[128,2048]{1,0:T(8,128)(2,1)S(1)} %add_pieces.1), channel_id=1, source_target_pairs={{0,2},{1,5},{2,0},{3,7},{4,6},{5,1},{6,4},{7,3},{8,10},{9,13},{10,... | collective-permute-start | bytes 1572872 | tf_op jit(solution)/shard_map/ppermute | solution.py:31
  34.8 2.4 %units_of.9.second = bf16[128,2048]{1,0:T(8,128)(2,1)S(1)} custom-call(bf16[16,16768]{1,0:T(8,128)(2,1)S(1)} %collective-permute-done.10.refs_0_, bf16[4,2048,512]{2,1,0:T(8,128)(2,1)S(1)} %copy-done, bf16[4,2048,512]{2,1,0:T(8,128)(2,1)S(1)} %bitcast.3), custom_call_target="tpu_custom_call" | custom-call | tf_op jit(solution)/shard_map/units_of/pallas_call | solution.py:251
  37.2 2.4 %sums_of.3 = (bf16[128,2048]{1,0:T(8,128)(2,1)S(1)}, bf16[128,2048]{1,0:T(8,128)(2,1)S(1)}) custom-call(bf16[128,2048]{1,0:T(8,128)(2,1)S(1)} %units_of.8.first, bf16[128,2048]{1,0:T(8,128)(2,1)S(1)} %units_of.9.second, bf16[4,2048,512]{2,1,0:T(8,128)(2,1)S(1)} %bitcast.5), custom_call_target="tpu_custom_call" | custom-call | tf_op jit(solution)/shard_map/sums_of/pallas_call | solution.py:303
  39.7 2.3 %hidden_units.1.hidden = bf16[256,2048]{1,0:T(8,128)(2,1)S(1)} custom-call(f32[256,2048]{1,0:T(8,128)S(1)} %get-tuple-element.69.gated, bf16[256,2048]{1,0:T(8,128)(2,1)S(1)} %get-tuple-element.70.rows, bf16[4,2048,512]{2,1,0:T(8,128)(2,1)S(1)} %bitcast.3), custom_call_target="tpu_custom_call" | custom-call | tf_op jit(solution)/shard_map/hidden_units/pallas_call | solution.py:229
  42.0 0.6 %collective-permute-done.15.refs_1_ = bf16[128,2048]{1,0:T(8,128)(2,1)S(1)} collective-permute-done((bf16[128,2048]{1,0:T(8,128)(2,1)S(1)}, bf16[128,2048]{1,0:T(8,128)(2,1)S(1)}, u32[]{:S(2)}, u32[]{:S(2)}) %collective-permute-start.15) | collective-permute-done | bytes 524320 | tf_op jit(solution)/shard_map/ppermute | solution.py:31
  42.8 1.6 %collective-permute-start.17 = (bf16[128,2048]{1,0:T(8,128)(2,1)S(1)}, bf16[128,2048]{1,0:T(8,128)(2,1)S(1)}, u32[]{:S(2)}, u32[]{:S(2)}) collective-permute-start(bf16[128,2048]{1,0:T(8,128)(2,1)S(1)} %add.5), channel_id=1, source_target_pairs={{0,4},{1,3},{2,6},{3,1},{4,0},{5,7},{6,2},{7,5},{8,12},{9,11},{10,... | collective-permute-start | bytes 1572872 | tf_op jit(solution)/shard_map/ppermute | solution.py:31
  44.4 2.4 %down_units.1 = (bf16[128,2048]{1,0:T(8,128)(2,1)S(1)}, bf16[64,2048]{1,0:T(8,128)(2,1)S(1)}, bf16[64,2048]{1,0:T(8,128)(2,1)S(1)}) custom-call(bf16[256,2048]{1,0:T(8,128)(2,1)S(1)} %hidden_units.1.hidden, bf16[4,2048,512]{2,1,0:T(8,128)(2,1)S(1)} %bitcast.5), custom_call_target="tpu_custom_call" | custom-call | tf_op jit(solution)/shard_map/down_units/pallas_call | solution.py:338
  46.9 0.5 collective-permute-start.14
  47.4 1.0 %collective-permute-done.13.refs_0_ = bf16[64,2048]{1,0:T(8,128)(2,1)S(1)} collective-permute-done((bf16[64,2048]{1,0:T(8,128)(2,1)S(1)}, bf16[64,2048]{1,0:T(8,128)(2,1)S(1)}, u32[]{:S(2)}, u32[]{:S(2)}) %collective-permute-start.13) | collective-permute-done | bytes 262176 | tf_op jit(solution)/shard_map/ppermute | solution.py:26
  48.8 3.3 %collective-permute-done.17.refs_4_ = bf16[128,2048]{1,0:T(8,128)(2,1)S(1)} collective-permute-done((bf16[128,2048]{1,0:T(8,128)(2,1)S(1)}, bf16[128,2048]{1,0:T(8,128)(2,1)S(1)}, u32[]{:S(2)}, u32[]{:S(2)}) %collective-permute-start.17) | collective-permute-done | bytes 524320 | tf_op jit(solution)/shard_map/ppermute | solution.py:31
  52.1 0.9 %finish.1 = bf16[128,2048]{1,0:T(8,128)(2,1)} custom-call(bf16[64,2048]{1,0:T(8,128)(2,1)S(1)} %collective-permute-done.13.refs_0_, bf16[64,2048]{1,0:T(8,128)(2,1)S(1)} %collective-permute-done.14.refs_1_, bf16[128,2048]{1,0:T(8,128)(2,1)S(1)} %get-tuple-element.74.refs_2_, bf16[128,2048]{1,0:T(8,128)(2,1)S(1)} %collective-permute-done.12.refs_3_, ...), custom_call_target="tpu_custom_call" | custom-call | tf_op jit(solution)/shard_map/finish/pallas_call | solution.py:394
  (43 shorter events, 4.4 us)
Async XLA Ops:
  0.0 10.4 %collective-permute-start.1 = (bf16[128,2048]{1,0:T(8,128)(2,1)}, bf16[128,2048]{1,0:T(8,128)(2,1)S(1)}, u32[]{:S(2)}, u32[]{:S(2)}) collective-permute-start(bf16[128,2048]{1,0:T(8,128)(2,1)} %tokens.1), channel_id=1, source_target_pairs={{0,2},{1,5},{2,0},{3,7},{4,6},{5,1},{6,4},{7,3},{8,10},{9,13},{10,... | collective-permute-start | bytes 1572872 | tf_op jit(solution)/shard_map/ppermute | solution.py:31
  2.9 9.8 %slice-start = ((s8[8388608]{0:T(1024)(128)(4,1)}), s8[4194304]{0:T(1024)(128)(4,1)S(1)}, s32[]{:S(2)}) async-start(s8[8388608]{0:T(1024)(128)(4,1)} %bitcast.2), calls=%async_computation | async-start | bytes 8388608
  2.9 9.8 %slice-start.2 = ((s8[8388608]{0:T(1024)(128)(4,1)}), s8[4194304]{0:T(1024)(128)(4,1)S(1)}, s32[]{:S(2)}) async-start(s8[8388608]{0:T(1024)(128)(4,1)} %bitcast.4), calls=%async_computation.2 | async-start | bytes 8388608
  2.9 3.8 %copy-start = (bf16[4,2048,512]{2,1,0:T(8,128)(2,1)S(1)}, bf16[4,2048,512]{2,1,0:T(8,128)(2,1)}, u32[]{:S(2)}) copy-start(bf16[4,2048,512]{2,1,0:T(8,128)(2,1)} %refs_1_.9) | copy-start | bytes 25165828
  2.9 9.8 %slice-start.1 = ((s8[8388608]{0:T(1024)(128)(4,1)}), s8[4194304]{0:T(1024)(128)(4,1)S(1)}, s32[]{:S(2)}) async-start(s8[8388608]{0:T(1024)(128)(4,1)} %bitcast.2), calls=%async_computation.1 | async-start | bytes 8388608
  3.0 9.8 %slice-start.3 = ((s8[8388608]{0:T(1024)(128)(4,1)}), s8[4194304]{0:T(1024)(128)(4,1)S(1)}, s32[]{:S(2)}) async-start(s8[8388608]{0:T(1024)(128)(4,1)} %bitcast.4), calls=%async_computation.3 | async-start | bytes 8388608
  4.3 1.6 %collective-permute-start.2 = (bf16[16,8320]{1,0:T(8,128)(2,1)S(1)}, bf16[16,8320]{1,0:T(8,128)(2,1)S(1)}, u32[]{:S(2)}, u32[]{:S(2)}) collective-permute-start(bf16[16,8320]{1,0:T(8,128)(2,1)S(1)} %get-tuple-element.43.refs_0_.low), channel_id=1, source_target_pairs={{0,1},{1,0},{2,3},{3,2},{4,5},{5,4},{6,7},{7,6},{8,9},{9,8},{10,11... | collective-permute-start | bytes 798728 | tf_op jit(solution)/shard_map/ppermute | solution.py:26
  4.4 1.9 %collective-permute-start.3 = (bf16[16,8320]{1,0:T(8,128)(2,1)S(1)}, bf16[16,8320]{1,0:T(8,128)(2,1)S(1)}, u32[]{:S(2)}, u32[]{:S(2)}) collective-permute-start(bf16[16,8320]{1,0:T(8,128)(2,1)S(1)} %get-tuple-element.44.refs_1_.high), channel_id=1, source_target_pairs={{0,1},{1,0},{2,3},{3,2},{4,5},{5,4},{6,7},{7,6},{8,9},{9,8},{10,11... | collective-permute-start | bytes 798728 | tf_op jit(solution)/shard_map/ppermute | solution.py:26
  4.9 5.5 %collective-permute-start = (bf16[16,256]{1,0:T(8,128)(2,1)S(1)}, bf16[16,256]{1,0:T(8,128)(2,1)S(1)}, u32[]{:S(2)}, u32[]{:S(2)}) collective-permute-start(bf16[16,256]{1,0:T(8,128)(2,1)S(1)} %get-tuple-element.42.table), channel_id=1, source_target_pairs={{0,2},{1,5},{2,0},{3,7},{4,6},{5,1},{6,4},{7,3},{8,10},{9,13},{10,... | collective-permute-start | bytes 24584 | tf_op jit(solution)/shard_map/ppermute | solution.py:31
  10.4 4.8 %collective-permute-start.5 = (bf16[16,16640]{1,0:T(8,128)(2,1)S(1)}, bf16[16,16640]{1,0:T(8,128)(2,1)S(1)}, u32[]{:S(2)}, u32[]{:S(2)}) collective-permute-start(bf16[16,16640]{1,0:T(8,128)(2,1)S(1)} %pack.1.refs_0_), channel_id=1, source_target_pairs={{0,1},{1,0},{2,3},{3,2},{4,5},{5,4},{6,7},{7,6},{8,9},{9,8},{10,11... | collective-permute-start | bytes 1597448 | tf_op jit(solution)/shard_map/ppermute | solution.py:26
  10.5 9.4 %collective-permute-start.4 = (bf16[16,16640]{1,0:T(8,128)(2,1)S(1)}, bf16[16,16640]{1,0:T(8,128)(2,1)S(1)}, u32[]{:S(2)}, u32[]{:S(2)}) collective-permute-start(bf16[16,16640]{1,0:T(8,128)(2,1)S(1)} %pack.1.refs_0_), channel_id=1, source_target_pairs={{0,4},{1,3},{2,6},{3,1},{4,0},{5,7},{6,2},{7,5},{8,12},{9,11},{10,... | collective-permute-start | bytes 1597448 | tf_op jit(solution)/shard_map/ppermute | solution.py:31
  12.7 13.0 %collective-permute-start.7 = (bf16[16,16768]{1,0:T(8,128)(2,1)S(1)}, bf16[16,16768]{1,0:T(8,128)(2,1)S(1)}, u32[]{:S(2)}, u32[]{:S(2)}) collective-permute-start(bf16[16,16768]{1,0:T(8,128)(2,1)S(1)} %join.1), channel_id=1, source_target_pairs={{0,4},{1,3},{2,6},{3,1},{4,0},{5,7},{6,2},{7,5},{8,12},{9,11},{10,... | collective-permute-start | bytes 1609736 | tf_op jit(solution)/shard_map/ppermute | solution.py:31
  19.9 3.0 %collective-permute-start.6 = (bf16[16,16640]{1,0:T(8,128)(2,1)S(1)}, bf16[16,16640]{1,0:T(8,128)(2,1)S(1)}, u32[]{:S(2)}, u32[]{:S(2)}) collective-permute-start(bf16[16,16640]{1,0:T(8,128)(2,1)S(1)} %collective-permute-done.4.refs_0_), channel_id=1, source_target_pairs={{0,1},{1,0},{2,3},{3,2},{4,5},{5,4},{6,7},{7,6},{8,9},{9,8},{10,11... | collective-permute-start | bytes 1597448 | tf_op jit(solution)/shard_map/ppermute | solution.py:26
  20.0 5.6 %collective-permute-start.11 = (bf16[128,2048]{1,0:T(8,128)(2,1)S(1)}, bf16[128,2048]{1,0:T(8,128)(2,1)S(1)}, u32[]{:S(2)}, u32[]{:S(2)}) collective-permute-start(bf16[128,2048]{1,0:T(8,128)(2,1)S(1)} %get-tuple-element.64), channel_id=1, source_target_pairs={{0,1},{1,0},{2,3},{3,2},{4,5},{5,4},{6,7},{7,6},{8,9},{9,8},{10,11... | collective-permute-start | bytes 1572872 | tf_op jit(solution)/shard_map/ppermute | solution.py:26
  25.6 7.7 %collective-permute-start.10 = (bf16[16,16768]{1,0:T(8,128)(2,1)S(1)}, bf16[16,16768]{1,0:T(8,128)(2,1)S(1)}, u32[]{:S(2)}, u32[]{:S(2)}) collective-permute-start(bf16[16,16768]{1,0:T(8,128)(2,1)S(1)} %collective-permute-done.7.refs_0_), channel_id=1, source_target_pairs={{0,1},{1,0},{2,3},{3,2},{4,5},{5,4},{6,7},{7,6},{8,9},{9,8},{10,11... | collective-permute-start | bytes 1609736 | tf_op jit(solution)/shard_map/ppermute | solution.py:26
  25.8 11.4 %collective-permute-start.12 = (bf16[128,2048]{1,0:T(8,128)(2,1)S(1)}, bf16[128,2048]{1,0:T(8,128)(2,1)S(1)}, u32[]{:S(2)}, u32[]{:S(2)}) collective-permute-start(bf16[128,2048]{1,0:T(8,128)(2,1)S(1)} %add.3), channel_id=1, source_target_pairs={{0,2},{1,5},{2,0},{3,7},{4,6},{5,1},{6,4},{7,3},{8,10},{9,13},{10,... | collective-permute-start | bytes 1572872 | tf_op jit(solution)/shard_map/ppermute | solution.py:31
  30.2 3.0 %collective-permute-start.8 = (bf16[64,2048]{1,0:T(8,128)(2,1)S(1)}, bf16[64,2048]{1,0:T(8,128)(2,1)S(1)}, u32[]{:S(2)}, u32[]{:S(2)}) collective-permute-start(bf16[64,2048]{1,0:T(8,128)(2,1)S(1)} %get-tuple-element.58), channel_id=1, source_target_pairs={{0,1},{1,0},{2,3},{3,2},{4,5},{5,4},{6,7},{7,6},{8,9},{9,8},{10,11... | collective-permute-start | bytes 786440 | tf_op jit(solution)/shard_map/ppermute | solution.py:26
  30.5 2.7 %collective-permute-start.9 = (bf16[64,2048]{1,0:T(8,128)(2,1)S(1)}, bf16[64,2048]{1,0:T(8,128)(2,1)S(1)}, u32[]{:S(2)}, u32[]{:S(2)}) collective-permute-start(bf16[64,2048]{1,0:T(8,128)(2,1)S(1)} %get-tuple-element.59), channel_id=1, source_target_pairs={{0,1},{1,0},{2,3},{3,2},{4,5},{5,4},{6,7},{7,6},{8,9},{9,8},{10,11... | collective-permute-start | bytes 786440 | tf_op jit(solution)/shard_map/ppermute | solution.py:26
  33.4 9.2 %collective-permute-start.15 = (bf16[128,2048]{1,0:T(8,128)(2,1)S(1)}, bf16[128,2048]{1,0:T(8,128)(2,1)S(1)}, u32[]{:S(2)}, u32[]{:S(2)}) collective-permute-start(bf16[128,2048]{1,0:T(8,128)(2,1)S(1)} %add_pieces.1), channel_id=1, source_target_pairs={{0,2},{1,5},{2,0},{3,7},{4,6},{5,1},{6,4},{7,3},{8,10},{9,13},{10,... | collective-permute-start | bytes 1572872 | tf_op jit(solution)/shard_map/ppermute | solution.py:31
  39.6 3.2 %collective-permute-start.16 = (bf16[128,2048]{1,0:T(8,128)(2,1)S(1)}, bf16[128,2048]{1,0:T(8,128)(2,1)S(1)}, u32[]{:S(2)}, u32[]{:S(2)}) collective-permute-start(bf16[128,2048]{1,0:T(8,128)(2,1)S(1)} %get-tuple-element.78), channel_id=1, source_target_pairs={{0,1},{1,0},{2,3},{3,2},{4,5},{5,4},{6,7},{7,6},{8,9},{9,8},{10,11... | collective-permute-start | bytes 1572872 | tf_op jit(solution)/shard_map/ppermute | solution.py:26
  42.8 9.2 %collective-permute-start.17 = (bf16[128,2048]{1,0:T(8,128)(2,1)S(1)}, bf16[128,2048]{1,0:T(8,128)(2,1)S(1)}, u32[]{:S(2)}, u32[]{:S(2)}) collective-permute-start(bf16[128,2048]{1,0:T(8,128)(2,1)S(1)} %add.5), channel_id=1, source_target_pairs={{0,4},{1,3},{2,6},{3,1},{4,0},{5,7},{6,2},{7,5},{8,12},{9,11},{10,... | collective-permute-start | bytes 1572872 | tf_op jit(solution)/shard_map/ppermute | solution.py:31
  46.8 1.6 %collective-permute-start.13 = (bf16[64,2048]{1,0:T(8,128)(2,1)S(1)}, bf16[64,2048]{1,0:T(8,128)(2,1)S(1)}, u32[]{:S(2)}, u32[]{:S(2)}) collective-permute-start(bf16[64,2048]{1,0:T(8,128)(2,1)S(1)} %get-tuple-element.72), channel_id=1, source_target_pairs={{0,1},{1,0},{2,3},{3,2},{4,5},{5,4},{6,7},{7,6},{8,9},{9,8},{10,11... | collective-permute-start | bytes 786440 | tf_op jit(solution)/shard_map/ppermute | solution.py:26
  46.9 1.9 %collective-permute-start.14 = (bf16[64,2048]{1,0:T(8,128)(2,1)S(1)}, bf16[64,2048]{1,0:T(8,128)(2,1)S(1)}, u32[]{:S(2)}, u32[]{:S(2)}) collective-permute-start(bf16[64,2048]{1,0:T(8,128)(2,1)S(1)} %get-tuple-element.73), channel_id=1, source_target_pairs={{0,1},{1,0},{2,3},{3,2},{4,5},{5,4},{6,7},{7,6},{8,9},{9,8},{10,11... | collective-permute-start | bytes 786440 | tf_op jit(solution)/shard_map/ppermute | solution.py:26

commit v8 on v7

--- a/solution.py
+++ b/solution.py
@@ -260,6 +260,30 @@
     )(*in_vmem(*parts, w_gate, w_up, *others))
 
 
+def both_kernel(gated, gated_rows, part, w_gate, w_up, first, second, rows):
+    held, _, units = w_gate.shape
+    weights = gather_inputs([part], rows, held)
+    for e in range(held):
+        block = slice(e * units, (e + 1) * units)
+        up_act = jnp.dot(gated_rows[...], w_up[e], preferred_element_type=jnp.float32)
+        first[:, block] = (gated[:, block] * up_act).astype(jnp.bfloat16)
+        second[:, block] = hidden_of(rows[...], w_gate[e], w_up[e], weights[e])
+
+
+def both_units(gated, gated_rows, part, w_gate, w_up):
+    half = pltpu.VMEM(gated.shape, jnp.bfloat16)
+    return pl.pallas_call(
+        both_kernel,
+        in_specs=[VMEM_SPEC] * 5,
+        out_specs=[VMEM_SPEC] * 2,
+        out_shape=[half, half],
+        scratch_shapes=[pltpu.VMEM(gated_rows.shape, jnp.bfloat16)],
+        cost_estimate=COST,
+        compiler_params=params(),
+        name="both_units",
+    )(*in_vmem(gated, gated_rows, part, w_gate, w_up))
+
+
 def rest_kernel(first, part, w_gate, w_up, w_down, mine, other, rows, hidden):
     held, _, units = w_gate.shape
     count = first.shape[0]
@@ -431,19 +455,17 @@
     mine_far, *other_far = sums_of(first, second, w_down, pieces=2)
 
     following_twin = flip(following, CORE)
-    first = units_of([following], w_gate, w_up)
+    first, first_rows = gated_units([following], w_gate)
     mine_far, first = barrier((mine_far, first))
     sum_far = add_pieces(mine_far, [flip(other, CORE) for other in other_far])
     sum_far, following_twin, first = barrier((sum_far, following_twin, first))
     relay = cross(sum_far, x, y)
-    second = units_of([following_twin], w_gate, w_up)
+    first, second = both_units(first, first_rows, following_twin, w_gate, w_up)
     second, back = barrier((second, back))
     mine_last, other_last = sums_of(first, second, w_down)
-    mine_last, gated = barrier((mine_last, gated))
-    hidden = hidden_units(gated, rows, w_up)
-    mine_last, hidden = barrier((mine_last, hidden))
     sum_last = add(add(mine_last, relay, dtype=jnp.float32, cost=RELAY), flip(other_last, CORE))
     last = cross(sum_last, y, x)
+    hidden = hidden_units(gated, rows, w_up)
     mine_own, *other_own = down_units(hidden, w_down, pieces=2)
     return finish([flip(other, CORE) for other in other_own], mine_own, back, last)
 

time: 53.3 us -> 52.4 us (0.983)
  waiting for transfers between devices: 7.36 us -> 6.26 us
    pallas_call x5 -> x3, Pallas kernels: 12.3 us -> 7.4 us  [units_of(): pl.pallas_call(functools.partial(units_kernel, parts=len(parts)), in_spec...]
    pallas_call x0 -> x1, Pallas kernels: none -> 3.71 us  [both_units(): pl.pallas_call(both_kernel, in_specs=[VMEM_SPEC] * 5, out_specs=[VMEM_SPE...]
    pallas_call x1 -> x2, Pallas kernels: 2.63 us -> 4.1 us  [gated_units(): pl.pallas_call(functools.partial(gated_kernel, parts=len(parts)), in_spec...]
    ppermute x7, waiting for transfers between devices: 5.18 us -> 3.98 us  [cross(): lax.ppermute(x, 'ep', [(i, i ^ (odd if i % 2 else even)) for i in range(n)])]
  transfers between devices with their start and end apart: 18 -> 18, of which waited for: 8 -> 9; matrix products, arithmetic and copies ran while one was open for 0% -> 0% of each run, Pallas kernels for 58% -> 59%
where the time goes in v8:
time: 52.4 us; the launch traced here: 52.3 us
  Pallas kernels  32 us (61%)
  starting transfers between devices  13.1 us (25%)
  waiting for transfers between devices  6.26 us (12%)
    ppermute x7, starting transfers between devices, cross(): lax.ppermute(x, 'ep', [(i, i ^ (odd if i % 2 else even)) for i in range(n)])  10.7 us
    pallas_call x3, Pallas kernels, units_of(): pl.pallas_call(functools.partial(units_kernel, parts=len(parts)), in_spec...  7.4 us
    pallas_call x2, Pallas kernels, sums_of(): pl.pallas_call(sums_kernel, in_specs=[VMEM_SPEC] * 3, out_specs=[VMEM_SPE...  4.71 us
    pallas_call x1, Pallas kernels, rest_of(): pl.pallas_call(rest_kernel, in_specs=[VMEM_SPEC] * 5, out_specs=[VMEM_SPE...  4.62 us
    pallas_call x2, Pallas kernels, gated_units(): pl.pallas_call(functools.partial(gated_kernel, parts=len(parts)), in_spec...  4.1 us
    ppermute x7, waiting for transfers between devices, cross(): lax.ppermute(x, 'ep', [(i, i ^ (odd if i % 2 else even)) for i in range(n)])  3.98 us
    pallas_call x1, Pallas kernels, both_units(): pl.pallas_call(both_kernel, in_specs=[VMEM_SPEC] * 5, out_specs=[VMEM_SPE...  3.71 us
    ppermute x11, starting transfers between devices, flip(): return lax.ppermute(x, 'ep', [(i, i ^ mask) for i in range(n)])  2.43 us
  transfers between devices with their start and end apart: 18, of which 9 were waited for; matrix products, arithmetic and copies ran while one was open for 0% of the time, Pallas kernels for 59%

profile of v8, /device:TPU:0, one launch (start us, length us, event | category | flops | bytes accessed | tf_op | source)
XLA Modules:
  0.0 52.3 jit_solution(5513050809217687992)
XLA Ops:
  0.0 2.9 %collective-permute-start.1 = (bf16[128,2048]{1,0:T(8,128)(2,1)}, bf16[128,2048]{1,0:T(8,128)(2,1)S(1)}, u32[]{:S(2)}, u32[]{:S(2)}) collective-permute-start(bf16[128,2048]{1,0:T(8,128)(2,1)} %tokens.1), channel_id=1, source_target_pairs={{0,2},{1,5},{2,0},{3,7},{4,6},{5,1},{6,4},{7,3},{8,10},{9,13},{10,... | collective-permute-start | bytes 1572872 | tf_op jit(solution)/shard_map/ppermute | solution.py:31
  3.0 1.3 %prepare.1 = (bf16[16,8320]{1,0:T(8,128)(2,1)S(1)}, bf16[16,8320]{1,0:T(8,128)(2,1)S(1)}, bf16[16,256]{1,0:T(8,128)(2,1)S(1)}) custom-call(bf16[128,2048]{1,0:T(8,128)(2,1)} %tokens.1, s32[10,128]{1,0:T(8,128)} %bitcast.6, bf16[10,128]{1,0:T(8,128)(2,1)} %bitcast.7), custom_call_target="tpu_custom_call" | custom-call | flops 99999997952 | bytes 100000000 | tf_op jit(solution)/shard_map/prepare/pallas_call | solution.py:87
  4.9 0.6 %collective-permute-start = (bf16[16,256]{1,0:T(8,128)(2,1)S(1)}, bf16[16,256]{1,0:T(8,128)(2,1)S(1)}, u32[]{:S(2)}, u32[]{:S(2)}) collective-permute-start(bf16[16,256]{1,0:T(8,128)(2,1)S(1)} %get-tuple-element.42.table), channel_id=1, source_target_pairs={{0,2},{1,5},{2,0},{3,7},{4,6},{5,1},{6,4},{7,3},{8,10},{9,13},{10,... | collective-permute-start | bytes 24584 | tf_op jit(solution)/shard_map/ppermute | solution.py:31
  6.8 2.6 %gated_units.2 = (f32[256,2048]{1,0:T(8,128)S(1)}, bf16[256,2048]{1,0:T(8,128)(2,1)S(1)}) custom-call(bf16[16,8320]{1,0:T(8,128)(2,1)S(1)} %get-tuple-element.43.refs_0_.low, bf16[16,8320]{1,0:T(8,128)(2,1)S(1)} %get-tuple-element.44.refs_1_.high, bf16[16,8320]{1,0:T(8,128)(2,1)S(1)} %collective-permute-done.2.refs_2_, ...), custom_call_target="tpu_custom_call" | custom-call | tf_op jit(solution)/shard_map/gated_units/pallas_call | solution.py:209
  9.4 1.0 %collective-permute-done.table = bf16[16,256]{1,0:T(8,128)(2,1)S(1)} collective-permute-done((bf16[16,256]{1,0:T(8,128)(2,1)S(1)}, bf16[16,256]{1,0:T(8,128)(2,1)S(1)}, u32[]{:S(2)}, u32[]{:S(2)}) %collective-permute-start) | collective-permute-done | bytes 8224 | tf_op jit(solution)/shard_map/ppermute | solution.py:31
  10.5 2.1 %collective-permute-start.6 = (bf16[16,16640]{1,0:T(8,128)(2,1)S(1)}, bf16[16,16640]{1,0:T(8,128)(2,1)S(1)}, u32[]{:S(2)}, u32[]{:S(2)}) collective-permute-start(bf16[16,16640]{1,0:T(8,128)(2,1)S(1)} %pack.1.refs_0_), channel_id=1, source_target_pairs={{0,4},{1,3},{2,6},{3,1},{4,0},{5,7},{6,2},{7,5},{8,12},{9,11},{10,... | collective-permute-start | bytes 1597448 | tf_op jit(solution)/shard_map/ppermute | solution.py:31
  12.8 2.4 %units_of.3.first = bf16[128,2048]{1,0:T(8,128)(2,1)S(1)} custom-call(bf16[16,16640]{1,0:T(8,128)(2,1)S(1)} %pack.1.refs_0_, bf16[4,2048,512]{2,1,0:T(8,128)(2,1)S(1)} %copy-done, bf16[4,2048,512]{2,1,0:T(8,128)(2,1)S(1)} %bitcast.3, bf16[4,2048,512]{2,1,0:T(8,128)(2,1)S(1)} %bitcast.5), custom_call_target="tpu_custom_call" | custom-call | tf_op jit(solution)/shard_map/units_of/pallas_call | solution.py:251
  15.2 4.6 %rest_of.1 = (bf16[128,2048]{1,0:T(8,128)(2,1)S(1)}, bf16[128,2048]{1,0:T(8,128)(2,1)S(1)}) custom-call(bf16[128,2048]{1,0:T(8,128)(2,1)S(1)} %units_of.3.first, bf16[16,16640]{1,0:T(8,128)(2,1)S(1)} %collective-permute-done.7.part, bf16[4,2048,512]{2,1,0:T(8,128)(2,1)S(1)} %copy-done, bf16[4,2048,512]{2,1,0:T(8,128)(2,1)S(1)} %bitcast.3, ...), custom_call_target="tpu_custom_call" | custom-call | tf_op jit(solution)/shard_map/rest_of/pallas_call | solution.py:301
  20.4 2.4 %units_of.4.first = bf16[128,2048]{1,0:T(8,128)(2,1)S(1)} custom-call(bf16[16,16640]{1,0:T(8,128)(2,1)S(1)} %collective-permute-done.6.refs_0_, bf16[4,2048,512]{2,1,0:T(8,128)(2,1)S(1)} %copy-done, bf16[4,2048,512]{2,1,0:T(8,128)(2,1)S(1)} %bitcast.3), custom_call_target="tpu_custom_call" | custom-call | tf_op jit(solution)/shard_map/units_of/pallas_call | solution.py:251
  22.9 2.6 %units_of.5.second = bf16[128,2048]{1,0:T(8,128)(2,1)S(1)} custom-call(bf16[16,16640]{1,0:T(8,128)(2,1)S(1)} %collective-permute-done.8.refs_0_, bf16[4,2048,512]{2,1,0:T(8,128)(2,1)S(1)} %copy-done, bf16[4,2048,512]{2,1,0:T(8,128)(2,1)S(1)} %bitcast.3), custom_call_target="tpu_custom_call" | custom-call | tf_op jit(solution)/shard_map/units_of/pallas_call | solution.py:251
  25.8 2.0 %collective-permute-start.14 = (bf16[128,2048]{1,0:T(8,128)(2,1)S(1)}, bf16[128,2048]{1,0:T(8,128)(2,1)S(1)}, u32[]{:S(2)}, u32[]{:S(2)}) collective-permute-start(bf16[128,2048]{1,0:T(8,128)(2,1)S(1)} %add.3), channel_id=1, source_target_pairs={{0,2},{1,5},{2,0},{3,7},{4,6},{5,1},{6,4},{7,3},{8,10},{9,13},{10,... | collective-permute-start | bytes 1572872 | tf_op jit(solution)/shard_map/ppermute | solution.py:31
  27.8 2.4 %sums_of.2 = (bf16[128,2048]{1,0:T(8,128)(2,1)S(1)}, bf16[64,2048]{1,0:T(8,128)(2,1)S(1)}, bf16[64,2048]{1,0:T(8,128)(2,1)S(1)}) custom-call(bf16[128,2048]{1,0:T(8,128)(2,1)S(1)} %units_of.4.first, bf16[128,2048]{1,0:T(8,128)(2,1)S(1)} %units_of.5.second, bf16[4,2048,512]{2,1,0:T(8,128)(2,1)S(1)} %bitcast.5), custom_call_target="tpu_custom_call" | custom-call | tf_op jit(solution)/shard_map/sums_of/pallas_call | solution.py:327
  30.8 1.5 %gated_units.3 = (f32[128,2048]{1,0:T(8,128)S(1)}, bf16[128,2048]{1,0:T(8,128)(2,1)S(1)}) custom-call(bf16[16,16768]{1,0:T(8,128)(2,1)S(1)} %collective-permute-done.9.refs_0_, bf16[4,2048,512]{2,1,0:T(8,128)(2,1)S(1)} %copy-done), custom_call_target="tpu_custom_call" | custom-call | tf_op jit(solution)/shard_map/gated_units/pallas_call | solution.py:209
  32.4 1.4 %collective-permute-start.15 = (bf16[128,2048]{1,0:T(8,128)(2,1)S(1)}, bf16[128,2048]{1,0:T(8,128)(2,1)S(1)}, u32[]{:S(2)}, u32[]{:S(2)}) collective-permute-start(bf16[128,2048]{1,0:T(8,128)(2,1)S(1)} %add_pieces.1), channel_id=1, source_target_pairs={{0,2},{1,5},{2,0},{3,7},{4,6},{5,1},{6,4},{7,3},{8,10},{9,13},{10,... | collective-permute-start | bytes 1572872 | tf_op jit(solution)/shard_map/ppermute | solution.py:31
  33.8 3.7 %both_units.1 = (bf16[128,2048]{1,0:T(8,128)(2,1)S(1)}, bf16[128,2048]{1,0:T(8,128)(2,1)S(1)}) custom-call(f32[128,2048]{1,0:T(8,128)S(1)} %get-tuple-element.67.gated, bf16[128,2048]{1,0:T(8,128)(2,1)S(1)} %get-tuple-element.68.gated_rows, bf16[16,16768]{1,0:T(8,128)(2,1)S(1)} %collective-permute-done.12.part, bf16[4,2048,512]{2,1,0:T(8,128)(2,1)S(1)} %copy-done, ...), custom_call_target="tpu_custom_call" | custom-call | tf_op jit(solution)/shard_map/both_units/pallas_call | solution.py:275
  37.5 2.4 %sums_of.3 = (bf16[128,2048]{1,0:T(8,128)(2,1)S(1)}, bf16[128,2048]{1,0:T(8,128)(2,1)S(1)}) custom-call(bf16[128,2048]{1,0:T(8,128)(2,1)S(1)} %get-tuple-element.74.first, bf16[128,2048]{1,0:T(8,128)(2,1)S(1)} %get-tuple-element.75.second, bf16[4,2048,512]{2,1,0:T(8,128)(2,1)S(1)} %bitcast.5), custom_call_target="tpu_custom_call" | custom-call | tf_op jit(solution)/shard_map/sums_of/pallas_call | solution.py:327
  40.0 1.7 %collective-permute-done.15.refs_1_ = bf16[128,2048]{1,0:T(8,128)(2,1)S(1)} collective-permute-done((bf16[128,2048]{1,0:T(8,128)(2,1)S(1)}, bf16[128,2048]{1,0:T(8,128)(2,1)S(1)}, u32[]{:S(2)}, u32[]{:S(2)}) %collective-permute-start.15) | collective-permute-done | bytes 524320 | tf_op jit(solution)/shard_map/ppermute | solution.py:31
  41.9 1.5 %collective-permute-start.17 = (bf16[128,2048]{1,0:T(8,128)(2,1)S(1)}, bf16[128,2048]{1,0:T(8,128)(2,1)S(1)}, u32[]{:S(2)}, u32[]{:S(2)}) collective-permute-start(bf16[128,2048]{1,0:T(8,128)(2,1)S(1)} %add.5), channel_id=1, source_target_pairs={{0,4},{1,3},{2,6},{3,1},{4,0},{5,7},{6,2},{7,5},{8,12},{9,11},{10,... | collective-permute-start | bytes 1572872 | tf_op jit(solution)/shard_map/ppermute | solution.py:31
  43.4 2.3 %hidden_units.1.hidden = bf16[256,2048]{1,0:T(8,128)(2,1)S(1)} custom-call(f32[256,2048]{1,0:T(8,128)S(1)} %get-tuple-element.46.gated, bf16[256,2048]{1,0:T(8,128)(2,1)S(1)} %get-tuple-element.47.rows, bf16[4,2048,512]{2,1,0:T(8,128)(2,1)S(1)} %bitcast.3), custom_call_target="tpu_custom_call" | custom-call | tf_op jit(solution)/shard_map/hidden_units/pallas_call | solution.py:229
  45.8 2.4 %down_units.1 = (bf16[128,2048]{1,0:T(8,128)(2,1)S(1)}, bf16[64,2048]{1,0:T(8,128)(2,1)S(1)}, bf16[64,2048]{1,0:T(8,128)(2,1)S(1)}) custom-call(bf16[256,2048]{1,0:T(8,128)(2,1)S(1)} %hidden_units.1.hidden, bf16[4,2048,512]{2,1,0:T(8,128)(2,1)S(1)} %bitcast.5), custom_call_target="tpu_custom_call" | custom-call | tf_op jit(solution)/shard_map/down_units/pallas_call | solution.py:362
  48.2 0.5 collective-permute-start.5
  48.7 1.0 %collective-permute-done.4.refs_0_ = bf16[64,2048]{1,0:T(8,128)(2,1)S(1)} collective-permute-done((bf16[64,2048]{1,0:T(8,128)(2,1)S(1)}, bf16[64,2048]{1,0:T(8,128)(2,1)S(1)}, u32[]{:S(2)}, u32[]{:S(2)}) %collective-permute-start.4) | collective-permute-done | bytes 262176 | tf_op jit(solution)/shard_map/ppermute | solution.py:26
  50.1 1.1 %collective-permute-done.17.refs_4_ = bf16[128,2048]{1,0:T(8,128)(2,1)S(1)} collective-permute-done((bf16[128,2048]{1,0:T(8,128)(2,1)S(1)}, bf16[128,2048]{1,0:T(8,128)(2,1)S(1)}, u32[]{:S(2)}, u32[]{:S(2)}) %collective-permute-start.17) | collective-permute-done | bytes 524320 | tf_op jit(solution)/shard_map/ppermute | solution.py:31
  51.2 0.9 %finish.1 = bf16[128,2048]{1,0:T(8,128)(2,1)} custom-call(bf16[64,2048]{1,0:T(8,128)(2,1)S(1)} %collective-permute-done.4.refs_0_, bf16[64,2048]{1,0:T(8,128)(2,1)S(1)} %collective-permute-done.5.refs_1_, bf16[128,2048]{1,0:T(8,128)(2,1)S(1)} %get-tuple-element.50.refs_2_, bf16[128,2048]{1,0:T(8,128)(2,1)S(1)} %collective-permute-done.14.refs_3_, ...), custom_call_target="tpu_custom_call" | custom-call | tf_op jit(solution)/shard_map/finish/pallas_call | solution.py:418
  (43 shorter events, 4.5 us)
Async XLA Ops:
  0.0 10.4 %collective-permute-start.1 = (bf16[128,2048]{1,0:T(8,128)(2,1)}, bf16[128,2048]{1,0:T(8,128)(2,1)S(1)}, u32[]{:S(2)}, u32[]{:S(2)}) collective-permute-start(bf16[128,2048]{1,0:T(8,128)(2,1)} %tokens.1), channel_id=1, source_target_pairs={{0,2},{1,5},{2,0},{3,7},{4,6},{5,1},{6,4},{7,3},{8,10},{9,13},{10,... | collective-permute-start | bytes 1572872 | tf_op jit(solution)/shard_map/ppermute | solution.py:31
  2.9 9.8 %slice-start = ((s8[8388608]{0:T(1024)(128)(4,1)}), s8[4194304]{0:T(1024)(128)(4,1)S(1)}, s32[]{:S(2)}) async-start(s8[8388608]{0:T(1024)(128)(4,1)} %bitcast.2), calls=%async_computation | async-start | bytes 8388608
  2.9 9.8 %slice-start.2 = ((s8[8388608]{0:T(1024)(128)(4,1)}), s8[4194304]{0:T(1024)(128)(4,1)S(1)}, s32[]{:S(2)}) async-start(s8[8388608]{0:T(1024)(128)(4,1)} %bitcast.4), calls=%async_computation.2 | async-start | bytes 8388608
  2.9 3.8 %copy-start = (bf16[4,2048,512]{2,1,0:T(8,128)(2,1)S(1)}, bf16[4,2048,512]{2,1,0:T(8,128)(2,1)}, u32[]{:S(2)}) copy-start(bf16[4,2048,512]{2,1,0:T(8,128)(2,1)} %w_gate.3) | copy-start | bytes 25165828
  2.9 9.8 %slice-start.1 = ((s8[8388608]{0:T(1024)(128)(4,1)}), s8[4194304]{0:T(1024)(128)(4,1)S(1)}, s32[]{:S(2)}) async-start(s8[8388608]{0:T(1024)(128)(4,1)} %bitcast.2), calls=%async_computation.1 | async-start | bytes 8388608
  3.0 9.8 %slice-start.3 = ((s8[8388608]{0:T(1024)(128)(4,1)}), s8[4194304]{0:T(1024)(128)(4,1)S(1)}, s32[]{:S(2)}) async-start(s8[8388608]{0:T(1024)(128)(4,1)} %bitcast.4), calls=%async_computation.3 | async-start | bytes 8388608
  4.3 1.6 %collective-permute-start.2 = (bf16[16,8320]{1,0:T(8,128)(2,1)S(1)}, bf16[16,8320]{1,0:T(8,128)(2,1)S(1)}, u32[]{:S(2)}, u32[]{:S(2)}) collective-permute-start(bf16[16,8320]{1,0:T(8,128)(2,1)S(1)} %get-tuple-element.43.refs_0_.low), channel_id=1, source_target_pairs={{0,1},{1,0},{2,3},{3,2},{4,5},{5,4},{6,7},{7,6},{8,9},{9,8},{10,11... | collective-permute-start | bytes 798728 | tf_op jit(solution)/shard_map/ppermute | solution.py:26
  4.4 1.9 %collective-permute-start.3 = (bf16[16,8320]{1,0:T(8,128)(2,1)S(1)}, bf16[16,8320]{1,0:T(8,128)(2,1)S(1)}, u32[]{:S(2)}, u32[]{:S(2)}) collective-permute-start(bf16[16,8320]{1,0:T(8,128)(2,1)S(1)} %get-tuple-element.44.refs_1_.high), channel_id=1, source_target_pairs={{0,1},{1,0},{2,3},{3,2},{4,5},{5,4},{6,7},{7,6},{8,9},{9,8},{10,11... | collective-permute-start | bytes 798728 | tf_op jit(solution)/shard_map/ppermute | solution.py:26
  4.9 5.5 %collective-permute-start = (bf16[16,256]{1,0:T(8,128)(2,1)S(1)}, bf16[16,256]{1,0:T(8,128)(2,1)S(1)}, u32[]{:S(2)}, u32[]{:S(2)}) collective-permute-start(bf16[16,256]{1,0:T(8,128)(2,1)S(1)} %get-tuple-element.42.table), channel_id=1, source_target_pairs={{0,2},{1,5},{2,0},{3,7},{4,6},{5,1},{6,4},{7,3},{8,10},{9,13},{10,... | collective-permute-start | bytes 24584 | tf_op jit(solution)/shard_map/ppermute | solution.py:31
  10.4 4.8 %collective-permute-start.7 = (bf16[16,16640]{1,0:T(8,128)(2,1)S(1)}, bf16[16,16640]{1,0:T(8,128)(2,1)S(1)}, u32[]{:S(2)}, u32[]{:S(2)}) collective-permute-start(bf16[16,16640]{1,0:T(8,128)(2,1)S(1)} %pack.1.refs_0_), channel_id=1, source_target_pairs={{0,1},{1,0},{2,3},{3,2},{4,5},{5,4},{6,7},{7,6},{8,9},{9,8},{10,11... | collective-permute-start | bytes 1597448 | tf_op jit(solution)/shard_map/ppermute | solution.py:26
  10.5 9.4 %collective-permute-start.6 = (bf16[16,16640]{1,0:T(8,128)(2,1)S(1)}, bf16[16,16640]{1,0:T(8,128)(2,1)S(1)}, u32[]{:S(2)}, u32[]{:S(2)}) collective-permute-start(bf16[16,16640]{1,0:T(8,128)(2,1)S(1)} %pack.1.refs_0_), channel_id=1, source_target_pairs={{0,4},{1,3},{2,6},{3,1},{4,0},{5,7},{6,2},{7,5},{8,12},{9,11},{10,... | collective-permute-start | bytes 1597448 | tf_op jit(solution)/shard_map/ppermute | solution.py:31
  12.7 13.0 %collective-permute-start.9 = (bf16[16,16768]{1,0:T(8,128)(2,1)S(1)}, bf16[16,16768]{1,0:T(8,128)(2,1)S(1)}, u32[]{:S(2)}, u32[]{:S(2)}) collective-permute-start(bf16[16,16768]{1,0:T(8,128)(2,1)S(1)} %join.1), channel_id=1, source_target_pairs={{0,4},{1,3},{2,6},{3,1},{4,0},{5,7},{6,2},{7,5},{8,12},{9,11},{10,... | collective-permute-start | bytes 1609736 | tf_op jit(solution)/shard_map/ppermute | solution.py:31
  19.9 3.0 %collective-permute-start.8 = (bf16[16,16640]{1,0:T(8,128)(2,1)S(1)}, bf16[16,16640]{1,0:T(8,128)(2,1)S(1)}, u32[]{:S(2)}, u32[]{:S(2)}) collective-permute-start(bf16[16,16640]{1,0:T(8,128)(2,1)S(1)} %collective-permute-done.6.refs_0_), channel_id=1, source_target_pairs={{0,1},{1,0},{2,3},{3,2},{4,5},{5,4},{6,7},{7,6},{8,9},{9,8},{10,11... | collective-permute-start | bytes 1597448 | tf_op jit(solution)/shard_map/ppermute | solution.py:26
  20.0 5.6 %collective-permute-start.13 = (bf16[128,2048]{1,0:T(8,128)(2,1)S(1)}, bf16[128,2048]{1,0:T(8,128)(2,1)S(1)}, u32[]{:S(2)}, u32[]{:S(2)}) collective-permute-start(bf16[128,2048]{1,0:T(8,128)(2,1)S(1)} %get-tuple-element.72), channel_id=1, source_target_pairs={{0,1},{1,0},{2,3},{3,2},{4,5},{5,4},{6,7},{7,6},{8,9},{9,8},{10,11... | collective-permute-start | bytes 1572872 | tf_op jit(solution)/shard_map/ppermute | solution.py:26
  25.6 6.8 %collective-permute-start.12 = (bf16[16,16768]{1,0:T(8,128)(2,1)S(1)}, bf16[16,16768]{1,0:T(8,128)(2,1)S(1)}, u32[]{:S(2)}, u32[]{:S(2)}) collective-permute-start(bf16[16,16768]{1,0:T(8,128)(2,1)S(1)} %collective-permute-done.9.refs_0_), channel_id=1, source_target_pairs={{0,1},{1,0},{2,3},{3,2},{4,5},{5,4},{6,7},{7,6},{8,9},{9,8},{10,11... | collective-permute-start | bytes 1609736 | tf_op jit(solution)/shard_map/ppermute | solution.py:26
  25.8 11.7 %collective-permute-start.14 = (bf16[128,2048]{1,0:T(8,128)(2,1)S(1)}, bf16[128,2048]{1,0:T(8,128)(2,1)S(1)}, u32[]{:S(2)}, u32[]{:S(2)}) collective-permute-start(bf16[128,2048]{1,0:T(8,128)(2,1)S(1)} %add.3), channel_id=1, source_target_pairs={{0,2},{1,5},{2,0},{3,7},{4,6},{5,1},{6,4},{7,3},{8,10},{9,13},{10,... | collective-permute-start | bytes 1572872 | tf_op jit(solution)/shard_map/ppermute | solution.py:31
  30.2 2.1 %collective-permute-start.10 = (bf16[64,2048]{1,0:T(8,128)(2,1)S(1)}, bf16[64,2048]{1,0:T(8,128)(2,1)S(1)}, u32[]{:S(2)}, u32[]{:S(2)}) collective-permute-start(bf16[64,2048]{1,0:T(8,128)(2,1)S(1)} %get-tuple-element.64), channel_id=1, source_target_pairs={{0,1},{1,0},{2,3},{3,2},{4,5},{5,4},{6,7},{7,6},{8,9},{9,8},{10,11... | collective-permute-start | bytes 786440 | tf_op jit(solution)/shard_map/ppermute | solution.py:26
  30.5 1.7 %collective-permute-start.11 = (bf16[64,2048]{1,0:T(8,128)(2,1)S(1)}, bf16[64,2048]{1,0:T(8,128)(2,1)S(1)}, u32[]{:S(2)}, u32[]{:S(2)}) collective-permute-start(bf16[64,2048]{1,0:T(8,128)(2,1)S(1)} %get-tuple-element.65), channel_id=1, source_target_pairs={{0,1},{1,0},{2,3},{3,2},{4,5},{5,4},{6,7},{7,6},{8,9},{9,8},{10,11... | collective-permute-start | bytes 786440 | tf_op jit(solution)/shard_map/ppermute | solution.py:26
  32.4 9.2 %collective-permute-start.15 = (bf16[128,2048]{1,0:T(8,128)(2,1)S(1)}, bf16[128,2048]{1,0:T(8,128)(2,1)S(1)}, u32[]{:S(2)}, u32[]{:S(2)}) collective-permute-start(bf16[128,2048]{1,0:T(8,128)(2,1)S(1)} %add_pieces.1), channel_id=1, source_target_pairs={{0,2},{1,5},{2,0},{3,7},{4,6},{5,1},{6,4},{7,3},{8,10},{9,13},{10,... | collective-permute-start | bytes 1572872 | tf_op jit(solution)/shard_map/ppermute | solution.py:31
  39.9 2.0 %collective-permute-start.16 = (bf16[128,2048]{1,0:T(8,128)(2,1)S(1)}, bf16[128,2048]{1,0:T(8,128)(2,1)S(1)}, u32[]{:S(2)}, u32[]{:S(2)}) collective-permute-start(bf16[128,2048]{1,0:T(8,128)(2,1)S(1)} %get-tuple-element.78), channel_id=1, source_target_pairs={{0,1},{1,0},{2,3},{3,2},{4,5},{5,4},{6,7},{7,6},{8,9},{9,8},{10,11... | collective-permute-start | bytes 1572872 | tf_op jit(solution)/shard_map/ppermute | solution.py:26
  41.9 9.2 %collective-permute-start.17 = (bf16[128,2048]{1,0:T(8,128)(2,1)S(1)}, bf16[128,2048]{1,0:T(8,128)(2,1)S(1)}, u32[]{:S(2)}, u32[]{:S(2)}) collective-permute-start(bf16[128,2048]{1,0:T(8,128)(2,1)S(1)} %add.5), channel_id=1, source_target_pairs={{0,4},{1,3},{2,6},{3,1},{4,0},{5,7},{6,2},{7,5},{8,12},{9,11},{10,... | collective-permute-start | bytes 1572872 | tf_op jit(solution)/shard_map/ppermute | solution.py:31
  48.1 1.6 %collective-permute-start.4 = (bf16[64,2048]{1,0:T(8,128)(2,1)S(1)}, bf16[64,2048]{1,0:T(8,128)(2,1)S(1)}, u32[]{:S(2)}, u32[]{:S(2)}) collective-permute-start(bf16[64,2048]{1,0:T(8,128)(2,1)S(1)} %get-tuple-element.48), channel_id=1, source_target_pairs={{0,1},{1,0},{2,3},{3,2},{4,5},{5,4},{6,7},{7,6},{8,9},{9,8},{10,11... | collective-permute-start | bytes 786440 | tf_op jit(solution)/shard_map/ppermute | solution.py:26
  48.2 1.9 %collective-permute-start.5 = (bf16[64,2048]{1,0:T(8,128)(2,1)S(1)}, bf16[64,2048]{1,0:T(8,128)(2,1)S(1)}, u32[]{:S(2)}, u32[]{:S(2)}) collective-permute-start(bf16[64,2048]{1,0:T(8,128)(2,1)S(1)} %get-tuple-element.49), channel_id=1, source_target_pairs={{0,1},{1,0},{2,3},{3,2},{4,5},{5,4},{6,7},{7,6},{8,9},{9,8},{10,11... | collective-permute-start | bytes 786440 | tf_op jit(solution)/shard_map/ppermute | solution.py:26

commit v9 on v8

--- a/solution.py
+++ b/solution.py
@@ -260,6 +260,29 @@
     )(*in_vmem(*parts, w_gate, w_up, *others))
 
 
+def units_sum_kernel(part, w_gate, w_up, mine, twin, hidden, total, rows):
+    total[...] = (mine[...].astype(jnp.float32) + twin[...].astype(jnp.float32)).astype(total.dtype)
+    held, _, units = w_gate.shape
+    weights = gather_inputs([part], rows, held)
+    for e in range(held):
+        hidden[:, e * units : (e + 1) * units] = hidden_of(rows[...], w_gate[e], w_up[e], weights[e])
+
+
+def units_and_sum(part, w_gate, w_up, mine, twin):
+    held, width, units = w_gate.shape
+    count = rows_in(part, width)
+    return pl.pallas_call(
+        units_sum_kernel,
+        in_specs=[VMEM_SPEC] * 5,
+        out_specs=[VMEM_SPEC] * 2,
+        out_shape=[pltpu.VMEM((count, held * units), jnp.bfloat16), pltpu.VMEM(mine.shape, mine.dtype)],
+        scratch_shapes=[pltpu.VMEM((count, width), jnp.bfloat16)],
+        cost_estimate=COST,
+        compiler_params=params(),
+        name="units_and_sum",
+    )(*in_vmem(part, w_gate, w_up, mine, twin))
+
+
 def both_kernel(gated, gated_rows, part, w_gate, w_up, first, second, rows):
     held, _, units = w_gate.shape
     weights = gather_inputs([part], rows, held)
@@ -436,20 +459,19 @@
     weights = (w_gate, w_up, w_down)
     near_rows, near_table = cross(tokens, x, y), cross(table, x, y)
     gated, rows = gated_units([low, high, flip(low, CORE), flip(high, CORE)], w_gate)
-    near_table, near_rows, gated = barrier((near_table, near_rows, gated))
+    wide = join(low, high, table, tokens.shape[1], SPARE)
+    near_table, near_rows, gated, wide = barrier((near_table, near_rows, gated, wide))
     near = pack(near_rows, near_table)
 
     far = cross(near, y, x)
     mine_near, other_near = rest_of(units_of([near], *weights), flip(near, CORE), *weights)
-    following = cross(join(low, high, table, tokens.shape[1], SPARE), y, x)
+    following = cross(wide, y, x)
     far, mine_near = barrier((far, mine_near))
 
     far_twin = flip(far, CORE)
     first = units_of([far], w_gate, w_up)
     first, far_twin = barrier((first, far_twin))
-    second = units_of([far_twin], w_gate, w_up)
-    mine_near, second = barrier((mine_near, second))
-    sum_near = add(mine_near, flip(other_near, CORE))
+    second, sum_near = units_and_sum(far_twin, w_gate, w_up, mine_near, flip(other_near, CORE))
     back = cross(sum_near, x, y)
     following, second = barrier((following, second))
     mine_far, *other_far = sums_of(first, second, w_down, pieces=2)

time: 52.4 us -> 52.3 us (level)
    pallas_call x0 -> x1, Pallas kernels: none -> 2.79 us  [units_and_sum(): pl.pallas_call(units_sum_kernel, in_specs=[VMEM_SPEC] * 5, out_specs=[VME...]
    pallas_call x3 -> x2, Pallas kernels: 7.4 us -> 4.79 us  [units_of(): pl.pallas_call(functools.partial(units_kernel, parts=len(parts)), in_spec...]
where the time goes in v9:
time: 52.3 us; the launch traced here: 52.1 us
  Pallas kernels  32 us (61%)
  starting transfers between devices  13.2 us (25%)
  waiting for transfers between devices  6.09 us (12%)
    ppermute x7, starting transfers between devices, cross(): lax.ppermute(x, 'ep', [(i, i ^ (odd if i % 2 else even)) for i in range(n)])  10.7 us
    pallas_call x2, Pallas kernels, units_of(): pl.pallas_call(functools.partial(units_kernel, parts=len(parts)), in_spec...  4.79 us
    pallas_call x2, Pallas kernels, sums_of(): pl.pallas_call(sums_kernel, in_specs=[VMEM_SPEC] * 3, out_specs=[VMEM_SPE...  4.71 us
    pallas_call x1, Pallas kernels, rest_of(): pl.pallas_call(rest_kernel, in_specs=[VMEM_SPEC] * 5, out_specs=[VMEM_SPE...  4.62 us
    pallas_call x2, Pallas kernels, gated_units(): pl.pallas_call(functools.partial(gated_kernel, parts=len(parts)), in_spec...  3.98 us
    ppermute x7, waiting for transfers between devices, cross(): lax.ppermute(x, 'ep', [(i, i ^ (odd if i % 2 else even)) for i in range(n)])  3.82 us
    pallas_call x1, Pallas kernels, both_units(): pl.pallas_call(both_kernel, in_specs=[VMEM_SPEC] * 5, out_specs=[VMEM_SPE...  3.73 us
    pallas_call x1, Pallas kernels, units_and_sum(): pl.pallas_call(units_sum_kernel, in_specs=[VMEM_SPEC] * 5, out_specs=[VME...  2.79 us
  transfers between devices with their start and end apart: 18, of which 9 were waited for; matrix products, arithmetic and copies ran while one was open for 0% of the time, Pallas kernels for 59%

profile of v9, /device:TPU:0, one launch (start us, length us, event | category | flops | bytes accessed | tf_op | source)
XLA Modules:
  0.0 52.1 jit_solution(2538287040824740089)
XLA Ops:
  0.0 2.9 %collective-permute-start.1 = (bf16[128,2048]{1,0:T(8,128)(2,1)}, bf16[128,2048]{1,0:T(8,128)(2,1)S(1)}, u32[]{:S(2)}, u32[]{:S(2)}) collective-permute-start(bf16[128,2048]{1,0:T(8,128)(2,1)} %tokens.1), channel_id=1, source_target_pairs={{0,2},{1,5},{2,0},{3,7},{4,6},{5,1},{6,4},{7,3},{8,10},{9,13},{10,... | collective-permute-start | bytes 1572872 | tf_op jit(solution)/shard_map/ppermute | solution.py:31
  3.0 1.3 %prepare.1 = (bf16[16,8320]{1,0:T(8,128)(2,1)S(1)}, bf16[16,8320]{1,0:T(8,128)(2,1)S(1)}, bf16[16,256]{1,0:T(8,128)(2,1)S(1)}) custom-call(bf16[128,2048]{1,0:T(8,128)(2,1)} %tokens.1, s32[10,128]{1,0:T(8,128)} %bitcast.6, bf16[10,128]{1,0:T(8,128)(2,1)} %bitcast.7), custom_call_target="tpu_custom_call" | custom-call | flops 99999997952 | bytes 100000000 | tf_op jit(solution)/shard_map/prepare/pallas_call | solution.py:87
  4.4 0.5 collective-permute-start.3
  4.9 0.6 %collective-permute-start = (bf16[16,256]{1,0:T(8,128)(2,1)S(1)}, bf16[16,256]{1,0:T(8,128)(2,1)S(1)}, u32[]{:S(2)}, u32[]{:S(2)}) collective-permute-start(bf16[16,256]{1,0:T(8,128)(2,1)S(1)} %get-tuple-element.43.table), channel_id=1, source_target_pairs={{0,2},{1,5},{2,0},{3,7},{4,6},{5,1},{6,4},{7,3},{8,10},{9,13},{10,... | collective-permute-start | bytes 24584 | tf_op jit(solution)/shard_map/ppermute | solution.py:31
  6.8 2.6 %gated_units.2 = (f32[256,2048]{1,0:T(8,128)S(1)}, bf16[256,2048]{1,0:T(8,128)(2,1)S(1)}) custom-call(bf16[16,8320]{1,0:T(8,128)(2,1)S(1)} %get-tuple-element.44.refs_0_.low, bf16[16,8320]{1,0:T(8,128)(2,1)S(1)} %get-tuple-element.45.refs_1_.high, bf16[16,8320]{1,0:T(8,128)(2,1)S(1)} %collective-permute-done.2.refs_2_, ...), custom_call_target="tpu_custom_call" | custom-call | tf_op jit(solution)/shard_map/gated_units/pallas_call | solution.py:209
  9.4 1.0 %collective-permute-done.table = bf16[16,256]{1,0:T(8,128)(2,1)S(1)} collective-permute-done((bf16[16,256]{1,0:T(8,128)(2,1)S(1)}, bf16[16,256]{1,0:T(8,128)(2,1)S(1)}, u32[]{:S(2)}, u32[]{:S(2)}) %collective-permute-start) | collective-permute-done | bytes 8224 | tf_op jit(solution)/shard_map/ppermute | solution.py:31
  10.5 2.1 %collective-permute-start.6 = (bf16[16,16640]{1,0:T(8,128)(2,1)S(1)}, bf16[16,16640]{1,0:T(8,128)(2,1)S(1)}, u32[]{:S(2)}, u32[]{:S(2)}) collective-permute-start(bf16[16,16640]{1,0:T(8,128)(2,1)S(1)} %pack.1.refs_0_), channel_id=1, source_target_pairs={{0,4},{1,3},{2,6},{3,1},{4,0},{5,7},{6,2},{7,5},{8,12},{9,11},{10,... | collective-permute-start | bytes 1597448 | tf_op jit(solution)/shard_map/ppermute | solution.py:31
  12.7 2.4 %units_of.2.first = bf16[128,2048]{1,0:T(8,128)(2,1)S(1)} custom-call(bf16[16,16640]{1,0:T(8,128)(2,1)S(1)} %pack.1.refs_0_, bf16[4,2048,512]{2,1,0:T(8,128)(2,1)S(1)} %copy-done, bf16[4,2048,512]{2,1,0:T(8,128)(2,1)S(1)} %bitcast.3, bf16[4,2048,512]{2,1,0:T(8,128)(2,1)S(1)} %bitcast.5), custom_call_target="tpu_custom_call" | custom-call | tf_op jit(solution)/shard_map/units_of/pallas_call | solution.py:251
  15.2 4.6 %rest_of.1 = (bf16[128,2048]{1,0:T(8,128)(2,1)S(1)}, bf16[128,2048]{1,0:T(8,128)(2,1)S(1)}) custom-call(bf16[128,2048]{1,0:T(8,128)(2,1)S(1)} %units_of.2.first, bf16[16,16640]{1,0:T(8,128)(2,1)S(1)} %collective-permute-done.7.part, bf16[4,2048,512]{2,1,0:T(8,128)(2,1)S(1)} %copy-done, bf16[4,2048,512]{2,1,0:T(8,128)(2,1)S(1)} %bitcast.3, ...), custom_call_target="tpu_custom_call" | custom-call | tf_op jit(solution)/shard_map/rest_of/pallas_call | solution.py:324
  20.4 2.4 %units_of.3.first = bf16[128,2048]{1,0:T(8,128)(2,1)S(1)} custom-call(bf16[16,16640]{1,0:T(8,128)(2,1)S(1)} %collective-permute-done.6.refs_0_, bf16[4,2048,512]{2,1,0:T(8,128)(2,1)S(1)} %copy-done, bf16[4,2048,512]{2,1,0:T(8,128)(2,1)S(1)} %bitcast.3), custom_call_target="tpu_custom_call" | custom-call | tf_op jit(solution)/shard_map/units_of/pallas_call | solution.py:251
  22.8 2.8 %units_and_sum.1 = (bf16[128,2048]{1,0:T(8,128)(2,1)S(1)}, bf16[128,2048]{1,0:T(8,128)(2,1)S(1)}) custom-call(bf16[16,16640]{1,0:T(8,128)(2,1)S(1)} %collective-permute-done.8.part, bf16[4,2048,512]{2,1,0:T(8,128)(2,1)S(1)} %copy-done, bf16[4,2048,512]{2,1,0:T(8,128)(2,1)S(1)} %bitcast.3, bf16[128,2048]{1,0:T(8,128)(2,1)S(1)} %get-tuple-element.59.mine, ...), custom_call_target="tpu_custom_call" | custom-call | tf_op jit(solution)/shard_map/units_and_sum/pallas_call | solution.py:274
  25.8 2.0 %collective-permute-start.14 = (bf16[128,2048]{1,0:T(8,128)(2,1)S(1)}, bf16[128,2048]{1,0:T(8,128)(2,1)S(1)}, u32[]{:S(2)}, u32[]{:S(2)}) collective-permute-start(bf16[128,2048]{1,0:T(8,128)(2,1)S(1)} %get-tuple-element.74), channel_id=1, source_target_pairs={{0,2},{1,5},{2,0},{3,7},{4,6},{5,1},{6,4},{7,3},{8,10},{9,13},{10,... | collective-permute-start | bytes 1572872 | tf_op jit(solution)/shard_map/ppermute | solution.py:31
  27.8 2.4 %sums_of.2 = (bf16[128,2048]{1,0:T(8,128)(2,1)S(1)}, bf16[64,2048]{1,0:T(8,128)(2,1)S(1)}, bf16[64,2048]{1,0:T(8,128)(2,1)S(1)}) custom-call(bf16[128,2048]{1,0:T(8,128)(2,1)S(1)} %units_of.3.first, bf16[128,2048]{1,0:T(8,128)(2,1)S(1)} %get-tuple-element.62.second, bf16[4,2048,512]{2,1,0:T(8,128)(2,1)S(1)} %bitcast.5), custom_call_target="tpu_custom_call" | custom-call | tf_op jit(solution)/shard_map/sums_of/pallas_call | solution.py:350
  30.7 1.4 %gated_units.3 = (f32[128,2048]{1,0:T(8,128)S(1)}, bf16[128,2048]{1,0:T(8,128)(2,1)S(1)}) custom-call(bf16[16,16768]{1,0:T(8,128)(2,1)S(1)} %collective-permute-done.9.refs_0_, bf16[4,2048,512]{2,1,0:T(8,128)(2,1)S(1)} %copy-done), custom_call_target="tpu_custom_call" | custom-call | tf_op jit(solution)/shard_map/gated_units/pallas_call | solution.py:209
  32.2 1.4 %collective-permute-start.15 = (bf16[128,2048]{1,0:T(8,128)(2,1)S(1)}, bf16[128,2048]{1,0:T(8,128)(2,1)S(1)}, u32[]{:S(2)}, u32[]{:S(2)}) collective-permute-start(bf16[128,2048]{1,0:T(8,128)(2,1)S(1)} %add_pieces.1), channel_id=1, source_target_pairs={{0,2},{1,5},{2,0},{3,7},{4,6},{5,1},{6,4},{7,3},{8,10},{9,13},{10,... | collective-permute-start | bytes 1572872 | tf_op jit(solution)/shard_map/ppermute | solution.py:31
  33.6 3.7 %both_units.1 = (bf16[128,2048]{1,0:T(8,128)(2,1)S(1)}, bf16[128,2048]{1,0:T(8,128)(2,1)S(1)}) custom-call(f32[128,2048]{1,0:T(8,128)S(1)} %get-tuple-element.70.gated, bf16[128,2048]{1,0:T(8,128)(2,1)S(1)} %get-tuple-element.71.gated_rows, bf16[16,16768]{1,0:T(8,128)(2,1)S(1)} %collective-permute-done.13.part, bf16[4,2048,512]{2,1,0:T(8,128)(2,1)S(1)} %copy-done, ...), custom_call_target="tpu_custom_call" | custom-call | tf_op jit(solution)/shard_map/both_units/pallas_call | solution.py:298
  37.4 2.4 %sums_of.3 = (bf16[128,2048]{1,0:T(8,128)(2,1)S(1)}, bf16[128,2048]{1,0:T(8,128)(2,1)S(1)}) custom-call(bf16[128,2048]{1,0:T(8,128)(2,1)S(1)} %get-tuple-element.76.first, bf16[128,2048]{1,0:T(8,128)(2,1)S(1)} %get-tuple-element.77.second, bf16[4,2048,512]{2,1,0:T(8,128)(2,1)S(1)} %bitcast.5), custom_call_target="tpu_custom_call" | custom-call | tf_op jit(solution)/shard_map/sums_of/pallas_call | solution.py:350
  39.9 1.6 %collective-permute-done.15.refs_1_ = bf16[128,2048]{1,0:T(8,128)(2,1)S(1)} collective-permute-done((bf16[128,2048]{1,0:T(8,128)(2,1)S(1)}, bf16[128,2048]{1,0:T(8,128)(2,1)S(1)}, u32[]{:S(2)}, u32[]{:S(2)}) %collective-permute-start.15) | collective-permute-done | bytes 524320 | tf_op jit(solution)/shard_map/ppermute | solution.py:31
  41.8 1.5 %collective-permute-start.17 = (bf16[128,2048]{1,0:T(8,128)(2,1)S(1)}, bf16[128,2048]{1,0:T(8,128)(2,1)S(1)}, u32[]{:S(2)}, u32[]{:S(2)}) collective-permute-start(bf16[128,2048]{1,0:T(8,128)(2,1)S(1)} %add.3), channel_id=1, source_target_pairs={{0,4},{1,3},{2,6},{3,1},{4,0},{5,7},{6,2},{7,5},{8,12},{9,11},{10,... | collective-permute-start | bytes 1572872 | tf_op jit(solution)/shard_map/ppermute | solution.py:31
  43.3 2.3 %hidden_units.1.hidden = bf16[256,2048]{1,0:T(8,128)(2,1)S(1)} custom-call(f32[256,2048]{1,0:T(8,128)S(1)} %get-tuple-element.47.gated, bf16[256,2048]{1,0:T(8,128)(2,1)S(1)} %get-tuple-element.48.rows, bf16[4,2048,512]{2,1,0:T(8,128)(2,1)S(1)} %bitcast.3), custom_call_target="tpu_custom_call" | custom-call | tf_op jit(solution)/shard_map/hidden_units/pallas_call | solution.py:229
  45.6 2.4 %down_units.1 = (bf16[128,2048]{1,0:T(8,128)(2,1)S(1)}, bf16[64,2048]{1,0:T(8,128)(2,1)S(1)}, bf16[64,2048]{1,0:T(8,128)(2,1)S(1)}) custom-call(bf16[256,2048]{1,0:T(8,128)(2,1)S(1)} %hidden_units.1.hidden, bf16[4,2048,512]{2,1,0:T(8,128)(2,1)S(1)} %bitcast.5), custom_call_target="tpu_custom_call" | custom-call | tf_op jit(solution)/shard_map/down_units/pallas_call | solution.py:385
  48.6 1.0 %collective-permute-done.4.refs_0_ = bf16[64,2048]{1,0:T(8,128)(2,1)S(1)} collective-permute-done((bf16[64,2048]{1,0:T(8,128)(2,1)S(1)}, bf16[64,2048]{1,0:T(8,128)(2,1)S(1)}, u32[]{:S(2)}, u32[]{:S(2)}) %collective-permute-start.4) | collective-permute-done | bytes 262176 | tf_op jit(solution)/shard_map/ppermute | solution.py:26
  50.0 1.1 %collective-permute-done.17.refs_4_ = bf16[128,2048]{1,0:T(8,128)(2,1)S(1)} collective-permute-done((bf16[128,2048]{1,0:T(8,128)(2,1)S(1)}, bf16[128,2048]{1,0:T(8,128)(2,1)S(1)}, u32[]{:S(2)}, u32[]{:S(2)}) %collective-permute-start.17) | collective-permute-done | bytes 524320 | tf_op jit(solution)/shard_map/ppermute | solution.py:31
  51.0 0.9 %finish.1 = bf16[128,2048]{1,0:T(8,128)(2,1)} custom-call(bf16[64,2048]{1,0:T(8,128)(2,1)S(1)} %collective-permute-done.4.refs_0_, bf16[64,2048]{1,0:T(8,128)(2,1)S(1)} %collective-permute-done.5.refs_1_, bf16[128,2048]{1,0:T(8,128)(2,1)S(1)} %get-tuple-element.51.refs_2_, bf16[128,2048]{1,0:T(8,128)(2,1)S(1)} %collective-permute-done.14.refs_3_, ...), custom_call_target="tpu_custom_call" | custom-call | tf_op jit(solution)/shard_map/finish/pallas_call | solution.py:441
  (42 shorter events, 4.3 us)
Async XLA Ops:
  0.0 10.4 %collective-permute-start.1 = (bf16[128,2048]{1,0:T(8,128)(2,1)}, bf16[128,2048]{1,0:T(8,128)(2,1)S(1)}, u32[]{:S(2)}, u32[]{:S(2)}) collective-permute-start(bf16[128,2048]{1,0:T(8,128)(2,1)} %tokens.1), channel_id=1, source_target_pairs={{0,2},{1,5},{2,0},{3,7},{4,6},{5,1},{6,4},{7,3},{8,10},{9,13},{10,... | collective-permute-start | bytes 1572872 | tf_op jit(solution)/shard_map/ppermute | solution.py:31
  2.9 9.8 %slice-start = ((s8[8388608]{0:T(1024)(128)(4,1)}), s8[4194304]{0:T(1024)(128)(4,1)S(1)}, s32[]{:S(2)}) async-start(s8[8388608]{0:T(1024)(128)(4,1)} %bitcast.2), calls=%async_computation | async-start | bytes 8388608
  2.9 9.8 %slice-start.2 = ((s8[8388608]{0:T(1024)(128)(4,1)}), s8[4194304]{0:T(1024)(128)(4,1)S(1)}, s32[]{:S(2)}) async-start(s8[8388608]{0:T(1024)(128)(4,1)} %bitcast.4), calls=%async_computation.2 | async-start | bytes 8388608
  2.9 3.8 %copy-start = (bf16[4,2048,512]{2,1,0:T(8,128)(2,1)S(1)}, bf16[4,2048,512]{2,1,0:T(8,128)(2,1)}, u32[]{:S(2)}) copy-start(bf16[4,2048,512]{2,1,0:T(8,128)(2,1)} %w_gate.5) | copy-start | bytes 25165828
  2.9 9.8 %slice-start.1 = ((s8[8388608]{0:T(1024)(128)(4,1)}), s8[4194304]{0:T(1024)(128)(4,1)S(1)}, s32[]{:S(2)}) async-start(s8[8388608]{0:T(1024)(128)(4,1)} %bitcast.2), calls=%async_computation.1 | async-start | bytes 8388608
  3.0 9.8 %slice-start.3 = ((s8[8388608]{0:T(1024)(128)(4,1)}), s8[4194304]{0:T(1024)(128)(4,1)S(1)}, s32[]{:S(2)}) async-start(s8[8388608]{0:T(1024)(128)(4,1)} %bitcast.4), calls=%async_computation.3 | async-start | bytes 8388608
  4.3 1.6 %collective-permute-start.2 = (bf16[16,8320]{1,0:T(8,128)(2,1)S(1)}, bf16[16,8320]{1,0:T(8,128)(2,1)S(1)}, u32[]{:S(2)}, u32[]{:S(2)}) collective-permute-start(bf16[16,8320]{1,0:T(8,128)(2,1)S(1)} %get-tuple-element.44.refs_0_.low), channel_id=1, source_target_pairs={{0,1},{1,0},{2,3},{3,2},{4,5},{5,4},{6,7},{7,6},{8,9},{9,8},{10,11... | collective-permute-start | bytes 798728 | tf_op jit(solution)/shard_map/ppermute | solution.py:26
  4.4 1.9 %collective-permute-start.3 = (bf16[16,8320]{1,0:T(8,128)(2,1)S(1)}, bf16[16,8320]{1,0:T(8,128)(2,1)S(1)}, u32[]{:S(2)}, u32[]{:S(2)}) collective-permute-start(bf16[16,8320]{1,0:T(8,128)(2,1)S(1)} %get-tuple-element.45.refs_1_.high), channel_id=1, source_target_pairs={{0,1},{1,0},{2,3},{3,2},{4,5},{5,4},{6,7},{7,6},{8,9},{9,8},{10,11... | collective-permute-start | bytes 798728 | tf_op jit(solution)/shard_map/ppermute | solution.py:26
  4.9 5.5 %collective-permute-start = (bf16[16,256]{1,0:T(8,128)(2,1)S(1)}, bf16[16,256]{1,0:T(8,128)(2,1)S(1)}, u32[]{:S(2)}, u32[]{:S(2)}) collective-permute-start(bf16[16,256]{1,0:T(8,128)(2,1)S(1)} %get-tuple-element.43.table), channel_id=1, source_target_pairs={{0,2},{1,5},{2,0},{3,7},{4,6},{5,1},{6,4},{7,3},{8,10},{9,13},{10,... | collective-permute-start | bytes 24584 | tf_op jit(solution)/shard_map/ppermute | solution.py:31
  10.4 4.7 %collective-permute-start.7 = (bf16[16,16640]{1,0:T(8,128)(2,1)S(1)}, bf16[16,16640]{1,0:T(8,128)(2,1)S(1)}, u32[]{:S(2)}, u32[]{:S(2)}) collective-permute-start(bf16[16,16640]{1,0:T(8,128)(2,1)S(1)} %pack.1.refs_0_), channel_id=1, source_target_pairs={{0,1},{1,0},{2,3},{3,2},{4,5},{5,4},{6,7},{7,6},{8,9},{9,8},{10,11... | collective-permute-start | bytes 1597448 | tf_op jit(solution)/shard_map/ppermute | solution.py:26
  10.5 9.4 %collective-permute-start.6 = (bf16[16,16640]{1,0:T(8,128)(2,1)S(1)}, bf16[16,16640]{1,0:T(8,128)(2,1)S(1)}, u32[]{:S(2)}, u32[]{:S(2)}) collective-permute-start(bf16[16,16640]{1,0:T(8,128)(2,1)S(1)} %pack.1.refs_0_), channel_id=1, source_target_pairs={{0,4},{1,3},{2,6},{3,1},{4,0},{5,7},{6,2},{7,5},{8,12},{9,11},{10,... | collective-permute-start | bytes 1597448 | tf_op jit(solution)/shard_map/ppermute | solution.py:31
  12.6 13.0 %collective-permute-start.9 = (bf16[16,16768]{1,0:T(8,128)(2,1)S(1)}, bf16[16,16768]{1,0:T(8,128)(2,1)S(1)}, u32[]{:S(2)}, u32[]{:S(2)}) collective-permute-start(bf16[16,16768]{1,0:T(8,128)(2,1)S(1)} %join.1), channel_id=1, source_target_pairs={{0,4},{1,3},{2,6},{3,1},{4,0},{5,7},{6,2},{7,5},{8,12},{9,11},{10,... | collective-permute-start | bytes 1609736 | tf_op jit(solution)/shard_map/ppermute | solution.py:31
  19.9 2.9 %collective-permute-start.8 = (bf16[16,16640]{1,0:T(8,128)(2,1)S(1)}, bf16[16,16640]{1,0:T(8,128)(2,1)S(1)}, u32[]{:S(2)}, u32[]{:S(2)}) collective-permute-start(bf16[16,16640]{1,0:T(8,128)(2,1)S(1)} %collective-permute-done.6.refs_0_), channel_id=1, source_target_pairs={{0,1},{1,0},{2,3},{3,2},{4,5},{5,4},{6,7},{7,6},{8,9},{9,8},{10,11... | collective-permute-start | bytes 1597448 | tf_op jit(solution)/shard_map/ppermute | solution.py:26
  19.9 2.9 %collective-permute-start.10 = (bf16[128,2048]{1,0:T(8,128)(2,1)S(1)}, bf16[128,2048]{1,0:T(8,128)(2,1)S(1)}, u32[]{:S(2)}, u32[]{:S(2)}) collective-permute-start(bf16[128,2048]{1,0:T(8,128)(2,1)S(1)} %get-tuple-element.60), channel_id=1, source_target_pairs={{0,1},{1,0},{2,3},{3,2},{4,5},{5,4},{6,7},{7,6},{8,9},{9,8},{10,11... | collective-permute-start | bytes 1572872 | tf_op jit(solution)/shard_map/ppermute | solution.py:26
  25.6 6.6 %collective-permute-start.13 = (bf16[16,16768]{1,0:T(8,128)(2,1)S(1)}, bf16[16,16768]{1,0:T(8,128)(2,1)S(1)}, u32[]{:S(2)}, u32[]{:S(2)}) collective-permute-start(bf16[16,16768]{1,0:T(8,128)(2,1)S(1)} %collective-permute-done.9.refs_0_), channel_id=1, source_target_pairs={{0,1},{1,0},{2,3},{3,2},{4,5},{5,4},{6,7},{7,6},{8,9},{9,8},{10,11... | collective-permute-start | bytes 1609736 | tf_op jit(solution)/shard_map/ppermute | solution.py:26
  25.8 11.6 %collective-permute-start.14 = (bf16[128,2048]{1,0:T(8,128)(2,1)S(1)}, bf16[128,2048]{1,0:T(8,128)(2,1)S(1)}, u32[]{:S(2)}, u32[]{:S(2)}) collective-permute-start(bf16[128,2048]{1,0:T(8,128)(2,1)S(1)} %get-tuple-element.74), channel_id=1, source_target_pairs={{0,2},{1,5},{2,0},{3,7},{4,6},{5,1},{6,4},{7,3},{8,10},{9,13},{10,... | collective-permute-start | bytes 1572872 | tf_op jit(solution)/shard_map/ppermute | solution.py:31
  30.1 1.9 %collective-permute-start.11 = (bf16[64,2048]{1,0:T(8,128)(2,1)S(1)}, bf16[64,2048]{1,0:T(8,128)(2,1)S(1)}, u32[]{:S(2)}, u32[]{:S(2)}) collective-permute-start(bf16[64,2048]{1,0:T(8,128)(2,1)S(1)} %get-tuple-element.67), channel_id=1, source_target_pairs={{0,1},{1,0},{2,3},{3,2},{4,5},{5,4},{6,7},{7,6},{8,9},{9,8},{10,11... | collective-permute-start | bytes 786440 | tf_op jit(solution)/shard_map/ppermute | solution.py:26
  30.4 1.7 %collective-permute-start.12 = (bf16[64,2048]{1,0:T(8,128)(2,1)S(1)}, bf16[64,2048]{1,0:T(8,128)(2,1)S(1)}, u32[]{:S(2)}, u32[]{:S(2)}) collective-permute-start(bf16[64,2048]{1,0:T(8,128)(2,1)S(1)} %get-tuple-element.68), channel_id=1, source_target_pairs={{0,1},{1,0},{2,3},{3,2},{4,5},{5,4},{6,7},{7,6},{8,9},{9,8},{10,11... | collective-permute-start | bytes 786440 | tf_op jit(solution)/shard_map/ppermute | solution.py:26
  32.2 9.2 %collective-permute-start.15 = (bf16[128,2048]{1,0:T(8,128)(2,1)S(1)}, bf16[128,2048]{1,0:T(8,128)(2,1)S(1)}, u32[]{:S(2)}, u32[]{:S(2)}) collective-permute-start(bf16[128,2048]{1,0:T(8,128)(2,1)S(1)} %add_pieces.1), channel_id=1, source_target_pairs={{0,2},{1,5},{2,0},{3,7},{4,6},{5,1},{6,4},{7,3},{8,10},{9,13},{10,... | collective-permute-start | bytes 1572872 | tf_op jit(solution)/shard_map/ppermute | solution.py:31
  39.7 2.0 %collective-permute-start.16 = (bf16[128,2048]{1,0:T(8,128)(2,1)S(1)}, bf16[128,2048]{1,0:T(8,128)(2,1)S(1)}, u32[]{:S(2)}, u32[]{:S(2)}) collective-permute-start(bf16[128,2048]{1,0:T(8,128)(2,1)S(1)} %get-tuple-element.80), channel_id=1, source_target_pairs={{0,1},{1,0},{2,3},{3,2},{4,5},{5,4},{6,7},{7,6},{8,9},{9,8},{10,11... | collective-permute-start | bytes 1572872 | tf_op jit(solution)/shard_map/ppermute | solution.py:26
  41.8 9.2 %collective-permute-start.17 = (bf16[128,2048]{1,0:T(8,128)(2,1)S(1)}, bf16[128,2048]{1,0:T(8,128)(2,1)S(1)}, u32[]{:S(2)}, u32[]{:S(2)}) collective-permute-start(bf16[128,2048]{1,0:T(8,128)(2,1)S(1)} %add.3), channel_id=1, source_target_pairs={{0,4},{1,3},{2,6},{3,1},{4,0},{5,7},{6,2},{7,5},{8,12},{9,11},{10,... | collective-permute-start | bytes 1572872 | tf_op jit(solution)/shard_map/ppermute | solution.py:31
  48.0 1.6 %collective-permute-start.4 = (bf16[64,2048]{1,0:T(8,128)(2,1)S(1)}, bf16[64,2048]{1,0:T(8,128)(2,1)S(1)}, u32[]{:S(2)}, u32[]{:S(2)}) collective-permute-start(bf16[64,2048]{1,0:T(8,128)(2,1)S(1)} %get-tuple-element.49), channel_id=1, source_target_pairs={{0,1},{1,0},{2,3},{3,2},{4,5},{5,4},{6,7},{7,6},{8,9},{9,8},{10,11... | collective-permute-start | bytes 786440 | tf_op jit(solution)/shard_map/ppermute | solution.py:26
  48.1 1.9 %collective-permute-start.5 = (bf16[64,2048]{1,0:T(8,128)(2,1)S(1)}, bf16[64,2048]{1,0:T(8,128)(2,1)S(1)}, u32[]{:S(2)}, u32[]{:S(2)}) collective-permute-start(bf16[64,2048]{1,0:T(8,128)(2,1)S(1)} %get-tuple-element.50), channel_id=1, source_target_pairs={{0,1},{1,0},{2,3},{3,2},{4,5},{5,4},{6,7},{7,6},{8,9},{9,8},{10,11... | collective-permute-start | bytes 786440 | tf_op jit(solution)/shard_map/ppermute | solution.py:26

commit v10 on v8

--- a/solution.py
+++ b/solution.py
@@ -16,7 +16,7 @@
 PACK = 16
 SPARE = LANES
 MEDIUM = pl.CostEstimate(flops=0, bytes_accessed=3 * 10**6, transcendentals=0)
-RELAY = pl.CostEstimate(flops=2 * 10**9, bytes_accessed=3 * 10**6, transcendentals=0)
+RELAY = pl.CostEstimate(flops=2 * 10**8, bytes_accessed=3 * 10**6, transcendentals=0)
 LONG = pl.CostEstimate(flops=10**11, bytes_accessed=10**8, transcendentals=0)
 COST = pl.CostEstimate(flops=0, bytes_accessed=0, transcendentals=0)
 
@@ -405,7 +405,7 @@
         size = twins[0].shape[0]
         total = twins[start // size][pl.ds(start % size, count)].astype(jnp.float32)
         for part in parts:
-            total += part[rows].astype(jnp.float32)
+            total += part[rows, : block.shape[2]].astype(jnp.float32)
         block[i] = total.astype(block.dtype)
         copies.append(pltpu.make_async_copy(block.at[i], out.at[rows], sems.at[i]))
         copies[-1].start()
@@ -449,10 +449,10 @@
     first, far_twin = barrier((first, far_twin))
     second = units_of([far_twin], w_gate, w_up)
     mine_near, second = barrier((mine_near, second))
-    sum_near = add(mine_near, flip(other_near, CORE))
+    sum_near = add(mine_near, flip(other_near, CORE), spare=LANES)
     back = cross(sum_near, x, y)
     following, second = barrier((following, second))
-    mine_far, *other_far = sums_of(first, second, w_down, pieces=2)
+    mine_far, *other_far = sums_of(first, second, w_down)
 
     following_twin = flip(following, CORE)
     first, first_rows = gated_units([following], w_gate)

time: 52.4 us -> 52.2 us (level)
    ppermute x7, waiting for transfers between devices: 3.98 us -> 3.43 us  [cross(): lax.ppermute(x, 'ep', [(i, i ^ (odd if i % 2 else even)) for i in range(n)])]
    ppermute x11 -> x10, starting transfers between devices: 2.43 us -> 2.86 us  [flip(): return lax.ppermute(x, 'ep', [(i, i ^ mask) for i in range(n)])]
    ppermute x11 -> x10, waiting for transfers between devices: 2.28 us -> 2.3 us  [flip(): return lax.ppermute(x, 'ep', [(i, i ^ mask) for i in range(n)])]
  transfers between devices with their start and end apart: 18 -> 17, of which waited for: 9 -> 9; matrix products, arithmetic and copies ran while one was open for 0% -> 0% of each run, Pallas kernels for 59% -> 59%
where the time goes in v10:
time: 52.2 us; the launch traced here: 52.1 us
  Pallas kernels  32.1 us (61%)
  starting transfers between devices  13.4 us (26%)
  waiting for transfers between devices  5.74 us (11%)
    ppermute x7, starting transfers between devices, cross(): lax.ppermute(x, 'ep', [(i, i ^ (odd if i % 2 else even)) for i in range(n)])  10.6 us
    pallas_call x3, Pallas kernels, units_of(): pl.pallas_call(functools.partial(units_kernel, parts=len(parts)), in_spec...  7.39 us
    pallas_call x2, Pallas kernels, sums_of(): pl.pallas_call(sums_kernel, in_specs=[VMEM_SPEC] * 3, out_specs=[VMEM_SPE...  4.71 us
    pallas_call x1, Pallas kernels, rest_of(): pl.pallas_call(rest_kernel, in_specs=[VMEM_SPEC] * 5, out_specs=[VMEM_SPE...  4.62 us
    pallas_call x2, Pallas kernels, gated_units(): pl.pallas_call(functools.partial(gated_kernel, parts=len(parts)), in_spec...  4.1 us
    pallas_call x1, Pallas kernels, both_units(): pl.pallas_call(both_kernel, in_specs=[VMEM_SPEC] * 5, out_specs=[VMEM_SPE...  3.74 us
    ppermute x7, waiting for transfers between devices, cross(): lax.ppermute(x, 'ep', [(i, i ^ (odd if i % 2 else even)) for i in range(n)])  3.43 us
    ppermute x10, starting transfers between devices, flip(): return lax.ppermute(x, 'ep', [(i, i ^ mask) for i in range(n)])  2.86 us
  transfers between devices with their start and end apart: 17, of which 9 were waited for; matrix products, arithmetic and copies ran while one was open for 0% of the time, Pallas kernels for 59%

profile of v10, /device:TPU:0, one launch (start us, length us, event | category | flops | bytes accessed | tf_op | source)
XLA Modules:
  0.0 52.1 jit_solution(14519518527842231351)
XLA Ops:
  0.0 2.9 %collective-permute-start.1 = (bf16[128,2048]{1,0:T(8,128)(2,1)}, bf16[128,2048]{1,0:T(8,128)(2,1)S(1)}, u32[]{:S(2)}, u32[]{:S(2)}) collective-permute-start(bf16[128,2048]{1,0:T(8,128)(2,1)} %tokens.1), channel_id=1, source_target_pairs={{0,2},{1,5},{2,0},{3,7},{4,6},{5,1},{6,4},{7,3},{8,10},{9,13},{10,... | collective-permute-start | bytes 1572872 | tf_op jit(solution)/shard_map/ppermute | solution.py:31
  3.0 1.3 %prepare.1 = (bf16[16,8320]{1,0:T(8,128)(2,1)S(1)}, bf16[16,8320]{1,0:T(8,128)(2,1)S(1)}, bf16[16,256]{1,0:T(8,128)(2,1)S(1)}) custom-call(bf16[128,2048]{1,0:T(8,128)(2,1)} %tokens.1, s32[10,128]{1,0:T(8,128)} %bitcast.6, bf16[10,128]{1,0:T(8,128)(2,1)} %bitcast.7), custom_call_target="tpu_custom_call" | custom-call | flops 99999997952 | bytes 100000000 | tf_op jit(solution)/shard_map/prepare/pallas_call | solution.py:87
  4.9 0.6 %collective-permute-start = (bf16[16,256]{1,0:T(8,128)(2,1)S(1)}, bf16[16,256]{1,0:T(8,128)(2,1)S(1)}, u32[]{:S(2)}, u32[]{:S(2)}) collective-permute-start(bf16[16,256]{1,0:T(8,128)(2,1)S(1)} %get-tuple-element.41.table), channel_id=1, source_target_pairs={{0,2},{1,5},{2,0},{3,7},{4,6},{5,1},{6,4},{7,3},{8,10},{9,13},{10,... | collective-permute-start | bytes 24584 | tf_op jit(solution)/shard_map/ppermute | solution.py:31
  6.8 2.6 %gated_units.2 = (f32[256,2048]{1,0:T(8,128)S(1)}, bf16[256,2048]{1,0:T(8,128)(2,1)S(1)}) custom-call(bf16[16,8320]{1,0:T(8,128)(2,1)S(1)} %get-tuple-element.42.refs_0_.low, bf16[16,8320]{1,0:T(8,128)(2,1)S(1)} %get-tuple-element.43.refs_1_.high, bf16[16,8320]{1,0:T(8,128)(2,1)S(1)} %collective-permute-done.2.refs_2_, ...), custom_call_target="tpu_custom_call" | custom-call | tf_op jit(solution)/shard_map/gated_units/pallas_call | solution.py:209
  9.4 1.0 %collective-permute-done.table = bf16[16,256]{1,0:T(8,128)(2,1)S(1)} collective-permute-done((bf16[16,256]{1,0:T(8,128)(2,1)S(1)}, bf16[16,256]{1,0:T(8,128)(2,1)S(1)}, u32[]{:S(2)}, u32[]{:S(2)}) %collective-permute-start) | collective-permute-done | bytes 8224 | tf_op jit(solution)/shard_map/ppermute | solution.py:31
  10.5 2.1 %collective-permute-start.6 = (bf16[16,16640]{1,0:T(8,128)(2,1)S(1)}, bf16[16,16640]{1,0:T(8,128)(2,1)S(1)}, u32[]{:S(2)}, u32[]{:S(2)}) collective-permute-start(bf16[16,16640]{1,0:T(8,128)(2,1)S(1)} %pack.1.refs_0_), channel_id=1, source_target_pairs={{0,4},{1,3},{2,6},{3,1},{4,0},{5,7},{6,2},{7,5},{8,12},{9,11},{10,... | collective-permute-start | bytes 1597448 | tf_op jit(solution)/shard_map/ppermute | solution.py:31
  12.8 2.4 %units_of.3.first = bf16[128,2048]{1,0:T(8,128)(2,1)S(1)} custom-call(bf16[16,16640]{1,0:T(8,128)(2,1)S(1)} %pack.1.refs_0_, bf16[4,2048,512]{2,1,0:T(8,128)(2,1)S(1)} %copy-done, bf16[4,2048,512]{2,1,0:T(8,128)(2,1)S(1)} %bitcast.3, bf16[4,2048,512]{2,1,0:T(8,128)(2,1)S(1)} %bitcast.5), custom_call_target="tpu_custom_call" | custom-call | tf_op jit(solution)/shard_map/units_of/pallas_call | solution.py:251
  15.2 4.6 %rest_of.1 = (bf16[128,2048]{1,0:T(8,128)(2,1)S(1)}, bf16[128,2048]{1,0:T(8,128)(2,1)S(1)}) custom-call(bf16[128,2048]{1,0:T(8,128)(2,1)S(1)} %units_of.3.first, bf16[16,16640]{1,0:T(8,128)(2,1)S(1)} %collective-permute-done.7.part, bf16[4,2048,512]{2,1,0:T(8,128)(2,1)S(1)} %copy-done, bf16[4,2048,512]{2,1,0:T(8,128)(2,1)S(1)} %bitcast.3, ...), custom_call_target="tpu_custom_call" | custom-call | tf_op jit(solution)/shard_map/rest_of/pallas_call | solution.py:301
  20.4 2.4 %units_of.4.first = bf16[128,2048]{1,0:T(8,128)(2,1)S(1)} custom-call(bf16[16,16640]{1,0:T(8,128)(2,1)S(1)} %collective-permute-done.6.refs_0_, bf16[4,2048,512]{2,1,0:T(8,128)(2,1)S(1)} %copy-done, bf16[4,2048,512]{2,1,0:T(8,128)(2,1)S(1)} %bitcast.3), custom_call_target="tpu_custom_call" | custom-call | tf_op jit(solution)/shard_map/units_of/pallas_call | solution.py:251
  22.8 2.6 %units_of.5.second = bf16[128,2048]{1,0:T(8,128)(2,1)S(1)} custom-call(bf16[16,16640]{1,0:T(8,128)(2,1)S(1)} %collective-permute-done.8.refs_0_, bf16[4,2048,512]{2,1,0:T(8,128)(2,1)S(1)} %copy-done, bf16[4,2048,512]{2,1,0:T(8,128)(2,1)S(1)} %bitcast.3), custom_call_target="tpu_custom_call" | custom-call | tf_op jit(solution)/shard_map/units_of/pallas_call | solution.py:251
  25.6 2.0 %collective-permute-start.13 = (bf16[128,2176]{1,0:T(8,128)(2,1)S(1)}, bf16[128,2176]{1,0:T(8,128)(2,1)S(1)}, u32[]{:S(2)}, u32[]{:S(2)}) collective-permute-start(bf16[128,2176]{1,0:T(8,128)(2,1)S(1)} %add.3), channel_id=1, source_target_pairs={{0,2},{1,5},{2,0},{3,7},{4,6},{5,1},{6,4},{7,3},{8,10},{9,13},{10,... | collective-permute-start | bytes 1671176 | tf_op jit(solution)/shard_map/ppermute | solution.py:31
  27.6 2.4 %sums_of.2 = (bf16[128,2048]{1,0:T(8,128)(2,1)S(1)}, bf16[128,2048]{1,0:T(8,128)(2,1)S(1)}) custom-call(bf16[128,2048]{1,0:T(8,128)(2,1)S(1)} %units_of.4.first, bf16[128,2048]{1,0:T(8,128)(2,1)S(1)} %units_of.5.second, bf16[4,2048,512]{2,1,0:T(8,128)(2,1)S(1)} %bitcast.5), custom_call_target="tpu_custom_call" | custom-call | tf_op jit(solution)/shard_map/sums_of/pallas_call | solution.py:327
  30.0 0.6 %collective-permute-start.10 = (bf16[128,2048]{1,0:T(8,128)(2,1)S(1)}, bf16[128,2048]{1,0:T(8,128)(2,1)S(1)}, u32[]{:S(2)}, u32[]{:S(2)}) collective-permute-start(bf16[128,2048]{1,0:T(8,128)(2,1)S(1)} %get-tuple-element.63), channel_id=1, source_target_pairs={{0,1},{1,0},{2,3},{3,2},{4,5},{5,4},{6,7},{7,6},{8,9},{9,8},{10,11... | collective-permute-start | bytes 1572872 | tf_op jit(solution)/shard_map/ppermute | solution.py:26
  30.6 1.5 %gated_units.3 = (f32[128,2048]{1,0:T(8,128)S(1)}, bf16[128,2048]{1,0:T(8,128)(2,1)S(1)}) custom-call(bf16[16,16768]{1,0:T(8,128)(2,1)S(1)} %collective-permute-done.9.refs_0_, bf16[4,2048,512]{2,1,0:T(8,128)(2,1)S(1)} %copy-done), custom_call_target="tpu_custom_call" | custom-call | tf_op jit(solution)/shard_map/gated_units/pallas_call | solution.py:209
  32.2 1.2 %collective-permute-start.14 = (bf16[128,2048]{1,0:T(8,128)(2,1)S(1)}, bf16[128,2048]{1,0:T(8,128)(2,1)S(1)}, u32[]{:S(2)}, u32[]{:S(2)}) collective-permute-start(bf16[128,2048]{1,0:T(8,128)(2,1)S(1)} %add_pieces.1), channel_id=1, source_target_pairs={{0,2},{1,5},{2,0},{3,7},{4,6},{5,1},{6,4},{7,3},{8,10},{9,13},{10,... | collective-permute-start | bytes 1572872 | tf_op jit(solution)/shard_map/ppermute | solution.py:31
  33.5 3.7 %both_units.1 = (bf16[128,2048]{1,0:T(8,128)(2,1)S(1)}, bf16[128,2048]{1,0:T(8,128)(2,1)S(1)}) custom-call(f32[128,2048]{1,0:T(8,128)S(1)} %get-tuple-element.65.gated, bf16[128,2048]{1,0:T(8,128)(2,1)S(1)} %get-tuple-element.66.gated_rows, bf16[16,16768]{1,0:T(8,128)(2,1)S(1)} %collective-permute-done.11.part, bf16[4,2048,512]{2,1,0:T(8,128)(2,1)S(1)} %copy-done, ...), custom_call_target="tpu_custom_call" | custom-call | tf_op jit(solution)/shard_map/both_units/pallas_call | solution.py:275
  37.2 2.4 %sums_of.3 = (bf16[128,2048]{1,0:T(8,128)(2,1)S(1)}, bf16[128,2048]{1,0:T(8,128)(2,1)S(1)}) custom-call(bf16[128,2048]{1,0:T(8,128)(2,1)S(1)} %get-tuple-element.72.first, bf16[128,2048]{1,0:T(8,128)(2,1)S(1)} %get-tuple-element.73.second, bf16[4,2048,512]{2,1,0:T(8,128)(2,1)S(1)} %bitcast.5), custom_call_target="tpu_custom_call" | custom-call | tf_op jit(solution)/shard_map/sums_of/pallas_call | solution.py:327
  40.1 1.4 %collective-permute-done.14.refs_1_ = bf16[128,2048]{1,0:T(8,128)(2,1)S(1)} collective-permute-done((bf16[128,2048]{1,0:T(8,128)(2,1)S(1)}, bf16[128,2048]{1,0:T(8,128)(2,1)S(1)}, u32[]{:S(2)}, u32[]{:S(2)}) %collective-permute-start.14) | collective-permute-done | bytes 524320 | tf_op jit(solution)/shard_map/ppermute | solution.py:31
  41.7 1.5 %collective-permute-start.16 = (bf16[128,2048]{1,0:T(8,128)(2,1)S(1)}, bf16[128,2048]{1,0:T(8,128)(2,1)S(1)}, u32[]{:S(2)}, u32[]{:S(2)}) collective-permute-start(bf16[128,2048]{1,0:T(8,128)(2,1)S(1)} %add.5), channel_id=1, source_target_pairs={{0,4},{1,3},{2,6},{3,1},{4,0},{5,7},{6,2},{7,5},{8,12},{9,11},{10,... | collective-permute-start | bytes 1572872 | tf_op jit(solution)/shard_map/ppermute | solution.py:31
  43.3 2.3 %hidden_units.1.hidden = bf16[256,2048]{1,0:T(8,128)(2,1)S(1)} custom-call(f32[256,2048]{1,0:T(8,128)S(1)} %get-tuple-element.45.gated, bf16[256,2048]{1,0:T(8,128)(2,1)S(1)} %get-tuple-element.46.rows, bf16[4,2048,512]{2,1,0:T(8,128)(2,1)S(1)} %bitcast.3), custom_call_target="tpu_custom_call" | custom-call | tf_op jit(solution)/shard_map/hidden_units/pallas_call | solution.py:229
  45.6 2.4 %down_units.1 = (bf16[128,2048]{1,0:T(8,128)(2,1)S(1)}, bf16[64,2048]{1,0:T(8,128)(2,1)S(1)}, bf16[64,2048]{1,0:T(8,128)(2,1)S(1)}) custom-call(bf16[256,2048]{1,0:T(8,128)(2,1)S(1)} %hidden_units.1.hidden, bf16[4,2048,512]{2,1,0:T(8,128)(2,1)S(1)} %bitcast.5), custom_call_target="tpu_custom_call" | custom-call | tf_op jit(solution)/shard_map/down_units/pallas_call | solution.py:362
  48.6 1.0 %collective-permute-done.4.refs_0_ = bf16[64,2048]{1,0:T(8,128)(2,1)S(1)} collective-permute-done((bf16[64,2048]{1,0:T(8,128)(2,1)S(1)}, bf16[64,2048]{1,0:T(8,128)(2,1)S(1)}, u32[]{:S(2)}, u32[]{:S(2)}) %collective-permute-start.4) | collective-permute-done | bytes 262176 | tf_op jit(solution)/shard_map/ppermute | solution.py:26
  50.0 1.0 %collective-permute-done.16.refs_4_ = bf16[128,2048]{1,0:T(8,128)(2,1)S(1)} collective-permute-done((bf16[128,2048]{1,0:T(8,128)(2,1)S(1)}, bf16[128,2048]{1,0:T(8,128)(2,1)S(1)}, u32[]{:S(2)}, u32[]{:S(2)}) %collective-permute-start.16) | collective-permute-done | bytes 524320 | tf_op jit(solution)/shard_map/ppermute | solution.py:31
  51.0 1.0 %finish.1 = bf16[128,2048]{1,0:T(8,128)(2,1)} custom-call(bf16[64,2048]{1,0:T(8,128)(2,1)S(1)} %collective-permute-done.4.refs_0_, bf16[64,2048]{1,0:T(8,128)(2,1)S(1)} %collective-permute-done.5.refs_1_, bf16[128,2048]{1,0:T(8,128)(2,1)S(1)} %get-tuple-element.49.refs_2_, bf16[128,2176]{1,0:T(8,128)(2,1)S(1)} %collective-permute-done.13.refs_3_, ...), custom_call_target="tpu_custom_call" | custom-call | tf_op jit(solution)/shard_map/finish/pallas_call | solution.py:418
  (41 shorter events, 4.7 us)
Async XLA Ops:
  0.0 10.4 %collective-permute-start.1 = (bf16[128,2048]{1,0:T(8,128)(2,1)}, bf16[128,2048]{1,0:T(8,128)(2,1)S(1)}, u32[]{:S(2)}, u32[]{:S(2)}) collective-permute-start(bf16[128,2048]{1,0:T(8,128)(2,1)} %tokens.1), channel_id=1, source_target_pairs={{0,2},{1,5},{2,0},{3,7},{4,6},{5,1},{6,4},{7,3},{8,10},{9,13},{10,... | collective-permute-start | bytes 1572872 | tf_op jit(solution)/shard_map/ppermute | solution.py:31
  2.9 9.8 %slice-start = ((s8[8388608]{0:T(1024)(128)(4,1)}), s8[4194304]{0:T(1024)(128)(4,1)S(1)}, s32[]{:S(2)}) async-start(s8[8388608]{0:T(1024)(128)(4,1)} %bitcast.2), calls=%async_computation | async-start | bytes 8388608
  2.9 9.8 %slice-start.2 = ((s8[8388608]{0:T(1024)(128)(4,1)}), s8[4194304]{0:T(1024)(128)(4,1)S(1)}, s32[]{:S(2)}) async-start(s8[8388608]{0:T(1024)(128)(4,1)} %bitcast.4), calls=%async_computation.2 | async-start | bytes 8388608
  2.9 3.8 %copy-start = (bf16[4,2048,512]{2,1,0:T(8,128)(2,1)S(1)}, bf16[4,2048,512]{2,1,0:T(8,128)(2,1)}, u32[]{:S(2)}) copy-start(bf16[4,2048,512]{2,1,0:T(8,128)(2,1)} %w_gate.3) | copy-start | bytes 25165828
  2.9 9.8 %slice-start.1 = ((s8[8388608]{0:T(1024)(128)(4,1)}), s8[4194304]{0:T(1024)(128)(4,1)S(1)}, s32[]{:S(2)}) async-start(s8[8388608]{0:T(1024)(128)(4,1)} %bitcast.2), calls=%async_computation.1 | async-start | bytes 8388608
  3.0 9.8 %slice-start.3 = ((s8[8388608]{0:T(1024)(128)(4,1)}), s8[4194304]{0:T(1024)(128)(4,1)S(1)}, s32[]{:S(2)}) async-start(s8[8388608]{0:T(1024)(128)(4,1)} %bitcast.4), calls=%async_computation.3 | async-start | bytes 8388608
  4.3 1.6 %collective-permute-start.2 = (bf16[16,8320]{1,0:T(8,128)(2,1)S(1)}, bf16[16,8320]{1,0:T(8,128)(2,1)S(1)}, u32[]{:S(2)}, u32[]{:S(2)}) collective-permute-start(bf16[16,8320]{1,0:T(8,128)(2,1)S(1)} %get-tuple-element.42.refs_0_.low), channel_id=1, source_target_pairs={{0,1},{1,0},{2,3},{3,2},{4,5},{5,4},{6,7},{7,6},{8,9},{9,8},{10,11... | collective-permute-start | bytes 798728 | tf_op jit(solution)/shard_map/ppermute | solution.py:26
  4.4 1.9 %collective-permute-start.3 = (bf16[16,8320]{1,0:T(8,128)(2,1)S(1)}, bf16[16,8320]{1,0:T(8,128)(2,1)S(1)}, u32[]{:S(2)}, u32[]{:S(2)}) collective-permute-start(bf16[16,8320]{1,0:T(8,128)(2,1)S(1)} %get-tuple-element.43.refs_1_.high), channel_id=1, source_target_pairs={{0,1},{1,0},{2,3},{3,2},{4,5},{5,4},{6,7},{7,6},{8,9},{9,8},{10,11... | collective-permute-start | bytes 798728 | tf_op jit(solution)/shard_map/ppermute | solution.py:26
  4.9 5.5 %collective-permute-start = (bf16[16,256]{1,0:T(8,128)(2,1)S(1)}, bf16[16,256]{1,0:T(8,128)(2,1)S(1)}, u32[]{:S(2)}, u32[]{:S(2)}) collective-permute-start(bf16[16,256]{1,0:T(8,128)(2,1)S(1)} %get-tuple-element.41.table), channel_id=1, source_target_pairs={{0,2},{1,5},{2,0},{3,7},{4,6},{5,1},{6,4},{7,3},{8,10},{9,13},{10,... | collective-permute-start | bytes 24584 | tf_op jit(solution)/shard_map/ppermute | solution.py:31
  10.4 4.8 %collective-permute-start.7 = (bf16[16,16640]{1,0:T(8,128)(2,1)S(1)}, bf16[16,16640]{1,0:T(8,128)(2,1)S(1)}, u32[]{:S(2)}, u32[]{:S(2)}) collective-permute-start(bf16[16,16640]{1,0:T(8,128)(2,1)S(1)} %pack.1.refs_0_), channel_id=1, source_target_pairs={{0,1},{1,0},{2,3},{3,2},{4,5},{5,4},{6,7},{7,6},{8,9},{9,8},{10,11... | collective-permute-start | bytes 1597448 | tf_op jit(solution)/shard_map/ppermute | solution.py:26
  10.5 9.4 %collective-permute-start.6 = (bf16[16,16640]{1,0:T(8,128)(2,1)S(1)}, bf16[16,16640]{1,0:T(8,128)(2,1)S(1)}, u32[]{:S(2)}, u32[]{:S(2)}) collective-permute-start(bf16[16,16640]{1,0:T(8,128)(2,1)S(1)} %pack.1.refs_0_), channel_id=1, source_target_pairs={{0,4},{1,3},{2,6},{3,1},{4,0},{5,7},{6,2},{7,5},{8,12},{9,11},{10,... | collective-permute-start | bytes 1597448 | tf_op jit(solution)/shard_map/ppermute | solution.py:31
  12.7 14.9 %collective-permute-start.9 = (bf16[16,16768]{1,0:T(8,128)(2,1)S(1)}, bf16[16,16768]{1,0:T(8,128)(2,1)S(1)}, u32[]{:S(2)}, u32[]{:S(2)}) collective-permute-start(bf16[16,16768]{1,0:T(8,128)(2,1)S(1)} %join.1), channel_id=1, source_target_pairs={{0,4},{1,3},{2,6},{3,1},{4,0},{5,7},{6,2},{7,5},{8,12},{9,11},{10,... | collective-permute-start | bytes 1609736 | tf_op jit(solution)/shard_map/ppermute | solution.py:31
  19.9 3.0 %collective-permute-start.8 = (bf16[16,16640]{1,0:T(8,128)(2,1)S(1)}, bf16[16,16640]{1,0:T(8,128)(2,1)S(1)}, u32[]{:S(2)}, u32[]{:S(2)}) collective-permute-start(bf16[16,16640]{1,0:T(8,128)(2,1)S(1)} %collective-permute-done.6.refs_0_), channel_id=1, source_target_pairs={{0,1},{1,0},{2,3},{3,2},{4,5},{5,4},{6,7},{7,6},{8,9},{9,8},{10,11... | collective-permute-start | bytes 1597448 | tf_op jit(solution)/shard_map/ppermute | solution.py:26
  20.0 5.4 %collective-permute-start.12 = (bf16[128,2048]{1,0:T(8,128)(2,1)S(1)}, bf16[128,2048]{1,0:T(8,128)(2,1)S(1)}, u32[]{:S(2)}, u32[]{:S(2)}) collective-permute-start(bf16[128,2048]{1,0:T(8,128)(2,1)S(1)} %get-tuple-element.70), channel_id=1, source_target_pairs={{0,1},{1,0},{2,3},{3,2},{4,5},{5,4},{6,7},{7,6},{8,9},{9,8},{10,11... | collective-permute-start | bytes 1572872 | tf_op jit(solution)/shard_map/ppermute | solution.py:26
  25.6 11.6 %collective-permute-start.13 = (bf16[128,2176]{1,0:T(8,128)(2,1)S(1)}, bf16[128,2176]{1,0:T(8,128)(2,1)S(1)}, u32[]{:S(2)}, u32[]{:S(2)}) collective-permute-start(bf16[128,2176]{1,0:T(8,128)(2,1)S(1)} %add.3), channel_id=1, source_target_pairs={{0,2},{1,5},{2,0},{3,7},{4,6},{5,1},{6,4},{7,3},{8,10},{9,13},{10,... | collective-permute-start | bytes 1671176 | tf_op jit(solution)/shard_map/ppermute | solution.py:31
  27.6 4.6 %collective-permute-start.11 = (bf16[16,16768]{1,0:T(8,128)(2,1)S(1)}, bf16[16,16768]{1,0:T(8,128)(2,1)S(1)}, u32[]{:S(2)}, u32[]{:S(2)}) collective-permute-start(bf16[16,16768]{1,0:T(8,128)(2,1)S(1)} %collective-permute-done.9.refs_0_), channel_id=1, source_target_pairs={{0,1},{1,0},{2,3},{3,2},{4,5},{5,4},{6,7},{7,6},{8,9},{9,8},{10,11... | collective-permute-start | bytes 1609736 | tf_op jit(solution)/shard_map/ppermute | solution.py:26
  30.0 2.1 %collective-permute-start.10 = (bf16[128,2048]{1,0:T(8,128)(2,1)S(1)}, bf16[128,2048]{1,0:T(8,128)(2,1)S(1)}, u32[]{:S(2)}, u32[]{:S(2)}) collective-permute-start(bf16[128,2048]{1,0:T(8,128)(2,1)S(1)} %get-tuple-element.63), channel_id=1, source_target_pairs={{0,1},{1,0},{2,3},{3,2},{4,5},{5,4},{6,7},{7,6},{8,9},{9,8},{10,11... | collective-permute-start | bytes 1572872 | tf_op jit(solution)/shard_map/ppermute | solution.py:26
  32.2 9.2 %collective-permute-start.14 = (bf16[128,2048]{1,0:T(8,128)(2,1)S(1)}, bf16[128,2048]{1,0:T(8,128)(2,1)S(1)}, u32[]{:S(2)}, u32[]{:S(2)}) collective-permute-start(bf16[128,2048]{1,0:T(8,128)(2,1)S(1)} %add_pieces.1), channel_id=1, source_target_pairs={{0,2},{1,5},{2,0},{3,7},{4,6},{5,1},{6,4},{7,3},{8,10},{9,13},{10,... | collective-permute-start | bytes 1572872 | tf_op jit(solution)/shard_map/ppermute | solution.py:31
  39.6 2.1 %collective-permute-start.15 = (bf16[128,2048]{1,0:T(8,128)(2,1)S(1)}, bf16[128,2048]{1,0:T(8,128)(2,1)S(1)}, u32[]{:S(2)}, u32[]{:S(2)}) collective-permute-start(bf16[128,2048]{1,0:T(8,128)(2,1)S(1)} %get-tuple-element.76), channel_id=1, source_target_pairs={{0,1},{1,0},{2,3},{3,2},{4,5},{5,4},{6,7},{7,6},{8,9},{9,8},{10,11... | collective-permute-start | bytes 1572872 | tf_op jit(solution)/shard_map/ppermute | solution.py:26
  41.7 9.2 %collective-permute-start.16 = (bf16[128,2048]{1,0:T(8,128)(2,1)S(1)}, bf16[128,2048]{1,0:T(8,128)(2,1)S(1)}, u32[]{:S(2)}, u32[]{:S(2)}) collective-permute-start(bf16[128,2048]{1,0:T(8,128)(2,1)S(1)} %add.5), channel_id=1, source_target_pairs={{0,4},{1,3},{2,6},{3,1},{4,0},{5,7},{6,2},{7,5},{8,12},{9,11},{10,... | collective-permute-start | bytes 1572872 | tf_op jit(solution)/shard_map/ppermute | solution.py:31
  48.0 1.6 %collective-permute-start.4 = (bf16[64,2048]{1,0:T(8,128)(2,1)S(1)}, bf16[64,2048]{1,0:T(8,128)(2,1)S(1)}, u32[]{:S(2)}, u32[]{:S(2)}) collective-permute-start(bf16[64,2048]{1,0:T(8,128)(2,1)S(1)} %get-tuple-element.47), channel_id=1, source_target_pairs={{0,1},{1,0},{2,3},{3,2},{4,5},{5,4},{6,7},{7,6},{8,9},{9,8},{10,11... | collective-permute-start | bytes 786440 | tf_op jit(solution)/shard_map/ppermute | solution.py:26
  48.1 1.9 %collective-permute-start.5 = (bf16[64,2048]{1,0:T(8,128)(2,1)S(1)}, bf16[64,2048]{1,0:T(8,128)(2,1)S(1)}, u32[]{:S(2)}, u32[]{:S(2)}) collective-permute-start(bf16[64,2048]{1,0:T(8,128)(2,1)S(1)} %get-tuple-element.48), channel_id=1, source_target_pairs={{0,1},{1,0},{2,3},{3,2},{4,5},{5,4},{6,7},{7,6},{8,9},{9,8},{10,11... | collective-permute-start | bytes 786440 | tf_op jit(solution)/shard_map/ppermute | solution.py:26

commit v11 on v10

--- a/solution.py
+++ b/solution.py
@@ -436,12 +436,13 @@
     weights = (w_gate, w_up, w_down)
     near_rows, near_table = cross(tokens, x, y), cross(table, x, y)
     gated, rows = gated_units([low, high, flip(low, CORE), flip(high, CORE)], w_gate)
-    near_table, near_rows, gated = barrier((near_table, near_rows, gated))
+    wide = join(low, high, table, tokens.shape[1], SPARE)
+    near_table, near_rows, gated, wide = barrier((near_table, near_rows, gated, wide))
     near = pack(near_rows, near_table)
 
     far = cross(near, y, x)
     mine_near, other_near = rest_of(units_of([near], *weights), flip(near, CORE), *weights)
-    following = cross(join(low, high, table, tokens.shape[1], SPARE), y, x)
+    following = cross(wide, y, x)
     far, mine_near = barrier((far, mine_near))
 
     far_twin = flip(far, CORE)

time: 52.2 us -> 52.2 us (level)
  transfers between devices with their start and end apart: 17 -> 17, of which waited for: 9 -> 10; matrix products, arithmetic and copies ran while one was open for 0% -> 0% of each run, Pallas kernels for 59% -> 59%
where the time goes in v11:
time: 52.2 us; the launch traced here: 52.1 us
  Pallas kernels  32 us (61%)
  starting transfers between devices  13.4 us (26%)
  waiting for transfers between devices  5.79 us (11%)
    ppermute x7, starting transfers between devices, cross(): lax.ppermute(x, 'ep', [(i, i ^ (odd if i % 2 else even)) for i in range(n)])  10.5 us
    pallas_call x3, Pallas kernels, units_of(): pl.pallas_call(functools.partial(units_kernel, parts=len(parts)), in_spec...  7.38 us
    pallas_call x2, Pallas kernels, sums_of(): pl.pallas_call(sums_kernel, in_specs=[VMEM_SPEC] * 3, out_specs=[VMEM_SPE...  4.72 us
    pallas_call x1, Pallas kernels, rest_of(): pl.pallas_call(rest_kernel, in_specs=[VMEM_SPEC] * 5, out_specs=[VMEM_SPE...  4.62 us
    pallas_call x2, Pallas kernels, gated_units(): pl.pallas_call(functools.partial(gated_kernel, parts=len(parts)), in_spec...  4.08 us
    pallas_call x1, Pallas kernels, both_units(): pl.pallas_call(both_kernel, in_specs=[VMEM_SPEC] * 5, out_specs=[VMEM_SPE...  3.74 us
    ppermute x7, waiting for transfers between devices, cross(): lax.ppermute(x, 'ep', [(i, i ^ (odd if i % 2 else even)) for i in range(n)])  3.52 us
    ppermute x10, starting transfers between devices, flip(): return lax.ppermute(x, 'ep', [(i, i ^ mask) for i in range(n)])  2.87 us
  transfers between devices with their start and end apart: 17, of which 10 were waited for; matrix products, arithmetic and copies ran while one was open for 0% of the time, Pallas kernels for 59%

profile of v11, /device:TPU:0, one launch (start us, length us, event | category | flops | bytes accessed | tf_op | source)
XLA Modules:
  0.0 52.1 jit_solution(15305641317642818579)
XLA Ops:
  0.0 2.9 %collective-permute-start.1 = (bf16[128,2048]{1,0:T(8,128)(2,1)}, bf16[128,2048]{1,0:T(8,128)(2,1)S(1)}, u32[]{:S(2)}, u32[]{:S(2)}) collective-permute-start(bf16[128,2048]{1,0:T(8,128)(2,1)} %tokens.1), channel_id=1, source_target_pairs={{0,2},{1,5},{2,0},{3,7},{4,6},{5,1},{6,4},{7,3},{8,10},{9,13},{10,... | collective-permute-start | bytes 1572872 | tf_op jit(solution)/shard_map/ppermute | solution.py:31
  3.0 1.3 %prepare.1 = (bf16[16,8320]{1,0:T(8,128)(2,1)S(1)}, bf16[16,8320]{1,0:T(8,128)(2,1)S(1)}, bf16[16,256]{1,0:T(8,128)(2,1)S(1)}) custom-call(bf16[128,2048]{1,0:T(8,128)(2,1)} %tokens.1, s32[10,128]{1,0:T(8,128)} %bitcast.6, bf16[10,128]{1,0:T(8,128)(2,1)} %bitcast.7), custom_call_target="tpu_custom_call" | custom-call | flops 99999997952 | bytes 100000000 | tf_op jit(solution)/shard_map/prepare/pallas_call | solution.py:87
  4.9 0.6 %collective-permute-start = (bf16[16,256]{1,0:T(8,128)(2,1)S(1)}, bf16[16,256]{1,0:T(8,128)(2,1)S(1)}, u32[]{:S(2)}, u32[]{:S(2)}) collective-permute-start(bf16[16,256]{1,0:T(8,128)(2,1)S(1)} %get-tuple-element.42.table), channel_id=1, source_target_pairs={{0,2},{1,5},{2,0},{3,7},{4,6},{5,1},{6,4},{7,3},{8,10},{9,13},{10,... | collective-permute-start | bytes 24584 | tf_op jit(solution)/shard_map/ppermute | solution.py:31
  6.8 2.6 %gated_units.2 = (f32[256,2048]{1,0:T(8,128)S(1)}, bf16[256,2048]{1,0:T(8,128)(2,1)S(1)}) custom-call(bf16[16,8320]{1,0:T(8,128)(2,1)S(1)} %get-tuple-element.43.refs_0_.low, bf16[16,8320]{1,0:T(8,128)(2,1)S(1)} %get-tuple-element.44.refs_1_.high, bf16[16,8320]{1,0:T(8,128)(2,1)S(1)} %collective-permute-done.2.refs_2_, ...), custom_call_target="tpu_custom_call" | custom-call | tf_op jit(solution)/shard_map/gated_units/pallas_call | solution.py:209
  9.4 1.0 %collective-permute-done.table = bf16[16,256]{1,0:T(8,128)(2,1)S(1)} collective-permute-done((bf16[16,256]{1,0:T(8,128)(2,1)S(1)}, bf16[16,256]{1,0:T(8,128)(2,1)S(1)}, u32[]{:S(2)}, u32[]{:S(2)}) %collective-permute-start) | collective-permute-done | bytes 8224 | tf_op jit(solution)/shard_map/ppermute | solution.py:31
  10.5 2.1 %collective-permute-start.6 = (bf16[16,16640]{1,0:T(8,128)(2,1)S(1)}, bf16[16,16640]{1,0:T(8,128)(2,1)S(1)}, u32[]{:S(2)}, u32[]{:S(2)}) collective-permute-start(bf16[16,16640]{1,0:T(8,128)(2,1)S(1)} %pack.1.refs_0_), channel_id=1, source_target_pairs={{0,4},{1,3},{2,6},{3,1},{4,0},{5,7},{6,2},{7,5},{8,12},{9,11},{10,... | collective-permute-start | bytes 1597448 | tf_op jit(solution)/shard_map/ppermute | solution.py:31
  12.7 2.4 %units_of.3.first = bf16[128,2048]{1,0:T(8,128)(2,1)S(1)} custom-call(bf16[16,16640]{1,0:T(8,128)(2,1)S(1)} %pack.1.refs_0_, bf16[4,2048,512]{2,1,0:T(8,128)(2,1)S(1)} %copy-done, bf16[4,2048,512]{2,1,0:T(8,128)(2,1)S(1)} %bitcast.3, bf16[4,2048,512]{2,1,0:T(8,128)(2,1)S(1)} %bitcast.5), custom_call_target="tpu_custom_call" | custom-call | tf_op jit(solution)/shard_map/units_of/pallas_call | solution.py:251
  15.2 4.6 %rest_of.1 = (bf16[128,2048]{1,0:T(8,128)(2,1)S(1)}, bf16[128,2048]{1,0:T(8,128)(2,1)S(1)}) custom-call(bf16[128,2048]{1,0:T(8,128)(2,1)S(1)} %units_of.3.first, bf16[16,16640]{1,0:T(8,128)(2,1)S(1)} %collective-permute-done.7.part, bf16[4,2048,512]{2,1,0:T(8,128)(2,1)S(1)} %copy-done, bf16[4,2048,512]{2,1,0:T(8,128)(2,1)S(1)} %bitcast.3, ...), custom_call_target="tpu_custom_call" | custom-call | tf_op jit(solution)/shard_map/rest_of/pallas_call | solution.py:301
  20.4 2.4 %units_of.4.first = bf16[128,2048]{1,0:T(8,128)(2,1)S(1)} custom-call(bf16[16,16640]{1,0:T(8,128)(2,1)S(1)} %collective-permute-done.6.refs_0_, bf16[4,2048,512]{2,1,0:T(8,128)(2,1)S(1)} %copy-done, bf16[4,2048,512]{2,1,0:T(8,128)(2,1)S(1)} %bitcast.3), custom_call_target="tpu_custom_call" | custom-call | tf_op jit(solution)/shard_map/units_of/pallas_call | solution.py:251
  22.8 2.6 %units_of.5.second = bf16[128,2048]{1,0:T(8,128)(2,1)S(1)} custom-call(bf16[16,16640]{1,0:T(8,128)(2,1)S(1)} %collective-permute-done.8.refs_0_, bf16[4,2048,512]{2,1,0:T(8,128)(2,1)S(1)} %copy-done, bf16[4,2048,512]{2,1,0:T(8,128)(2,1)S(1)} %bitcast.3), custom_call_target="tpu_custom_call" | custom-call | tf_op jit(solution)/shard_map/units_of/pallas_call | solution.py:251
  25.6 2.1 %collective-permute-start.13 = (bf16[128,2176]{1,0:T(8,128)(2,1)S(1)}, bf16[128,2176]{1,0:T(8,128)(2,1)S(1)}, u32[]{:S(2)}, u32[]{:S(2)}) collective-permute-start(bf16[128,2176]{1,0:T(8,128)(2,1)S(1)} %add.3), channel_id=1, source_target_pairs={{0,2},{1,5},{2,0},{3,7},{4,6},{5,1},{6,4},{7,3},{8,10},{9,13},{10,... | collective-permute-start | bytes 1671176 | tf_op jit(solution)/shard_map/ppermute | solution.py:31
  27.6 2.4 %sums_of.2 = (bf16[128,2048]{1,0:T(8,128)(2,1)S(1)}, bf16[128,2048]{1,0:T(8,128)(2,1)S(1)}) custom-call(bf16[128,2048]{1,0:T(8,128)(2,1)S(1)} %units_of.4.first, bf16[128,2048]{1,0:T(8,128)(2,1)S(1)} %units_of.5.second, bf16[4,2048,512]{2,1,0:T(8,128)(2,1)S(1)} %bitcast.5), custom_call_target="tpu_custom_call" | custom-call | tf_op jit(solution)/shard_map/sums_of/pallas_call | solution.py:327
  30.6 1.5 %gated_units.3 = (f32[128,2048]{1,0:T(8,128)S(1)}, bf16[128,2048]{1,0:T(8,128)(2,1)S(1)}) custom-call(bf16[16,16768]{1,0:T(8,128)(2,1)S(1)} %collective-permute-done.9.refs_0_, bf16[4,2048,512]{2,1,0:T(8,128)(2,1)S(1)} %copy-done), custom_call_target="tpu_custom_call" | custom-call | tf_op jit(solution)/shard_map/gated_units/pallas_call | solution.py:209
  32.2 1.2 %collective-permute-start.14 = (bf16[128,2048]{1,0:T(8,128)(2,1)S(1)}, bf16[128,2048]{1,0:T(8,128)(2,1)S(1)}, u32[]{:S(2)}, u32[]{:S(2)}) collective-permute-start(bf16[128,2048]{1,0:T(8,128)(2,1)S(1)} %add_pieces.1), channel_id=1, source_target_pairs={{0,2},{1,5},{2,0},{3,7},{4,6},{5,1},{6,4},{7,3},{8,10},{9,13},{10,... | collective-permute-start | bytes 1572872 | tf_op jit(solution)/shard_map/ppermute | solution.py:31
  33.4 3.7 %both_units.1 = (bf16[128,2048]{1,0:T(8,128)(2,1)S(1)}, bf16[128,2048]{1,0:T(8,128)(2,1)S(1)}) custom-call(f32[128,2048]{1,0:T(8,128)S(1)} %get-tuple-element.67.gated, bf16[128,2048]{1,0:T(8,128)(2,1)S(1)} %get-tuple-element.68.gated_rows, bf16[16,16768]{1,0:T(8,128)(2,1)S(1)} %collective-permute-done.11.part, bf16[4,2048,512]{2,1,0:T(8,128)(2,1)S(1)} %copy-done, ...), custom_call_target="tpu_custom_call" | custom-call | tf_op jit(solution)/shard_map/both_units/pallas_call | solution.py:275
  37.2 2.4 %sums_of.3 = (bf16[128,2048]{1,0:T(8,128)(2,1)S(1)}, bf16[128,2048]{1,0:T(8,128)(2,1)S(1)}) custom-call(bf16[128,2048]{1,0:T(8,128)(2,1)S(1)} %get-tuple-element.74.first, bf16[128,2048]{1,0:T(8,128)(2,1)S(1)} %get-tuple-element.75.second, bf16[4,2048,512]{2,1,0:T(8,128)(2,1)S(1)} %bitcast.5), custom_call_target="tpu_custom_call" | custom-call | tf_op jit(solution)/shard_map/sums_of/pallas_call | solution.py:327
  39.5 0.6 %collective-permute-start.15 = (bf16[128,2048]{1,0:T(8,128)(2,1)S(1)}, bf16[128,2048]{1,0:T(8,128)(2,1)S(1)}, u32[]{:S(2)}, u32[]{:S(2)}) collective-permute-start(bf16[128,2048]{1,0:T(8,128)(2,1)S(1)} %get-tuple-element.78), channel_id=1, source_target_pairs={{0,1},{1,0},{2,3},{3,2},{4,5},{5,4},{6,7},{7,6},{8,9},{9,8},{10,11... | collective-permute-start | bytes 1572872 | tf_op jit(solution)/shard_map/ppermute | solution.py:26
  40.1 1.4 %collective-permute-done.14.refs_1_ = bf16[128,2048]{1,0:T(8,128)(2,1)S(1)} collective-permute-done((bf16[128,2048]{1,0:T(8,128)(2,1)S(1)}, bf16[128,2048]{1,0:T(8,128)(2,1)S(1)}, u32[]{:S(2)}, u32[]{:S(2)}) %collective-permute-start.14) | collective-permute-done | bytes 524320 | tf_op jit(solution)/shard_map/ppermute | solution.py:31
  41.7 1.5 %collective-permute-start.16 = (bf16[128,2048]{1,0:T(8,128)(2,1)S(1)}, bf16[128,2048]{1,0:T(8,128)(2,1)S(1)}, u32[]{:S(2)}, u32[]{:S(2)}) collective-permute-start(bf16[128,2048]{1,0:T(8,128)(2,1)S(1)} %add.5), channel_id=1, source_target_pairs={{0,4},{1,3},{2,6},{3,1},{4,0},{5,7},{6,2},{7,5},{8,12},{9,11},{10,... | collective-permute-start | bytes 1572872 | tf_op jit(solution)/shard_map/ppermute | solution.py:31
  43.3 2.3 %hidden_units.1.hidden = bf16[256,2048]{1,0:T(8,128)(2,1)S(1)} custom-call(f32[256,2048]{1,0:T(8,128)S(1)} %get-tuple-element.46.gated, bf16[256,2048]{1,0:T(8,128)(2,1)S(1)} %get-tuple-element.47.rows, bf16[4,2048,512]{2,1,0:T(8,128)(2,1)S(1)} %bitcast.3), custom_call_target="tpu_custom_call" | custom-call | tf_op jit(solution)/shard_map/hidden_units/pallas_call | solution.py:229
  45.6 2.4 %down_units.1 = (bf16[128,2048]{1,0:T(8,128)(2,1)S(1)}, bf16[64,2048]{1,0:T(8,128)(2,1)S(1)}, bf16[64,2048]{1,0:T(8,128)(2,1)S(1)}) custom-call(bf16[256,2048]{1,0:T(8,128)(2,1)S(1)} %hidden_units.1.hidden, bf16[4,2048,512]{2,1,0:T(8,128)(2,1)S(1)} %bitcast.5), custom_call_target="tpu_custom_call" | custom-call | tf_op jit(solution)/shard_map/down_units/pallas_call | solution.py:362
  48.6 1.0 %collective-permute-done.4.refs_0_ = bf16[64,2048]{1,0:T(8,128)(2,1)S(1)} collective-permute-done((bf16[64,2048]{1,0:T(8,128)(2,1)S(1)}, bf16[64,2048]{1,0:T(8,128)(2,1)S(1)}, u32[]{:S(2)}, u32[]{:S(2)}) %collective-permute-start.4) | collective-permute-done | bytes 262176 | tf_op jit(solution)/shard_map/ppermute | solution.py:26
  50.0 1.0 %collective-permute-done.16.refs_4_ = bf16[128,2048]{1,0:T(8,128)(2,1)S(1)} collective-permute-done((bf16[128,2048]{1,0:T(8,128)(2,1)S(1)}, bf16[128,2048]{1,0:T(8,128)(2,1)S(1)}, u32[]{:S(2)}, u32[]{:S(2)}) %collective-permute-start.16) | collective-permute-done | bytes 524320 | tf_op jit(solution)/shard_map/ppermute | solution.py:31
  51.0 1.0 %finish.1 = bf16[128,2048]{1,0:T(8,128)(2,1)} custom-call(bf16[64,2048]{1,0:T(8,128)(2,1)S(1)} %collective-permute-done.4.refs_0_, bf16[64,2048]{1,0:T(8,128)(2,1)S(1)} %collective-permute-done.5.refs_1_, bf16[128,2048]{1,0:T(8,128)(2,1)S(1)} %get-tuple-element.50.refs_2_, bf16[128,2176]{1,0:T(8,128)(2,1)S(1)} %collective-permute-done.13.refs_3_, ...), custom_call_target="tpu_custom_call" | custom-call | tf_op jit(solution)/shard_map/finish/pallas_call | solution.py:418
  (41 shorter events, 4.7 us)
Async XLA Ops:
  0.0 10.4 %collective-permute-start.1 = (bf16[128,2048]{1,0:T(8,128)(2,1)}, bf16[128,2048]{1,0:T(8,128)(2,1)S(1)}, u32[]{:S(2)}, u32[]{:S(2)}) collective-permute-start(bf16[128,2048]{1,0:T(8,128)(2,1)} %tokens.1), channel_id=1, source_target_pairs={{0,2},{1,5},{2,0},{3,7},{4,6},{5,1},{6,4},{7,3},{8,10},{9,13},{10,... | collective-permute-start | bytes 1572872 | tf_op jit(solution)/shard_map/ppermute | solution.py:31
  2.9 9.8 %slice-start = ((s8[8388608]{0:T(1024)(128)(4,1)}), s8[4194304]{0:T(1024)(128)(4,1)S(1)}, s32[]{:S(2)}) async-start(s8[8388608]{0:T(1024)(128)(4,1)} %bitcast.2), calls=%async_computation | async-start | bytes 8388608
  2.9 9.8 %slice-start.2 = ((s8[8388608]{0:T(1024)(128)(4,1)}), s8[4194304]{0:T(1024)(128)(4,1)S(1)}, s32[]{:S(2)}) async-start(s8[8388608]{0:T(1024)(128)(4,1)} %bitcast.4), calls=%async_computation.2 | async-start | bytes 8388608
  2.9 3.8 %copy-start = (bf16[4,2048,512]{2,1,0:T(8,128)(2,1)S(1)}, bf16[4,2048,512]{2,1,0:T(8,128)(2,1)}, u32[]{:S(2)}) copy-start(bf16[4,2048,512]{2,1,0:T(8,128)(2,1)} %w_gate.3) | copy-start | bytes 25165828
  2.9 9.8 %slice-start.1 = ((s8[8388608]{0:T(1024)(128)(4,1)}), s8[4194304]{0:T(1024)(128)(4,1)S(1)}, s32[]{:S(2)}) async-start(s8[8388608]{0:T(1024)(128)(4,1)} %bitcast.2), calls=%async_computation.1 | async-start | bytes 8388608
  3.0 9.8 %slice-start.3 = ((s8[8388608]{0:T(1024)(128)(4,1)}), s8[4194304]{0:T(1024)(128)(4,1)S(1)}, s32[]{:S(2)}) async-start(s8[8388608]{0:T(1024)(128)(4,1)} %bitcast.4), calls=%async_computation.3 | async-start | bytes 8388608
  4.3 1.6 %collective-permute-start.2 = (bf16[16,8320]{1,0:T(8,128)(2,1)S(1)}, bf16[16,8320]{1,0:T(8,128)(2,1)S(1)}, u32[]{:S(2)}, u32[]{:S(2)}) collective-permute-start(bf16[16,8320]{1,0:T(8,128)(2,1)S(1)} %get-tuple-element.43.refs_0_.low), channel_id=1, source_target_pairs={{0,1},{1,0},{2,3},{3,2},{4,5},{5,4},{6,7},{7,6},{8,9},{9,8},{10,11... | collective-permute-start | bytes 798728 | tf_op jit(solution)/shard_map/ppermute | solution.py:26
  4.4 1.9 %collective-permute-start.3 = (bf16[16,8320]{1,0:T(8,128)(2,1)S(1)}, bf16[16,8320]{1,0:T(8,128)(2,1)S(1)}, u32[]{:S(2)}, u32[]{:S(2)}) collective-permute-start(bf16[16,8320]{1,0:T(8,128)(2,1)S(1)} %get-tuple-element.44.refs_1_.high), channel_id=1, source_target_pairs={{0,1},{1,0},{2,3},{3,2},{4,5},{5,4},{6,7},{7,6},{8,9},{9,8},{10,11... | collective-permute-start | bytes 798728 | tf_op jit(solution)/shard_map/ppermute | solution.py:26
  4.9 5.5 %collective-permute-start = (bf16[16,256]{1,0:T(8,128)(2,1)S(1)}, bf16[16,256]{1,0:T(8,128)(2,1)S(1)}, u32[]{:S(2)}, u32[]{:S(2)}) collective-permute-start(bf16[16,256]{1,0:T(8,128)(2,1)S(1)} %get-tuple-element.42.table), channel_id=1, source_target_pairs={{0,2},{1,5},{2,0},{3,7},{4,6},{5,1},{6,4},{7,3},{8,10},{9,13},{10,... | collective-permute-start | bytes 24584 | tf_op jit(solution)/shard_map/ppermute | solution.py:31
  10.4 4.7 %collective-permute-start.7 = (bf16[16,16640]{1,0:T(8,128)(2,1)S(1)}, bf16[16,16640]{1,0:T(8,128)(2,1)S(1)}, u32[]{:S(2)}, u32[]{:S(2)}) collective-permute-start(bf16[16,16640]{1,0:T(8,128)(2,1)S(1)} %pack.1.refs_0_), channel_id=1, source_target_pairs={{0,1},{1,0},{2,3},{3,2},{4,5},{5,4},{6,7},{7,6},{8,9},{9,8},{10,11... | collective-permute-start | bytes 1597448 | tf_op jit(solution)/shard_map/ppermute | solution.py:26
  10.5 9.4 %collective-permute-start.6 = (bf16[16,16640]{1,0:T(8,128)(2,1)S(1)}, bf16[16,16640]{1,0:T(8,128)(2,1)S(1)}, u32[]{:S(2)}, u32[]{:S(2)}) collective-permute-start(bf16[16,16640]{1,0:T(8,128)(2,1)S(1)} %pack.1.refs_0_), channel_id=1, source_target_pairs={{0,4},{1,3},{2,6},{3,1},{4,0},{5,7},{6,2},{7,5},{8,12},{9,11},{10,... | collective-permute-start | bytes 1597448 | tf_op jit(solution)/shard_map/ppermute | solution.py:31
  12.6 15.0 %collective-permute-start.9 = (bf16[16,16768]{1,0:T(8,128)(2,1)S(1)}, bf16[16,16768]{1,0:T(8,128)(2,1)S(1)}, u32[]{:S(2)}, u32[]{:S(2)}) collective-permute-start(bf16[16,16768]{1,0:T(8,128)(2,1)S(1)} %join.1), channel_id=1, source_target_pairs={{0,4},{1,3},{2,6},{3,1},{4,0},{5,7},{6,2},{7,5},{8,12},{9,11},{10,... | collective-permute-start | bytes 1609736 | tf_op jit(solution)/shard_map/ppermute | solution.py:31
  19.9 2.9 %collective-permute-start.8 = (bf16[16,16640]{1,0:T(8,128)(2,1)S(1)}, bf16[16,16640]{1,0:T(8,128)(2,1)S(1)}, u32[]{:S(2)}, u32[]{:S(2)}) collective-permute-start(bf16[16,16640]{1,0:T(8,128)(2,1)S(1)} %collective-permute-done.6.refs_0_), channel_id=1, source_target_pairs={{0,1},{1,0},{2,3},{3,2},{4,5},{5,4},{6,7},{7,6},{8,9},{9,8},{10,11... | collective-permute-start | bytes 1597448 | tf_op jit(solution)/shard_map/ppermute | solution.py:26
  19.9 5.5 %collective-permute-start.12 = (bf16[128,2048]{1,0:T(8,128)(2,1)S(1)}, bf16[128,2048]{1,0:T(8,128)(2,1)S(1)}, u32[]{:S(2)}, u32[]{:S(2)}) collective-permute-start(bf16[128,2048]{1,0:T(8,128)(2,1)S(1)} %get-tuple-element.72), channel_id=1, source_target_pairs={{0,1},{1,0},{2,3},{3,2},{4,5},{5,4},{6,7},{7,6},{8,9},{9,8},{10,11... | collective-permute-start | bytes 1572872 | tf_op jit(solution)/shard_map/ppermute | solution.py:26
  25.6 11.6 %collective-permute-start.13 = (bf16[128,2176]{1,0:T(8,128)(2,1)S(1)}, bf16[128,2176]{1,0:T(8,128)(2,1)S(1)}, u32[]{:S(2)}, u32[]{:S(2)}) collective-permute-start(bf16[128,2176]{1,0:T(8,128)(2,1)S(1)} %add.3), channel_id=1, source_target_pairs={{0,2},{1,5},{2,0},{3,7},{4,6},{5,1},{6,4},{7,3},{8,10},{9,13},{10,... | collective-permute-start | bytes 1671176 | tf_op jit(solution)/shard_map/ppermute | solution.py:31
  27.6 4.6 %collective-permute-start.11 = (bf16[16,16768]{1,0:T(8,128)(2,1)S(1)}, bf16[16,16768]{1,0:T(8,128)(2,1)S(1)}, u32[]{:S(2)}, u32[]{:S(2)}) collective-permute-start(bf16[16,16768]{1,0:T(8,128)(2,1)S(1)} %collective-permute-done.9.refs_0_), channel_id=1, source_target_pairs={{0,1},{1,0},{2,3},{3,2},{4,5},{5,4},{6,7},{7,6},{8,9},{9,8},{10,11... | collective-permute-start | bytes 1609736 | tf_op jit(solution)/shard_map/ppermute | solution.py:26
  30.0 2.1 %collective-permute-start.10 = (bf16[128,2048]{1,0:T(8,128)(2,1)S(1)}, bf16[128,2048]{1,0:T(8,128)(2,1)S(1)}, u32[]{:S(2)}, u32[]{:S(2)}) collective-permute-start(bf16[128,2048]{1,0:T(8,128)(2,1)S(1)} %get-tuple-element.65), channel_id=1, source_target_pairs={{0,1},{1,0},{2,3},{3,2},{4,5},{5,4},{6,7},{7,6},{8,9},{9,8},{10,11... | collective-permute-start | bytes 1572872 | tf_op jit(solution)/shard_map/ppermute | solution.py:26
  32.2 9.2 %collective-permute-start.14 = (bf16[128,2048]{1,0:T(8,128)(2,1)S(1)}, bf16[128,2048]{1,0:T(8,128)(2,1)S(1)}, u32[]{:S(2)}, u32[]{:S(2)}) collective-permute-start(bf16[128,2048]{1,0:T(8,128)(2,1)S(1)} %add_pieces.1), channel_id=1, source_target_pairs={{0,2},{1,5},{2,0},{3,7},{4,6},{5,1},{6,4},{7,3},{8,10},{9,13},{10,... | collective-permute-start | bytes 1572872 | tf_op jit(solution)/shard_map/ppermute | solution.py:31
  39.5 2.1 %collective-permute-start.15 = (bf16[128,2048]{1,0:T(8,128)(2,1)S(1)}, bf16[128,2048]{1,0:T(8,128)(2,1)S(1)}, u32[]{:S(2)}, u32[]{:S(2)}) collective-permute-start(bf16[128,2048]{1,0:T(8,128)(2,1)S(1)} %get-tuple-element.78), channel_id=1, source_target_pairs={{0,1},{1,0},{2,3},{3,2},{4,5},{5,4},{6,7},{7,6},{8,9},{9,8},{10,11... | collective-permute-start | bytes 1572872 | tf_op jit(solution)/shard_map/ppermute | solution.py:26
  41.7 9.2 %collective-permute-start.16 = (bf16[128,2048]{1,0:T(8,128)(2,1)S(1)}, bf16[128,2048]{1,0:T(8,128)(2,1)S(1)}, u32[]{:S(2)}, u32[]{:S(2)}) collective-permute-start(bf16[128,2048]{1,0:T(8,128)(2,1)S(1)} %add.5), channel_id=1, source_target_pairs={{0,4},{1,3},{2,6},{3,1},{4,0},{5,7},{6,2},{7,5},{8,12},{9,11},{10,... | collective-permute-start | bytes 1572872 | tf_op jit(solution)/shard_map/ppermute | solution.py:31
  48.0 1.6 %collective-permute-start.4 = (bf16[64,2048]{1,0:T(8,128)(2,1)S(1)}, bf16[64,2048]{1,0:T(8,128)(2,1)S(1)}, u32[]{:S(2)}, u32[]{:S(2)}) collective-permute-start(bf16[64,2048]{1,0:T(8,128)(2,1)S(1)} %get-tuple-element.48), channel_id=1, source_target_pairs={{0,1},{1,0},{2,3},{3,2},{4,5},{5,4},{6,7},{7,6},{8,9},{9,8},{10,11... | collective-permute-start | bytes 786440 | tf_op jit(solution)/shard_map/ppermute | solution.py:26
  48.1 1.9 %collective-permute-start.5 = (bf16[64,2048]{1,0:T(8,128)(2,1)S(1)}, bf16[64,2048]{1,0:T(8,128)(2,1)S(1)}, u32[]{:S(2)}, u32[]{:S(2)}) collective-permute-start(bf16[64,2048]{1,0:T(8,128)(2,1)S(1)} %get-tuple-element.49), channel_id=1, source_target_pairs={{0,1},{1,0},{2,3},{3,2},{4,5},{5,4},{6,7},{7,6},{8,9},{9,8},{10,11... | collective-permute-start | bytes 786440 | tf_op jit(solution)/shard_map/ppermute | solution.py:26
